TPU v7x, 512 devices: a whole 4x4x16 slice. The times are simulated.
512 devices in a mesh: slide: 16 (over z_lo, core), seq: 32 (over y, x, z_hi).
Axes of the slice: x: 4, y: 4, z: 16 (z_hi: 2, z_lo: 8; z = z_hi * 8 + z_lo), core: 2. Of those that a mesh axis runs over, the one named last changes fastest.
Arguments:
- ctx_in: bfloat16 [16, 6144, 1536], P('slide', 'seq'), may hold values from -6 to 6
- resid: bfloat16 [16, 6144, 1536], P('slide', 'seq'), may hold values from -6 to 6
- enc_out_w: bfloat16 [1536, 1536], P(None, 'seq'), may hold values from -0.15625 to 0.15625
- slide_proj: bfloat16 [1536, 768], P(None, 'seq'), may hold values from -0.15625 to 0.15625
- qkv_w: bfloat16 [768, 2304], P(None, 'seq'), may hold values from -0.75 to 0.75
- tissue: int32 [16, 32, 192], P('slide', 'seq'), may hold values from 0 to 191, each once within a row
- kept_count: int32 [16, 32], P('slide'), may hold values from 64 to 192, as said below
- dilation: int32 [16, 2], P('slide'), may hold values from 4 to 64, as said below
Outputs:
- slide_out: bfloat16 [16, 6144, 768], P('slide', 'seq')
Inputs may be any that keep to these rules, and one draw needn't show every extreme that they name: `kept_count`: for every slide the counts sum to 4096, and for every block b the counts of blocks 0 to b together exceed (b + 1) * 128 by 0 to 64, by 0 for the last block. `dilation`: column 0 is a local segment length from a quarter of 64 to 64; column 1 is a rate of 4, 8 or 16.
All inputs are finite; a program needn't handle non-finite values.
Results may differ from a plain program's by a relative error of at most 0.009.
Values may be sent and summed in bfloat16 or wider, within the bound.
No kernel may reach another device: no remote copies, remote signals or barrier semaphores. Data moves between devices by JAX's collectives and lax.ppermute only.
A program may use at most 64 MiB of HBM per device.

v0:
```python
import jax
import jax.numpy as jnp
from jax import lax
from jax.sharding import PartitionSpec as P

HEADS = 16
RATE_MIN = 4


NORM_EPS = 1e-06
BIG_NEGATIVE = -1e30


def with_halo(x, sides, width):
    for axis, dim in sides:
        devices, length = (lax.axis_size(axis), x.shape[dim])
        up = [(i, (i + 1) % devices) for i in range(devices - 1)]
        down = [(j, i) for i, j in up]
        last = lax.slice_in_dim(x, length - width, length, axis=dim)
        first = lax.slice_in_dim(x, 0, width, axis=dim)
        before = lax.ppermute(last, axis, up)
        after = lax.ppermute(first, axis, down)
        x = jnp.concatenate([before, x, after], axis=dim)
    return x


def norm_rows(values):
    center = values - jnp.mean(values, axis=-1, keepdims=True)
    spread = jnp.mean(center * center, axis=-1, keepdims=True)
    return center * lax.rsqrt(spread + NORM_EPS)


def pick_table(table, owners, device_parts):
    match = owners[:, None] == jnp.arange(device_parts, dtype=jnp.int32)[None, :]
    return jnp.sum(jnp.where(match, table[None, :], 0), axis=1)


def attend_slide(
    blended_output,
    start_position,
    active_count,
    every_start,
    every_count,
    segment_length,
    dilation_rate,
    sequence_length,
    device_parts,
):
    row_cap = blended_output.shape[0]
    model_width = blended_output.shape[1] // 3
    head_dim = model_width // HEADS
    half_rows = sequence_length // device_parts // 2
    score_scale = float(head_dim) ** (-0.5)
    queries = blended_output[:, :model_width]
    keys_own = blended_output[:, model_width : 2 * model_width]
    values_own = blended_output[:, 2 * model_width :]
    head_keys = keys_own[:half_rows]
    tail_keys = lax.dynamic_slice_in_dim(keys_own, active_count - half_rows, half_rows, 0)
    head_vals = values_own[:half_rows]
    tail_vals = lax.dynamic_slice_in_dim(values_own, active_count - half_rows, half_rows, 0)
    rim_pack = jnp.stack(
        [
            jnp.concatenate([head_keys, tail_keys], axis=0),
            jnp.concatenate([head_vals, tail_vals], axis=0),
        ]
    )
    widened = with_halo(rim_pack, (("seq", 1),), half_rows)
    key_rows = jnp.concatenate(
        [widened[0, :half_rows], keys_own, widened[0, 3 * half_rows :]], axis=0
    )
    value_rows = jnp.concatenate(
        [widened[1, :half_rows], values_own, widened[1, 3 * half_rows :]], axis=0
    )
    row_ids = jnp.arange(row_cap, dtype=jnp.int32)
    rim_ids = jnp.arange(half_rows, dtype=jnp.int32)
    query_pos = start_position + row_ids
    query_live = row_ids < active_count
    lower_pos = start_position - half_rows + rim_ids
    upper_pos = start_position + active_count + rim_ids
    key_pos = jnp.concatenate([lower_pos, query_pos, upper_pos])
    key_live = jnp.concatenate([lower_pos >= 0, query_live, upper_pos < sequence_length])
    allowed = (
        (query_pos // segment_length)[:, None] == (key_pos // segment_length)[None, :]
    ) & key_live[None, :]
    query3 = queries.reshape(row_cap, HEADS, head_dim)
    key3 = key_rows.reshape(-1, HEADS, head_dim)
    value3 = value_rows.reshape(-1, HEADS, head_dim)
    scores = (
        jnp.einsum("qhd,khd->qhk", query3, key3, preferred_element_type=jnp.float32) * score_scale
    )
    local_best = jnp.max(jnp.where(allowed[:, None, :], scores, BIG_NEGATIVE), axis=-1)
    weights = jnp.where(allowed[:, None, :], jnp.exp(scores - local_best[..., None]), 0.0)
    local_total = jnp.sum(weights, axis=-1)
    local_sum = jnp.einsum(
        "qhk,khd->qhd", weights.astype(jnp.bfloat16), value3, preferred_element_type=jnp.float32
    )
    place_count = row_cap // RATE_MIN
    head_numbers = jnp.arange(HEADS, dtype=jnp.int32)
    place_numbers = jnp.arange(place_count, dtype=jnp.int32)
    leading_local = jnp.mod(head_numbers - start_position, dilation_rate)
    selected_rows = leading_local[None, :] + dilation_rate * place_numbers[:, None]
    chosen_live = selected_rows < active_count
    selector = (jnp.transpose(selected_rows)[:, :, None] == row_ids[None, None, :]).astype(
        jnp.bfloat16
    )
    picked_q = jnp.einsum(
        "hpr,rhd->phd", selector, query3, preferred_element_type=jnp.float32
    ).astype(jnp.bfloat16)
    picked_k = jnp.einsum(
        "hpr,rhd->phd",
        selector,
        keys_own.reshape(row_cap, HEADS, head_dim),
        preferred_element_type=jnp.float32,
    ).astype(jnp.bfloat16)
    picked_v = jnp.einsum(
        "hpr,rhd->phd",
        selector,
        values_own.reshape(row_cap, HEADS, head_dim),
        preferred_element_type=jnp.float32,
    ).astype(jnp.bfloat16)
    picked_k = picked_k.reshape(place_count, model_width)
    picked_v = picked_v.reshape(place_count, model_width)
    best_so_far = jnp.full((place_count, HEADS), BIG_NEGATIVE, jnp.float32)
    key_block = lax.all_gather(picked_k, "seq", axis=0, tiled=True)
    value_block = lax.all_gather(picked_v, "seq", axis=0, tiled=True)
    block_rows = key_block.shape[0]
    block_ids = jnp.arange(block_rows, dtype=jnp.int32)
    owners = block_ids // place_count
    place_lookup = block_ids - owners * place_count
    holder_start = pick_table(every_start, owners, device_parts)
    owner_count = pick_table(every_count, owners, device_parts)
    local_of = (
        jnp.mod(head_numbers[None, :] - holder_start[:, None], dilation_rate)
        + dilation_rate * place_lookup[:, None]
    )
    key_ok = local_of < owner_count[:, None]
    block_keys = key_block.reshape(block_rows, HEADS, head_dim)
    block_vals = value_block.reshape(block_rows, HEADS, head_dim).astype(jnp.float32)
    scores_g = (
        jnp.einsum("ahd,bhd->ahb", picked_q, block_keys, preferred_element_type=jnp.float32)
        * score_scale
    )
    usable = chosen_live[:, :, None] & jnp.transpose(key_ok)[None, :, :]
    new_best = jnp.maximum(best_so_far, jnp.max(jnp.where(usable, scores_g, BIG_NEGATIVE), axis=-1))
    weights_g = jnp.where(usable, jnp.exp(scores_g - new_best[..., None]), 0.0)
    new_total = jnp.sum(weights_g, axis=-1)
    new_sum = jnp.einsum("ahb,bhd->ahd", weights_g, block_vals, precision=lax.Precision.HIGHEST)
    shift_amount = row_ids[:, None] - leading_local[None, :]
    inside_lattice = (shift_amount >= 0) & (jnp.mod(shift_amount, dilation_rate) == 0)
    lattice_slot = jnp.clip(shift_amount // dilation_rate, 0, place_count - 1)
    spreader = (
        (jnp.transpose(lattice_slot)[:, :, None] == place_numbers[None, None, :])
        & jnp.transpose(inside_lattice)[:, :, None]
    ).astype(jnp.float32)
    row_best = jnp.where(
        inside_lattice,
        jnp.einsum("hrp,ph->rh", spreader, new_best, precision=lax.Precision.HIGHEST),
        BIG_NEGATIVE,
    )
    row_total = jnp.einsum("hrp,ph->rh", spreader, new_total, precision=lax.Precision.HIGHEST)
    row_sum = jnp.einsum("hrp,phd->rhd", spreader, new_sum, precision=lax.Precision.HIGHEST)
    joint_best = jnp.maximum(local_best, row_best)
    near_factor = jnp.exp(local_best - joint_best)
    far_factor = jnp.exp(row_best - joint_best)
    numerator = near_factor[..., None] * local_sum + far_factor[..., None] * row_sum
    denominator = near_factor * local_total + far_factor * row_total
    denominator = jnp.where(query_live[:, None], denominator, 1.0)
    return (numerator / denominator[..., None]).reshape(row_cap, model_width).astype(jnp.bfloat16)


def on_device(ctx_in, resid, enc_out_w, slide_proj, qkv_w, tissue, kept_count, dilation):
    device_parts = lax.axis_size("seq")
    my_index = lax.axis_index("seq")
    tile_cap = ctx_in.shape[1]
    kept_dev = tile_cap * 2 // 3
    sequence_length = kept_dev * device_parts
    shard_ids = jnp.arange(device_parts, dtype=jnp.int32)
    counts = kept_count[0]
    count_ends = jnp.cumsum(counts)
    starts = count_ends - counts
    count_me = jnp.sum(jnp.where(shard_ids == my_index, counts, 0))
    start_me = jnp.sum(jnp.where(shard_ids == my_index, starts, 0))
    listing = tissue[0, 0]
    own_ctx = jnp.take(ctx_in[0], listing, axis=0)
    own_res = jnp.take(resid[0], listing, axis=0)
    hidden = own_res.astype(jnp.float32) + jnp.dot(
        own_ctx,
        lax.all_gather(enc_out_w, "seq", axis=1, tiled=True),
        preferred_element_type=jnp.float32,
    )
    normed = norm_rows(hidden).astype(jnp.bfloat16)
    embedded = jnp.dot(
        normed,
        lax.all_gather(slide_proj, "seq", axis=1, tiled=True),
        preferred_element_type=jnp.float32,
    ).astype(jnp.bfloat16)
    blended_output = jnp.dot(
        embedded,
        lax.all_gather(qkv_w, "seq", axis=1, tiled=True),
        preferred_element_type=jnp.float32,
    ).astype(jnp.bfloat16)
    attended = attend_slide(
        blended_output,
        start_me,
        count_me,
        starts,
        counts,
        dilation[0, 0],
        dilation[0, 1],
        sequence_length,
        device_parts,
    )
    live_rows = jnp.arange(tile_cap, dtype=jnp.int32) < count_me
    cleaned = jnp.where(live_rows[:, None], attended, jnp.zeros_like(attended))
    placed = jnp.zeros_like(cleaned).at[listing].set(cleaned)
    return placed[None]


def solution(mesh):
    return jax.shard_map(
        on_device,
        mesh=mesh,
        in_specs=(
            P("slide", "seq", None),
            P("slide", "seq", None),
            P(None, "seq"),
            P(None, "seq"),
            P(None, "seq"),
            P("slide", "seq", None),
            P("slide", None),
            P("slide", None),
        ),
        out_specs=P("slide", "seq", None),
        check_vma=False,
    )
```

profile of v0, /device:TPU:1, one launch (start us, length us, event | category | flops | bytes accessed | tf_op | source)
XLA Modules:
  0.0 784.4 jit_solution(14809408324199364053)
XLA Ops:
  8.8 1.3 fusion.115
  12.8 1.1 gather_fusion
  14.0 1.9 gather_fusion.1
  18.0 175.6 %all-gather.6.cloned.1.call-done = bf16[1536,1536]{0,1:T(8,128)(2,1)} async-done(((bf16[1536,48]{0,1:T(8,128)(2,1)}), bf16[1536,1536]{0,1:T(8,128)(2,1)}) %all-gather.6.cloned.1.call-update) | async-done | bytes 4718608 | tf_op jit(solution)/shard_map/all_gather | solution.py:188
  193.6 4.3 fusion.116
  198.2 128.9 %all-gather.8.cloned.1.call-done = bf16[1536,768]{0,1:T(8,128)(2,1)} async-done(((bf16[1536,24]{0,1:T(8,128)(2,1)}), bf16[1536,768]{0,1:T(8,128)(2,1)}) %all-gather.8.cloned.1.call-update) | async-done | bytes 2359312 | tf_op jit(solution)/shard_map/all_gather | solution.py:194
  327.2 150.4 %all-gather.10.cloned.1.call-done = bf16[768,2304]{0,1:T(8,128)(2,1)} async-done(((bf16[768,72]{0,1:T(8,128)(2,1)}), bf16[768,2304]{0,1:T(8,128)(2,1)}) %all-gather.10.cloned.1.call-update) | async-done | bytes 3538960 | tf_op jit(solution)/shard_map/all_gather | solution.py:199
  477.6 4.8 convolution_convert_fusion
  488.8 1.4 and_select_fusion.6
  490.2 0.9 add_select_fusion.5
  493.2 1.2 add_compare_fusion
  494.4 0.9 fusion.93
  495.3 1.4 fusion.76
  497.4 1.6 fusion.68
  499.2 1.3 collective-permute-start
  501.3 1.5 collective-permute-start.1
  502.7 22.3 %collective-permute-done = bf16[2,64,768]{2,1,0:T(8,128)(2,1)S(1)} collective-permute-done((bf16[2,64,768]{2,1,0:T(8,128)(2,1)S(1)}, bf16[2,64,768]{2,1,0:T(8,128)(2,1)S(1)}, u32[]{:S(2)}, u32[]{:S(2)}) %collective-permute-start) | collective-permute-done | bytes 196640 | tf_op jit(solution)/shard_map/ppermute | solution.py:21
  525.3 5.8 collective-permute-done.1
  531.3 0.8 copy.64
  532.1 0.8 copy.65
  532.9 1.4 fusion.2
  534.4 2.1 copy-done.2
  536.5 2.3 fusion.5
  538.8 94.6 %all-gather.12.cloned.1.call-done = bf16[1536,768]{1,0:T(8,128)(2,1)} async-done(((bf16[48,768]{1,0:T(8,128)(2,1)}), bf16[1536,768]{1,0:T(8,128)(2,1)}) %all-gather.12.cloned.1.call-update) | async-done | bytes 2359312 | tf_op jit(solution)/shard_map/all_gather | solution.py:124
  633.4 2.8 copy.49
  636.3 3.5 fusion
  639.8 3.2 fusion.7
  643.0 120.3 %all-gather.14.cloned.1.call-done = bf16[1536,768]{1,0:T(8,128)(2,1)} async-done(((bf16[48,768]{1,0:T(8,128)(2,1)}), bf16[1536,768]{1,0:T(8,128)(2,1)}) %all-gather.14.cloned.1.call-update) | async-done | bytes 2359312 | tf_op jit(solution)/shard_map/all_gather | solution.py:125
  763.4 2.9 copy.55
  766.4 5.6 fusion.27
  773.2 1.5 fusion.23
  775.6 2.3 scatter_custom_fusion
  (110 shorter events, 14.1 us)
Async XLA Ops:
  6.5 6.3 copy-start
  6.5 7.4 copy-start.1
  6.5 187.1 %all-gather.6.cloned.1.call-start = ((), (), s32[]{:S(2)}) async-start(), calls=%async_computation | async-start | bytes 4866048 | tf_op jit(solution)/shard_map/all_gather | solution.py:188
  7.3 319.9 %all-gather.8.cloned.1.call-start = ((), (), s32[]{:S(2)}) async-start(), calls=%async_computation.1 | async-start | bytes 2433024 | tf_op jit(solution)/shard_map/all_gather | solution.py:194
  8.0 469.6 %all-gather.10.cloned.1.call-start = ((), (), s32[]{:S(2)}) async-start(), calls=%async_computation.2 | async-start | bytes 3649536 | tf_op jit(solution)/shard_map/all_gather | solution.py:199
  8.7 624.7 %all-gather.12.cloned.1.call-start = ((), (), s32[]{:S(2)}) async-start(), calls=%async_computation.3 | async-start | bytes 2433024 | tf_op jit(solution)/shard_map/all_gather | solution.py:124
  13.9 2.5 copy-start.19
  13.9 3.9 copy-start.24
  17.9 477.4 %copy-start.12 = (s32[16]{0:T(128)}, s32[16]{0:T(128)S(1)}, u32[]{:S(2)}) copy-start(s32[16]{0:T(128)S(1)} %and_select_fusion.5) | copy-start | bytes 196
  18.0 474.0 %copy-start.17 = (s32[16,48]{1,0:T(8,128)}, s32[16,48]{1,0:T(8,128)S(1)}, u32[]{:S(2)}) copy-start(s32[16,48]{1,0:T(8,128)S(1)} %broadcast_add_fusion) | copy-start | bytes 9220
  483.8 279.6 %all-gather.14.cloned.1.call-start = ((), (), s32[]{:S(2)}) async-start(), calls=%async_computation.4 | async-start | bytes 2433024 | tf_op jit(solution)/shard_map/all_gather | solution.py:125
  492.0 42.4 %copy-start.3 = (bf16[192,768]{0,1:T(8,128)(2,1)}, bf16[192,768]{0,1:T(8,128)(2,1)S(1)}, u32[]{:S(2)}) copy-start(bf16[192,768]{0,1:T(8,128)(2,1)S(1)} %copy.51) | copy-start | bytes 884740
  499.1 33.8 %copy-start.5 = (pred[192,320]{1,0:T(8,128)(4,1)S(1)}, pred[192,320]{1,0:T(8,128)(4,1)}, u32[]{:S(2)}) copy-start(pred[192,320]{1,0:T(8,128)(4,1)} %compare_and_fusion) | copy-start | bytes 184324
  499.2 25.8 %collective-permute-start = (bf16[2,64,768]{2,1,0:T(8,128)(2,1)S(1)}, bf16[2,64,768]{2,1,0:T(8,128)(2,1)S(1)}, u32[]{:S(2)}, u32[]{:S(2)}) collective-permute-start(bf16[2,64,768]{2,1,0:T(8,128)(2,1)S(1)} %get-tuple-element.18), channel_id=1, source_target_pairs={{0,1},{1,2},{2,3},{3,4},{4,5},{5,6},{6,7},{7,8},{8,9},{9,10},{10,1... | collective-permute-start | bytes 589832 | tf_op jit(solution)/shard_map/ppermute | solution.py:21
  501.3 29.8 %collective-permute-start.1 = (bf16[2,64,768]{2,1,0:T(8,128)(2,1)S(1)}, bf16[2,64,768]{2,1,0:T(8,128)(2,1)S(1)}, u32[]{:S(2)}, u32[]{:S(2)}) collective-permute-start(bf16[2,64,768]{2,1,0:T(8,128)(2,1)S(1)} %get-tuple-element.19), channel_id=1, source_target_pairs={{1,0},{2,1},{3,2},{4,3},{5,4},{6,5},{7,6},{8,7},{9,8},{10,9},{11,1... | collective-permute-start | bytes 589832 | tf_op jit(solution)/shard_map/ppermute | solution.py:22
  534.4 2.1 copy-start.2
  538.8 97.5 %copy-start.9 = (pred[16,1536]{1,0:T(8,128)(4,1)S(1)}, pred[16,1536]{1,0:T(8,128)(4,1)}, u32[]{:S(2)}) copy-start(pred[16,1536]{1,0:T(8,128)(4,1)} %fusion.68) | copy-start | bytes 73732
  538.8 97.5 %copy-start.15 = (pred[48,16]{0,1:T(8,128)(4,1)S(1)}, pred[48,16]{0,1:T(8,128)(4,1)}, u32[]{:S(2)}) copy-start(pred[48,16]{0,1:T(8,128)(4,1)} %add_compare_fusion) | copy-start | bytes 2308
  538.8 97.5 %copy-start.18 = (s32[16,48]{1,0:T(8,128)S(1)}, s32[16,48]{1,0:T(8,128)}, u32[]{:S(2)}) copy-start(s32[16,48]{1,0:T(8,128)} %copy-done.17) | copy-start | bytes 9220
  643.0 123.2 %copy-start.10 = (pred[16,1536]{1,0:T(8,128)(4,1)S(1)}, pred[16,1536]{1,0:T(8,128)(4,1)}, u32[]{:S(2)}) copy-start(pred[16,1536]{1,0:T(8,128)(4,1)} %fusion.68) | copy-start | bytes 73732
  643.0 123.3 %copy-start.16 = (pred[48,16]{0,1:T(8,128)(4,1)S(1)}, pred[48,16]{0,1:T(8,128)(4,1)}, u32[]{:S(2)}) copy-start(pred[48,16]{0,1:T(8,128)(4,1)} %add_compare_fusion) | copy-start | bytes 2308
  763.4 9.8 %slice-start = ((s8[4718592]{0:T(1024)(128)(4,1)}), s8[524288]{0:T(1024)(128)(4,1)S(1)}, s32[]{:S(2)}) async-start(s8[4718592]{0:T(1024)(128)(4,1)} %bitcast.129), calls=%async_computation.5 | async-start | bytes 1048576
  766.3 5.7 copy-start.14
  766.3 5.7 copy-start.23
  766.3 6.5 copy-start.11
  766.3 6.5 copy-start.13
  766.3 6.5 copy-start.21
  766.3 6.8 slice-start.1
  766.4 6.8 copy-start.4
  766.4 6.8 copy-start.6
  766.4 6.8 copy-start.7
  766.4 6.8 copy-start.8
  (2 other events, 2.4 us)
Sparse Core Ops, SparseCore 0:
  11.7 181.8 all-gather.5
  198.0 129.1 all-gather.7
  331.5 146.0 all-gather.9
  483.9 149.4 all-gather.11
  637.6 125.7 all-gather.13
where the time goes:
time: 785 us; the launch traced here: 784 us
  waiting for transfers between devices  700 us (89%)
  matrix products  23.4 us (3%)
  other arithmetic  21.5 us (3%)
  between operations  19.1 us (2%)
  local copies, waits for them, and re-layouts  17.3 us (2%)
    all_gather x1, waiting for transfers between devices, on_device(): lax.all_gather(enc_out_w, 'seq', axis=1, tiled=True)  176 us
    all_gather x1, waiting for transfers between devices, on_device(): lax.all_gather(qkv_w, 'seq', axis=1, tiled=True)  150 us
    all_gather x1, waiting for transfers between devices, on_device(): lax.all_gather(slide_proj, 'seq', axis=1, tiled=True)  129 us
    all_gather x1, waiting for transfers between devices, attend_slide(): value_block = lax.all_gather(picked_v, 'seq', axis=0, tiled=True)  120 us
    all_gather x1, waiting for transfers between devices, attend_slide(): key_block = lax.all_gather(picked_k, 'seq', axis=0, tiled=True)  94.6 us
    ppermute x1, waiting for transfers between devices, with_halo(): before = lax.ppermute(last, axis, up)  22.3 us
  transfers between devices with their start and end apart: 7, of which 7 were waited for; matrix products, arithmetic and copies ran while one was open for 5% of the time, Pallas kernels for 0%

commit v1 on v0

v1 whole, which is shorter than its diff:
```python
import jax
import jax.numpy as jnp
from jax import lax
from jax.sharding import Mesh, PartitionSpec as P

HEADS = 16
HEAD_DIM = 48
D = 768
HALF = 64
RATE_MIN = 4
TILE_DEV = 192
SEQ_LEN = 4096
WINDOW = 384
KEY_SLOTS = 80
QUERY_SLOTS = 48
LANES = 128
PLANE = ("y", "x")
NORM_EPS = 1e-06
BIG_NEGATIVE = -1e30
SCALE = HEAD_DIM**-0.5


def dot_nt(a, b):
    return lax.dot_general(a, b, (((1,), (1,)), ((), ())), preferred_element_type=jnp.float32)


def mirrored(x):
    z_low = lax.axis_size("zlo")
    pairs = [
        (low * 2 + high, (z_low - 1 - low) * 2 + (1 - high))
        for low in range(z_low)
        for high in range(2)
    ]
    return lax.ppermute(x, ("zlo", "zhi"), pairs)


def across(x):
    return lax.ppermute(x, "zhi", [(0, 1), (1, 0)])


def both_halves(x, high):
    other = mirrored(x)
    return jnp.where(high == 0, jnp.stack([x, other]), jnp.stack([other, x]))


def gather_weight(x, high):
    pair = both_halves(x, high).reshape(2 * x.shape[0], x.shape[1])
    plane = lax.all_gather(pair, PLANE, axis=0, tiled=True)
    return lax.all_gather(plane, "core", axis=0, tiled=False)


def on_device(ctx_in, resid, enc_out_w, slide_proj, qkv_w, tissue, kept_count, dilation):
    core = lax.axis_index("core")
    high = lax.axis_index("zhi")
    plane_id = lax.axis_index("y") * lax.axis_size("x") + lax.axis_index("x")
    block_id = plane_id * 2 + high
    seg_len, rate = dilation[0, 0], dilation[0, 1]
    counts = kept_count[0]
    starts = jnp.cumsum(counts) - counts
    pair_counts = counts.reshape(-1, 2).sum(axis=1)
    pair_starts = starts.reshape(-1, 2)[:, 0]

    def pick(table, index):
        return jnp.sum(jnp.where(jnp.arange(table.shape[0]) == index, table, 0))

    count_me, start_me = pick(counts, block_id), pick(starts, block_id)
    count_other, start_other = pick(counts, block_id + 1 - 2 * high), pick(starts, block_id + 1 - 2 * high)
    pair_start, pair_count = pick(pair_starts, plane_id), pick(pair_counts, plane_id)
    base = jnp.where(high == 0, pair_start - HALF, pair_start)

    w_own = lax.dynamic_slice_in_dim(enc_out_w, core * D, D, 0).T
    p_own = lax.dynamic_slice_in_dim(slide_proj, core * D, D, 0).T
    q_own = lax.dynamic_slice_in_dim(qkv_w, core * (D // 2), D // 2, 0).T
    w_all = gather_weight(w_own, high)
    p_all = gather_weight(p_own, high)
    q_all = gather_weight(q_own, high)

    listing = tissue[0, 0]
    own_ctx = jnp.take(ctx_in[0], listing, axis=0)
    own_res = jnp.take(resid[0], listing, axis=0)
    hidden = own_res.astype(jnp.float32) + dot_nt(own_ctx[:, :D], w_all[0]) + dot_nt(own_ctx[:, D:], w_all[1])
    center = hidden - jnp.mean(hidden, axis=-1, keepdims=True)
    spread = jnp.mean(center * center, axis=-1, keepdims=True)
    normed = (center * lax.rsqrt(spread + NORM_EPS)).astype(jnp.bfloat16)
    embedded = (dot_nt(normed[:, :D], p_all[0]) + dot_nt(normed[:, D:], p_all[1])).astype(jnp.bfloat16)

    partner = across(embedded)
    rim_from = jnp.where(high == 0, count_other - HALF, 0)
    rim = lax.dynamic_slice_in_dim(partner, rim_from, HALF, 0)
    planes = lax.axis_size("y") * lax.axis_size("x")
    halo_pairs = [(p * 2, p * 2 + 2) for p in range(planes - 1)]
    halo_pairs += [(p * 2 + 1, p * 2 - 1) for p in range(1, planes)]
    halo = lax.ppermute(rim, ("y", "x", "zhi"), halo_pairs)

    rows = jnp.arange(TILE_DEV, dtype=jnp.int32)
    rim_rows = jnp.arange(HALF, dtype=jnp.int32)
    window = jnp.arange(WINDOW, dtype=jnp.int32)
    live = rows < count_me
    place_to = jnp.concatenate(
        [
            jnp.where(live, start_me - base + rows, -1),
            jnp.where(rows < count_other, start_other - base + rows, -1),
            rim_rows + jnp.where(high == 0, 0, pair_count),
        ]
    )
    place = (window[:, None] == place_to[None, :]).astype(jnp.bfloat16)
    sources = jnp.concatenate([embedded, partner, halo], axis=0)
    spanned = jnp.dot(place, sources, preferred_element_type=jnp.float32).astype(jnp.bfloat16)

    half = D // 2
    q_rows = (
        dot_nt(q_all[0, :D], embedded[:, :half]) + dot_nt(q_all[1, :D], embedded[:, half:])
    ).astype(jnp.bfloat16).reshape(HEADS, HEAD_DIM, TILE_DEV)
    kv_rows = (
        dot_nt(q_all[0, D:], spanned[:, :half]) + dot_nt(q_all[1, D:], spanned[:, half:])
    ).astype(jnp.bfloat16)
    keys = kv_rows[:D].reshape(HEADS, HEAD_DIM, WINDOW)
    vals = kv_rows[D:].reshape(HEADS, HEAD_DIM, WINDOW)

    heads = jnp.arange(HEADS, dtype=jnp.int32)
    key_slots = jnp.arange(KEY_SLOTS, dtype=jnp.int32)
    query_slots = jnp.arange(QUERY_SLOTS, dtype=jnp.int32)
    key_phase = jnp.mod(heads - pair_start, rate)
    query_phase = jnp.mod(heads - start_me, rate)
    key_lane = pair_start - base + key_phase[:, None] + rate * key_slots[None, :]
    key_pick = (key_lane[:, :, None] == window[None, None, :]).astype(jnp.bfloat16)
    query_row = query_phase[:, None] + rate * query_slots[None, :]
    query_pick = (query_row[:, :, None] == rows[None, None, :]).astype(jnp.bfloat16)
    kv_heads = jnp.concatenate(
        [keys, vals, jnp.zeros((HEADS, LANES - 2 * HEAD_DIM, WINDOW), jnp.bfloat16)], axis=1
    )
    q_heads = jnp.concatenate(
        [q_rows, jnp.zeros((HEADS, LANES - HEAD_DIM, TILE_DEV), jnp.bfloat16)], axis=1
    )
    payload = jnp.concatenate(
        [
            jnp.einsum("hsw,hfw->hsf", key_pick, kv_heads, preferred_element_type=jnp.float32),
            jnp.einsum("hsw,hfw->hsf", query_pick, q_heads, preferred_element_type=jnp.float32),
        ],
        axis=1,
    ).astype(jnp.bfloat16)
    arrived = lax.all_to_all(payload, PLANE, 0, 0)
    far_kv = arrived[:, :KEY_SLOTS].reshape(-1, LANES)
    far_q = arrived[:, KEY_SLOTS:].reshape(-1, LANES)
    far_phase = jnp.mod(plane_id - pair_starts, rate)
    far_live = (far_phase[:, None] + rate * key_slots[None, :] < pair_counts[:, None]).reshape(-1, 1)
    far_scores = jnp.where(far_live, dot_nt(far_kv, far_q) * SCALE, BIG_NEGATIVE)
    far_best = jnp.max(far_scores, axis=0, keepdims=True)
    far_weights = jnp.where(far_live, jnp.exp(far_scores - far_best), 0.0)
    far_total = jnp.sum(far_weights, axis=0)
    far_sum = jnp.einsum(
        "kq,kd->qd", far_weights.astype(jnp.bfloat16), far_kv, preferred_element_type=jnp.float32
    )[:, HEAD_DIM : 2 * HEAD_DIM]
    far_log = far_best[0] + jnp.log(far_total)
    log_a = lax.reduce_precision(far_log, 8, 7)
    log_b = lax.reduce_precision(far_log - log_a, 8, 7)
    log_c = lax.reduce_precision(far_log - log_a - log_b, 8, 7)
    answer = jnp.concatenate(
        [
            far_sum / far_total[:, None],
            jnp.stack([log_a, log_b, log_c], axis=1),
            jnp.zeros((far_q.shape[0], LANES - HEAD_DIM - 3), jnp.float32),
        ],
        axis=1,
    ).astype(jnp.bfloat16)
    answers = lax.all_to_all(answer.reshape(-1, QUERY_SLOTS, LANES), PLANE, 0, 0)

    key_pos = base + window
    key_ok = (key_pos >= 0) & (key_pos < SEQ_LEN)
    query_pos = start_me + rows
    allowed = (key_pos // seg_len)[:, None] == (query_pos // seg_len)[None, :]
    allowed = (allowed & key_ok[:, None])[None]
    scores = jnp.einsum("hdk,hdq->hkq", keys, q_rows, preferred_element_type=jnp.float32) * SCALE
    local_best = jnp.max(jnp.where(allowed, scores, BIG_NEGATIVE), axis=1)
    weights = jnp.where(allowed, jnp.exp(scores - local_best[:, None]), 0.0)
    local_total = jnp.sum(weights, axis=1)
    local_sum = jnp.einsum(
        "hdk,hkq->hdq", vals, weights.astype(jnp.bfloat16), preferred_element_type=jnp.float32
    )

    spread_rows = jnp.einsum("hsf,hsr->hfr", answers, query_pick, preferred_element_type=jnp.float32)
    shift = rows[None, :] - query_phase[:, None]
    inside = (shift >= 0) & (jnp.mod(shift, rate) == 0)
    row_log = spread_rows[:, HEAD_DIM] + spread_rows[:, HEAD_DIM + 1] + spread_rows[:, HEAD_DIM + 2]
    row_log = jnp.where(inside, row_log, BIG_NEGATIVE)
    joint = jnp.maximum(local_best, row_log)
    near = jnp.exp(local_best - joint)
    far = jnp.exp(row_log - joint)
    below = jnp.where(live[None], near * local_total + far, 1.0)
    attended = (near[:, None] * local_sum + far[:, None] * spread_rows[:, :HEAD_DIM]) / below[:, None]
    attended = jnp.where(live[None, None], attended, 0.0).astype(jnp.bfloat16).reshape(D, TILE_DEV)
    back = (listing[None, :] == rows[:, None]).astype(jnp.bfloat16)
    return dot_nt(back, attended).astype(jnp.bfloat16)[None]


def solution(mesh):
    devices = mesh.devices.reshape(-1, 2, 4, 4, 2)
    split = Mesh(devices, ("zlo", "core", "y", "x", "zhi"))
    slide, seq = ("zlo", "core"), ("y", "x", "zhi")
    return jax.shard_map(
        on_device,
        mesh=split,
        in_specs=(
            P(slide, seq, None),
            P(slide, seq, None),
            P(None, seq),
            P(None, seq),
            P(None, seq),
            P(slide, seq, None),
            P(slide, None),
            P(slide, None),
        ),
        out_specs=P(slide, seq, None),
        check_vma=False,
    )
```

time: 785 us -> 379 us (0.48)
  the two profiles are of different devices: /device:TPU:1 before, /device:TPU:192 now
where the time goes in v1:
time: 379 us; the launch traced here: 378 us
  waiting for transfers between devices  240 us (63%)
  starting transfers between devices  41.8 us (11%)
  other arithmetic  37.2 us (10%)
  matrix products  24.5 us (6%)
  between operations  20.3 us (5%)
  local copies, waits for them, and re-layouts  13.4 us (4%)
    all_gather x3, waiting for transfers between devices, gather_weight(): plane = lax.all_gather(pair, PLANE, axis=0, tiled=True)  149 us
    all_gather x3, waiting for transfers between devices, gather_weight(): return lax.all_gather(plane, 'core', axis=0, tiled=False)  59.2 us
    ppermute x3, starting transfers between devices, mirrored(): return lax.ppermute(x, ('zlo', 'zhi'), pairs)  20.6 us
    exp x1, other arithmetic, on_device(): near = jnp.exp(local_best - joint)  19.4 us
    dot_general x10, matrix products, dot_nt(): lax.dot_general(a, b, (((1,), (1,)), ((), ())), preferred_element_type=jn...  14.3 us
    ppermute x1, waiting for transfers between devices, across(): return lax.ppermute(x, 'zhi', [(0, 1), (1, 0)])  12.2 us
    ppermute x3, waiting for transfers between devices, mirrored(): return lax.ppermute(x, ('zlo', 'zhi'), pairs)  10.2 us
    all_to_all x1, starting transfers between devices, on_device(): arrived = lax.all_to_all(payload, PLANE, 0, 0)  7.76 us
  transfers between devices with their start and end apart: 13, of which 13 were waited for; matrix products, arithmetic and copies ran while one was open for 10% of the time, Pallas kernels for 0%

profile of v1, /device:TPU:192, one launch (start us, length us, event | category | flops | bytes accessed | tf_op | source)
XLA Modules:
  0.0 377.6 jit_solution(14204058716264880550)
XLA Ops:
  7.5 6.8 %collective-permute-start.1 = (bf16[48,768]{1,0:T(8,128)(2,1)S(1)}, bf16[48,768]{1,0:T(8,128)(2,1)S(1)}, u32[]{:S(2)}, u32[]{:S(2)}) collective-permute-start(bf16[48,768]{1,0:T(8,128)(2,1)S(1)} %get-tuple-element.18), channel_id=1, source_target_pairs={{0,449},{1,448},{64,385},{65,384},{128,321},{129,320},{192,257},{1... | collective-permute-start | bytes 221192 | tf_op jit(solution)/shard_map/ppermute | solution.py:34
  14.4 5.5 %collective-permute-done.1 = bf16[48,768]{1,0:T(8,128)(2,1)S(1)} collective-permute-done((bf16[48,768]{1,0:T(8,128)(2,1)S(1)}, bf16[48,768]{1,0:T(8,128)(2,1)S(1)}, u32[]{:S(2)}, u32[]{:S(2)}) %collective-permute-start.1) | collective-permute-done | bytes 73760 | tf_op jit(solution)/shard_map/ppermute | solution.py:34
  21.4 6.9 %collective-permute-start.2 = (bf16[24,768]{1,0:T(8,128)(2,1)S(1)}, bf16[24,768]{1,0:T(8,128)(2,1)S(1)}, u32[]{:S(2)}, u32[]{:S(2)}) collective-permute-start(bf16[24,768]{1,0:T(8,128)(2,1)S(1)} %get-tuple-element.22), channel_id=1, source_target_pairs={{0,449},{1,448},{64,385},{65,384},{128,321},{129,320},{192,257},{1... | collective-permute-start | bytes 110600 | tf_op jit(solution)/shard_map/ppermute | solution.py:34
  28.3 2.1 collective-permute-done.2
  32.0 6.8 %collective-permute-start = (bf16[72,384]{1,0:T(8,128)(2,1)S(1)}, bf16[72,384]{1,0:T(8,128)(2,1)S(1)}, u32[]{:S(2)}, u32[]{:S(2)}) collective-permute-start(bf16[72,384]{1,0:T(8,128)(2,1)S(1)} %get-tuple-element.20), channel_id=1, source_target_pairs={{0,449},{1,448},{64,385},{65,384},{128,321},{129,320},{192,257},{1... | collective-permute-start | bytes 165896 | tf_op jit(solution)/shard_map/ppermute | solution.py:34
  38.8 2.7 collective-permute-done
  42.2 41.7 %all-gather.12.cloned.1.call-done = bf16[1536,768]{1,0:T(8,128)(2,1)} async-done(((bf16[96,768]{1,0:T(8,128)(2,1)}), bf16[1536,768]{1,0:T(8,128)(2,1)}) %all-gather.12.cloned.1.call-update) | async-done | bytes 2359312 | tf_op jit(solution)/shard_map/all_gather | solution.py:48
  83.9 60.9 %all-gather.14.cloned.1.call-done = bf16[768,768]{1,0:T(8,128)(2,1)} async-done(((bf16[48,768]{1,0:T(8,128)(2,1)}), bf16[768,768]{1,0:T(8,128)(2,1)}) %all-gather.14.cloned.1.call-update) | async-done | bytes 1179664 | tf_op jit(solution)/shard_map/all_gather | solution.py:48
  157.4 1.4 and_select_fusion.2
  160.8 46.3 %all-gather.10.cloned.1.call-done = bf16[2304,384]{1,0:T(8,128)(2,1)} async-done(((bf16[144,384]{1,0:T(8,128)(2,1)}), bf16[2304,384]{1,0:T(8,128)(2,1)}) %all-gather.10.cloned.1.call-update) | async-done | bytes 1769488 | tf_op jit(solution)/shard_map/all_gather | solution.py:48
  211.1 22.4 %all-gather.18.cloned.1.call-done = bf16[3072,768]{1,0:T(8,128)(2,1)} async-done(((bf16[1536,768]{1,0:T(8,128)(2,1)}), bf16[3072,768]{1,0:T(8,128)(2,1)}) %all-gather.18.cloned.1.call-update) | async-done | bytes 4718608 | tf_op jit(solution)/shard_map/all_gather | solution.py:49
  233.5 2.7 convolution_add_fusion.2
  238.0 20.2 %all-gather.20.cloned.1.call-done = bf16[1536,768]{1,0:T(8,128)(2,1)} async-done(((bf16[768,768]{1,0:T(8,128)(2,1)}), bf16[1536,768]{1,0:T(8,128)(2,1)}) %all-gather.20.cloned.1.call-update) | async-done | bytes 2359312 | tf_op jit(solution)/shard_map/all_gather | solution.py:49
  258.2 1.8 fusion.42
  260.0 1.8 fusion.39
  261.9 6.2 %collective-permute-start.3 = (bf16[192,768]{1,0:T(8,128)(2,1)S(1)}, bf16[192,768]{1,0:T(8,128)(2,1)S(1)}, u32[]{:S(2)}, u32[]{:S(2)}) collective-permute-start(bf16[192,768]{1,0:T(8,128)(2,1)S(1)} %fusion.39), channel_id=1, source_target_pairs={{0,1},{1,0},{2,3},{3,2},{4,5},{5,4},{6,7},{7,6},{8,9},{9,8},{10,11... | collective-permute-start | bytes 884744 | tf_op jit(solution)/shard_map/ppermute | solution.py:38
  268.1 16.6 %all-gather.16.cloned.1.call-done = bf16[4608,384]{1,0:T(8,128)(2,1)} async-done(((bf16[2304,384]{1,0:T(8,128)(2,1)}), bf16[4608,384]{1,0:T(8,128)(2,1)}) %all-gather.16.cloned.1.call-update) | async-done | bytes 3538960 | tf_op jit(solution)/shard_map/all_gather | solution.py:49
  284.7 1.4 fusion.70
  286.1 1.4 fusion.40
  288.1 12.2 %collective-permute-done.3 = bf16[192,768]{1,0:T(8,128)(2,1)S(1)} collective-permute-done((bf16[192,768]{1,0:T(8,128)(2,1)S(1)}, bf16[192,768]{1,0:T(8,128)(2,1)S(1)}, u32[]{:S(2)}, u32[]{:S(2)}) %collective-permute-start.3) | collective-permute-done | bytes 294944 | tf_op jit(solution)/shard_map/ppermute | solution.py:38
  300.4 3.5 collective-permute-start.4
  304.3 1.8 collective-permute-done.4
  310.3 7.8 %all-to-all-start = ((bf16[16,128,128]{2,1,0:T(8,128)(2,1)}), bf16[16,128,128]{2,1,0:T(8,128)(2,1)S(1)}, u32[]{:S(2)}, u32[]{:S(2)}) async-start(bf16[16,128,128]{2,1,0:T(8,128)(2,1)} %pad_maximum_fusion), calls=%async_computation | async-start | bytes 1048576 | tf_op jit(solution)/shard_map/all_to_all | solution.py:142
  318.9 3.1 select_reduce_fusion
  322.0 6.6 %all-to-all-done = bf16[16,128,128]{2,1,0:T(8,128)(2,1)S(1)} async-done(((bf16[16,128,128]{2,1,0:T(8,128)(2,1)}), bf16[16,128,128]{2,1,0:T(8,128)(2,1)S(1)}, u32[]{:S(2)}, u32[]{:S(2)}) %all-to-all-start) | async-done | bytes 524320 | tf_op jit(solution)/shard_map/all_to_all | solution.py:142
  333.5 3.5 all-to-all-start.1
  337.1 3.3 fusion.1
  340.3 1.7 copy.35
  342.0 1.7 copy.33
  343.7 1.6 all-to-all-done.1
  346.7 19.4 %fusion.72 = (f32[16,192]{1,0:T(8,128)S(1)}, f32[16,192]{1,0:T(8,128)S(1)}, f32[16,192]{1,0:T(8,128)S(1)}) fusion(f32[16,1,192]{1,2,0:T(8,128)} %copy.33, f32[16,1,192]{1,2,0:T(8,128)} %copy.35, pred[192]{0:T(512)(128)(4,1)S(1)} %iota_compare_fusion.11, f32[16,128,192]{1,2,0:T(8,128)S(1)} %fusion.64, pred[]{:T(512)S(6)} %lt.111, s32[]{:T(128)S(6)} %select_n.205, ...), kind=kLoop, calls=%fused_computation.86 | loop fusion | flops 61440 | bytes 98565 | tf_op jit(solution)/shard_map/exp | solution.py:187
  366.0 3.7 fusion.59
  (103 shorter events, 32.0 us)
Async XLA Ops:
  6.5 201.9 %copy-start = (bf16[1,192,1536]{2,1,0:T(8,128)(2,1)S(1)}, bf16[1,192,1536]{2,1,0:T(8,128)(2,1)}, u32[]{:S(2)}) copy-start(bf16[1,192,1536]{2,1,0:T(8,128)(2,1)} %param.10) | copy-start | bytes 1769476
  6.5 77.3 %all-gather.12.cloned.1.call-start = ((), (), s32[]{:S(2)}) async-start(), calls=%async_computation.3 | async-start | bytes 2506752 | tf_op jit(solution)/shard_map/all_gather | solution.py:48
  7.5 12.4 %collective-permute-start.1 = (bf16[48,768]{1,0:T(8,128)(2,1)S(1)}, bf16[48,768]{1,0:T(8,128)(2,1)S(1)}, u32[]{:S(2)}, u32[]{:S(2)}) collective-permute-start(bf16[48,768]{1,0:T(8,128)(2,1)S(1)} %get-tuple-element.18), channel_id=1, source_target_pairs={{0,449},{1,448},{64,385},{65,384},{128,321},{129,320},{192,257},{1... | collective-permute-start | bytes 221192 | tf_op jit(solution)/shard_map/ppermute | solution.py:34
  20.6 124.2 %all-gather.14.cloned.1.call-start = ((), (), s32[]{:S(2)}) async-start(), calls=%async_computation.4 | async-start | bytes 1253376 | tf_op jit(solution)/shard_map/all_gather | solution.py:48
  21.4 9.0 %collective-permute-start.2 = (bf16[24,768]{1,0:T(8,128)(2,1)S(1)}, bf16[24,768]{1,0:T(8,128)(2,1)S(1)}, u32[]{:S(2)}, u32[]{:S(2)}) collective-permute-start(bf16[24,768]{1,0:T(8,128)(2,1)S(1)} %get-tuple-element.22), channel_id=1, source_target_pairs={{0,449},{1,448},{64,385},{65,384},{128,321},{129,320},{192,257},{1... | collective-permute-start | bytes 110600 | tf_op jit(solution)/shard_map/ppermute | solution.py:34
  31.1 176.0 %all-gather.10.cloned.1.call-start = ((), (), s32[]{:S(2)}) async-start(), calls=%async_computation.2 | async-start | bytes 1880064 | tf_op jit(solution)/shard_map/all_gather | solution.py:48
  32.0 112.9 %copy-start.8 = (s32[1,32]{1,0:T(1,128)S(1)}, s32[1,32]{1,0:T(1,128)}, u32[]{:S(2)}) copy-start(s32[1,32]{1,0:T(1,128)} %param.16) | copy-start | bytes 388
  32.0 9.5 %collective-permute-start = (bf16[72,384]{1,0:T(8,128)(2,1)S(1)}, bf16[72,384]{1,0:T(8,128)(2,1)S(1)}, u32[]{:S(2)}, u32[]{:S(2)}) collective-permute-start(bf16[72,384]{1,0:T(8,128)(2,1)S(1)} %get-tuple-element.20), channel_id=1, source_target_pairs={{0,449},{1,448},{64,385},{65,384},{128,321},{129,320},{192,257},{1... | collective-permute-start | bytes 165896 | tf_op jit(solution)/shard_map/ppermute | solution.py:34
  41.4 103.7 %copy-start.7 = (s32[1,2]{1,0:T(1,128)S(1)}, s32[1,2]{1,0:T(1,128)}, u32[]{:S(2)}) copy-start(s32[1,2]{1,0:T(1,128)} %param.17) | copy-start | bytes 28
  42.1 118.7 %copy-start.6 = (s32[1,1,192]{2,1,0:T(1,128)S(1)}, s32[1,1,192]{2,1,0:T(1,128)}, u32[]{:S(2)}) copy-start(s32[1,1,192]{2,1,0:T(1,128)} %param.15) | copy-start | bytes 2308
  42.1 191.4 %all-gather.18.cloned.1.call-start = ((), (), s32[]{:S(2)}) async-start(), calls=%async_computation.6 | async-start | bytes 7077888 | tf_op jit(solution)/shard_map/all_gather | solution.py:49
  83.9 174.3 %all-gather.20.cloned.1.call-start = ((), (), s32[]{:S(2)}) async-start(), calls=%async_computation.7 | async-start | bytes 3538944 | tf_op jit(solution)/shard_map/all_gather | solution.py:49
  144.8 139.9 %all-gather.16.cloned.1.call-start = ((), (), s32[]{:S(2)}) async-start(), calls=%async_computation.5 | async-start | bytes 5308416 | tf_op jit(solution)/shard_map/all_gather | solution.py:49
  208.4 1.1 copy-start.1
  233.5 3.0 copy-start.3
  261.9 38.5 %collective-permute-start.3 = (bf16[192,768]{1,0:T(8,128)(2,1)S(1)}, bf16[192,768]{1,0:T(8,128)(2,1)S(1)}, u32[]{:S(2)}, u32[]{:S(2)}) collective-permute-start(bf16[192,768]{1,0:T(8,128)(2,1)S(1)} %fusion.39), channel_id=1, source_target_pairs={{0,1},{1,0},{2,3},{3,2},{4,5},{5,4},{6,7},{7,6},{8,9},{9,8},{10,11... | collective-permute-start | bytes 884744 | tf_op jit(solution)/shard_map/ppermute | solution.py:38
  288.1 18.5 %copy-start.2 = (bf16[4608,384]{1,0:T(8,128)(2,1)S(1)}, bf16[4608,384]{1,0:T(8,128)(2,1)}, u32[]{:S(2)}) copy-start(bf16[4608,384]{1,0:T(8,128)(2,1)} %all-gather.16.cloned.1.call-done) | copy-start | bytes 10616836
  300.4 5.7 %collective-permute-start.4 = (bf16[64,768]{1,0:T(8,128)(2,1)S(1)}, bf16[64,768]{1,0:T(8,128)(2,1)S(1)}, u32[]{:S(2)}, u32[]{:S(2)}) collective-permute-start(bf16[64,768]{1,0:T(8,128)(2,1)S(1)} %constant_dynamic-slice_fusion), channel_id=1, source_target_pairs={{0,2},{2,4},{4,6},{6,8},{8,10},{10,12},{12,14},{14,16},{16,18},{18... | collective-permute-start | bytes 294920 | tf_op jit(solution)/shard_map/ppermute | solution.py:93
  308.5 0.9 copy-start.4
  310.3 18.2 %all-to-all-start = ((bf16[16,128,128]{2,1,0:T(8,128)(2,1)}), bf16[16,128,128]{2,1,0:T(8,128)(2,1)S(1)}, u32[]{:S(2)}, u32[]{:S(2)}) async-start(bf16[16,128,128]{2,1,0:T(8,128)(2,1)} %pad_maximum_fusion), calls=%async_computation | async-start | bytes 1048576 | tf_op jit(solution)/shard_map/all_to_all | solution.py:142
  333.5 11.8 %all-to-all-start.1 = ((bf16[16,48,128]{2,1,0:T(8,128)(2,1)}), bf16[16,48,128]{2,1,0:T(8,128)(2,1)S(1)}, u32[]{:S(2)}, u32[]{:S(2)}) async-start(bf16[16,48,128]{2,1,0:T(8,128)(2,1)} %concatenate.29), calls=%async_computation.1 | async-start | bytes 393216 | tf_op jit(solution)/shard_map/all_to_all | solution.py:166
  346.7 19.4 %copy-start.5 = (bf16[768,384]{1,0:T(8,128)(2,1)S(1)}, bf16[768,384]{1,0:T(8,128)(2,1)}, u32[]{:S(2)}) copy-start(bf16[768,384]{1,0:T(8,128)(2,1)} %copy-done.4) | copy-start | bytes 1769476
Sparse Core Ops, SparseCore 0:
  20.7 63.0 all-gather.11
  86.8 57.8 all-gather.13
  147.8 59.2 all-gather.9
  209.1 24.3 all-gather.17
  235.4 22.7 all-gather.19
  260.2 24.4 all-gather.15

commit v2 on v1

v2 whole, which is shorter than its diff:
```python
import functools

import jax
import jax.numpy as jnp
from jax import lax
from jax.experimental import pallas as pl
from jax.experimental.pallas import tpu as pltpu
from jax.sharding import Mesh, PartitionSpec as P

HEADS = 16
HEAD_DIM = 48
D = 768
D_ENC = 1536
HALF = 64
TILE_DEV = 192
SEQ_LEN = 4096
WINDOW = 384
KEY_SLOTS = 80
QUERY_SLOTS = 48
LANES = 128
W_ROWS = 48
P_ROWS = 24
Q_ROWS = 72
PLANES = 16
PLANE = ("y", "x")
NORM_EPS = 1e-06
BIG_NEGATIVE = -1e30
SCALE = HEAD_DIM**-0.5
BF16 = jnp.bfloat16
F32 = jnp.float32
I32 = jnp.int32
VMEM_LIMIT = 48 * 1024 * 1024

CORE, HIGH, RATE, START_ME, COUNT_ME, START_OTHER, COUNT_OTHER, PAIR_START, PAIR_COUNT, BASE = range(10)
ALL_STARTS = 16
ALL_COUNTS = 32


def dot_nn(a, b):
    return lax.dot_general(a, b, (((1,), (0,)), ((), ())), preferred_element_type=F32)


def dot_nt(a, b):
    return lax.dot_general(a, b, (((1,), (1,)), ((), ())), preferred_element_type=F32)


def dot_tn(a, b):
    return lax.dot_general(a, b, (((0,), (0,)), ((), ())), preferred_element_type=F32)


def iota(shape, dim):
    return lax.broadcasted_iota(I32, shape, dim)


def embed_kernel(table, ctx, res, near_a, near_b, far_a, far_b, out, w, p, hidden, normed, sems):
    core, high = table[CORE], table[HIGH]
    loads = [
        pltpu.make_async_copy(near_a, w.at[core, :, high], sems.at[0]),
        pltpu.make_async_copy(near_b, w.at[1 - core, :, high], sems.at[1]),
        pltpu.make_async_copy(far_a.at[:, :W_ROWS], w.at[core, :, 1 - high], sems.at[2]),
        pltpu.make_async_copy(far_b.at[:, :W_ROWS], w.at[1 - core, :, 1 - high], sems.at[3]),
        pltpu.make_async_copy(far_a.at[:, W_ROWS:], p.at[core], sems.at[4]),
        pltpu.make_async_copy(far_b.at[:, W_ROWS:], p.at[1 - core], sems.at[5]),
    ]
    for load in loads:
        load.start()
    for load in loads[:4]:
        load.wait()
    group = 4
    width = group * 2 * W_ROWS
    total = jnp.zeros((TILE_DEV, 1), F32)
    for n in range(PLANES // group):
        columns = slice(n * width, (n + 1) * width)
        part = res[:, columns].astype(F32)
        for half in range(2):
            block = w[half, n * group : (n + 1) * group].reshape(width, D)
            part += dot_nt(ctx[:, half * D : (half + 1) * D], block)
        hidden[:, columns] = part
        total += jnp.sum(part, axis=1, keepdims=True)
    center = hidden[...] - total / D_ENC
    spread = jnp.sum(center * center, axis=1, keepdims=True) / D_ENC
    normed[...] = (center * lax.rsqrt(spread + NORM_EPS)).astype(BF16)
    for load in loads[4:]:
        load.wait()
    for n in range(2):
        rows = slice(n * PLANES // 2, (n + 1) * PLANES // 2)
        part = dot_nt(normed[:, :D], p[0, rows].reshape(D // 2, D))
        part += dot_nt(normed[:, D:], p[1, rows].reshape(D // 2, D))
        out[:, n * D // 2 : (n + 1) * D // 2] = part.astype(BF16)


def embed(table, ctx, res, near_a, near_b, far_a, far_b):
    vmem = pl.BlockSpec(memory_space=pltpu.VMEM)
    hbm = pl.BlockSpec(memory_space=pl.ANY)
    return pl.pallas_call(
        embed_kernel,
        out_shape=jax.ShapeDtypeStruct((TILE_DEV, D), BF16),
        in_specs=[pl.BlockSpec(memory_space=pltpu.SMEM), vmem, vmem, hbm, hbm, hbm, hbm],
        out_specs=vmem,
        scratch_shapes=[
            pltpu.VMEM((2, PLANES, 2, W_ROWS, D), BF16),
            pltpu.VMEM((2, PLANES, 2 * P_ROWS, D), BF16),
            pltpu.VMEM((TILE_DEV, D_ENC), F32),
            pltpu.VMEM((TILE_DEV, D_ENC), BF16),
            pltpu.SemaphoreType.DMA((6,)),
        ],
        compiler_params=pltpu.CompilerParams(vmem_limit_bytes=VMEM_LIMIT),
        cost_estimate=pl.CostEstimate(flops=1_400_000_000, bytes_accessed=9_000_000, transcendentals=0),
        name="embed_rows",
    )(table, ctx, res, near_a, near_b, far_a, far_b)


def project_kernel(table, own, partner, halo, qa, qb, payload, q_out, kv_out, spanned):
    core, rate, base = table[CORE], table[RATE], table[BASE]

    def placed(first, count, length):
        lane = iota((WINDOW, length), 1)
        hit = (iota((WINDOW, length), 0) == lane + first) & (lane < count)
        return hit.astype(BF16)

    spread = dot_nn(placed(table[START_ME] - base, table[COUNT_ME], TILE_DEV), own[...])
    spread += dot_nn(placed(table[START_OTHER] - base, table[COUNT_OTHER], TILE_DEV), partner[...])
    halo_at = jnp.where(table[HIGH] == 0, 0, table[PAIR_COUNT])
    spread += dot_nn(placed(halo_at, HALF, HALF), halo[...])
    spanned[...] = spread.astype(BF16)
    half = D // 2
    lanes_a = pl.ds(pl.multiple_of(core * half, LANES), half)
    lanes_b = pl.ds(pl.multiple_of((1 - core) * half, LANES), half)
    own_a, own_b = own[:, lanes_a], own[:, lanes_b]
    q_out[...] = (dot_nt(qa[:D], own_a) + dot_nt(qb[:D], own_b)).astype(BF16)
    span_a, span_b = spanned[:, lanes_a], spanned[:, lanes_b]
    for n in range(2):
        rows = slice((n + 1) * D, (n + 2) * D)
        kv_out[n * D : (n + 1) * D] = (dot_nt(qa[rows], span_a) + dot_nt(qb[rows], span_b)).astype(BF16)
    key_slot = iota((KEY_SLOTS, WINDOW), 0) * rate
    key_lane = iota((KEY_SLOTS, WINDOW), 1)
    query_slot = iota((QUERY_SLOTS, TILE_DEV), 0) * rate
    query_lane = iota((QUERY_SLOTS, TILE_DEV), 1)
    key_rest = jnp.zeros((LANES - 2 * HEAD_DIM, WINDOW), BF16)
    query_rest = jnp.zeros((LANES - HEAD_DIM, TILE_DEV), BF16)
    for h in range(HEADS):
        rows = slice(h * HEAD_DIM, (h + 1) * HEAD_DIM)
        key_first = table[PAIR_START] - base + ((h - table[PAIR_START]) & (rate - 1))
        key_pick = (key_lane == key_slot + key_first).astype(BF16)
        both = jnp.concatenate([kv_out[rows], kv_out[D + h * HEAD_DIM : D + (h + 1) * HEAD_DIM], key_rest], axis=0)
        payload[h, :KEY_SLOTS] = dot_nt(key_pick, both).astype(BF16)
        query_first = (h - table[START_ME]) & (rate - 1)
        query_pick = (query_lane == query_slot + query_first).astype(BF16)
        ask = jnp.concatenate([q_out[rows], query_rest], axis=0)
        payload[h, KEY_SLOTS:] = dot_nt(query_pick, ask).astype(BF16)


def project(table, own, partner, halo, qa, qb):
    vmem = pl.BlockSpec(memory_space=pltpu.VMEM)
    return pl.pallas_call(
        project_kernel,
        out_shape=(
            jax.ShapeDtypeStruct((HEADS, KEY_SLOTS + QUERY_SLOTS, LANES), BF16),
            jax.ShapeDtypeStruct((D, TILE_DEV), BF16),
            jax.ShapeDtypeStruct((2 * D, WINDOW), BF16),
        ),
        in_specs=[pl.BlockSpec(memory_space=pltpu.SMEM)] + [vmem] * 5,
        out_specs=(vmem, vmem, vmem),
        scratch_shapes=[pltpu.VMEM((WINDOW, D), BF16)],
        compiler_params=pltpu.CompilerParams(vmem_limit_bytes=VMEM_LIMIT),
        cost_estimate=pl.CostEstimate(flops=2_000_000_000, bytes_accessed=6_000_000, transcendentals=0),
        name="project_rows",
    )(table, own, partner, halo, qa, qb)


def local_kernel(q, kv, key_seg, query_seg, out_sum, out_best, out_total):
    allowed = key_seg[...] == query_seg[...]
    for h in range(HEADS):
        rows = slice(h * HEAD_DIM, (h + 1) * HEAD_DIM)
        scores = dot_tn(kv[rows], q[rows]) * SCALE
        scores = jnp.where(allowed, scores, BIG_NEGATIVE)
        best = jnp.max(scores, axis=0, keepdims=True)
        weights = jnp.exp(scores - best)
        out_best[h : h + 1] = best
        out_total[h : h + 1] = jnp.sum(weights, axis=0, keepdims=True)
        out_sum[rows] = dot_nn(kv[D + h * HEAD_DIM : D + (h + 1) * HEAD_DIM], weights.astype(BF16))


def local_branch(q, kv, key_seg, query_seg):
    vmem = pl.BlockSpec(memory_space=pltpu.VMEM)
    stat = jax.ShapeDtypeStruct((HEADS, TILE_DEV), F32)
    return pl.pallas_call(
        local_kernel,
        out_shape=(jax.ShapeDtypeStruct((D, TILE_DEV), F32), stat, stat),
        in_specs=[vmem] * 4,
        out_specs=(vmem, vmem, vmem),
        compiler_params=pltpu.CompilerParams(vmem_limit_bytes=VMEM_LIMIT),
        cost_estimate=pl.CostEstimate(flops=300_000_000, bytes_accessed=3_000_000, transcendentals=1_200_000),
        name="local_branch",
    )(q, kv, key_seg, query_seg)


def far_kernel(table, plane, arrived, answer, scores):
    rate = table[RATE]
    kv = arrived[:, :KEY_SLOTS].reshape(PLANES * KEY_SLOTS, LANES)
    group = 8
    width = group * QUERY_SLOTS
    slot = iota((KEY_SLOTS, width), 0) * rate
    for n in range(PLANES // group):
        asks = arrived[n * group : (n + 1) * group, KEY_SLOTS:].reshape(width, LANES)
        best = jnp.full((1, width), BIG_NEGATIVE, F32)
        for p in range(PLANES):
            phase = (plane[0] - table[ALL_STARTS + p]) & (rate - 1)
            piece = dot_nt(arrived[p, :KEY_SLOTS], asks) * SCALE
            piece = jnp.where(slot + phase < table[ALL_COUNTS + p], piece, BIG_NEGATIVE)
            scores[p * KEY_SLOTS : (p + 1) * KEY_SLOTS] = piece
            best = jnp.maximum(best, jnp.max(piece, axis=0, keepdims=True))
        weights = jnp.exp(scores[...] - best)
        total = jnp.sum(weights, axis=0, keepdims=True)
        summed = dot_tn(kv, weights.astype(BF16))
        shared = summed[HEAD_DIM : 2 * HEAD_DIM] / total
        log_all = best + jnp.log(total)
        log_a = log_all.astype(BF16).astype(F32)
        log_b = (log_all - log_a).astype(BF16).astype(F32)
        log_c = log_all - log_a - log_b
        row = iota((LANES - HEAD_DIM, width), 0)
        tail = jnp.where(row == 0, log_a, jnp.where(row == 1, log_b, jnp.where(row == 2, log_c, 0.0)))
        block = jnp.concatenate([shared, tail], axis=0)
        answer[n * group : (n + 1) * group] = block.T.astype(BF16).reshape(group, QUERY_SLOTS, LANES)


def far_branch(table, plane, arrived):
    vmem, smem = pl.BlockSpec(memory_space=pltpu.VMEM), pl.BlockSpec(memory_space=pltpu.SMEM)
    return pl.pallas_call(
        far_kernel,
        out_shape=jax.ShapeDtypeStruct((PLANES, QUERY_SLOTS, LANES), BF16),
        in_specs=[smem, smem, vmem],
        out_specs=vmem,
        scratch_shapes=[pltpu.VMEM((PLANES * KEY_SLOTS, PLANES // 2 * QUERY_SLOTS), F32)],
        compiler_params=pltpu.CompilerParams(vmem_limit_bytes=VMEM_LIMIT),
        cost_estimate=pl.CostEstimate(flops=500_000_000, bytes_accessed=1_000_000, transcendentals=1_000_000),
        name="far_branch",
    )(table, plane, arrived)


def finish_kernel(table, answers, local_sum, local_best, local_total, listing, out, attended):
    rate = table[RATE]
    slot = iota((QUERY_SLOTS, TILE_DEV), 0) * rate
    lane = iota((QUERY_SLOTS, TILE_DEV), 1)
    row = iota((1, TILE_DEV), 1)
    live = row < table[COUNT_ME]
    for h in range(HEADS):
        rows = slice(h * HEAD_DIM, (h + 1) * HEAD_DIM)
        phase = (h - table[START_ME]) & (rate - 1)
        pick = (lane == slot + phase).astype(BF16)
        wide = dot_tn(answers[h], pick)
        log_all = wide[HEAD_DIM : HEAD_DIM + 1] + wide[HEAD_DIM + 1 : HEAD_DIM + 2] + wide[HEAD_DIM + 2 : HEAD_DIM + 3]
        log_all = jnp.where((row & (rate - 1)) == phase, log_all, BIG_NEGATIVE)
        best = local_best[h : h + 1]
        joint = jnp.maximum(best, log_all)
        near = jnp.exp(best - joint)
        far = jnp.exp(log_all - joint)
        below = jnp.where(live, near * local_total[h : h + 1] + far, 1.0)
        mixed = (near * local_sum[rows] + far * wide[:HEAD_DIM]) / below
        attended[rows] = jnp.where(live, mixed, 0.0).astype(BF16)
    back = (listing[...] == iota((TILE_DEV, TILE_DEV), 0)).astype(BF16)
    out[0] = dot_nt(back, attended[...]).astype(BF16)


def finish(table, answers, local_sum, local_best, local_total, listing):
    vmem = pl.BlockSpec(memory_space=pltpu.VMEM)
    return pl.pallas_call(
        finish_kernel,
        out_shape=jax.ShapeDtypeStruct((1, TILE_DEV, D), BF16),
        in_specs=[pl.BlockSpec(memory_space=pltpu.SMEM)] + [vmem] * 5,
        out_specs=vmem,
        scratch_shapes=[pltpu.VMEM((D, TILE_DEV), BF16)],
        compiler_params=pltpu.CompilerParams(vmem_limit_bytes=VMEM_LIMIT),
        cost_estimate=pl.CostEstimate(flops=100_000_000, bytes_accessed=1_500_000, transcendentals=10_000),
        name="finish_rows",
    )(table, answers, local_sum, local_best, local_total, listing)


def mirrored(x):
    z_low = lax.axis_size("zlo")
    pairs = [
        (low * 2 + high, (z_low - 1 - low) * 2 + (1 - high))
        for low in range(z_low)
        for high in range(2)
    ]
    return lax.ppermute(x, ("zlo", "zhi"), pairs)


def across(x):
    return lax.ppermute(x, "zhi", [(0, 1), (1, 0)])


def other_core(x):
    return lax.ppermute(x, "core", [(0, 1), (1, 0)])


def over_plane(x):
    return lax.all_to_all(jnp.broadcast_to(x[None], (PLANES,) + x.shape), PLANE, 0, 0)


def in_order(own, other, high):
    return jnp.where(high == 0, jnp.concatenate([own, other]), jnp.concatenate([other, own]))


def on_device(ctx_in, resid, enc_out_w, slide_proj, qkv_w, tissue, kept_count, dilation):
    core = lax.axis_index("core")
    high = lax.axis_index("zhi")
    plane_id = lax.axis_index("y") * lax.axis_size("x") + lax.axis_index("x")
    block_id = plane_id * 2 + high
    seg_len, rate = dilation[0, 0], dilation[0, 1]

    w_own = lax.dynamic_slice_in_dim(enc_out_w, core * D, D, 0).T
    p_own = lax.dynamic_slice_in_dim(slide_proj, core * D, D, 0).T
    q_own = lax.dynamic_slice_in_dim(qkv_w, core * (D // 2), D // 2, 0).T
    near_a = over_plane(w_own)
    w_other = mirrored(w_own)
    p_other = mirrored(p_own)
    q_other = mirrored(q_own)
    near_b = other_core(near_a)
    far_a = over_plane(jnp.concatenate([w_other, in_order(p_own, p_other, high)]))
    far_b = other_core(far_a)
    q_pair, far_a = lax.optimization_barrier((in_order(q_own, q_other, high), far_a))
    q_a = over_plane(q_pair)
    q_b = other_core(q_a)

    counts = kept_count[0]
    starts = jnp.cumsum(counts) - counts
    pair_counts = counts.reshape(-1, 2).sum(axis=1)
    pair_starts = starts.reshape(-1, 2)[:, 0]

    def pick(values, index):
        return jnp.sum(jnp.where(jnp.arange(values.shape[0]) == index, values, 0))

    other_id = block_id + 1 - 2 * high
    count_me, start_me = pick(counts, block_id), pick(starts, block_id)
    count_other, start_other = pick(counts, other_id), pick(starts, other_id)
    pair_start, pair_count = pick(pair_starts, plane_id), pick(pair_counts, plane_id)
    base = jnp.where(high == 0, pair_start - HALF, pair_start)
    scalars = [core, high, rate, start_me, count_me, start_other, count_other, pair_start, pair_count, base]
    table = jnp.concatenate(
        [
            jnp.stack([jnp.asarray(s, I32) for s in scalars]),
            jnp.zeros((ALL_STARTS - len(scalars),), I32),
            pair_starts.astype(I32),
            pair_counts.astype(I32),
        ]
    )

    listing = tissue[0, 0]
    own_ctx = jnp.take(ctx_in[0], listing, axis=0)
    own_res = jnp.take(resid[0], listing, axis=0)
    embedded = embed(table, own_ctx, own_res, near_a, near_b, far_a, far_b)

    partner = across(embedded)
    rim_from = jnp.where(high == 0, count_other - HALF, 0)
    rim = lax.dynamic_slice_in_dim(partner, rim_from, HALF, 0)
    halo_pairs = [(p * 2, p * 2 + 2) for p in range(PLANES - 1)]
    halo_pairs += [(p * 2 + 1, p * 2 - 1) for p in range(1, PLANES)]
    halo = lax.ppermute(rim, ("y", "x", "zhi"), halo_pairs)

    payload, q_rows, kv_rows = project(
        table, embedded, partner, halo, q_a.reshape(3 * D, D // 2), q_b.reshape(3 * D, D // 2)
    )
    arrived = lax.all_to_all(payload, PLANE, 0, 0)

    key_pos = base + jnp.arange(WINDOW, dtype=I32)
    key_ok = (key_pos >= 0) & (key_pos < SEQ_LEN)
    key_seg = jnp.where(key_ok, key_pos // seg_len, -1)[:, None]
    query_seg = ((start_me + jnp.arange(TILE_DEV, dtype=I32)) // seg_len)[None, :]
    local_sum, local_best, local_total = local_branch(q_rows, kv_rows, key_seg, query_seg)

    answer = far_branch(table, jnp.asarray(plane_id, I32).reshape(1), arrived)
    answers = lax.all_to_all(answer, PLANE, 0, 0)
    return finish(table, answers, local_sum, local_best, local_total, listing[None, :])


def solution(mesh):
    devices = mesh.devices.reshape(-1, 2, 4, 4, 2)
    split = Mesh(devices, ("zlo", "core", "y", "x", "zhi"))
    slide, seq = ("zlo", "core"), ("y", "x", "zhi")
    return jax.shard_map(
        on_device,
        mesh=split,
        in_specs=(
            P(slide, seq, None),
            P(slide, seq, None),
            P(None, seq),
            P(None, seq),
            P(None, seq),
            P(slide, seq, None),
            P(slide, None),
            P(slide, None),
        ),
        out_specs=P(slide, seq, None),
        check_vma=False,
    )
```

time: 379 us -> 223 us (0.59)
  the two profiles are of different devices: /device:TPU:192 before, /device:TPU:1 now
where the time goes in v2:
time: 223 us; the launch traced here: 221 us
  waiting for transfers between devices  67.5 us (30%)
  starting transfers between devices  65.9 us (30%)
  blocking collectives  36.2 us (16%)
  Pallas kernels  22.9 us (10%)
  local copies, waits for them, and re-layouts  16.9 us (8%)
  other arithmetic  8.59 us (4%)
  between operations  2.74 us (1%)
    all_to_all x1, blocking collectives, over_plane(): lax.all_to_all(jnp.broadcast_to(x[None], (PLANES,) + x.shape), PLANE, 0, 0)  36.2 us
    ppermute x1, waiting for transfers between devices, across(): return lax.ppermute(x, 'zhi', [(0, 1), (1, 0)])  27.6 us
    all_to_all x2, waiting for transfers between devices, over_plane(): lax.all_to_all(jnp.broadcast_to(x[None], (PLANES,) + x.shape), PLANE, 0, 0)  19.9 us
    ppermute x3, starting transfers between devices, mirrored(): return lax.ppermute(x, ('zlo', 'zhi'), pairs)  19.7 us
    ppermute x3, starting transfers between devices, other_core(): return lax.ppermute(x, 'core', [(0, 1), (1, 0)])  15.3 us
    ppermute x1, starting transfers between devices, across(): return lax.ppermute(x, 'zhi', [(0, 1), (1, 0)])  10.1 us
    ppermute x3, waiting for transfers between devices, mirrored(): return lax.ppermute(x, ('zlo', 'zhi'), pairs)  9.61 us
    all_to_all x2, starting transfers between devices, over_plane(): lax.all_to_all(jnp.broadcast_to(x[None], (PLANES,) + x.shape), PLANE, 0, 0)  9.34 us
  transfers between devices with their start and end apart: 12, of which 7 were waited for; matrix products, arithmetic and copies ran while one was open for 10% of the time, Pallas kernels for 5%

profile of v2, /device:TPU:1, one launch (start us, length us, event | category | flops | bytes accessed | tf_op | source)
XLA Modules:
  0.0 220.6 jit_solution(13864124638029835361)
XLA Ops:
  0.8 11.9 %collective-permute-start.3 = (bf16[24,768]{1,0:T(8,128)(2,1)S(1)}, bf16[24,768]{1,0:T(8,128)(2,1)S(1)}, u32[]{:S(2)}, u32[]{:S(2)}) collective-permute-start(bf16[24,768]{1,0:T(8,128)(2,1)S(1)} %dynamic-slice_bitcast_fusion.2), channel_id=1, source_target_pairs={{0,449},{1,448},{64,385},{65,384},{128,321},{129,320},{192,257},{1... | collective-permute-start | bytes 110600 | tf_op jit(solution)/shard_map/ppermute | solution.py:286
  13.7 1.9 collective-permute-start.2
  15.6 7.7 %collective-permute-done.2 = bf16[48,768]{1,0:T(8,128)(2,1)S(1)} collective-permute-done((bf16[48,768]{1,0:T(8,128)(2,1)S(1)}, bf16[48,768]{1,0:T(8,128)(2,1)S(1)}, u32[]{:S(2)}, u32[]{:S(2)}) %collective-permute-start.2) | collective-permute-done | bytes 73760 | tf_op jit(solution)/shard_map/ppermute | solution.py:286
  23.6 36.2 %all_to_all.25.far_a = bf16[16,96,768]{2,1,0:T(8,128)(2,1)S(1)} all-to-all(bf16[16,96,768]{2,1,0:T(8,128)(2,1)S(1)} %broadcast_in_dim.46), channel_id=1, replica_groups=mesh['zlo'=8,'core'=2,'y'=4,'x'=4,'zhi'=2] {'y','x'}, dimensions={0} | all-to-all | bytes 4718592 | tf_op jit(solution)/shard_map/all_to_all | solution.py:298
  60.8 4.4 %all-to-all-start = ((bf16[16,48,768]{2,1,0:T(8,128)(2,1)}), bf16[16,48,768]{2,1,0:T(8,128)(2,1)}, u32[]{:S(2)}, u32[]{:S(2)}) async-start(bf16[16,48,768]{2,1,0:T(8,128)(2,1)} %broadcast_in_dim.45), calls=%async_computation | async-start | bytes 2359296 | tf_op jit(solution)/shard_map/all_to_all | solution.py:298
  65.3 5.9 %collective-permute-start.1 = (bf16[72,384]{1,0:T(8,128)(2,1)S(1)}, bf16[72,384]{1,0:T(8,128)(2,1)S(1)}, u32[]{:S(2)}, u32[]{:S(2)}) collective-permute-start(bf16[72,384]{1,0:T(8,128)(2,1)S(1)} %dynamic-slice_bitcast_fusion.1), channel_id=1, source_target_pairs={{0,449},{1,448},{64,385},{65,384},{128,321},{129,320},{192,257},{1... | collective-permute-start | bytes 165896 | tf_op jit(solution)/shard_map/ppermute | solution.py:286
  71.1 1.9 collective-permute-done.1
  73.1 8.2 %all-to-all-done.near_a = bf16[16,48,768]{2,1,0:T(8,128)(2,1)} async-done(((bf16[16,48,768]{2,1,0:T(8,128)(2,1)}), bf16[16,48,768]{2,1,0:T(8,128)(2,1)}, u32[]{:S(2)}, u32[]{:S(2)}) %all-to-all-start) | async-done | bytes 1179680 | tf_op jit(solution)/shard_map/all_to_all | solution.py:298
  81.3 1.4 broadcast_in_dim.47
  82.7 5.0 %all-to-all-start.2 = ((bf16[16,144,384]{2,1,0:T(8,128)(2,1)}), bf16[16,144,384]{2,1,0:T(8,128)(2,1)}, u32[]{:S(2)}, u32[]{:S(2)}) async-start(bf16[16,144,384]{2,1,0:T(8,128)(2,1)} %broadcast_in_dim.47), calls=%async_computation.2 | async-start | bytes 3538944 | tf_op jit(solution)/shard_map/all_to_all | solution.py:298
  87.7 5.5 %collective-permute-start.4 = (bf16[16,96,768]{2,1,0:T(8,128)(2,1)S(1)}, bf16[16,96,768]{2,1,0:T(8,128)(2,1)}, u32[]{:S(2)}, u32[]{:S(2)}) collective-permute-start(bf16[16,96,768]{2,1,0:T(8,128)(2,1)S(1)} %all_to_all.25.far_a), channel_id=1, source_target_pairs={{0,32},{32,0},{1,33},{33,1},{2,34},{34,2},{3,35},{35,3},{4,36},{36... | collective-permute-start | bytes 7077896 | tf_op jit(solution)/shard_map/ppermute | solution.py:294
  95.6 1.9 collective-permute-start
  97.5 11.7 %all-to-all-done.2 = bf16[16,144,384]{2,1,0:T(8,128)(2,1)} async-done(((bf16[16,144,384]{2,1,0:T(8,128)(2,1)}), bf16[16,144,384]{2,1,0:T(8,128)(2,1)}, u32[]{:S(2)}, u32[]{:S(2)}) %all-to-all-start.2) | async-done | bytes 1769504 | tf_op jit(solution)/shard_map/all_to_all | solution.py:298
  109.2 7.9 %collective-permute-start.7 = (bf16[16,144,384]{2,1,0:T(8,128)(2,1)}, bf16[16,144,384]{2,1,0:T(8,128)(2,1)}, u32[]{:S(2)}, u32[]{:S(2)}) collective-permute-start(bf16[16,144,384]{2,1,0:T(8,128)(2,1)} %all-to-all-done.2), channel_id=1, source_target_pairs={{0,32},{32,0},{1,33},{33,1},{2,34},{34,2},{3,35},{35,3},{4,36},{36... | collective-permute-start | bytes 5308424 | tf_op jit(solution)/shard_map/ppermute | solution.py:294
  118.5 2.0 gather_fusion
  120.5 3.7 %gather_fusion.1 = bf16[192,1536]{1,0:T(8,128)(2,1)} fusion(bf16[192,1536]{1,0:T(8,128)(2,1)} %bitcast.37, s32[1024]{0:T(1024)S(1)} %pad_clamp_fusion), kind=kCustom, calls=%fused_computation.1.clone | custom fusion | bytes 1180416 | tf_op jit(solution)/shard_map/jit(_take)/gather | solution.py:351
  126.2 4.5 %concatenate.18.table = s32[48]{0:T(128)S(1)} concatenate(s32[1]{0:T(128)} %bitcast, s32[1]{0:T(128)} %bitcast.1, s32[1]{0:T(128)} %bitcast.2, s32[1]{0:T(128)} %bitcast.5, s32[1]{0:T(128)} %bitcast.6, s32[1]{0:T(128)} %bitcast.7, s32[1]{0:T(128)} %bitcast.8, s32[1]{0:T(128)} %bitcast.9, s32[1]{0:T(128)} %bitcast.10, s32[1]{0:T(128)} %bitcast.11, s32[6]{0:T(128)S(1)} %broadcast.120, ...), dimensions={0} | concatenate | bytes 384 | tf_op jit(solution)/shard_map/concatenate | solution.py:340
  130.7 1.4 broadcast_select_fusion
  132.1 5.4 %embed_rows.1.own = bf16[192,768]{1,0:T(8,128)(2,1)S(1)} custom-call(s32[48]{0:T(128)S(1)} %concatenate.18.table, bf16[192,1536]{1,0:T(8,128)(2,1)S(1)} %get-tuple-element.29.ctx, bf16[192,1536]{1,0:T(8,128)(2,1)S(1)} %get-tuple-element.28.res, bf16[16,48,768]{2,1,0:T(8,128)(2,1)} %all-to-all-done.near_a, bf16[16,48,768]{2,1,0:T(8,128)(2,1)} %collective-permute-done.near_b, ...), custom_call_target="tpu_custom_call" | custom-call | flops 1400000000 | bytes 9000000 | tf_op jit(solution)/shard_map/embed_rows/pallas_call | solution.py:95
  137.6 10.1 %collective-permute-start.5 = (bf16[192,768]{1,0:T(8,128)(2,1)S(1)}, bf16[192,768]{1,0:T(8,128)(2,1)S(1)}, u32[]{:S(2)}, u32[]{:S(2)}) collective-permute-start(bf16[192,768]{1,0:T(8,128)(2,1)S(1)} %embed_rows.1.own), channel_id=1, source_target_pairs={{0,1},{1,0},{2,3},{3,2},{4,5},{5,4},{6,7},{7,6},{8,9},{9,8},{10,11... | collective-permute-start | bytes 884744 | tf_op jit(solution)/shard_map/ppermute | solution.py:290
  148.3 27.6 %collective-permute-done.5.partner = bf16[192,768]{1,0:T(8,128)(2,1)S(1)} collective-permute-done((bf16[192,768]{1,0:T(8,128)(2,1)S(1)}, bf16[192,768]{1,0:T(8,128)(2,1)S(1)}, u32[]{:S(2)}, u32[]{:S(2)}) %collective-permute-start.5) | collective-permute-done | bytes 294944 | tf_op jit(solution)/shard_map/ppermute | solution.py:290
  175.9 1.3 collective-permute-start.6
  177.2 1.6 collective-permute-done.6.halo
  178.8 6.1 %project_rows.1 = (bf16[16,128,128]{2,1,0:T(8,128)(2,1)}, bf16[768,192]{1,0:T(8,128)(2,1)S(1)}, bf16[1536,384]{1,0:T(8,128)(2,1)S(1)}) custom-call(s32[48]{0:T(128)S(1)} %concatenate.18.table, bf16[192,768]{1,0:T(8,128)(2,1)S(1)} %embed_rows.1.own, bf16[192,768]{1,0:T(8,128)(2,1)S(1)} %collective-permute-done.5.partner, ...), custom_call_target="tpu_custom_call" | custom-call | flops 2000000000 | bytes 6000000 | tf_op jit(solution)/shard_map/project_rows/pallas_call | solution.py:155
  185.7 6.6 %all-to-all-start.3 = ((bf16[16,128,128]{2,1,0:T(8,128)(2,1)}), bf16[16,128,128]{2,1,0:T(8,128)(2,1)S(1)}, u32[]{:S(2)}, u32[]{:S(2)}) async-start(bf16[16,128,128]{2,1,0:T(8,128)(2,1)} %get-tuple-element.16), calls=%async_computation.3 | async-start | bytes 1048576 | tf_op jit(solution)/shard_map/all_to_all | solution.py:364
  192.9 8.8 %all-to-all-done.3.arrived = bf16[16,128,128]{2,1,0:T(8,128)(2,1)S(1)} async-done(((bf16[16,128,128]{2,1,0:T(8,128)(2,1)}), bf16[16,128,128]{2,1,0:T(8,128)(2,1)S(1)}, u32[]{:S(2)}, u32[]{:S(2)}) %all-to-all-start.3) | async-done | bytes 524320 | tf_op jit(solution)/shard_map/all_to_all | solution.py:364
  201.7 4.0 %far_branch.1 = bf16[16,48,128]{2,1,0:T(8,128)(2,1)} custom-call(s32[48]{0:T(128)S(1)} %concatenate.18.table, s32[1]{0:T(128)} %bitcast.12.plane, bf16[16,128,128]{2,1,0:T(8,128)(2,1)S(1)} %all-to-all-done.3.arrived), custom_call_target="tpu_custom_call" | custom-call | flops 500000000 | bytes 1000000 | tf_op jit(solution)/shard_map/far_branch/pallas_call | solution.py:229
  205.7 3.5 %all-to-all-start.4 = ((bf16[16,48,128]{2,1,0:T(8,128)(2,1)}), bf16[16,48,128]{2,1,0:T(8,128)(2,1)S(1)}, u32[]{:S(2)}, u32[]{:S(2)}) async-start(bf16[16,48,128]{2,1,0:T(8,128)(2,1)} %far_branch.1), calls=%async_computation.4 | async-start | bytes 393216 | tf_op jit(solution)/shard_map/all_to_all | solution.py:373
  209.3 1.4 and_select_fusion.query_seg
  210.6 2.6 %fusion.key_seg = s32[384,1]{1,0:T(8,128)S(1)} fusion(s32[]{:T(128)} %bitcast.21, s32[]{:T(128)S(6)} %sign.29, s32[]{:T(128)} %select_n.101), kind=kLoop, calls=%fused_computation.5 | loop fusion | flops 4992 | bytes 1548 | tf_op jit(solution)/shard_map/jit(_where)/select_n | solution.py:368
  213.3 5.3 %local_branch.1 = (f32[768,192]{1,0:T(8,128)S(1)}, f32[16,192]{1,0:T(8,128)S(1)}, f32[16,192]{1,0:T(8,128)S(1)}) custom-call(bf16[768,192]{1,0:T(8,128)(2,1)S(1)} %copy-done.3, bf16[1536,384]{1,0:T(8,128)(2,1)S(1)} %get-tuple-element.18.kv, s32[384,1]{1,0:T(8,128)S(1)} %fusion.key_seg, s32[1,192]{1,0:T(1,128)S(1)} %and_select_fusion.query_seg), custom_call_target="tpu_custom_call" | custom-call | flops 300000000 | bytes 3000000 | tf_op jit(solution)/shard_map/local_branch/pallas_call | solution.py:187
  218.6 2.0 finish_rows.1
  (45 shorter events, 8.5 us)
Async XLA Ops:
  0.0 118.5 %copy-start = (bf16[1,192,1536]{2,1,0:T(8,128)(2,1)S(1)}, bf16[1,192,1536]{2,1,0:T(8,128)(2,1)}, u32[]{:S(2)}) copy-start(bf16[1,192,1536]{2,1,0:T(8,128)(2,1)} %param.10) | copy-start | bytes 1769476
  0.8 14.8 %collective-permute-start.3 = (bf16[24,768]{1,0:T(8,128)(2,1)S(1)}, bf16[24,768]{1,0:T(8,128)(2,1)S(1)}, u32[]{:S(2)}, u32[]{:S(2)}) collective-permute-start(bf16[24,768]{1,0:T(8,128)(2,1)S(1)} %dynamic-slice_bitcast_fusion.2), channel_id=1, source_target_pairs={{0,449},{1,448},{64,385},{65,384},{128,321},{129,320},{192,257},{1... | collective-permute-start | bytes 110600 | tf_op jit(solution)/shard_map/ppermute | solution.py:286
  13.7 9.6 %collective-permute-start.2 = (bf16[48,768]{1,0:T(8,128)(2,1)S(1)}, bf16[48,768]{1,0:T(8,128)(2,1)S(1)}, u32[]{:S(2)}, u32[]{:S(2)}) collective-permute-start(bf16[48,768]{1,0:T(8,128)(2,1)S(1)} %dynamic-slice_bitcast_fusion), channel_id=1, source_target_pairs={{0,449},{1,448},{64,385},{65,384},{128,321},{129,320},{192,257},{1... | collective-permute-start | bytes 221192 | tf_op jit(solution)/shard_map/ppermute | solution.py:286
  59.7 5.5 %copy-start.4 = (bf16[768,72]{0,1:T(8,128)(2,1)S(1)}, bf16[768,72]{0,1:T(8,128)(2,1)}, u32[]{:S(2)}) copy-start(bf16[768,72]{0,1:T(8,128)(2,1)} %param.14) | copy-start | bytes 331780
  60.8 20.5 %all-to-all-start = ((bf16[16,48,768]{2,1,0:T(8,128)(2,1)}), bf16[16,48,768]{2,1,0:T(8,128)(2,1)}, u32[]{:S(2)}, u32[]{:S(2)}) async-start(bf16[16,48,768]{2,1,0:T(8,128)(2,1)} %broadcast_in_dim.45), calls=%async_computation | async-start | bytes 2359296 | tf_op jit(solution)/shard_map/all_to_all | solution.py:298
  65.3 7.8 %collective-permute-start.1 = (bf16[72,384]{1,0:T(8,128)(2,1)S(1)}, bf16[72,384]{1,0:T(8,128)(2,1)S(1)}, u32[]{:S(2)}, u32[]{:S(2)}) collective-permute-start(bf16[72,384]{1,0:T(8,128)(2,1)S(1)} %dynamic-slice_bitcast_fusion.1), channel_id=1, source_target_pairs={{0,449},{1,448},{64,385},{65,384},{128,321},{129,320},{192,257},{1... | collective-permute-start | bytes 165896 | tf_op jit(solution)/shard_map/ppermute | solution.py:286
  82.7 10.5 %copy-start.6 = (s32[1,32]{1,0:T(1,128)S(1)}, s32[1,32]{1,0:T(1,128)}, u32[]{:S(2)}) copy-start(s32[1,32]{1,0:T(1,128)} %param.16) | copy-start | bytes 388
  82.7 12.9 %copy-start.1 = (s32[1,1,192]{2,1,0:T(1,128)S(1)}, s32[1,1,192]{2,1,0:T(1,128)}, u32[]{:S(2)}) copy-start(s32[1,1,192]{2,1,0:T(1,128)} %param.15) | copy-start | bytes 2308
  82.7 26.5 %all-to-all-start.2 = ((bf16[16,144,384]{2,1,0:T(8,128)(2,1)}), bf16[16,144,384]{2,1,0:T(8,128)(2,1)}, u32[]{:S(2)}, u32[]{:S(2)}) async-start(bf16[16,144,384]{2,1,0:T(8,128)(2,1)} %broadcast_in_dim.47), calls=%async_computation.2 | async-start | bytes 3538944 | tf_op jit(solution)/shard_map/all_to_all | solution.py:298
  87.7 44.5 %collective-permute-start.4 = (bf16[16,96,768]{2,1,0:T(8,128)(2,1)S(1)}, bf16[16,96,768]{2,1,0:T(8,128)(2,1)}, u32[]{:S(2)}, u32[]{:S(2)}) collective-permute-start(bf16[16,96,768]{2,1,0:T(8,128)(2,1)S(1)} %all_to_all.25.far_a), channel_id=1, source_target_pairs={{0,32},{32,0},{1,33},{33,1},{2,34},{34,2},{3,35},{35,3},{4,36},{36... | collective-permute-start | bytes 7077896 | tf_op jit(solution)/shard_map/ppermute | solution.py:294
  95.6 36.5 %collective-permute-start = (bf16[16,48,768]{2,1,0:T(8,128)(2,1)}, bf16[16,48,768]{2,1,0:T(8,128)(2,1)}, u32[]{:S(2)}, u32[]{:S(2)}) collective-permute-start(bf16[16,48,768]{2,1,0:T(8,128)(2,1)} %all-to-all-done.near_a), channel_id=1, source_target_pairs={{0,32},{32,0},{1,33},{33,1},{2,34},{34,2},{3,35},{35,3},{4,36},{36... | collective-permute-start | bytes 3538952 | tf_op jit(solution)/shard_map/ppermute | solution.py:294
  109.2 69.6 %collective-permute-start.7 = (bf16[16,144,384]{2,1,0:T(8,128)(2,1)}, bf16[16,144,384]{2,1,0:T(8,128)(2,1)}, u32[]{:S(2)}, u32[]{:S(2)}) collective-permute-start(bf16[16,144,384]{2,1,0:T(8,128)(2,1)} %all-to-all-done.2), channel_id=1, source_target_pairs={{0,32},{32,0},{1,33},{33,1},{2,34},{34,2},{3,35},{35,3},{4,36},{36... | collective-permute-start | bytes 5308424 | tf_op jit(solution)/shard_map/ppermute | solution.py:294
  120.5 4.4 %copy-start.5 = (s32[1,2]{1,0:T(1,128)S(1)}, s32[1,2]{1,0:T(1,128)}, u32[]{:S(2)}) copy-start(s32[1,2]{1,0:T(1,128)} %param.17) | copy-start | bytes 28
  137.6 38.3 %collective-permute-start.5 = (bf16[192,768]{1,0:T(8,128)(2,1)S(1)}, bf16[192,768]{1,0:T(8,128)(2,1)S(1)}, u32[]{:S(2)}, u32[]{:S(2)}) collective-permute-start(bf16[192,768]{1,0:T(8,128)(2,1)S(1)} %embed_rows.1.own), channel_id=1, source_target_pairs={{0,1},{1,0},{2,3},{3,2},{4,5},{5,4},{6,7},{7,6},{8,9},{9,8},{10,11... | collective-permute-start | bytes 884744 | tf_op jit(solution)/shard_map/ppermute | solution.py:290
  175.9 2.9 %collective-permute-start.6 = (bf16[64,768]{1,0:T(8,128)(2,1)S(1)}, bf16[64,768]{1,0:T(8,128)(2,1)S(1)}, u32[]{:S(2)}, u32[]{:S(2)}) collective-permute-start(bf16[64,768]{1,0:T(8,128)(2,1)S(1)} %constant_dynamic-slice_fusion), channel_id=1, source_target_pairs={{0,2},{2,4},{4,6},{6,8},{8,10},{10,12},{12,14},{14,16},{16,18},{18... | collective-permute-start | bytes 294920 | tf_op jit(solution)/shard_map/ppermute | solution.py:359
  184.9 0.8 copy-start.2
  185.7 27.6 %copy-start.3 = (bf16[768,192]{1,0:T(8,128)(2,1)S(1)}, bf16[768,192]{1,0:T(8,128)(2,1)}, u32[]{:S(2)}) copy-start(bf16[768,192]{1,0:T(8,128)(2,1)} %copy-done.2) | copy-start | bytes 884740
  185.7 16.0 %all-to-all-start.3 = ((bf16[16,128,128]{2,1,0:T(8,128)(2,1)}), bf16[16,128,128]{2,1,0:T(8,128)(2,1)S(1)}, u32[]{:S(2)}, u32[]{:S(2)}) async-start(bf16[16,128,128]{2,1,0:T(8,128)(2,1)} %get-tuple-element.16), calls=%async_computation.3 | async-start | bytes 1048576 | tf_op jit(solution)/shard_map/all_to_all | solution.py:364
  205.7 12.9 %all-to-all-start.4 = ((bf16[16,48,128]{2,1,0:T(8,128)(2,1)}), bf16[16,48,128]{2,1,0:T(8,128)(2,1)S(1)}, u32[]{:S(2)}, u32[]{:S(2)}) async-start(bf16[16,48,128]{2,1,0:T(8,128)(2,1)} %far_branch.1), calls=%async_computation.4 | async-start | bytes 393216 | tf_op jit(solution)/shard_map/all_to_all | solution.py:373

commit v3 on v2

--- a/solution.py
+++ b/solution.py
@@ -14,7 +14,7 @@
 HALF = 64
 TILE_DEV = 192
 SEQ_LEN = 4096
-WINDOW = 384
+WINDOW = 320
 KEY_SLOTS = 80
 QUERY_SLOTS = 48
 LANES = 128
@@ -31,7 +31,8 @@
 I32 = jnp.int32
 VMEM_LIMIT = 48 * 1024 * 1024
 
-CORE, HIGH, RATE, START_ME, COUNT_ME, START_OTHER, COUNT_OTHER, PAIR_START, PAIR_COUNT, BASE = range(10)
+CORE, HIGH, PLANE_ID, RATE, SEGMENT = range(5)
+START_ME, COUNT_ME, START_OTHER, COUNT_OTHER, PAIR_START, PAIR_COUNT = range(5, 11)
 ALL_STARTS = 16
 ALL_COUNTS = 32
 
@@ -50,6 +51,45 @@
 
 def iota(shape, dim):
     return lax.broadcasted_iota(I32, shape, dim)
+
+
+def prepare_kernel(place, counts, dilation, ctx, res, listing, own_ctx, own_res, table):
+    core, high, plane = place[0], place[1], place[2]
+    table[CORE], table[HIGH], table[PLANE_ID] = core, high, plane
+    table[SEGMENT], table[RATE] = dilation[0, 0], dilation[0, 1]
+    start = jnp.int32(0)
+    for p in range(PLANES):
+        first, second = counts[0, 2 * p], counts[0, 2 * p + 1]
+        table[ALL_STARTS + p] = start
+        table[ALL_COUNTS + p] = first + second
+
+        @pl.when(plane == p)
+        def _(first=first, second=second, start=start):
+            table[PAIR_START] = start
+            table[PAIR_COUNT] = first + second
+            table[COUNT_ME] = jnp.where(high == 0, first, second)
+            table[COUNT_OTHER] = jnp.where(high == 0, second, first)
+            table[START_ME] = jnp.where(high == 0, start, start + first)
+            table[START_OTHER] = jnp.where(high == 0, start + first, start)
+
+        start = start + first + second
+    order = (iota((TILE_DEV, TILE_DEV), 0) == listing[0]).astype(BF16)
+    own_ctx[...] = dot_tn(order, ctx[0]).astype(BF16)
+    own_res[...] = dot_tn(order, res[0]).astype(BF16)
+
+
+def prepare(place, counts, dilation, ctx, res, listing):
+    vmem, smem = pl.BlockSpec(memory_space=pltpu.VMEM), pl.BlockSpec(memory_space=pltpu.SMEM)
+    rows = jax.ShapeDtypeStruct((TILE_DEV, D_ENC), BF16)
+    return pl.pallas_call(
+        prepare_kernel,
+        out_shape=(rows, rows, jax.ShapeDtypeStruct((ALL_COUNTS + PLANES,), I32)),
+        in_specs=[smem, smem, smem, vmem, vmem, vmem],
+        out_specs=(vmem, vmem, smem),
+        compiler_params=pltpu.CompilerParams(vmem_limit_bytes=VMEM_LIMIT),
+        cost_estimate=pl.CostEstimate(flops=250_000_000, bytes_accessed=2_400_000, transcendentals=0),
+        name="prepare_rows",
+    )(place, counts, dilation, ctx, res, listing)
 
 
 def embed_kernel(table, ctx, res, near_a, near_b, far_a, far_b, out, w, p, hidden, normed, sems):
@@ -110,8 +150,8 @@
     )(table, ctx, res, near_a, near_b, far_a, far_b)
 
 
-def project_kernel(table, own, partner, halo, qa, qb, payload, q_out, kv_out, spanned):
-    core, rate, base = table[CORE], table[RATE], table[BASE]
+def project_kernel(table, own, partner, qa, qb, payload, q_out, kv_out, spanned):
+    core, rate, base = table[CORE], table[RATE], table[PAIR_START]
 
     def placed(first, count, length):
         lane = iota((WINDOW, length), 1)
@@ -120,8 +160,6 @@
 
     spread = dot_nn(placed(table[START_ME] - base, table[COUNT_ME], TILE_DEV), own[...])
     spread += dot_nn(placed(table[START_OTHER] - base, table[COUNT_OTHER], TILE_DEV), partner[...])
-    halo_at = jnp.where(table[HIGH] == 0, 0, table[PAIR_COUNT])
-    spread += dot_nn(placed(halo_at, HALF, HALF), halo[...])
     spanned[...] = spread.astype(BF16)
     half = D // 2
     lanes_a = pl.ds(pl.multiple_of(core * half, LANES), half)
@@ -140,7 +178,7 @@
     query_rest = jnp.zeros((LANES - HEAD_DIM, TILE_DEV), BF16)
     for h in range(HEADS):
         rows = slice(h * HEAD_DIM, (h + 1) * HEAD_DIM)
-        key_first = table[PAIR_START] - base + ((h - table[PAIR_START]) & (rate - 1))
+        key_first = (h - base) & (rate - 1)
         key_pick = (key_lane == key_slot + key_first).astype(BF16)
         both = jnp.concatenate([kv_out[rows], kv_out[D + h * HEAD_DIM : D + (h + 1) * HEAD_DIM], key_rest], axis=0)
         payload[h, :KEY_SLOTS] = dot_nt(key_pick, both).astype(BF16)
@@ -150,7 +188,7 @@
         payload[h, KEY_SLOTS:] = dot_nt(query_pick, ask).astype(BF16)
 
 
-def project(table, own, partner, halo, qa, qb):
+def project(table, own, partner, qa, qb):
     vmem = pl.BlockSpec(memory_space=pltpu.VMEM)
     return pl.pallas_call(
         project_kernel,
@@ -159,43 +197,61 @@
             jax.ShapeDtypeStruct((D, TILE_DEV), BF16),
             jax.ShapeDtypeStruct((2 * D, WINDOW), BF16),
         ),
+        in_specs=[pl.BlockSpec(memory_space=pltpu.SMEM)] + [vmem] * 4,
+        out_specs=(vmem, vmem, vmem),
+        scratch_shapes=[pltpu.VMEM((WINDOW, D), BF16)],
+        compiler_params=pltpu.CompilerParams(vmem_limit_bytes=VMEM_LIMIT),
+        cost_estimate=pl.CostEstimate(flops=2_000_000_000, bytes_accessed=6_000_000, transcendentals=0),
+        name="project_rows",
+    )(table, own, partner, qa, qb)
+
+
+def local_kernel(table, q, kv, halo, qa, qb, out_sum, out_best, out_total, rim):
+    core, high, start_me = table[CORE], table[HIGH], table[START_ME]
+    half = D // 2
+    halo_a = halo[:, pl.ds(pl.multiple_of(core * half, LANES), half)]
+    halo_b = halo[:, pl.ds(pl.multiple_of((1 - core) * half, LANES), half)]
+    rim[...] = (dot_nt(qa[D:], halo_a) + dot_nt(qb[D:], halo_b)).astype(BF16)
+    length = jnp.full((1, 1), table[SEGMENT], I32).astype(F32)
+
+    def segment(position):
+        return jnp.floor((position.astype(F32) + 0.5) / length)
+
+    query_seg = segment(start_me + iota((1, TILE_DEV), 1))
+    key_at = iota((WINDOW, 1), 0)
+    key_seg = jnp.where(key_at < table[PAIR_COUNT], segment(table[PAIR_START] + key_at), -1.0)
+    rim_first = table[PAIR_START] + jnp.where(high == 0, -HALF, table[PAIR_COUNT])
+    rim_at = rim_first + iota((HALF, 1), 0)
+    rim_seg = jnp.where((rim_at >= 0) & (rim_at < SEQ_LEN), segment(rim_at), -1.0)
+    key_ok, rim_ok = key_seg == query_seg, rim_seg == query_seg
+    for h in range(HEADS):
+        rows = slice(h * HEAD_DIM, (h + 1) * HEAD_DIM)
+        v_rows = slice(D + h * HEAD_DIM, D + (h + 1) * HEAD_DIM)
+        scores = jnp.where(key_ok, dot_tn(kv[rows], q[rows]) * SCALE, BIG_NEGATIVE)
+        rim_scores = jnp.where(rim_ok, dot_tn(rim[rows], q[rows]) * SCALE, BIG_NEGATIVE)
+        best = jnp.maximum(jnp.max(scores, axis=0, keepdims=True), jnp.max(rim_scores, axis=0, keepdims=True))
+        weights, rim_weights = jnp.exp(scores - best), jnp.exp(rim_scores - best)
+        out_best[h : h + 1] = best
+        out_total[h : h + 1] = jnp.sum(weights, axis=0, keepdims=True) + jnp.sum(rim_weights, axis=0, keepdims=True)
+        out_sum[rows] = dot_nn(kv[v_rows], weights.astype(BF16)) + dot_nn(rim[v_rows], rim_weights.astype(BF16))
+
+
+def local_branch(table, q, kv, halo, qa, qb):
+    vmem = pl.BlockSpec(memory_space=pltpu.VMEM)
+    stat = jax.ShapeDtypeStruct((HEADS, TILE_DEV), F32)
+    return pl.pallas_call(
+        local_kernel,
+        out_shape=(jax.ShapeDtypeStruct((D, TILE_DEV), F32), stat, stat),
         in_specs=[pl.BlockSpec(memory_space=pltpu.SMEM)] + [vmem] * 5,
         out_specs=(vmem, vmem, vmem),
-        scratch_shapes=[pltpu.VMEM((WINDOW, D), BF16)],
-        compiler_params=pltpu.CompilerParams(vmem_limit_bytes=VMEM_LIMIT),
-        cost_estimate=pl.CostEstimate(flops=2_000_000_000, bytes_accessed=6_000_000, transcendentals=0),
-        name="project_rows",
-    )(table, own, partner, halo, qa, qb)
-
-
-def local_kernel(q, kv, key_seg, query_seg, out_sum, out_best, out_total):
-    allowed = key_seg[...] == query_seg[...]
-    for h in range(HEADS):
-        rows = slice(h * HEAD_DIM, (h + 1) * HEAD_DIM)
-        scores = dot_tn(kv[rows], q[rows]) * SCALE
-        scores = jnp.where(allowed, scores, BIG_NEGATIVE)
-        best = jnp.max(scores, axis=0, keepdims=True)
-        weights = jnp.exp(scores - best)
-        out_best[h : h + 1] = best
-        out_total[h : h + 1] = jnp.sum(weights, axis=0, keepdims=True)
-        out_sum[rows] = dot_nn(kv[D + h * HEAD_DIM : D + (h + 1) * HEAD_DIM], weights.astype(BF16))
-
-
-def local_branch(q, kv, key_seg, query_seg):
-    vmem = pl.BlockSpec(memory_space=pltpu.VMEM)
-    stat = jax.ShapeDtypeStruct((HEADS, TILE_DEV), F32)
-    return pl.pallas_call(
-        local_kernel,
-        out_shape=(jax.ShapeDtypeStruct((D, TILE_DEV), F32), stat, stat),
-        in_specs=[vmem] * 4,
-        out_specs=(vmem, vmem, vmem),
-        compiler_params=pltpu.CompilerParams(vmem_limit_bytes=VMEM_LIMIT),
-        cost_estimate=pl.CostEstimate(flops=300_000_000, bytes_accessed=3_000_000, transcendentals=1_200_000),
+        scratch_shapes=[pltpu.VMEM((2 * D, HALF), BF16)],
+        compiler_params=pltpu.CompilerParams(vmem_limit_bytes=VMEM_LIMIT),
+        cost_estimate=pl.CostEstimate(flops=600_000_000, bytes_accessed=6_000_000, transcendentals=1_200_000),
         name="local_branch",
-    )(q, kv, key_seg, query_seg)
-
-
-def far_kernel(table, plane, arrived, answer, scores):
+    )(table, q, kv, halo, qa, qb)
+
+
+def far_kernel(table, arrived, answer, scores):
     rate = table[RATE]
     kv = arrived[:, :KEY_SLOTS].reshape(PLANES * KEY_SLOTS, LANES)
     group = 8
@@ -205,7 +261,7 @@
         asks = arrived[n * group : (n + 1) * group, KEY_SLOTS:].reshape(width, LANES)
         best = jnp.full((1, width), BIG_NEGATIVE, F32)
         for p in range(PLANES):
-            phase = (plane[0] - table[ALL_STARTS + p]) & (rate - 1)
+            phase = (table[PLANE_ID] - table[ALL_STARTS + p]) & (rate - 1)
             piece = dot_nt(arrived[p, :KEY_SLOTS], asks) * SCALE
             piece = jnp.where(slot + phase < table[ALL_COUNTS + p], piece, BIG_NEGATIVE)
             scores[p * KEY_SLOTS : (p + 1) * KEY_SLOTS] = piece
@@ -224,18 +280,18 @@
         answer[n * group : (n + 1) * group] = block.T.astype(BF16).reshape(group, QUERY_SLOTS, LANES)
 
 
-def far_branch(table, plane, arrived):
+def far_branch(table, arrived):
     vmem, smem = pl.BlockSpec(memory_space=pltpu.VMEM), pl.BlockSpec(memory_space=pltpu.SMEM)
     return pl.pallas_call(
         far_kernel,
         out_shape=jax.ShapeDtypeStruct((PLANES, QUERY_SLOTS, LANES), BF16),
-        in_specs=[smem, smem, vmem],
+        in_specs=[smem, vmem],
         out_specs=vmem,
         scratch_shapes=[pltpu.VMEM((PLANES * KEY_SLOTS, PLANES // 2 * QUERY_SLOTS), F32)],
         compiler_params=pltpu.CompilerParams(vmem_limit_bytes=VMEM_LIMIT),
         cost_estimate=pl.CostEstimate(flops=500_000_000, bytes_accessed=1_000_000, transcendentals=1_000_000),
         name="far_branch",
-    )(table, plane, arrived)
+    )(table, arrived)
 
 
 def finish_kernel(table, answers, local_sum, local_best, local_total, listing, out, attended):
@@ -258,7 +314,7 @@
         below = jnp.where(live, near * local_total[h : h + 1] + far, 1.0)
         mixed = (near * local_sum[rows] + far * wide[:HEAD_DIM]) / below
         attended[rows] = jnp.where(live, mixed, 0.0).astype(BF16)
-    back = (listing[...] == iota((TILE_DEV, TILE_DEV), 0)).astype(BF16)
+    back = (listing[0] == iota((TILE_DEV, TILE_DEV), 0)).astype(BF16)
     out[0] = dot_nt(back, attended[...]).astype(BF16)
 
 
@@ -295,7 +351,11 @@
 
 
 def over_plane(x):
-    return lax.all_to_all(jnp.broadcast_to(x[None], (PLANES,) + x.shape), PLANE, 0, 0)
+    return lax.all_to_all(x, PLANE, 0, 0)
+
+
+def copies(x):
+    return jnp.broadcast_to(x[None], (PLANES,) + x.shape)
 
 
 def in_order(own, other, high):
@@ -306,72 +366,43 @@
     core = lax.axis_index("core")
     high = lax.axis_index("zhi")
     plane_id = lax.axis_index("y") * lax.axis_size("x") + lax.axis_index("x")
-    block_id = plane_id * 2 + high
-    seg_len, rate = dilation[0, 0], dilation[0, 1]
 
     w_own = lax.dynamic_slice_in_dim(enc_out_w, core * D, D, 0).T
     p_own = lax.dynamic_slice_in_dim(slide_proj, core * D, D, 0).T
     q_own = lax.dynamic_slice_in_dim(qkv_w, core * (D // 2), D // 2, 0).T
-    near_a = over_plane(w_own)
+    near_a = over_plane(copies(w_own))
     w_other = mirrored(w_own)
     p_other = mirrored(p_own)
     q_other = mirrored(q_own)
+    place = jnp.stack([core, high, plane_id]).astype(I32)
+    own_ctx, own_res, table = prepare(place, kept_count, dilation, ctx_in, resid, tissue)
+    far = jnp.concatenate([w_other, in_order(p_own, p_other, high)])
+    far, near_a, own_ctx, own_res, table = lax.optimization_barrier((copies(far), near_a, own_ctx, own_res, table))
+    far_a = over_plane(far)
     near_b = other_core(near_a)
-    far_a = over_plane(jnp.concatenate([w_other, in_order(p_own, p_other, high)]))
+    q_both = copies(in_order(q_own, q_other, high))
+    far_a, near_b, q_both = lax.optimization_barrier((far_a, near_b, q_both))
     far_b = other_core(far_a)
-    q_pair, far_a = lax.optimization_barrier((in_order(q_own, q_other, high), far_a))
-    q_a = over_plane(q_pair)
+    embedded = embed(table, own_ctx, own_res, near_a, near_b, far_a, far_b)
+
+    q_both, embedded = lax.optimization_barrier((q_both, embedded))
+    partner = across(embedded)
+    q_a, partner = lax.optimization_barrier((over_plane(q_both), partner))
     q_b = other_core(q_a)
-
-    counts = kept_count[0]
-    starts = jnp.cumsum(counts) - counts
-    pair_counts = counts.reshape(-1, 2).sum(axis=1)
-    pair_starts = starts.reshape(-1, 2)[:, 0]
-
-    def pick(values, index):
-        return jnp.sum(jnp.where(jnp.arange(values.shape[0]) == index, values, 0))
-
-    other_id = block_id + 1 - 2 * high
-    count_me, start_me = pick(counts, block_id), pick(starts, block_id)
-    count_other, start_other = pick(counts, other_id), pick(starts, other_id)
-    pair_start, pair_count = pick(pair_starts, plane_id), pick(pair_counts, plane_id)
-    base = jnp.where(high == 0, pair_start - HALF, pair_start)
-    scalars = [core, high, rate, start_me, count_me, start_other, count_other, pair_start, pair_count, base]
-    table = jnp.concatenate(
-        [
-            jnp.stack([jnp.asarray(s, I32) for s in scalars]),
-            jnp.zeros((ALL_STARTS - len(scalars),), I32),
-            pair_starts.astype(I32),
-            pair_counts.astype(I32),
-        ]
-    )
-
-    listing = tissue[0, 0]
-    own_ctx = jnp.take(ctx_in[0], listing, axis=0)
-    own_res = jnp.take(resid[0], listing, axis=0)
-    embedded = embed(table, own_ctx, own_res, near_a, near_b, far_a, far_b)
-
-    partner = across(embedded)
-    rim_from = jnp.where(high == 0, count_other - HALF, 0)
+    q_a, q_b = q_a.reshape(3 * D, D // 2), q_b.reshape(3 * D, D // 2)
+    rim_from = jnp.where(high == 0, table[COUNT_OTHER] - HALF, 0)
     rim = lax.dynamic_slice_in_dim(partner, rim_from, HALF, 0)
     halo_pairs = [(p * 2, p * 2 + 2) for p in range(PLANES - 1)]
     halo_pairs += [(p * 2 + 1, p * 2 - 1) for p in range(1, PLANES)]
     halo = lax.ppermute(rim, ("y", "x", "zhi"), halo_pairs)
 
-    payload, q_rows, kv_rows = project(
-        table, embedded, partner, halo, q_a.reshape(3 * D, D // 2), q_b.reshape(3 * D, D // 2)
-    )
+    q_b, halo = lax.optimization_barrier((q_b, halo))
+    payload, q_rows, kv_rows = project(table, embedded, partner, q_a, q_b)
     arrived = lax.all_to_all(payload, PLANE, 0, 0)
-
-    key_pos = base + jnp.arange(WINDOW, dtype=I32)
-    key_ok = (key_pos >= 0) & (key_pos < SEQ_LEN)
-    key_seg = jnp.where(key_ok, key_pos // seg_len, -1)[:, None]
-    query_seg = ((start_me + jnp.arange(TILE_DEV, dtype=I32)) // seg_len)[None, :]
-    local_sum, local_best, local_total = local_branch(q_rows, kv_rows, key_seg, query_seg)
-
-    answer = far_branch(table, jnp.asarray(plane_id, I32).reshape(1), arrived)
+    local_sum, local_best, local_total = local_branch(table, q_rows, kv_rows, halo, q_a, q_b)
+    answer = far_branch(table, arrived)
     answers = lax.all_to_all(answer, PLANE, 0, 0)
-    return finish(table, answers, local_sum, local_best, local_total, listing[None, :])
+    return finish(table, answers, local_sum, local_best, local_total, tissue)
 
 
 def solution(mesh):

time: 223 us -> 187 us (0.84)
  the two profiles are of different devices: /device:TPU:1 before, /device:TPU:98 now
where the time goes in v3:
time: 187 us; the launch traced here: 186 us
  waiting for transfers between devices  69.4 us (37%)
  starting transfers between devices  59.5 us (32%)
  Pallas kernels  25.3 us (14%)
  blocking collectives  17.1 us (9%)
  local copies, waits for them, and re-layouts  13.5 us (7%)
    ppermute x1, waiting for transfers between devices, across(): return lax.ppermute(x, 'zhi', [(0, 1), (1, 0)])  30.2 us
    all_to_all x3, starting transfers between devices, over_plane(): return lax.all_to_all(x, PLANE, 0, 0)  22 us
    ppermute x3, waiting for transfers between devices, mirrored(): return lax.ppermute(x, ('zlo', 'zhi'), pairs)  17.6 us
    all_to_all x1, blocking collectives, on_device(): arrived = lax.all_to_all(payload, PLANE, 0, 0)  17.1 us
    ppermute x3, starting transfers between devices, mirrored(): return lax.ppermute(x, ('zlo', 'zhi'), pairs)  16.3 us
    all_to_all x3, waiting for transfers between devices, over_plane(): return lax.all_to_all(x, PLANE, 0, 0)  13.3 us
    unnamed x38, local copies, waits for them, and re-layouts  8.61 us
    pallas_call x1, Pallas kernels, local_branch(): pl.pallas_call(local_kernel, out_shape=(jax.ShapeDtypeStruct((D, TILE_DEV...  7.9 us
  transfers between devices with their start and end apart: 12, of which 6 were waited for; matrix products, arithmetic and copies ran while one was open for 0% of the time, Pallas kernels for 5%

profile of v3, /device:TPU:98, one launch (start us, length us, event | category | flops | bytes accessed | tf_op | source)
XLA Modules:
  0.0 185.8 jit_solution(14673436374365807369)
XLA Ops:
  1.0 1.1 broadcast_in_dim.7
  2.1 7.5 %all-to-all-start = ((bf16[16,48,768]{2,1,0:T(8,128)(2,1)}), bf16[16,48,768]{2,1,0:T(8,128)(2,1)S(1)}, u32[]{:S(2)}, u32[]{:S(2)}) async-start(bf16[16,48,768]{2,1,0:T(8,128)(2,1)} %broadcast_in_dim.7), calls=%async_computation | async-start | bytes 2359296 | tf_op jit(solution)/shard_map/all_to_all | solution.py:354
  9.6 11.4 %collective-permute-start = (bf16[48,768]{1,0:T(8,128)(2,1)S(1)}, bf16[48,768]{1,0:T(8,128)(2,1)S(1)}, u32[]{:S(2)}, u32[]{:S(2)}) collective-permute-start(bf16[48,768]{1,0:T(8,128)(2,1)S(1)} %dynamic-slice_bitcast_fusion), channel_id=1, source_target_pairs={{0,449},{1,448},{64,385},{65,384},{128,321},{129,320},{192,257},{1... | collective-permute-start | bytes 221192 | tf_op jit(solution)/shard_map/ppermute | solution.py:342
  21.0 1.9 %collective-permute-start.1 = (bf16[24,768]{1,0:T(8,128)(2,1)S(1)}, bf16[24,768]{1,0:T(8,128)(2,1)S(1)}, u32[]{:S(2)}, u32[]{:S(2)}) collective-permute-start(bf16[24,768]{1,0:T(8,128)(2,1)S(1)} %dynamic-slice_bitcast_fusion.2), channel_id=1, source_target_pairs={{0,449},{1,448},{64,385},{65,384},{128,321},{129,320},{192,257},{1... | collective-permute-start | bytes 110600 | tf_op jit(solution)/shard_map/ppermute | solution.py:342
  23.0 1.6 prepare_rows.1
  25.5 7.9 %collective-permute-done.1 = bf16[24,768]{1,0:T(8,128)(2,1)S(1)} collective-permute-done((bf16[24,768]{1,0:T(8,128)(2,1)S(1)}, bf16[24,768]{1,0:T(8,128)(2,1)S(1)}, u32[]{:S(2)}, u32[]{:S(2)}) %collective-permute-start.1) | collective-permute-done | bytes 36896 | tf_op jit(solution)/shard_map/ppermute | solution.py:342
  33.5 1.8 broadcast_in_dim.6
  35.3 7.4 %all-to-all-start.1 = ((bf16[16,96,768]{2,1,0:T(8,128)(2,1)}), bf16[16,96,768]{2,1,0:T(8,128)(2,1)S(1)}, u32[]{:S(2)}, u32[]{:S(2)}) async-start(bf16[16,96,768]{2,1,0:T(8,128)(2,1)} %broadcast_in_dim.6), calls=%async_computation.1 | async-start | bytes 4718592 | tf_op jit(solution)/shard_map/all_to_all | solution.py:354
  42.6 1.9 %collective-permute-start.2 = (bf16[16,48,768]{2,1,0:T(8,128)(2,1)}, bf16[16,48,768]{2,1,0:T(8,128)(2,1)}, u32[]{:S(2)}, u32[]{:S(2)}) collective-permute-start(bf16[16,48,768]{2,1,0:T(8,128)(2,1)} %copy-done.1), channel_id=1, source_target_pairs={{0,32},{32,0},{1,33},{33,1},{2,34},{34,2},{3,35},{35,3},{4,36},{36... | collective-permute-start | bytes 3538952 | tf_op jit(solution)/shard_map/ppermute | solution.py:350
  44.6 3.1 %collective-permute-start.3 = (bf16[72,384]{1,0:T(8,128)(2,1)S(1)}, bf16[72,384]{1,0:T(8,128)(2,1)S(1)}, u32[]{:S(2)}, u32[]{:S(2)}) collective-permute-start(bf16[72,384]{1,0:T(8,128)(2,1)S(1)} %dynamic-slice_bitcast_fusion.1), channel_id=1, source_target_pairs={{0,449},{1,448},{64,385},{65,384},{128,321},{129,320},{192,257},{1... | collective-permute-start | bytes 165896 | tf_op jit(solution)/shard_map/ppermute | solution.py:342
  47.6 9.7 %collective-permute-done.3 = bf16[72,384]{1,0:T(8,128)(2,1)S(1)} collective-permute-done((bf16[72,384]{1,0:T(8,128)(2,1)S(1)}, bf16[72,384]{1,0:T(8,128)(2,1)S(1)}, u32[]{:S(2)}, u32[]{:S(2)}) %collective-permute-start.3) | collective-permute-done | bytes 55328 | tf_op jit(solution)/shard_map/ppermute | solution.py:342
  57.4 13.3 %all-to-all-done.1.far_a = bf16[16,96,768]{2,1,0:T(8,128)(2,1)S(1)} async-done(((bf16[16,96,768]{2,1,0:T(8,128)(2,1)}), bf16[16,96,768]{2,1,0:T(8,128)(2,1)S(1)}, u32[]{:S(2)}, u32[]{:S(2)}) %all-to-all-start.1) | async-done | bytes 2359328 | tf_op jit(solution)/shard_map/all_to_all | solution.py:354
  70.7 1.4 broadcast_in_dim.8
  72.1 1.9 %collective-permute-start.4 = (bf16[16,96,768]{2,1,0:T(8,128)(2,1)S(1)}, bf16[16,96,768]{2,1,0:T(8,128)(2,1)S(1)}, u32[]{:S(2)}, u32[]{:S(2)}) collective-permute-start(bf16[16,96,768]{2,1,0:T(8,128)(2,1)S(1)} %all-to-all-done.1.far_a), channel_id=1, source_target_pairs={{0,32},{32,0},{1,33},{33,1},{2,34},{34,2},{3,35},{35,3},{4,36},{36... | collective-permute-start | bytes 7077896 | tf_op jit(solution)/shard_map/ppermute | solution.py:350
  74.0 4.5 %collective-permute-done.4.far_b = bf16[16,96,768]{2,1,0:T(8,128)(2,1)S(1)} collective-permute-done((bf16[16,96,768]{2,1,0:T(8,128)(2,1)S(1)}, bf16[16,96,768]{2,1,0:T(8,128)(2,1)S(1)}, u32[]{:S(2)}, u32[]{:S(2)}) %collective-permute-start.4) | collective-permute-done | bytes 2359328 | tf_op jit(solution)/shard_map/ppermute | solution.py:350
  78.5 1.4 copy-done.16
  79.9 5.2 %embed_rows.1.own = bf16[192,768]{1,0:T(8,128)(2,1)S(1)} custom-call(s32[48]{0:T(128)S(1)} %get-tuple-element.31.table, bf16[192,1536]{1,0:T(8,128)(2,1)S(1)} %get-tuple-element.35.ctx, bf16[192,1536]{1,0:T(8,128)(2,1)S(1)} %copy-done.6, bf16[16,48,768]{2,1,0:T(8,128)(2,1)S(1)} %copy-done.2, bf16[16,48,768]{2,1,0:T(8,128)(2,1)} %collective-permute-done.2.near_b, ...), custom_call_target="tpu_custom_call" | custom-call | flops 1400000000 | bytes 9000000 | tf_op jit(solution)/shard_map/embed_rows/pallas_call | solution.py:135
  85.1 7.2 %all-to-all-start.2 = ((bf16[16,144,384]{2,1,0:T(8,128)(2,1)}), bf16[16,144,384]{2,1,0:T(8,128)(2,1)S(1)}, u32[]{:S(2)}, u32[]{:S(2)}) async-start(bf16[16,144,384]{2,1,0:T(8,128)(2,1)} %broadcast_in_dim.8), calls=%async_computation.2 | async-start | bytes 3538944 | tf_op jit(solution)/shard_map/all_to_all | solution.py:354
  92.3 7.3 %collective-permute-start.5 = (bf16[192,768]{1,0:T(8,128)(2,1)S(1)}, bf16[192,768]{1,0:T(8,128)(2,1)S(1)}, u32[]{:S(2)}, u32[]{:S(2)}) collective-permute-start(bf16[192,768]{1,0:T(8,128)(2,1)S(1)} %embed_rows.1.own), channel_id=1, source_target_pairs={{0,1},{1,0},{2,3},{3,2},{4,5},{5,4},{6,7},{7,6},{8,9},{9,8},{10,11... | collective-permute-start | bytes 884744 | tf_op jit(solution)/shard_map/ppermute | solution.py:346
  99.5 30.2 %collective-permute-done.5.partner = bf16[192,768]{1,0:T(8,128)(2,1)S(1)} collective-permute-done((bf16[192,768]{1,0:T(8,128)(2,1)S(1)}, bf16[192,768]{1,0:T(8,128)(2,1)S(1)}, u32[]{:S(2)}, u32[]{:S(2)}) %collective-permute-start.5) | collective-permute-done | bytes 294944 | tf_op jit(solution)/shard_map/ppermute | solution.py:346
  129.7 1.9 %collective-permute-start.6 = (bf16[16,144,384]{2,1,0:T(8,128)(2,1)S(1)}, bf16[16,144,384]{2,1,0:T(8,128)(2,1)}, u32[]{:S(2)}, u32[]{:S(2)}) collective-permute-start(bf16[16,144,384]{2,1,0:T(8,128)(2,1)S(1)} %all-to-all-done.2), channel_id=1, source_target_pairs={{0,32},{32,0},{1,33},{33,1},{2,34},{34,2},{3,35},{35,3},{4,36},{36... | collective-permute-start | bytes 5308424 | tf_op jit(solution)/shard_map/ppermute | solution.py:350
  133.6 3.4 %collective-permute-start.7 = (bf16[64,768]{1,0:T(8,128)(2,1)S(1)}, bf16[64,768]{1,0:T(8,128)(2,1)S(1)}, u32[]{:S(2)}, u32[]{:S(2)}) collective-permute-start(bf16[64,768]{1,0:T(8,128)(2,1)S(1)} %constant_dynamic-slice_fusion), channel_id=1, source_target_pairs={{0,2},{2,4},{4,6},{6,8},{8,10},{10,12},{12,14},{14,16},{16,18},{18... | collective-permute-start | bytes 294920 | tf_op jit(solution)/shard_map/ppermute | solution.py:397
  137.0 3.7 %collective-permute-done.7.halo = bf16[64,768]{1,0:T(8,128)(2,1)S(1)} collective-permute-done((bf16[64,768]{1,0:T(8,128)(2,1)S(1)}, bf16[64,768]{1,0:T(8,128)(2,1)S(1)}, u32[]{:S(2)}, u32[]{:S(2)}) %collective-permute-start.7) | collective-permute-done | bytes 98336 | tf_op jit(solution)/shard_map/ppermute | solution.py:397
  140.7 1.0 copy-done.12
  141.7 4.6 %project_rows.1 = (bf16[16,128,128]{2,1,0:T(8,128)(2,1)S(1)}, bf16[768,192]{1,0:T(8,128)(2,1)S(1)}, bf16[1536,320]{1,0:T(8,128)(2,1)S(1)}) custom-call(s32[48]{0:T(128)S(1)} %get-tuple-element.31.table, bf16[192,768]{1,0:T(8,128)(2,1)S(1)} %embed_rows.1.own, bf16[192,768]{1,0:T(8,128)(2,1)S(1)} %copy-done.12, bf16[2304,384]{1,0:T(8,128)(2,1)S(1)} %bitcast.12, ...), custom_call_target="tpu_custom_call" | custom-call | flops 2000000000 | bytes 6000000 | tf_op jit(solution)/shard_map/project_rows/pallas_call | solution.py:193
  147.0 17.1 %all_to_all.25.arrived = bf16[16,128,128]{2,1,0:T(8,128)(2,1)S(1)} all-to-all(bf16[16,128,128]{2,1,0:T(8,128)(2,1)S(1)} %get-tuple-element.44), channel_id=1, replica_groups=mesh['zlo'=8,'core'=2,'y'=4,'x'=4,'zhi'=2] {'y','x'}, dimensions={0} | all-to-all | bytes 1048576 | tf_op jit(solution)/shard_map/all_to_all | solution.py:401
  164.1 4.0 %far_branch.1 = bf16[16,48,128]{2,1,0:T(8,128)(2,1)} custom-call(s32[48]{0:T(128)S(1)} %get-tuple-element.31.table, bf16[16,128,128]{2,1,0:T(8,128)(2,1)S(1)} %all_to_all.25.arrived), custom_call_target="tpu_custom_call" | custom-call | flops 500000000 | bytes 1000000 | tf_op jit(solution)/shard_map/far_branch/pallas_call | solution.py:285
  168.1 4.8 %all-to-all-start.4 = ((bf16[16,48,128]{2,1,0:T(8,128)(2,1)}), bf16[16,48,128]{2,1,0:T(8,128)(2,1)S(1)}, u32[]{:S(2)}, u32[]{:S(2)}) async-start(bf16[16,48,128]{2,1,0:T(8,128)(2,1)} %far_branch.1), calls=%async_computation.4 | async-start | bytes 393216 | tf_op jit(solution)/shard_map/all_to_all | solution.py:404
  172.9 1.0 copy-done.10
  173.9 7.9 %local_branch.1 = (f32[768,192]{1,0:T(8,128)S(1)}, f32[16,192]{1,0:T(8,128)S(1)}, f32[16,192]{1,0:T(8,128)S(1)}) custom-call(s32[48]{0:T(128)S(1)} %get-tuple-element.31.table, bf16[768,192]{1,0:T(8,128)(2,1)S(1)} %copy-done.10, bf16[1536,320]{1,0:T(8,128)(2,1)S(1)} %get-tuple-element.46.kv, bf16[64,768]{1,0:T(8,128)(2,1)S(1)} %collective-permute-done.7.halo, ...), custom_call_target="tpu_custom_call" | custom-call | flops 600000000 | bytes 6000000 | tf_op jit(solution)/shard_map/local_branch/pallas_call | solution.py:242
  182.7 1.1 copy-done.4
  183.9 2.0 %finish_rows.1 = bf16[1,192,768]{2,1,0:T(8,128)(2,1)} custom-call(s32[48]{0:T(128)S(1)} %get-tuple-element.31.table, bf16[16,48,128]{2,1,0:T(8,128)(2,1)S(1)} %all-to-all-done.4.answers, f32[768,192]{1,0:T(8,128)S(1)} %copy-done.4, f32[16,192]{1,0:T(8,128)S(1)} %get-tuple-element.49.local_best, f32[16,192]{1,0:T(8,128)S(1)} %get-tuple-element.50.local_total, ...), custom_call_target="tpu_custom_call" | custom-call | flops 100000000 | bytes 1500000 | tf_op jit(solution)/shard_map/finish_rows/pallas_call | solution.py:323
  (49 shorter events, 4.9 us)
Async XLA Ops:
  0.0 0.9 copy-start
  0.9 20.0 %copy-start.18 = (bf16[1536,24]{0,1:T(8,128)(2,1)S(1)}, bf16[1536,24]{0,1:T(8,128)(2,1)}, u32[]{:S(2)}) copy-start(bf16[1536,24]{0,1:T(8,128)(2,1)} %param.11) | copy-start | bytes 221188
  0.9 22.1 %copy-start.7 = (bf16[1,192,1536]{2,1,0:T(8,128)(2,1)S(1)}, bf16[1,192,1536]{2,1,0:T(8,128)(2,1)}, u32[]{:S(2)}) copy-start(bf16[1,192,1536]{2,1,0:T(8,128)(2,1)} %ctx.1) | copy-start | bytes 1769476
  0.9 22.1 %copy-start.8 = (bf16[1,192,1536]{2,1,0:T(8,128)(2,1)S(1)}, bf16[1,192,1536]{2,1,0:T(8,128)(2,1)}, u32[]{:S(2)}) copy-start(bf16[1,192,1536]{2,1,0:T(8,128)(2,1)} %res.1) | copy-start | bytes 1769476
  0.9 22.0 %copy-start.13 = (s32[1,1,192]{2,1,0:T(1,128)S(1)}, s32[1,1,192]{2,1,0:T(1,128)}, u32[]{:S(2)}) copy-start(s32[1,1,192]{2,1,0:T(1,128)} %listing.3) | copy-start | bytes 2308
  1.0 22.0 %copy-start.14 = (s32[1,32]{1,0:T(1,128)S(1)}, s32[1,32]{1,0:T(1,128)}, u32[]{:S(2)}) copy-start(s32[1,32]{1,0:T(1,128)} %counts.1) | copy-start | bytes 388
  1.0 22.0 %copy-start.15 = (s32[1,2]{1,0:T(1,128)S(1)}, s32[1,2]{1,0:T(1,128)}, u32[]{:S(2)}) copy-start(s32[1,2]{1,0:T(1,128)} %dilation.1) | copy-start | bytes 28
  2.1 31.4 %all-to-all-start = ((bf16[16,48,768]{2,1,0:T(8,128)(2,1)}), bf16[16,48,768]{2,1,0:T(8,128)(2,1)S(1)}, u32[]{:S(2)}, u32[]{:S(2)}) async-start(bf16[16,48,768]{2,1,0:T(8,128)(2,1)} %broadcast_in_dim.7), calls=%async_computation | async-start | bytes 2359296 | tf_op jit(solution)/shard_map/all_to_all | solution.py:354
  9.6 23.9 %collective-permute-start = (bf16[48,768]{1,0:T(8,128)(2,1)S(1)}, bf16[48,768]{1,0:T(8,128)(2,1)S(1)}, u32[]{:S(2)}, u32[]{:S(2)}) collective-permute-start(bf16[48,768]{1,0:T(8,128)(2,1)S(1)} %dynamic-slice_bitcast_fusion), channel_id=1, source_target_pairs={{0,449},{1,448},{64,385},{65,384},{128,321},{129,320},{192,257},{1... | collective-permute-start | bytes 221192 | tf_op jit(solution)/shard_map/ppermute | solution.py:342
  21.0 12.5 %collective-permute-start.1 = (bf16[24,768]{1,0:T(8,128)(2,1)S(1)}, bf16[24,768]{1,0:T(8,128)(2,1)S(1)}, u32[]{:S(2)}, u32[]{:S(2)}) collective-permute-start(bf16[24,768]{1,0:T(8,128)(2,1)S(1)} %dynamic-slice_bitcast_fusion.2), channel_id=1, source_target_pairs={{0,449},{1,448},{64,385},{65,384},{128,321},{129,320},{192,257},{1... | collective-permute-start | bytes 110600 | tf_op jit(solution)/shard_map/ppermute | solution.py:342
  24.7 0.8 copy-start.5
  33.5 1.8 copy-start.1
  35.3 9.3 %copy-start.17 = (bf16[768,72]{0,1:T(8,128)(2,1)S(1)}, bf16[768,72]{0,1:T(8,128)(2,1)}, u32[]{:S(2)}) copy-start(bf16[768,72]{0,1:T(8,128)(2,1)} %param.12) | copy-start | bytes 331780
  35.3 35.4 %all-to-all-start.1 = ((bf16[16,96,768]{2,1,0:T(8,128)(2,1)}), bf16[16,96,768]{2,1,0:T(8,128)(2,1)S(1)}, u32[]{:S(2)}, u32[]{:S(2)}) async-start(bf16[16,96,768]{2,1,0:T(8,128)(2,1)} %broadcast_in_dim.6), calls=%async_computation.1 | async-start | bytes 4718592 | tf_op jit(solution)/shard_map/all_to_all | solution.py:354
  42.6 14.8 %collective-permute-start.2 = (bf16[16,48,768]{2,1,0:T(8,128)(2,1)}, bf16[16,48,768]{2,1,0:T(8,128)(2,1)}, u32[]{:S(2)}, u32[]{:S(2)}) collective-permute-start(bf16[16,48,768]{2,1,0:T(8,128)(2,1)} %copy-done.1), channel_id=1, source_target_pairs={{0,32},{32,0},{1,33},{33,1},{2,34},{34,2},{3,35},{35,3},{4,36},{36... | collective-permute-start | bytes 3538952 | tf_op jit(solution)/shard_map/ppermute | solution.py:350
  44.6 12.8 %collective-permute-start.3 = (bf16[72,384]{1,0:T(8,128)(2,1)S(1)}, bf16[72,384]{1,0:T(8,128)(2,1)S(1)}, u32[]{:S(2)}, u32[]{:S(2)}) collective-permute-start(bf16[72,384]{1,0:T(8,128)(2,1)S(1)} %dynamic-slice_bitcast_fusion.1), channel_id=1, source_target_pairs={{0,449},{1,448},{64,385},{65,384},{128,321},{129,320},{192,257},{1... | collective-permute-start | bytes 165896 | tf_op jit(solution)/shard_map/ppermute | solution.py:342
  70.7 9.2 %copy-start.2 = (bf16[16,48,768]{2,1,0:T(8,128)(2,1)S(1)}, bf16[16,48,768]{2,1,0:T(8,128)(2,1)}, u32[]{:S(2)}) copy-start(bf16[16,48,768]{2,1,0:T(8,128)(2,1)} %copy-done.1) | copy-start | bytes 3538948
  70.7 9.2 %copy-start.6 = (bf16[192,1536]{1,0:T(8,128)(2,1)S(1)}, bf16[192,1536]{1,0:T(8,128)(2,1)}, u32[]{:S(2)}) copy-start(bf16[192,1536]{1,0:T(8,128)(2,1)} %copy-done.5) | copy-start | bytes 1769476
  72.1 6.4 %collective-permute-start.4 = (bf16[16,96,768]{2,1,0:T(8,128)(2,1)S(1)}, bf16[16,96,768]{2,1,0:T(8,128)(2,1)S(1)}, u32[]{:S(2)}, u32[]{:S(2)}) collective-permute-start(bf16[16,96,768]{2,1,0:T(8,128)(2,1)S(1)} %all-to-all-done.1.far_a), channel_id=1, source_target_pairs={{0,32},{32,0},{1,33},{33,1},{2,34},{34,2},{3,35},{35,3},{4,36},{36... | collective-permute-start | bytes 7077896 | tf_op jit(solution)/shard_map/ppermute | solution.py:350
  78.5 1.4 copy-start.16
  85.1 44.6 %all-to-all-start.2 = ((bf16[16,144,384]{2,1,0:T(8,128)(2,1)}), bf16[16,144,384]{2,1,0:T(8,128)(2,1)S(1)}, u32[]{:S(2)}, u32[]{:S(2)}) async-start(bf16[16,144,384]{2,1,0:T(8,128)(2,1)} %broadcast_in_dim.8), calls=%async_computation.2 | async-start | bytes 3538944 | tf_op jit(solution)/shard_map/all_to_all | solution.py:354
  92.3 37.4 %collective-permute-start.5 = (bf16[192,768]{1,0:T(8,128)(2,1)S(1)}, bf16[192,768]{1,0:T(8,128)(2,1)S(1)}, u32[]{:S(2)}, u32[]{:S(2)}) collective-permute-start(bf16[192,768]{1,0:T(8,128)(2,1)S(1)} %embed_rows.1.own), channel_id=1, source_target_pairs={{0,1},{1,0},{2,3},{3,2},{4,5},{5,4},{6,7},{7,6},{8,9},{9,8},{10,11... | collective-permute-start | bytes 884744 | tf_op jit(solution)/shard_map/ppermute | solution.py:346
  129.7 11.0 %collective-permute-start.6 = (bf16[16,144,384]{2,1,0:T(8,128)(2,1)S(1)}, bf16[16,144,384]{2,1,0:T(8,128)(2,1)}, u32[]{:S(2)}, u32[]{:S(2)}) collective-permute-start(bf16[16,144,384]{2,1,0:T(8,128)(2,1)S(1)} %all-to-all-done.2), channel_id=1, source_target_pairs={{0,32},{32,0},{1,33},{33,1},{2,34},{34,2},{3,35},{35,3},{4,36},{36... | collective-permute-start | bytes 5308424 | tf_op jit(solution)/shard_map/ppermute | solution.py:350
  132.9 0.7 copy-start.11
  133.6 7.1 %collective-permute-start.7 = (bf16[64,768]{1,0:T(8,128)(2,1)S(1)}, bf16[64,768]{1,0:T(8,128)(2,1)S(1)}, u32[]{:S(2)}, u32[]{:S(2)}) collective-permute-start(bf16[64,768]{1,0:T(8,128)(2,1)S(1)} %constant_dynamic-slice_fusion), channel_id=1, source_target_pairs={{0,2},{2,4},{4,6},{6,8},{8,10},{10,12},{12,14},{14,16},{16,18},{18... | collective-permute-start | bytes 294920 | tf_op jit(solution)/shard_map/ppermute | solution.py:397
  140.7 1.0 copy-start.12
  146.3 0.7 copy-start.9
  168.1 14.6 %all-to-all-start.4 = ((bf16[16,48,128]{2,1,0:T(8,128)(2,1)}), bf16[16,48,128]{2,1,0:T(8,128)(2,1)S(1)}, u32[]{:S(2)}, u32[]{:S(2)}) async-start(bf16[16,48,128]{2,1,0:T(8,128)(2,1)} %far_branch.1), calls=%async_computation.4 | async-start | bytes 393216 | tf_op jit(solution)/shard_map/all_to_all | solution.py:404
  172.9 1.0 copy-start.10
  181.8 0.9 copy-start.3
  182.7 1.1 copy-start.4

commit v4 on v3

v4 whole, which is shorter than its diff:
```python
import jax
import jax.numpy as jnp
from jax import lax
from jax.experimental import pallas as pl
from jax.experimental.pallas import tpu as pltpu
from jax.sharding import Mesh, PartitionSpec as P

HEADS = 16
HEAD_DIM = 48
D = 768
D_ENC = 1536
HALF = 64
TILE_DEV = 192
SEQ_LEN = 4096
SLOTS = 48
LANES = 128
W_ROWS = 48
P_ROWS = 24
PLANES = 16
PLANE = ("y", "x")
EVERY = ("zlo", "core", "y", "x", "zhi")
NORM_EPS = 1e-06
BIG_NEGATIVE = -1e30
SCALE = HEAD_DIM**-0.5
BF16 = jnp.bfloat16
F32 = jnp.float32
I32 = jnp.int32
VMEM_LIMIT = 48 * 1024 * 1024

CORE, HIGH, PLANE_ID, RATE, SEGMENT, START_ME, COUNT_ME = range(7)
ALL_STARTS = 8
ALL_COUNTS = 40
BLOCKS = 32


def dot_nn(a, b):
    return lax.dot_general(a, b, (((1,), (0,)), ((), ())), preferred_element_type=F32)


def dot_nt(a, b):
    return lax.dot_general(a, b, (((1,), (1,)), ((), ())), preferred_element_type=F32)


def dot_tn(a, b):
    return lax.dot_general(a, b, (((0,), (0,)), ((), ())), preferred_element_type=F32)


def iota(shape, dim):
    return lax.broadcasted_iota(I32, shape, dim)


def call(kernel, name, out_shape, specs, scratch, flops, size, exps=0):
    vmem = pl.BlockSpec(memory_space=pltpu.VMEM)
    smem = pl.BlockSpec(memory_space=pltpu.SMEM)
    hbm = pl.BlockSpec(memory_space=pl.ANY)
    kinds = {"s": smem, "v": vmem, "h": hbm}
    ins, outs = specs.split("-")
    return pl.pallas_call(
        kernel,
        out_shape=tuple(jax.ShapeDtypeStruct(shape, dtype) for shape, dtype in out_shape),
        in_specs=[kinds[c] for c in ins],
        out_specs=tuple(kinds[c] for c in outs),
        scratch_shapes=scratch,
        compiler_params=pltpu.CompilerParams(vmem_limit_bytes=VMEM_LIMIT),
        cost_estimate=pl.CostEstimate(flops=flops, bytes_accessed=size, transcendentals=exps),
        name=name,
    )


def prepare_kernel(place, counts, dilation, ctx, res, listing, own_ctx, own_res, table):
    table[CORE], table[HIGH], table[PLANE_ID] = place[0], place[1], place[2]
    table[RATE], table[SEGMENT] = dilation[0, 1], dilation[0, 0]
    me = place[2] * 2 + place[1]
    start = jnp.int32(0)
    for b in range(BLOCKS):
        count = counts[0, b]
        table[ALL_STARTS + b] = start
        table[ALL_COUNTS + b] = count

        @pl.when(me == b)
        def _(start=start, count=count):
            table[START_ME] = start
            table[COUNT_ME] = count

        start = start + count
    order = (iota((TILE_DEV, TILE_DEV), 0) == listing[0]).astype(BF16)
    own_ctx[...] = dot_tn(order, ctx[0]).astype(BF16)
    own_res[...] = dot_tn(order, res[0]).astype(BF16)


def prepare(*args):
    rows = ((TILE_DEV, D_ENC), BF16)
    shapes = (rows, rows, ((ALL_COUNTS + BLOCKS,), I32))
    return call(prepare_kernel, "prepare_rows", shapes, "sssvvv-vvs", [], 250_000_000, 2_400_000)(*args)


def embed_kernel(table, ctx, res, near_a, near_b, far_a, far_b, out, rims, w, p, hidden, normed, sems):
    core, high = table[CORE], table[HIGH]
    loads = [
        pltpu.make_async_copy(near_a, w.at[core, :, high], sems.at[0]),
        pltpu.make_async_copy(near_b, w.at[1 - core, :, high], sems.at[1]),
        pltpu.make_async_copy(far_a.at[:, :W_ROWS], w.at[core, :, 1 - high], sems.at[2]),
        pltpu.make_async_copy(far_b.at[:, :W_ROWS], w.at[1 - core, :, 1 - high], sems.at[3]),
        pltpu.make_async_copy(far_a.at[:, W_ROWS:], p.at[core], sems.at[4]),
        pltpu.make_async_copy(far_b.at[:, W_ROWS:], p.at[1 - core], sems.at[5]),
    ]
    for load in loads:
        load.start()
    for load in loads[:4]:
        load.wait()
    group = 4
    width = group * 2 * W_ROWS
    total = jnp.zeros((TILE_DEV, 1), F32)
    for n in range(PLANES // group):
        columns = slice(n * width, (n + 1) * width)
        part = res[:, columns].astype(F32)
        for half in range(2):
            block = w[half, n * group : (n + 1) * group].reshape(width, D)
            part += dot_nt(ctx[:, half * D : (half + 1) * D], block)
        hidden[:, columns] = part
        total += jnp.sum(part, axis=1, keepdims=True)
    center = hidden[...] - total / D_ENC
    spread = jnp.sum(center * center, axis=1, keepdims=True) / D_ENC
    normed[...] = (center * lax.rsqrt(spread + NORM_EPS)).astype(BF16)
    for load in loads[4:]:
        load.wait()
    for n in range(2):
        rows = slice(n * PLANES // 2, (n + 1) * PLANES // 2)
        part = dot_nt(normed[:, :D], p[0, rows].reshape(D // 2, D))
        part += dot_nt(normed[:, D:], p[1, rows].reshape(D // 2, D))
        out[:, n * D // 2 : (n + 1) * D // 2] = part.astype(BF16)
    lane = iota((HALF, TILE_DEV), 1)
    pick = (lane == iota((HALF, TILE_DEV), 0) + (table[COUNT_ME] - HALF)).astype(BF16)
    rims[:HALF] = dot_nn(pick, out[...]).astype(BF16)
    rims[HALF:] = out[:HALF]


def embed(*args):
    scratch = [
        pltpu.VMEM((2, PLANES, 2, W_ROWS, D), BF16),
        pltpu.VMEM((2, PLANES, 2 * P_ROWS, D), BF16),
        pltpu.VMEM((TILE_DEV, D_ENC), F32),
        pltpu.VMEM((TILE_DEV, D_ENC), BF16),
        pltpu.SemaphoreType.DMA((6,)),
    ]
    shapes = (((TILE_DEV, D), BF16), ((2 * HALF, D), BF16))
    return call(embed_kernel, "embed_rows", shapes, "svvhhhh-vv", scratch, 1_400_000_000, 9_000_000)(*args)


def halves(table, ref, width):
    core = table[CORE]
    first = ref[:, pl.ds(pl.multiple_of(core * width, LANES), width)]
    second = ref[:, pl.ds(pl.multiple_of((1 - core) * width, LANES), width)]
    return first, second


def project_kernel(table, own, q_a, q_b, payload, q_out, kv_out):
    rate, start_me = table[RATE], table[START_ME]
    first, second = halves(table, own, D // 2)
    q_out[...] = (dot_nt(q_a[:D], first) + dot_nt(q_b[:D], second)).astype(BF16)
    for n in range(2):
        rows = slice((n + 1) * D, (n + 2) * D)
        kv_out[n * D : (n + 1) * D] = (dot_nt(q_a[rows], first) + dot_nt(q_b[rows], second)).astype(BF16)
    slot = iota((SLOTS, TILE_DEV), 0) * rate
    lane = iota((SLOTS, TILE_DEV), 1)
    key_rest = jnp.zeros((LANES - 2 * HEAD_DIM, TILE_DEV), BF16)
    query_rest = jnp.zeros((LANES - HEAD_DIM, TILE_DEV), BF16)
    for h in range(HEADS):
        rows = slice(h * HEAD_DIM, (h + 1) * HEAD_DIM)
        pick = (lane == slot + ((h - start_me) & (rate - 1))).astype(BF16)
        both = jnp.concatenate([kv_out[rows], kv_out[D + h * HEAD_DIM : D + (h + 1) * HEAD_DIM], key_rest], axis=0)
        ask = jnp.concatenate([q_out[rows], query_rest], axis=0)
        payload[h, :SLOTS] = dot_nt(pick, both).astype(BF16)
        payload[h, SLOTS:] = dot_nt(pick, ask).astype(BF16)


def project(*args):
    shapes = (((HEADS, 2 * SLOTS, LANES), BF16), ((D, TILE_DEV), BF16), ((2 * D, TILE_DEV), BF16))
    return call(project_kernel, "project_rows", shapes, "svvv-vvv", [], 1_000_000_000, 5_000_000)(*args)


def pack_kernel(arrived, out):
    rows = arrived[:, :SLOTS].reshape(PLANES * SLOTS, LANES)
    out[...] = rows.T[: 2 * HEAD_DIM]


def pack(*args):
    shapes = (((2 * HEAD_DIM, PLANES * SLOTS), BF16),)
    return call(pack_kernel, "pack_keys", shapes, "v-v", [], 1_000_000, 500_000)(*args)[0]


def local_kernel(table, q, kv, before, after, q_a, q_b, out_sum, out_best, out_total, rims, rim):
    start_me, count_me = table[START_ME], table[COUNT_ME]
    rims[:HALF] = before[...]
    rims[HALF:] = after[...]
    first, second = halves(table, rims, D // 2)
    rim[...] = (dot_nt(q_a[D:], first) + dot_nt(q_b[D:], second)).astype(BF16)
    length = jnp.full((1, 1), table[SEGMENT], I32).astype(F32)

    def segment(position):
        return jnp.floor((position.astype(F32) + 0.5) / length)

    query_seg = segment(start_me + iota((1, TILE_DEV), 1))
    key_at = iota((TILE_DEV, 1), 0)
    key_seg = jnp.where(key_at < count_me, segment(start_me + key_at), -1.0)
    rim_id = iota((2 * HALF, 1), 0)
    rim_at = start_me + jnp.where(rim_id < HALF, rim_id - HALF, rim_id - HALF + count_me)
    rim_seg = jnp.where((rim_at >= 0) & (rim_at < SEQ_LEN), segment(rim_at), -1.0)
    key_ok, rim_ok = key_seg == query_seg, rim_seg == query_seg
    for h in range(HEADS):
        rows = slice(h * HEAD_DIM, (h + 1) * HEAD_DIM)
        v_rows = slice(D + h * HEAD_DIM, D + (h + 1) * HEAD_DIM)
        scores = jnp.where(key_ok, dot_tn(kv[rows], q[rows]) * SCALE, BIG_NEGATIVE)
        rim_scores = jnp.where(rim_ok, dot_tn(rim[rows], q[rows]) * SCALE, BIG_NEGATIVE)
        best = jnp.maximum(jnp.max(scores, axis=0, keepdims=True), jnp.max(rim_scores, axis=0, keepdims=True))
        weights, rim_weights = jnp.exp(scores - best), jnp.exp(rim_scores - best)
        out_best[h : h + 1] = best
        out_total[h : h + 1] = jnp.sum(weights, axis=0, keepdims=True) + jnp.sum(rim_weights, axis=0, keepdims=True)
        out_sum[rows] = dot_nn(kv[v_rows], weights.astype(BF16)) + dot_nn(rim[v_rows], rim_weights.astype(BF16))


def local_branch(*args):
    stat = ((HEADS, TILE_DEV), F32)
    shapes = (((D, TILE_DEV), F32), stat, stat)
    scratch = [pltpu.VMEM((2 * HALF, D), BF16), pltpu.VMEM((2 * D, 2 * HALF), BF16)]
    return call(local_kernel, "local_branch", shapes, "svvvvvv-vvv", scratch, 600_000_000, 5_000_000, 1_000_000)(*args)


def far_scores(table, high, keys, asks, scores):
    rate = table[RATE]
    slot = iota((SLOTS, asks.shape[0]), 0) * rate
    best = jnp.full((1, asks.shape[0]), BIG_NEGATIVE, F32)
    for p in range(PLANES):
        block = 2 * p + high
        phase = (table[PLANE_ID] - table[ALL_STARTS + block]) & (rate - 1)
        piece = dot_nt(keys[p * SLOTS : (p + 1) * SLOTS], asks) * SCALE
        piece = jnp.where(slot + phase < table[ALL_COUNTS + block], piece, BIG_NEGATIVE)
        scores[p * SLOTS : (p + 1) * SLOTS] = piece
        best = jnp.maximum(best, jnp.max(piece, axis=0, keepdims=True))
    return best


FAR_GROUP = 8
FAR_WIDTH = FAR_GROUP * SLOTS


def far_own_kernel(table, arrived, out_sum, out_best, out_total, scores):
    keys = arrived[:, :SLOTS].reshape(PLANES * SLOTS, LANES)
    for n in range(PLANES // FAR_GROUP):
        lanes = slice(n * FAR_WIDTH, (n + 1) * FAR_WIDTH)
        asks = arrived[n * FAR_GROUP : (n + 1) * FAR_GROUP, SLOTS:].reshape(FAR_WIDTH, LANES)
        best = far_scores(table, table[HIGH], keys, asks, scores)
        weights = jnp.exp(scores[...] - best)
        out_best[:, lanes] = best
        out_total[:, lanes] = jnp.sum(weights, axis=0, keepdims=True)
        out_sum[:, lanes] = dot_tn(keys, weights.astype(BF16))[HEAD_DIM : 2 * HEAD_DIM]


def far_own(*args):
    width = PLANES * SLOTS
    shapes = (((HEAD_DIM, width), F32), ((1, width), F32), ((1, width), F32))
    scratch = [pltpu.VMEM((width, FAR_WIDTH), F32)]
    return call(far_own_kernel, "far_own", shapes, "sv-vvv", scratch, 300_000_000, 700_000, 600_000)(*args)


def far_rest_kernel(table, arrived, other, own_sum, own_best, own_total, answer, scores):
    other_t = other[...]
    keys = other_t.T
    values = other_t[HEAD_DIM:]
    for n in range(PLANES // FAR_GROUP):
        lanes = slice(n * FAR_WIDTH, (n + 1) * FAR_WIDTH)
        asks = arrived[n * FAR_GROUP : (n + 1) * FAR_GROUP, SLOTS:].reshape(FAR_WIDTH, LANES)[:, : 2 * HEAD_DIM]
        best_o = own_best[:, lanes]
        best = jnp.maximum(best_o, far_scores(table, 1 - table[HIGH], keys, asks, scores))
        weights = jnp.exp(scores[...] - best)
        scale_o = jnp.exp(best_o - best)
        total = jnp.sum(weights, axis=0, keepdims=True) + scale_o * own_total[:, lanes]
        summed = dot_nn(values, weights.astype(BF16)) + scale_o * own_sum[:, lanes]
        shared = summed / total
        log_all = best + jnp.log(total)
        log_a = log_all.astype(BF16).astype(F32)
        log_b = (log_all - log_a).astype(BF16).astype(F32)
        log_c = log_all - log_a - log_b
        row = iota((LANES - HEAD_DIM, FAR_WIDTH), 0)
        tail = jnp.where(row == 0, log_a, jnp.where(row == 1, log_b, jnp.where(row == 2, log_c, 0.0)))
        block = jnp.concatenate([shared, tail], axis=0)
        answer[n * FAR_GROUP : (n + 1) * FAR_GROUP] = block.T.astype(BF16).reshape(FAR_GROUP, SLOTS, LANES)


def far_rest(*args):
    shapes = (((PLANES, SLOTS, LANES), BF16),)
    scratch = [pltpu.VMEM((PLANES * SLOTS, FAR_WIDTH), F32)]
    return call(far_rest_kernel, "far_rest", shapes, "svvvvv-v", scratch, 300_000_000, 1_000_000, 600_000)(*args)[0]


def finish_kernel(table, answers, local_sum, local_best, local_total, listing, out, attended):
    rate = table[RATE]
    slot = iota((SLOTS, TILE_DEV), 0) * rate
    lane = iota((SLOTS, TILE_DEV), 1)
    row = iota((1, TILE_DEV), 1)
    live = row < table[COUNT_ME]
    for h in range(HEADS):
        rows = slice(h * HEAD_DIM, (h + 1) * HEAD_DIM)
        phase = (h - table[START_ME]) & (rate - 1)
        pick = (lane == slot + phase).astype(BF16)
        wide = dot_tn(answers[h], pick)
        log_all = wide[HEAD_DIM : HEAD_DIM + 1] + wide[HEAD_DIM + 1 : HEAD_DIM + 2] + wide[HEAD_DIM + 2 : HEAD_DIM + 3]
        log_all = jnp.where((row & (rate - 1)) == phase, log_all, BIG_NEGATIVE)
        best = local_best[h : h + 1]
        joint = jnp.maximum(best, log_all)
        near = jnp.exp(best - joint)
        far = jnp.exp(log_all - joint)
        below = jnp.where(live, near * local_total[h : h + 1] + far, 1.0)
        mixed = (near * local_sum[rows] + far * wide[:HEAD_DIM]) / below
        attended[rows] = jnp.where(live, mixed, 0.0).astype(BF16)
    back = (listing[0] == iota((TILE_DEV, TILE_DEV), 0)).astype(BF16)
    out[0] = dot_nt(back, attended[...]).astype(BF16)


def finish(*args):
    shapes = (((1, TILE_DEV, D), BF16),)
    scratch = [pltpu.VMEM((D, TILE_DEV), BF16)]
    return call(finish_kernel, "finish_rows", shapes, "svvvvv-v", scratch, 100_000_000, 1_500_000, 10_000)(*args)[0]


def mirrored(x):
    z_low = lax.axis_size("zlo")
    pairs = [
        (low * 2 + high, (z_low - 1 - low) * 2 + (1 - high))
        for low in range(z_low)
        for high in range(2)
    ]
    return lax.ppermute(x, ("zlo", "zhi"), pairs)


def across(x):
    return lax.ppermute(x, "zhi", [(0, 1), (1, 0)])


def rank(z, core, plane):
    z_low = lax.axis_size("zlo")
    return ((z % z_low * 2 + core) * PLANES + plane) * 2 + z // z_low


def all_places():
    z_size = 2 * lax.axis_size("zlo")
    return [(z, core, plane) for z in range(z_size) for core in range(2) for plane in range(PLANES)]


def toward(z, core):
    z_size = 2 * lax.axis_size("zlo")
    step = z_size // 4
    return (z + (step if core == 0 else -step)) % z_size


def quarter_way(x):
    pairs = [(rank(z, core, plane), rank(toward(z, core), core, plane)) for z, core, plane in all_places()]
    return lax.ppermute(x, EVERY, pairs)


def to_next(x, sign):
    pairs = []
    z_low = lax.axis_size("zlo")
    for z, core, plane in all_places():
        half_way = toward(z, core)
        block = 2 * plane + z // z_low + sign
        if 0 <= block < 2 * PLANES:
            target = rank(z % z_low + z_low * (block % 2), core, block // 2)
            pairs.append((rank(half_way, core, plane), target))
    return lax.ppermute(x, EVERY, pairs)


def other_core(x):
    return lax.ppermute(x, "core", [(0, 1), (1, 0)])


def over_plane(x):
    return lax.all_to_all(x, PLANE, 0, 0)


def hold(*values):
    return lax.optimization_barrier(values)


def copies(x):
    return jnp.broadcast_to(x[None], (PLANES,) + x.shape)


def in_order(own, other, high):
    return jnp.where(high == 0, jnp.concatenate([own, other]), jnp.concatenate([other, own]))


def on_device(ctx_in, resid, enc_out_w, slide_proj, qkv_w, tissue, kept_count, dilation):
    core = lax.axis_index("core")
    high = lax.axis_index("zhi")
    plane_id = lax.axis_index("y") * lax.axis_size("x") + lax.axis_index("x")

    w_own = lax.dynamic_slice_in_dim(enc_out_w, core * D, D, 0).T
    p_own = lax.dynamic_slice_in_dim(slide_proj, core * D, D, 0).T
    q_own = lax.dynamic_slice_in_dim(qkv_w, core * (D // 2), D // 2, 0).T
    near_a = over_plane(copies(w_own))
    w_other = mirrored(w_own)
    p_other = mirrored(p_own)
    q_other = mirrored(q_own)
    place = jnp.stack([core, high, plane_id]).astype(I32)
    own_ctx, own_res, table = prepare(place, kept_count, dilation, ctx_in, resid, tissue)
    far = jnp.concatenate([w_other, in_order(p_own, p_other, high)])
    far, near_a, own_ctx, own_res, table = hold(copies(far), near_a, own_ctx, own_res, table)
    far_a = over_plane(far)
    near_b = other_core(near_a)
    q_both = copies(in_order(q_own, q_other, high))
    far_a, near_b, q_both = hold(far_a, near_b, q_both)
    q_a = over_plane(q_both)
    far_b = other_core(far_a)
    embedded, rims = embed(table, own_ctx, own_res, near_a, near_b, far_a, far_b)
    rims = quarter_way(rims)
    q_a, embedded, rims = hold(q_a, embedded, rims)
    before, after = to_next(rims[:HALF], 1), to_next(rims[HALF:], -1)
    q_b = other_core(q_a)
    q_a, q_b = q_a.reshape(3 * D, D // 2), q_b.reshape(3 * D, D // 2)
    payload, q_rows, kv_rows = project(table, embedded, q_a, q_b)
    arrived = lax.all_to_all(payload, PLANE, 0, 0)
    other = across(pack(arrived))
    own_sum, own_best, own_total = far_own(table, arrived)
    local_sum, local_best, local_total = local_branch(table, q_rows, kv_rows, before, after, q_a, q_b)
    other, own_sum, local_sum = hold(other, own_sum, local_sum)
    answer = far_rest(table, arrived, other, own_sum, own_best, own_total)
    answers = lax.all_to_all(answer, PLANE, 0, 0)
    return finish(table, answers, local_sum, local_best, local_total, tissue)


def solution(mesh):
    devices = mesh.devices.reshape(-1, 2, 4, 4, 2)
    split = Mesh(devices, ("zlo", "core", "y", "x", "zhi"))
    slide, seq = ("zlo", "core"), ("y", "x", "zhi")
    return jax.shard_map(
        on_device,
        mesh=split,
        in_specs=(
            P(slide, seq, None),
            P(slide, seq, None),
            P(None, seq),
            P(None, seq),
            P(None, seq),
            P(slide, seq, None),
            P(slide, None),
            P(slide, None),
        ),
        out_specs=P(slide, seq, None),
        check_vma=False,
    )
```

time: 187 us -> 190 us (1.016)
  the two profiles are of different devices: /device:TPU:98 before, /device:TPU:1 now
where the time goes in v4:
time: 190 us; the launch traced here: 189 us
  starting transfers between devices  89.3 us (47%)
  waiting for transfers between devices  31.6 us (17%)
  blocking collectives  27.8 us (15%)
  Pallas kernels  23.6 us (12%)
  local copies, waits for them, and re-layouts  16 us (8%)
    all_to_all x1, blocking collectives, on_device(): answers = lax.all_to_all(answer, PLANE, 0, 0)  27.8 us
    all_to_all x3, waiting for transfers between devices, over_plane(): return lax.all_to_all(x, PLANE, 0, 0)  21.2 us
    ppermute x3, starting transfers between devices, mirrored(): return lax.ppermute(x, ('zlo', 'zhi'), pairs)  19.7 us
    all_to_all x3, starting transfers between devices, over_plane(): return lax.all_to_all(x, PLANE, 0, 0)  18.1 us
    ppermute x3, starting transfers between devices, other_core(): return lax.ppermute(x, 'core', [(0, 1), (1, 0)])  17.4 us
    unnamed x40, local copies, waits for them, and re-layouts  10.1 us
    ppermute x1, starting transfers between devices, quarter_way(): return lax.ppermute(x, EVERY, pairs)  9.92 us
    ppermute x1, starting transfers between devices, across(): return lax.ppermute(x, 'zhi', [(0, 1), (1, 0)])  9.5 us
  transfers between devices with their start and end apart: 14, of which 7 were waited for; matrix products, arithmetic and copies ran while one was open for 1% of the time, Pallas kernels for 8%

profile of v4, /device:TPU:1, one launch (start us, length us, event | category | flops | bytes accessed | tf_op | source)
XLA Modules:
  0.0 188.7 jit_solution(5539662532479300913)
XLA Ops:
  2.1 7.6 %all-to-all-start = ((bf16[16,48,768]{2,1,0:T(8,128)(2,1)}), bf16[16,48,768]{2,1,0:T(8,128)(2,1)S(1)}, u32[]{:S(2)}, u32[]{:S(2)}) async-start(bf16[16,48,768]{2,1,0:T(8,128)(2,1)} %broadcast_in_dim.7), calls=%async_computation | async-start | bytes 2359296 | tf_op jit(solution)/shard_map/all_to_all | solution.py:378
  9.7 11.1 %collective-permute-start = (bf16[48,768]{1,0:T(8,128)(2,1)S(1)}, bf16[48,768]{1,0:T(8,128)(2,1)S(1)}, u32[]{:S(2)}, u32[]{:S(2)}) collective-permute-start(bf16[48,768]{1,0:T(8,128)(2,1)S(1)} %dynamic-slice_bitcast_fusion), channel_id=1, source_target_pairs={{0,449},{1,448},{64,385},{65,384},{128,321},{129,320},{192,257},{1... | collective-permute-start | bytes 221192 | tf_op jit(solution)/shard_map/ppermute | solution.py:333
  20.8 1.9 %collective-permute-start.1 = (bf16[24,768]{1,0:T(8,128)(2,1)S(1)}, bf16[24,768]{1,0:T(8,128)(2,1)S(1)}, u32[]{:S(2)}, u32[]{:S(2)}) collective-permute-start(bf16[24,768]{1,0:T(8,128)(2,1)S(1)} %dynamic-slice_bitcast_fusion.2), channel_id=1, source_target_pairs={{0,449},{1,448},{64,385},{65,384},{128,321},{129,320},{192,257},{1... | collective-permute-start | bytes 110600 | tf_op jit(solution)/shard_map/ppermute | solution.py:333
  22.9 1.5 prepare_rows.1
  26.2 2.4 %collective-permute-done.1 = bf16[24,768]{1,0:T(8,128)(2,1)S(1)} collective-permute-done((bf16[24,768]{1,0:T(8,128)(2,1)S(1)}, bf16[24,768]{1,0:T(8,128)(2,1)S(1)}, u32[]{:S(2)}, u32[]{:S(2)}) %collective-permute-start.1) | collective-permute-done | bytes 36896 | tf_op jit(solution)/shard_map/ppermute | solution.py:333
  28.7 1.7 broadcast_in_dim.6
  30.3 6.8 %all-to-all-start.1 = ((bf16[16,96,768]{2,1,0:T(8,128)(2,1)}), bf16[16,96,768]{2,1,0:T(8,128)(2,1)}, u32[]{:S(2)}, u32[]{:S(2)}) async-start(bf16[16,96,768]{2,1,0:T(8,128)(2,1)} %broadcast_in_dim.6), calls=%async_computation.1 | async-start | bytes 4718592 | tf_op jit(solution)/shard_map/all_to_all | solution.py:378
  37.1 5.4 %collective-permute-start.2 = (bf16[16,48,768]{2,1,0:T(8,128)(2,1)S(1)}, bf16[16,48,768]{2,1,0:T(8,128)(2,1)S(1)}, u32[]{:S(2)}, u32[]{:S(2)}) collective-permute-start(bf16[16,48,768]{2,1,0:T(8,128)(2,1)S(1)} %all-to-all-done.near_a), channel_id=1, source_target_pairs={{0,32},{32,0},{1,33},{33,1},{2,34},{34,2},{3,35},{35,3},{4,36},{36... | collective-permute-start | bytes 3538952 | tf_op jit(solution)/shard_map/ppermute | solution.py:374
  42.5 6.6 %collective-permute-start.3 = (bf16[72,384]{1,0:T(8,128)(2,1)S(1)}, bf16[72,384]{1,0:T(8,128)(2,1)S(1)}, u32[]{:S(2)}, u32[]{:S(2)}) collective-permute-start(bf16[72,384]{1,0:T(8,128)(2,1)S(1)} %dynamic-slice_bitcast_fusion.1), channel_id=1, source_target_pairs={{0,449},{1,448},{64,385},{65,384},{128,321},{129,320},{192,257},{1... | collective-permute-start | bytes 165896 | tf_op jit(solution)/shard_map/ppermute | solution.py:333
  49.2 3.5 %collective-permute-done.3 = bf16[72,384]{1,0:T(8,128)(2,1)S(1)} collective-permute-done((bf16[72,384]{1,0:T(8,128)(2,1)S(1)}, bf16[72,384]{1,0:T(8,128)(2,1)S(1)}, u32[]{:S(2)}, u32[]{:S(2)}) %collective-permute-start.3) | collective-permute-done | bytes 55328 | tf_op jit(solution)/shard_map/ppermute | solution.py:333
  52.7 12.1 %all-to-all-done.1.far_a = bf16[16,96,768]{2,1,0:T(8,128)(2,1)} async-done(((bf16[16,96,768]{2,1,0:T(8,128)(2,1)}), bf16[16,96,768]{2,1,0:T(8,128)(2,1)}, u32[]{:S(2)}, u32[]{:S(2)}) %all-to-all-start.1) | async-done | bytes 2359328 | tf_op jit(solution)/shard_map/all_to_all | solution.py:378
  64.8 1.4 broadcast_in_dim.8
  66.2 8.4 %collective-permute-start.4 = (bf16[16,96,768]{2,1,0:T(8,128)(2,1)}, bf16[16,96,768]{2,1,0:T(8,128)(2,1)}, u32[]{:S(2)}, u32[]{:S(2)}) collective-permute-start(bf16[16,96,768]{2,1,0:T(8,128)(2,1)} %all-to-all-done.1.far_a), channel_id=1, source_target_pairs={{0,32},{32,0},{1,33},{33,1},{2,34},{34,2},{3,35},{35,3},{4,36},{36... | collective-permute-start | bytes 7077896 | tf_op jit(solution)/shard_map/ppermute | solution.py:374
  74.6 3.7 %all-to-all-start.2 = ((bf16[16,144,384]{2,1,0:T(8,128)(2,1)}), bf16[16,144,384]{2,1,0:T(8,128)(2,1)S(1)}, u32[]{:S(2)}, u32[]{:S(2)}) async-start(bf16[16,144,384]{2,1,0:T(8,128)(2,1)} %broadcast_in_dim.8), calls=%async_computation.2 | async-start | bytes 3538944 | tf_op jit(solution)/shard_map/all_to_all | solution.py:378
  79.1 1.3 copy-done.4
  82.5 5.4 %embed_rows.1 = (bf16[192,768]{1,0:T(8,128)(2,1)S(1)}, bf16[128,768]{1,0:T(8,128)(2,1)S(1)}) custom-call(s32[72]{0:T(128)S(1)} %get-tuple-element.36.table, bf16[192,1536]{1,0:T(8,128)(2,1)S(1)} %copy-done.6, bf16[192,1536]{1,0:T(8,128)(2,1)S(1)} %copy-done.8, bf16[16,48,768]{2,1,0:T(8,128)(2,1)S(1)} %all-to-all-done.near_a, ...), custom_call_target="tpu_custom_call" | custom-call | flops 1400000000 | bytes 9000000 | tf_op jit(solution)/shard_map/embed_rows/pallas_call | solution.py:147
  88.6 9.9 %collective-permute-start.5 = (bf16[128,768]{1,0:T(8,128)(2,1)S(1)}, bf16[128,768]{1,0:T(8,128)(2,1)S(1)}, u32[]{:S(2)}, u32[]{:S(2)}) collective-permute-start(bf16[128,768]{1,0:T(8,128)(2,1)S(1)} %get-tuple-element.45), channel_id=1, source_target_pairs={{0,256},{2,258},{4,260},{6,262},{8,264},{10,266},{12,268},{14,270}... | collective-permute-start | bytes 589832 | tf_op jit(solution)/shard_map/ppermute | solution.py:358
  98.6 9.1 %all-to-all-done.2 = bf16[16,144,384]{2,1,0:T(8,128)(2,1)S(1)} async-done(((bf16[16,144,384]{2,1,0:T(8,128)(2,1)}), bf16[16,144,384]{2,1,0:T(8,128)(2,1)S(1)}, u32[]{:S(2)}, u32[]{:S(2)}) %all-to-all-start.2) | async-done | bytes 1769504 | tf_op jit(solution)/shard_map/all_to_all | solution.py:378
  108.1 3.6 %collective-permute-start.6 = (bf16[16,144,384]{2,1,0:T(8,128)(2,1)S(1)}, bf16[16,144,384]{2,1,0:T(8,128)(2,1)S(1)}, u32[]{:S(2)}, u32[]{:S(2)}) collective-permute-start(bf16[16,144,384]{2,1,0:T(8,128)(2,1)S(1)} %all-to-all-done.2), channel_id=1, source_target_pairs={{0,32},{32,0},{1,33},{33,1},{2,34},{34,2},{3,35},{35,3},{4,36},{36... | collective-permute-start | bytes 5308424 | tf_op jit(solution)/shard_map/ppermute | solution.py:374
  111.7 3.3 %collective-permute-done.6 = bf16[16,144,384]{2,1,0:T(8,128)(2,1)S(1)} collective-permute-done((bf16[16,144,384]{2,1,0:T(8,128)(2,1)S(1)}, bf16[16,144,384]{2,1,0:T(8,128)(2,1)S(1)}, u32[]{:S(2)}, u32[]{:S(2)}) %collective-permute-start.6) | collective-permute-done | bytes 1769504 | tf_op jit(solution)/shard_map/ppermute | solution.py:374
  116.2 2.8 %project_rows.1 = (bf16[16,96,128]{2,1,0:T(8,128)(2,1)S(1)}, bf16[768,192]{1,0:T(8,128)(2,1)S(1)}, bf16[1536,192]{1,0:T(8,128)(2,1)S(1)}) custom-call(s32[72]{0:T(128)S(1)} %get-tuple-element.36.table, bf16[192,768]{1,0:T(8,128)(2,1)S(1)} %copy-done.13, bf16[2304,384]{1,0:T(8,128)(2,1)S(1)} %bitcast.11, bf16[2304,384]{1,0:T(8,128)(2,1)S(1)} %bitcast.13), custom_call_target="tpu_custom_call" | custom-call | flops 1000000000 | bytes 5000000 | tf_op jit(solution)/shard_map/project_rows/pallas_call | solution.py:179
  119.7 5.8 %all-to-all-start.3 = ((bf16[16,96,128]{2,1,0:T(8,128)(2,1)}), bf16[16,96,128]{2,1,0:T(8,128)(2,1)S(1)}, u32[]{:S(2)}, u32[]{:S(2)}) async-start(bf16[16,96,128]{2,1,0:T(8,128)(2,1)} %copy-done.11), calls=%async_computation.3 | async-start | bytes 786432 | tf_op jit(solution)/shard_map/all_to_all | solution.py:422
  125.5 1.6 fusion
  127.1 1.3 collective-permute-start.9
  128.4 7.6 %collective-permute-start.8 = (bf16[64,768]{1,0:T(8,128)(2,1)}, bf16[64,768]{1,0:T(8,128)(2,1)}, u32[]{:S(2)}, u32[]{:S(2)}) collective-permute-start(bf16[64,768]{1,0:T(8,128)(2,1)} %get-tuple-element.62), channel_id=1, source_target_pairs={{256,1},{258,3},{260,5},{262,7},{264,9},{266,11},{268,13},{270,15}... | collective-permute-start | bytes 294920 | tf_op jit(solution)/shard_map/ppermute | solution.py:370
  136.2 9.5 %collective-permute-start.7 = (bf16[96,768]{1,0:T(8,128)(2,1)S(1)}, bf16[96,768]{1,0:T(8,128)(2,1)S(1)}, u32[]{:S(2)}, u32[]{:S(2)}) collective-permute-start(bf16[96,768]{1,0:T(8,128)(2,1)S(1)} %pack_keys.1), channel_id=1, source_target_pairs={{0,1},{1,0},{2,3},{3,2},{4,5},{5,4},{6,7},{7,6},{8,9},{9,8},{10,11... | collective-permute-start | bytes 442376 | tf_op jit(solution)/shard_map/ppermute | solution.py:337
  145.7 1.5 copy-done.2
  147.2 6.1 %local_branch.1 = (f32[768,192]{1,0:T(8,128)S(1)}, f32[16,192]{1,0:T(8,128)S(1)}, f32[16,192]{1,0:T(8,128)S(1)}) custom-call(s32[72]{0:T(128)S(1)} %get-tuple-element.36.table, bf16[768,192]{1,0:T(8,128)(2,1)S(1)} %get-tuple-element.50.q, bf16[1536,192]{1,0:T(8,128)(2,1)S(1)} %get-tuple-element.51.kv, bf16[64,768]{1,0:T(8,128)(2,1)} %collective-permute-done.8.before, ...), custom_call_target="tpu_custom_call" | custom-call | flops 600000000 | bytes 5000000 | tf_op jit(solution)/shard_map/local_branch/pallas_call | solution.py:226
  153.3 2.8 %far_own.1 = (f32[48,768]{1,0:T(8,128)S(1)}, f32[1,768]{1,0:T(1,128)S(1)}, f32[1,768]{1,0:T(1,128)S(1)}) custom-call(s32[72]{0:T(128)S(1)} %get-tuple-element.36.table, bf16[16,96,128]{2,1,0:T(8,128)(2,1)S(1)} %all-to-all-done.3.arrived), custom_call_target="tpu_custom_call" | custom-call | flops 300000000 | bytes 700000 | tf_op jit(solution)/shard_map/far_own/pallas_call | solution.py:263
  156.0 3.0 %far_rest.1 = bf16[16,48,128]{2,1,0:T(8,128)(2,1)S(1)} custom-call(s32[72]{0:T(128)S(1)} %get-tuple-element.36.table, bf16[16,96,128]{2,1,0:T(8,128)(2,1)S(1)} %all-to-all-done.3.arrived, bf16[96,768]{1,0:T(8,128)(2,1)S(1)} %collective-permute-done.7.other, f32[48,768]{1,0:T(8,128)S(1)} %get-tuple-element.55.own_sum, ...), custom_call_target="tpu_custom_call" | custom-call | flops 300000000 | bytes 1000000 | tf_op jit(solution)/shard_map/far_rest/pallas_call | solution.py:293
  159.0 27.8 %all_to_all.25.answers = bf16[16,48,128]{2,1,0:T(8,128)(2,1)S(1)} all-to-all(bf16[16,48,128]{2,1,0:T(8,128)(2,1)S(1)} %far_rest.1), channel_id=1, replica_groups=mesh['zlo'=8,'core'=2,'y'=4,'x'=4,'zhi'=2] {'y','x'}, dimensions={0} | all-to-all | bytes 393216 | tf_op jit(solution)/shard_map/all_to_all | solution.py:428
  186.8 2.0 %finish_rows.1 = bf16[1,192,768]{2,1,0:T(8,128)(2,1)} custom-call(s32[72]{0:T(128)S(1)} %get-tuple-element.36.table, bf16[16,48,128]{2,1,0:T(8,128)(2,1)S(1)} %all_to_all.25.answers, f32[768,192]{1,0:T(8,128)S(1)} %get-tuple-element.58.local_sum, f32[16,192]{1,0:T(8,128)S(1)} %get-tuple-element.59.local_best, f32[16,192]{1,0:T(8,128)S(1)} %get-tuple-element.60.local_total, ...), custom_call_target="tpu_custom_call" | custom-call | flops 100000000 | bytes 1500000 | tf_op jit(solution)/shard_map/finish_rows/pallas_call | solution.py:323
  (56 shorter events, 9.9 us)
Async XLA Ops:
  0.0 0.9 copy-start
  0.9 19.9 %copy-start.19 = (bf16[1536,24]{0,1:T(8,128)(2,1)S(1)}, bf16[1536,24]{0,1:T(8,128)(2,1)}, u32[]{:S(2)}) copy-start(bf16[1536,24]{0,1:T(8,128)(2,1)} %param.11) | copy-start | bytes 221188
  0.9 21.9 %copy-start.9 = (bf16[1,192,1536]{2,1,0:T(8,128)(2,1)S(1)}, bf16[1,192,1536]{2,1,0:T(8,128)(2,1)}, u32[]{:S(2)}) copy-start(bf16[1,192,1536]{2,1,0:T(8,128)(2,1)} %ctx.1) | copy-start | bytes 1769476
  0.9 21.9 %copy-start.10 = (bf16[1,192,1536]{2,1,0:T(8,128)(2,1)S(1)}, bf16[1,192,1536]{2,1,0:T(8,128)(2,1)}, u32[]{:S(2)}) copy-start(bf16[1,192,1536]{2,1,0:T(8,128)(2,1)} %res.1) | copy-start | bytes 1769476
  0.9 21.9 %copy-start.14 = (s32[1,1,192]{2,1,0:T(1,128)S(1)}, s32[1,1,192]{2,1,0:T(1,128)}, u32[]{:S(2)}) copy-start(s32[1,1,192]{2,1,0:T(1,128)} %listing.3) | copy-start | bytes 2308
  1.0 21.9 %copy-start.15 = (s32[1,32]{1,0:T(1,128)S(1)}, s32[1,32]{1,0:T(1,128)}, u32[]{:S(2)}) copy-start(s32[1,32]{1,0:T(1,128)} %counts.1) | copy-start | bytes 388
  1.0 21.9 %copy-start.16 = (s32[1,2]{1,0:T(1,128)S(1)}, s32[1,2]{1,0:T(1,128)}, u32[]{:S(2)}) copy-start(s32[1,2]{1,0:T(1,128)} %dilation.1) | copy-start | bytes 28
  2.1 26.6 %all-to-all-start = ((bf16[16,48,768]{2,1,0:T(8,128)(2,1)}), bf16[16,48,768]{2,1,0:T(8,128)(2,1)S(1)}, u32[]{:S(2)}, u32[]{:S(2)}) async-start(bf16[16,48,768]{2,1,0:T(8,128)(2,1)} %broadcast_in_dim.7), calls=%async_computation | async-start | bytes 2359296 | tf_op jit(solution)/shard_map/all_to_all | solution.py:378
  9.7 18.9 %collective-permute-start = (bf16[48,768]{1,0:T(8,128)(2,1)S(1)}, bf16[48,768]{1,0:T(8,128)(2,1)S(1)}, u32[]{:S(2)}, u32[]{:S(2)}) collective-permute-start(bf16[48,768]{1,0:T(8,128)(2,1)S(1)} %dynamic-slice_bitcast_fusion), channel_id=1, source_target_pairs={{0,449},{1,448},{64,385},{65,384},{128,321},{129,320},{192,257},{1... | collective-permute-start | bytes 221192 | tf_op jit(solution)/shard_map/ppermute | solution.py:333
  20.8 7.8 %collective-permute-start.1 = (bf16[24,768]{1,0:T(8,128)(2,1)S(1)}, bf16[24,768]{1,0:T(8,128)(2,1)S(1)}, u32[]{:S(2)}, u32[]{:S(2)}) collective-permute-start(bf16[24,768]{1,0:T(8,128)(2,1)S(1)} %dynamic-slice_bitcast_fusion.2), channel_id=1, source_target_pairs={{0,449},{1,448},{64,385},{65,384},{128,321},{129,320},{192,257},{1... | collective-permute-start | bytes 110600 | tf_op jit(solution)/shard_map/ppermute | solution.py:333
  24.4 0.9 copy-start.5
  25.3 0.9 copy-start.7
  30.3 12.2 %copy-start.18 = (bf16[768,72]{0,1:T(8,128)(2,1)S(1)}, bf16[768,72]{0,1:T(8,128)(2,1)}, u32[]{:S(2)}) copy-start(bf16[768,72]{0,1:T(8,128)(2,1)} %param.12) | copy-start | bytes 331780
  30.3 34.5 %all-to-all-start.1 = ((bf16[16,96,768]{2,1,0:T(8,128)(2,1)}), bf16[16,96,768]{2,1,0:T(8,128)(2,1)}, u32[]{:S(2)}, u32[]{:S(2)}) async-start(bf16[16,96,768]{2,1,0:T(8,128)(2,1)} %broadcast_in_dim.6), calls=%async_computation.1 | async-start | bytes 4718592 | tf_op jit(solution)/shard_map/all_to_all | solution.py:378
  37.1 15.6 %collective-permute-start.2 = (bf16[16,48,768]{2,1,0:T(8,128)(2,1)S(1)}, bf16[16,48,768]{2,1,0:T(8,128)(2,1)S(1)}, u32[]{:S(2)}, u32[]{:S(2)}) collective-permute-start(bf16[16,48,768]{2,1,0:T(8,128)(2,1)S(1)} %all-to-all-done.near_a), channel_id=1, source_target_pairs={{0,32},{32,0},{1,33},{33,1},{2,34},{34,2},{3,35},{35,3},{4,36},{36... | collective-permute-start | bytes 3538952 | tf_op jit(solution)/shard_map/ppermute | solution.py:374
  42.5 10.2 %collective-permute-start.3 = (bf16[72,384]{1,0:T(8,128)(2,1)S(1)}, bf16[72,384]{1,0:T(8,128)(2,1)S(1)}, u32[]{:S(2)}, u32[]{:S(2)}) collective-permute-start(bf16[72,384]{1,0:T(8,128)(2,1)S(1)} %dynamic-slice_bitcast_fusion.1), channel_id=1, source_target_pairs={{0,449},{1,448},{64,385},{65,384},{128,321},{129,320},{192,257},{1... | collective-permute-start | bytes 165896 | tf_op jit(solution)/shard_map/ppermute | solution.py:333
  52.7 21.9 %copy-start.3 = (bf16[16,48,768]{2,1,0:T(8,128)(2,1)}, bf16[16,48,768]{2,1,0:T(8,128)(2,1)S(1)}, u32[]{:S(2)}) copy-start(bf16[16,48,768]{2,1,0:T(8,128)(2,1)S(1)} %collective-permute-done.2.near_b) | copy-start | bytes 3538948
  66.2 12.9 %collective-permute-start.4 = (bf16[16,96,768]{2,1,0:T(8,128)(2,1)}, bf16[16,96,768]{2,1,0:T(8,128)(2,1)}, u32[]{:S(2)}, u32[]{:S(2)}) collective-permute-start(bf16[16,96,768]{2,1,0:T(8,128)(2,1)} %all-to-all-done.1.far_a), channel_id=1, source_target_pairs={{0,32},{32,0},{1,33},{33,1},{2,34},{34,2},{3,35},{35,3},{4,36},{36... | collective-permute-start | bytes 7077896 | tf_op jit(solution)/shard_map/ppermute | solution.py:374
  74.6 33.1 %all-to-all-start.2 = ((bf16[16,144,384]{2,1,0:T(8,128)(2,1)}), bf16[16,144,384]{2,1,0:T(8,128)(2,1)S(1)}, u32[]{:S(2)}, u32[]{:S(2)}) async-start(bf16[16,144,384]{2,1,0:T(8,128)(2,1)} %broadcast_in_dim.8), calls=%async_computation.2 | async-start | bytes 3538944 | tf_op jit(solution)/shard_map/all_to_all | solution.py:378
  79.1 1.3 copy-start.4
  80.4 1.1 copy-start.6
  81.4 1.1 copy-start.8
  88.6 19.5 %collective-permute-start.5 = (bf16[128,768]{1,0:T(8,128)(2,1)S(1)}, bf16[128,768]{1,0:T(8,128)(2,1)S(1)}, u32[]{:S(2)}, u32[]{:S(2)}) collective-permute-start(bf16[128,768]{1,0:T(8,128)(2,1)S(1)} %get-tuple-element.45), channel_id=1, source_target_pairs={{0,256},{2,258},{4,260},{6,262},{8,264},{10,266},{12,268},{14,270}... | collective-permute-start | bytes 589832 | tf_op jit(solution)/shard_map/ppermute | solution.py:358
  108.1 10.9 %copy-start.17 = (bf16[128,768]{1,0:T(8,128)(2,1)}, bf16[128,768]{1,0:T(8,128)(2,1)S(1)}, u32[]{:S(2)}) copy-start(bf16[128,768]{1,0:T(8,128)(2,1)S(1)} %collective-permute-done.5) | copy-start | bytes 589828
  108.1 6.9 %collective-permute-start.6 = (bf16[16,144,384]{2,1,0:T(8,128)(2,1)S(1)}, bf16[16,144,384]{2,1,0:T(8,128)(2,1)S(1)}, u32[]{:S(2)}, u32[]{:S(2)}) collective-permute-start(bf16[16,144,384]{2,1,0:T(8,128)(2,1)S(1)} %all-to-all-done.2), channel_id=1, source_target_pairs={{0,32},{32,0},{1,33},{33,1},{2,34},{34,2},{3,35},{35,3},{4,36},{36... | collective-permute-start | bytes 5308424 | tf_op jit(solution)/shard_map/ppermute | solution.py:374
  115.0 4.0 %copy-start.1 = (bf16[16,144,384]{2,1,0:T(8,128)(2,1)}, bf16[16,144,384]{2,1,0:T(8,128)(2,1)S(1)}, u32[]{:S(2)}) copy-start(bf16[16,144,384]{2,1,0:T(8,128)(2,1)S(1)} %collective-permute-done.6) | copy-start | bytes 5308420
  115.0 1.2 copy-start.13
  119.7 16.3 %all-to-all-start.3 = ((bf16[16,96,128]{2,1,0:T(8,128)(2,1)}), bf16[16,96,128]{2,1,0:T(8,128)(2,1)S(1)}, u32[]{:S(2)}, u32[]{:S(2)}) async-start(bf16[16,96,128]{2,1,0:T(8,128)(2,1)} %copy-done.11), calls=%async_computation.3 | async-start | bytes 786432 | tf_op jit(solution)/shard_map/all_to_all | solution.py:422
  127.1 18.5 %collective-permute-start.9 = (bf16[64,768]{1,0:T(8,128)(2,1)}, bf16[64,768]{1,0:T(8,128)(2,1)}, u32[]{:S(2)}, u32[]{:S(2)}) collective-permute-start(bf16[64,768]{1,0:T(8,128)(2,1)} %get-tuple-element.61), channel_id=1, source_target_pairs={{258,1},{260,3},{262,5},{264,7},{266,9},{268,11},{270,13},{272,15}... | collective-permute-start | bytes 294920 | tf_op jit(solution)/shard_map/ppermute | solution.py:370
  128.4 17.3 %collective-permute-start.8 = (bf16[64,768]{1,0:T(8,128)(2,1)}, bf16[64,768]{1,0:T(8,128)(2,1)}, u32[]{:S(2)}, u32[]{:S(2)}) collective-permute-start(bf16[64,768]{1,0:T(8,128)(2,1)} %get-tuple-element.62), channel_id=1, source_target_pairs={{256,1},{258,3},{260,5},{262,7},{264,9},{266,11},{268,13},{270,15}... | collective-permute-start | bytes 294920 | tf_op jit(solution)/shard_map/ppermute | solution.py:370
  136.2 19.8 %collective-permute-start.7 = (bf16[96,768]{1,0:T(8,128)(2,1)S(1)}, bf16[96,768]{1,0:T(8,128)(2,1)S(1)}, u32[]{:S(2)}, u32[]{:S(2)}) collective-permute-start(bf16[96,768]{1,0:T(8,128)(2,1)S(1)} %pack_keys.1), channel_id=1, source_target_pairs={{0,1},{1,0},{2,3},{3,2},{4,5},{5,4},{6,7},{7,6},{8,9},{9,8},{10,11... | collective-permute-start | bytes 442376 | tf_op jit(solution)/shard_map/ppermute | solution.py:337
  145.7 1.5 copy-start.2
  (2 other events, 1.5 us)

commit v5 on v4

--- a/solution.py
+++ b/solution.py
@@ -85,66 +85,13 @@
         start = start + count
     order = (iota((TILE_DEV, TILE_DEV), 0) == listing[0]).astype(BF16)
     own_ctx[...] = dot_tn(order, ctx[0]).astype(BF16)
-    own_res[...] = dot_tn(order, res[0]).astype(BF16)
+    for z in range(2):
+        own_res[z] = dot_tn(order, res[z]).astype(BF16)
 
 
 def prepare(*args):
-    rows = ((TILE_DEV, D_ENC), BF16)
-    shapes = (rows, rows, ((ALL_COUNTS + BLOCKS,), I32))
+    shapes = (((TILE_DEV, D_ENC), BF16), ((2, TILE_DEV, D), BF16), ((ALL_COUNTS + BLOCKS,), I32))
     return call(prepare_kernel, "prepare_rows", shapes, "sssvvv-vvs", [], 250_000_000, 2_400_000)(*args)
-
-
-def embed_kernel(table, ctx, res, near_a, near_b, far_a, far_b, out, rims, w, p, hidden, normed, sems):
-    core, high = table[CORE], table[HIGH]
-    loads = [
-        pltpu.make_async_copy(near_a, w.at[core, :, high], sems.at[0]),
-        pltpu.make_async_copy(near_b, w.at[1 - core, :, high], sems.at[1]),
-        pltpu.make_async_copy(far_a.at[:, :W_ROWS], w.at[core, :, 1 - high], sems.at[2]),
-        pltpu.make_async_copy(far_b.at[:, :W_ROWS], w.at[1 - core, :, 1 - high], sems.at[3]),
-        pltpu.make_async_copy(far_a.at[:, W_ROWS:], p.at[core], sems.at[4]),
-        pltpu.make_async_copy(far_b.at[:, W_ROWS:], p.at[1 - core], sems.at[5]),
-    ]
-    for load in loads:
-        load.start()
-    for load in loads[:4]:
-        load.wait()
-    group = 4
-    width = group * 2 * W_ROWS
-    total = jnp.zeros((TILE_DEV, 1), F32)
-    for n in range(PLANES // group):
-        columns = slice(n * width, (n + 1) * width)
-        part = res[:, columns].astype(F32)
-        for half in range(2):
-            block = w[half, n * group : (n + 1) * group].reshape(width, D)
-            part += dot_nt(ctx[:, half * D : (half + 1) * D], block)
-        hidden[:, columns] = part
-        total += jnp.sum(part, axis=1, keepdims=True)
-    center = hidden[...] - total / D_ENC
-    spread = jnp.sum(center * center, axis=1, keepdims=True) / D_ENC
-    normed[...] = (center * lax.rsqrt(spread + NORM_EPS)).astype(BF16)
-    for load in loads[4:]:
-        load.wait()
-    for n in range(2):
-        rows = slice(n * PLANES // 2, (n + 1) * PLANES // 2)
-        part = dot_nt(normed[:, :D], p[0, rows].reshape(D // 2, D))
-        part += dot_nt(normed[:, D:], p[1, rows].reshape(D // 2, D))
-        out[:, n * D // 2 : (n + 1) * D // 2] = part.astype(BF16)
-    lane = iota((HALF, TILE_DEV), 1)
-    pick = (lane == iota((HALF, TILE_DEV), 0) + (table[COUNT_ME] - HALF)).astype(BF16)
-    rims[:HALF] = dot_nn(pick, out[...]).astype(BF16)
-    rims[HALF:] = out[:HALF]
-
-
-def embed(*args):
-    scratch = [
-        pltpu.VMEM((2, PLANES, 2, W_ROWS, D), BF16),
-        pltpu.VMEM((2, PLANES, 2 * P_ROWS, D), BF16),
-        pltpu.VMEM((TILE_DEV, D_ENC), F32),
-        pltpu.VMEM((TILE_DEV, D_ENC), BF16),
-        pltpu.SemaphoreType.DMA((6,)),
-    ]
-    shapes = (((TILE_DEV, D), BF16), ((2 * HALF, D), BF16))
-    return call(embed_kernel, "embed_rows", shapes, "svvhhhh-vv", scratch, 1_400_000_000, 9_000_000)(*args)
 
 
 def halves(table, ref, width):
@@ -152,6 +99,35 @@
     first = ref[:, pl.ds(pl.multiple_of(core * width, LANES), width)]
     second = ref[:, pl.ds(pl.multiple_of((1 - core) * width, LANES), width)]
     return first, second
+
+
+def embed_kernel(table, ctx, res, near_a, near_b, far_a, far_b, out, rims, hidden, normed):
+    core, high = table[CORE], table[HIGH]
+    first, second = halves(table, ctx, D)
+    near = dot_nt(first, near_a[...]) + dot_nt(second, near_b[...]) + res[high].astype(F32)
+    hidden[0] = near
+    far = dot_nt(first, far_a[:, :W_ROWS].reshape(D, D)) + dot_nt(second, far_b[:, :W_ROWS].reshape(D, D))
+    far += res[1 - high].astype(F32)
+    hidden[1] = far
+    mean = (jnp.sum(near, axis=1, keepdims=True) + jnp.sum(far, axis=1, keepdims=True)) / D_ENC
+    near, far = hidden[0] - mean, hidden[1] - mean
+    spread = (jnp.sum(near * near, axis=1, keepdims=True) + jnp.sum(far * far, axis=1, keepdims=True)) / D_ENC
+    scale = lax.rsqrt(spread + NORM_EPS)
+    normed[high] = (near * scale).astype(BF16)
+    normed[1 - high] = (far * scale).astype(BF16)
+    total = dot_nt(normed[core], far_a[:, W_ROWS:].reshape(D, D))
+    total += dot_nt(normed[1 - core], far_b[:, W_ROWS:].reshape(D, D))
+    out[...] = total.astype(BF16)
+    lane = iota((HALF, TILE_DEV), 1)
+    pick = (lane == iota((HALF, TILE_DEV), 0) + (table[COUNT_ME] - HALF)).astype(BF16)
+    rims[:HALF] = dot_nn(pick, out[...]).astype(BF16)
+    rims[HALF:] = out[:HALF]
+
+
+def embed(*args):
+    scratch = [pltpu.VMEM((2, TILE_DEV, D), F32), pltpu.VMEM((2, TILE_DEV, D), BF16)]
+    shapes = (((TILE_DEV, D), BF16), ((2 * HALF, D), BF16))
+    return call(embed_kernel, "embed_rows", shapes, "svvvvvv-vv", scratch, 1_400_000_000, 9_000_000)(*args)
 
 
 def project_kernel(table, own, q_a, q_b, payload, q_out, kv_out):
@@ -396,35 +372,38 @@
     plane_id = lax.axis_index("y") * lax.axis_size("x") + lax.axis_index("x")
 
     w_own = lax.dynamic_slice_in_dim(enc_out_w, core * D, D, 0).T
-    p_own = lax.dynamic_slice_in_dim(slide_proj, core * D, D, 0).T
+    p_split = slide_proj.reshape(PLANES, 2, W_ROWS, P_ROWS)
+    p_own = lax.dynamic_index_in_dim(p_split, core, 1, keepdims=False).reshape(D, P_ROWS).T
     q_own = lax.dynamic_slice_in_dim(qkv_w, core * (D // 2), D // 2, 0).T
     near_a = over_plane(copies(w_own))
     w_other = mirrored(w_own)
     p_other = mirrored(p_own)
     q_other = mirrored(q_own)
+    q_pair = in_order(q_own, q_other, high)
     place = jnp.stack([core, high, plane_id]).astype(I32)
-    own_ctx, own_res, table = prepare(place, kept_count, dilation, ctx_in, resid, tissue)
-    far = jnp.concatenate([w_other, in_order(p_own, p_other, high)])
-    far, near_a, own_ctx, own_res, table = hold(copies(far), near_a, own_ctx, own_res, table)
-    far_a = over_plane(far)
+    res_split = resid[0].reshape(TILE_DEV, PLANES, 2, W_ROWS).transpose(2, 0, 1, 3).reshape(2, TILE_DEV, D)
+    own_ctx, own_res, table = prepare(place, kept_count, dilation, ctx_in, res_split, tissue)
+    far = copies(jnp.concatenate([w_other, in_order(p_own, p_other, high)]))
+    far, near_a, own_ctx, own_res, table, q_pair = hold(far, near_a, own_ctx, own_res, table, q_pair)
+    q_a = lax.all_gather(q_pair, PLANE, axis=0, tiled=True)
+    far_a, near_a = hold(over_plane(far), near_a)
+    near_a = near_a.reshape(D, D)
     near_b = other_core(near_a)
-    q_both = copies(in_order(q_own, q_other, high))
-    far_a, near_b, q_both = hold(far_a, near_b, q_both)
-    q_a = over_plane(q_both)
     far_b = other_core(far_a)
     embedded, rims = embed(table, own_ctx, own_res, near_a, near_b, far_a, far_b)
     rims = quarter_way(rims)
-    q_a, embedded, rims = hold(q_a, embedded, rims)
-    before, after = to_next(rims[:HALF], 1), to_next(rims[HALF:], -1)
+    q_a, embedded = hold(q_a, embedded)
     q_b = other_core(q_a)
-    q_a, q_b = q_a.reshape(3 * D, D // 2), q_b.reshape(3 * D, D // 2)
+    q_b, rims = hold(q_b, rims)
     payload, q_rows, kv_rows = project(table, embedded, q_a, q_b)
-    arrived = lax.all_to_all(payload, PLANE, 0, 0)
+    arrived, rims = hold(lax.all_to_all(payload, PLANE, 0, 0), rims)
     other = across(pack(arrived))
     own_sum, own_best, own_total = far_own(table, arrived)
+    before, after = to_next(rims[:HALF], 1), to_next(rims[HALF:], -1)
+    other, own_sum, before, after = hold(other, own_sum, before, after)
+    answer = far_rest(table, arrived, other, own_sum, own_best, own_total)
+    q_rows, answer = hold(q_rows, answer)
     local_sum, local_best, local_total = local_branch(table, q_rows, kv_rows, before, after, q_a, q_b)
-    other, own_sum, local_sum = hold(other, own_sum, local_sum)
-    answer = far_rest(table, arrived, other, own_sum, own_best, own_total)
     answers = lax.all_to_all(answer, PLANE, 0, 0)
     return finish(table, answers, local_sum, local_best, local_total, tissue)
 

time: 190 us -> 216 us (1.14)
  waiting for transfers between devices: 31.6 us -> 73.7 us
  starting transfers between devices: 89.3 us -> 72.5 us
  blocking collectives: 27.8 us -> 12.7 us
  between operations: 0.41 us -> 13.7 us
    all_gather x0 -> x1, waiting for transfers between devices: none -> 18.9 us  [on_device(): q_a = lax.all_gather(q_pair, PLANE, axis=0, tiled=True)]
    all_to_all x1, blocking collectives: 27.8 us -> 12.7 us  [on_device(): arrived, rims = hold(lax.all_to_all(payload, PLANE, 0, 0), rims)]
    ppermute x2, waiting for transfers between devices: 0.01 us -> 11.9 us  [to_next(): return lax.ppermute(x, EVERY, pairs)]
    ppermute x1, waiting for transfers between devices: 0.4 us -> 8.91 us  [quarter_way(): return lax.ppermute(x, EVERY, pairs)]
    all_to_all x3 -> x2, waiting for transfers between devices: 21.2 us -> 29.3 us  [over_plane(): return lax.all_to_all(x, PLANE, 0, 0)]
    ppermute x3, waiting for transfers between devices: 5.94 us -> 0.01 us  [mirrored(): return lax.ppermute(x, ('zlo', 'zhi'), pairs)]
    ppermute x2, starting transfers between devices: 8.91 us -> 3.22 us  [to_next(): return lax.ppermute(x, EVERY, pairs)]
    ppermute x3, starting transfers between devices: 17.4 us -> 12.5 us  [other_core(): return lax.ppermute(x, 'core', [(0, 1), (1, 0)])]
  transfers between devices with their start and end apart: 14 -> 14, of which waited for: 7 -> 6; matrix products, arithmetic and copies ran while one was open for 1% -> 2% of each run, Pallas kernels for 8% -> 7%
where the time goes in v5:
time: 216 us; the launch traced here: 215 us
  waiting for transfers between devices  73.7 us (34%)
  starting transfers between devices  72.5 us (34%)
  Pallas kernels  24.4 us (11%)
  local copies, waits for them, and re-layouts  16.8 us (8%)
  between operations  13.7 us (6%)
  blocking collectives  12.7 us (6%)
    all_to_all x2, waiting for transfers between devices, over_plane(): return lax.all_to_all(x, PLANE, 0, 0)  29.3 us
    all_gather x1, waiting for transfers between devices, on_device(): q_a = lax.all_gather(q_pair, PLANE, axis=0, tiled=True)  18.9 us
    ppermute x3, starting transfers between devices, mirrored(): return lax.ppermute(x, ('zlo', 'zhi'), pairs)  17.6 us
    all_to_all x2, starting transfers between devices, over_plane(): return lax.all_to_all(x, PLANE, 0, 0)  14.4 us
    all_to_all x1, blocking collectives, on_device(): arrived, rims = hold(lax.all_to_all(payload, PLANE, 0, 0), rims)  12.7 us
    ppermute x3, starting transfers between devices, other_core(): return lax.ppermute(x, 'core', [(0, 1), (1, 0)])  12.5 us
    ppermute x1, starting transfers between devices, across(): return lax.ppermute(x, 'zhi', [(0, 1), (1, 0)])  12.3 us
    ppermute x2, waiting for transfers between devices, to_next(): return lax.ppermute(x, EVERY, pairs)  11.9 us
  transfers between devices with their start and end apart: 14, of which 6 were waited for; matrix products, arithmetic and copies ran while one was open for 2% of the time, Pallas kernels for 7%

profile of v5, /device:TPU:1, one launch (start us, length us, event | category | flops | bytes accessed | tf_op | source)
XLA Modules:
  0.0 214.7 jit_solution(11614227153722342175)
XLA Ops:
  8.6 7.7 %all-to-all-start = ((bf16[16,48,768]{2,1,0:T(8,128)(2,1)}), bf16[16,48,768]{2,1,0:T(8,128)(2,1)S(1)}, u32[]{:S(2)}, u32[]{:S(2)}) async-start(bf16[16,48,768]{2,1,0:T(8,128)(2,1)} %broadcast_in_dim.5), calls=%async_computation | async-start | bytes 2359296 | tf_op jit(solution)/shard_map/all_to_all | solution.py:354
  16.3 11.1 %collective-permute-start = (bf16[48,768]{1,0:T(8,128)(2,1)S(1)}, bf16[48,768]{1,0:T(8,128)(2,1)S(1)}, u32[]{:S(2)}, u32[]{:S(2)}) collective-permute-start(bf16[48,768]{1,0:T(8,128)(2,1)S(1)} %dynamic-slice_bitcast_fusion), channel_id=1, source_target_pairs={{0,449},{1,448},{64,385},{65,384},{128,321},{129,320},{192,257},{1... | collective-permute-start | bytes 221192 | tf_op jit(solution)/shard_map/ppermute | solution.py:309
  28.4 1.9 collective-permute-start.1
  30.4 4.6 %collective-permute-start.2 = (bf16[72,384]{1,0:T(8,128)(2,1)S(1)}, bf16[72,384]{1,0:T(8,128)(2,1)S(1)}, u32[]{:S(2)}, u32[]{:S(2)}) collective-permute-start(bf16[72,384]{1,0:T(8,128)(2,1)S(1)} %dynamic-slice_bitcast_fusion.1), channel_id=1, source_target_pairs={{0,449},{1,448},{64,385},{65,384},{128,321},{129,320},{192,257},{1... | collective-permute-start | bytes 165896 | tf_op jit(solution)/shard_map/ppermute | solution.py:309
  36.2 1.2 copy.12
  38.8 1.5 prepare_rows.1
  41.1 1.7 broadcast_in_dim.4
  42.8 6.7 %all-to-all-start.1 = ((bf16[16,96,768]{2,1,0:T(8,128)(2,1)}), bf16[16,96,768]{2,1,0:T(8,128)(2,1)}, u32[]{:S(2)}, u32[]{:S(2)}) async-start(bf16[16,96,768]{2,1,0:T(8,128)(2,1)} %broadcast_in_dim.4), calls=%async_computation.1 | async-start | bytes 4718592 | tf_op jit(solution)/shard_map/all_to_all | solution.py:354
  50.2 29.3 %all-to-all-done.1.far_a = bf16[16,96,768]{2,1,0:T(8,128)(2,1)} async-done(((bf16[16,96,768]{2,1,0:T(8,128)(2,1)}), bf16[16,96,768]{2,1,0:T(8,128)(2,1)}, u32[]{:S(2)}, u32[]{:S(2)}) %all-to-all-start.1) | async-done | bytes 2359328 | tf_op jit(solution)/shard_map/all_to_all | solution.py:354
  79.5 6.7 %collective-permute-start.4 = (bf16[16,96,768]{2,1,0:T(8,128)(2,1)}, bf16[16,96,768]{2,1,0:T(8,128)(2,1)S(1)}, u32[]{:S(2)}, u32[]{:S(2)}) collective-permute-start(bf16[16,96,768]{2,1,0:T(8,128)(2,1)} %all-to-all-done.1.far_a), channel_id=1, source_target_pairs={{0,32},{32,0},{1,33},{33,1},{2,34},{34,2},{3,35},{35,3},{4,36},{36... | collective-permute-start | bytes 7077896 | tf_op jit(solution)/shard_map/ppermute | solution.py:350
  86.2 1.9 collective-permute-start.3
  88.1 3.9 %collective-permute-done.3.near_b = bf16[768,768]{1,0:T(8,128)(2,1)S(1)} collective-permute-done((bf16[768,768]{1,0:T(8,128)(2,1)S(1)}, bf16[768,768]{1,0:T(8,128)(2,1)S(1)}, u32[]{:S(2)}, u32[]{:S(2)}) %collective-permute-start.3) | collective-permute-done | bytes 1179680 | tf_op jit(solution)/shard_map/ppermute | solution.py:350
  92.0 1.4 copy-done.15
  93.5 5.6 %embed_rows.1 = (bf16[192,768]{1,0:T(8,128)(2,1)S(1)}, bf16[128,768]{1,0:T(8,128)(2,1)S(1)}) custom-call(s32[72]{0:T(128)S(1)} %get-tuple-element.42.table, bf16[192,1536]{1,0:T(8,128)(2,1)S(1)} %get-tuple-element.44.ctx, bf16[2,192,768]{2,1,0:T(8,128)(2,1)S(1)} %get-tuple-element.45.res, bf16[768,768]{1,0:T(8,128)(2,1)S(1)} %bitcast.18, ...), custom_call_target="tpu_custom_call" | custom-call | flops 1400000000 | bytes 9000000 | tf_op jit(solution)/shard_map/embed_rows/pallas_call | solution.py:130
  99.1 18.9 %all-gather.2.cloned.1.call-done.q_a = bf16[2304,384]{1,0:T(8,128)(2,1)} async-done(((bf16[144,384]{1,0:T(8,128)(2,1)}), bf16[2304,384]{1,0:T(8,128)(2,1)}) %all-gather.2.cloned.1.call-update) | async-done | bytes 1769488 | tf_op jit(solution)/shard_map/all_gather | solution.py:388
  118.0 3.9 %collective-permute-start.5 = (bf16[2304,384]{1,0:T(8,128)(2,1)}, bf16[2304,384]{1,0:T(8,128)(2,1)S(1)}, u32[]{:S(2)}, u32[]{:S(2)}) collective-permute-start(bf16[2304,384]{1,0:T(8,128)(2,1)} %all-gather.2.cloned.1.call-done.q_a), channel_id=1, source_target_pairs={{0,32},{32,0},{1,33},{33,1},{2,34},{34,2},{3,35},{35,3},{4,36},{36... | collective-permute-start | bytes 5308424 | tf_op jit(solution)/shard_map/ppermute | solution.py:350
  121.9 8.1 %collective-permute-start.6 = (bf16[128,768]{1,0:T(8,128)(2,1)S(1)}, bf16[128,768]{1,0:T(8,128)(2,1)S(1)}, u32[]{:S(2)}, u32[]{:S(2)}) collective-permute-start(bf16[128,768]{1,0:T(8,128)(2,1)S(1)} %get-tuple-element.53), channel_id=1, source_target_pairs={{0,256},{2,258},{4,260},{6,262},{8,264},{10,266},{12,268},{14,270}... | collective-permute-start | bytes 589832 | tf_op jit(solution)/shard_map/ppermute | solution.py:334
  130.0 8.9 %collective-permute-done.6 = bf16[128,768]{1,0:T(8,128)(2,1)S(1)} collective-permute-done((bf16[128,768]{1,0:T(8,128)(2,1)S(1)}, bf16[128,768]{1,0:T(8,128)(2,1)S(1)}, u32[]{:S(2)}, u32[]{:S(2)}) %collective-permute-start.6) | collective-permute-done | bytes 196640 | tf_op jit(solution)/shard_map/ppermute | solution.py:334
  138.9 1.5 copy-done.1
  140.4 2.8 %project_rows.1 = (bf16[16,96,128]{2,1,0:T(8,128)(2,1)S(1)}, bf16[768,192]{1,0:T(8,128)(2,1)S(1)}, bf16[1536,192]{1,0:T(8,128)(2,1)S(1)}) custom-call(s32[72]{0:T(128)S(1)} %get-tuple-element.42.table, bf16[192,768]{1,0:T(8,128)(2,1)S(1)} %get-tuple-element.51.own, bf16[2304,384]{1,0:T(8,128)(2,1)S(1)} %copy-done.1, ...), custom_call_target="tpu_custom_call" | custom-call | flops 1000000000 | bytes 5000000 | tf_op jit(solution)/shard_map/project_rows/pallas_call | solution.py:155
  143.2 12.7 %all_to_all.20.arrived = bf16[16,96,128]{2,1,0:T(8,128)(2,1)S(1)} all-to-all(bf16[16,96,128]{2,1,0:T(8,128)(2,1)S(1)} %get-tuple-element.56), channel_id=1, replica_groups=mesh['zlo'=8,'core'=2,'y'=4,'x'=4,'zhi'=2] {'y','x'}, dimensions={0} | all-to-all | bytes 786432 | tf_op jit(solution)/shard_map/all_to_all | solution.py:399
  156.1 12.3 %collective-permute-start.7 = (bf16[96,768]{1,0:T(8,128)(2,1)S(1)}, bf16[96,768]{1,0:T(8,128)(2,1)S(1)}, u32[]{:S(2)}, u32[]{:S(2)}) collective-permute-start(bf16[96,768]{1,0:T(8,128)(2,1)S(1)} %pack_keys.1), channel_id=1, source_target_pairs={{0,1},{1,0},{2,3},{3,2},{4,5},{5,4},{6,7},{7,6},{8,9},{9,8},{10,11... | collective-permute-start | bytes 442376 | tf_op jit(solution)/shard_map/ppermute | solution.py:313
  168.4 1.9 collective-permute-start.8
  170.3 1.3 collective-permute-start.9
  171.6 2.7 %far_own.1 = (f32[48,768]{1,0:T(8,128)S(1)}, f32[1,768]{1,0:T(1,128)S(1)}, f32[1,768]{1,0:T(1,128)S(1)}) custom-call(s32[72]{0:T(128)S(1)} %get-tuple-element.42.table, bf16[16,96,128]{2,1,0:T(8,128)(2,1)S(1)} %all_to_all.20.arrived), custom_call_target="tpu_custom_call" | custom-call | flops 300000000 | bytes 700000 | tf_op jit(solution)/shard_map/far_own/pallas_call | solution.py:239
  174.4 6.7 %collective-permute-done.8.before = bf16[64,768]{1,0:T(8,128)(2,1)S(1)} collective-permute-done((bf16[64,768]{1,0:T(8,128)(2,1)S(1)}, bf16[64,768]{1,0:T(8,128)(2,1)S(1)}, u32[]{:S(2)}, u32[]{:S(2)}) %collective-permute-start.8) | collective-permute-done | bytes 98336 | tf_op jit(solution)/shard_map/ppermute | solution.py:346
  181.7 5.2 %collective-permute-done.9.after = bf16[64,768]{1,0:T(8,128)(2,1)S(1)} collective-permute-done((bf16[64,768]{1,0:T(8,128)(2,1)S(1)}, bf16[64,768]{1,0:T(8,128)(2,1)S(1)}, u32[]{:S(2)}, u32[]{:S(2)}) %collective-permute-start.9) | collective-permute-done | bytes 98336 | tf_op jit(solution)/shard_map/ppermute | solution.py:346
  187.6 3.6 %far_rest.1 = bf16[16,48,128]{2,1,0:T(8,128)(2,1)} custom-call(s32[72]{0:T(128)S(1)} %get-tuple-element.42.table, bf16[16,96,128]{2,1,0:T(8,128)(2,1)S(1)} %all_to_all.20.arrived, bf16[96,768]{1,0:T(8,128)(2,1)S(1)} %collective-permute-done.7.other, f32[48,768]{1,0:T(8,128)S(1)} %get-tuple-element.62.own_sum, f32[1,768]{1,0:T(1,128)S(1)} %get-tuple-element.63.own_best, ...), custom_call_target="tpu_custom_call" | custom-call | flops 300000000 | bytes 1000000 | tf_op jit(solution)/shard_map/far_rest/pallas_call | solution.py:269
  191.2 4.4 %all-to-all-start.3 = ((bf16[16,48,128]{2,1,0:T(8,128)(2,1)}), bf16[16,48,128]{2,1,0:T(8,128)(2,1)}, u32[]{:S(2)}, u32[]{:S(2)}) async-start(bf16[16,48,128]{2,1,0:T(8,128)(2,1)} %far_rest.1), calls=%async_computation.3 | async-start | bytes 393216 | tf_op jit(solution)/shard_map/all_to_all | solution.py:407
  195.6 1.5 copy-done.4
  199.8 5.6 %local_branch.1 = (f32[768,192]{1,0:T(8,128)S(1)}, f32[16,192]{1,0:T(8,128)S(1)}, f32[16,192]{1,0:T(8,128)S(1)}) custom-call(s32[72]{0:T(128)S(1)} %get-tuple-element.42.table, bf16[768,192]{1,0:T(8,128)(2,1)S(1)} %copy-done.7, bf16[1536,192]{1,0:T(8,128)(2,1)S(1)} %get-tuple-element.67.kv, bf16[64,768]{1,0:T(8,128)(2,1)S(1)} %copy-done.9, ...), custom_call_target="tpu_custom_call" | custom-call | flops 600000000 | bytes 5000000 | tf_op jit(solution)/shard_map/local_branch/pallas_call | solution.py:202
  205.5 2.4 %finish_rows.1 = bf16[1,192,768]{2,1,0:T(8,128)(2,1)} custom-call(s32[72]{0:T(128)S(1)} %get-tuple-element.42.table, bf16[16,48,128]{2,1,0:T(8,128)(2,1)} %all-to-all-done.3.answers, f32[768,192]{1,0:T(8,128)S(1)} %get-tuple-element.70.local_sum, f32[16,192]{1,0:T(8,128)S(1)} %get-tuple-element.71.local_best, f32[16,192]{1,0:T(8,128)S(1)} %get-tuple-element.72.local_total, ...), custom_call_target="tpu_custom_call" | custom-call | flops 100000000 | bytes 1500000 | tf_op jit(solution)/shard_map/finish_rows/pallas_call | solution.py:299
  (59 shorter events, 11.2 us)
Async XLA Ops:
  6.5 0.9 copy-start
  7.5 20.0 %copy-start.17 = (bf16[1536,24]{0,1:T(8,128)(2,1)S(1)}, bf16[1536,24]{0,1:T(8,128)(2,1)}, u32[]{:S(2)}) copy-start(bf16[1536,24]{0,1:T(8,128)(2,1)} %param.11) | copy-start | bytes 221188
  8.6 21.8 %copy-start.18 = (bf16[768,72]{0,1:T(8,128)(2,1)S(1)}, bf16[768,72]{0,1:T(8,128)(2,1)}, u32[]{:S(2)}) copy-start(bf16[768,72]{0,1:T(8,128)(2,1)} %param.12) | copy-start | bytes 331780
  8.6 26.5 %copy-start.16 = (bf16[1,192,1536]{2,1,0:T(8,128)(2,1)S(1)}, bf16[1,192,1536]{2,1,0:T(8,128)(2,1)}, u32[]{:S(2)}) copy-start(bf16[1,192,1536]{2,1,0:T(8,128)(2,1)} %param.9) | copy-start | bytes 1769476
  8.6 32.5 %all-to-all-start = ((bf16[16,48,768]{2,1,0:T(8,128)(2,1)}), bf16[16,48,768]{2,1,0:T(8,128)(2,1)S(1)}, u32[]{:S(2)}, u32[]{:S(2)}) async-start(bf16[16,48,768]{2,1,0:T(8,128)(2,1)} %broadcast_in_dim.5), calls=%async_computation | async-start | bytes 2359296 | tf_op jit(solution)/shard_map/all_to_all | solution.py:354
  16.3 24.8 %collective-permute-start = (bf16[48,768]{1,0:T(8,128)(2,1)S(1)}, bf16[48,768]{1,0:T(8,128)(2,1)S(1)}, u32[]{:S(2)}, u32[]{:S(2)}) collective-permute-start(bf16[48,768]{1,0:T(8,128)(2,1)S(1)} %dynamic-slice_bitcast_fusion), channel_id=1, source_target_pairs={{0,449},{1,448},{64,385},{65,384},{128,321},{129,320},{192,257},{1... | collective-permute-start | bytes 221192 | tf_op jit(solution)/shard_map/ppermute | solution.py:309
  28.4 11.9 %collective-permute-start.1 = (bf16[24,768]{1,0:T(8,128)(2,1)S(1)}, bf16[24,768]{1,0:T(8,128)(2,1)S(1)}, u32[]{:S(2)}, u32[]{:S(2)}) collective-permute-start(bf16[24,768]{1,0:T(8,128)(2,1)S(1)} %bitcast.21), channel_id=1, source_target_pairs={{0,449},{1,448},{64,385},{65,384},{128,321},{129,320},{192,257},{1... | collective-permute-start | bytes 110600 | tf_op jit(solution)/shard_map/ppermute | solution.py:309
  30.4 10.0 %collective-permute-start.2 = (bf16[72,384]{1,0:T(8,128)(2,1)S(1)}, bf16[72,384]{1,0:T(8,128)(2,1)S(1)}, u32[]{:S(2)}, u32[]{:S(2)}) collective-permute-start(bf16[72,384]{1,0:T(8,128)(2,1)S(1)} %dynamic-slice_bitcast_fusion.1), channel_id=1, source_target_pairs={{0,449},{1,448},{64,385},{65,384},{128,321},{129,320},{192,257},{1... | collective-permute-start | bytes 165896 | tf_op jit(solution)/shard_map/ppermute | solution.py:309
  36.2 1.5 copy-start.12
  36.2 1.5 copy-start.13
  36.2 1.5 copy-start.14
  37.8 1.1 copy-start.5
  42.8 36.8 %all-to-all-start.1 = ((bf16[16,96,768]{2,1,0:T(8,128)(2,1)}), bf16[16,96,768]{2,1,0:T(8,128)(2,1)}, u32[]{:S(2)}, u32[]{:S(2)}) async-start(bf16[16,96,768]{2,1,0:T(8,128)(2,1)} %broadcast_in_dim.4), calls=%async_computation.1 | async-start | bytes 4718592 | tf_op jit(solution)/shard_map/all_to_all | solution.py:354
  49.5 68.6 %all-gather.2.cloned.1.call-start = ((), (), s32[]{:S(2)}) async-start(), calls=%async_computation.4 | async-start | bytes 1880064 | tf_op jit(solution)/shard_map/all_gather | solution.py:388
  79.5 12.5 %collective-permute-start.4 = (bf16[16,96,768]{2,1,0:T(8,128)(2,1)}, bf16[16,96,768]{2,1,0:T(8,128)(2,1)S(1)}, u32[]{:S(2)}, u32[]{:S(2)}) collective-permute-start(bf16[16,96,768]{2,1,0:T(8,128)(2,1)} %all-to-all-done.1.far_a), channel_id=1, source_target_pairs={{0,32},{32,0},{1,33},{33,1},{2,34},{34,2},{3,35},{35,3},{4,36},{36... | collective-permute-start | bytes 7077896 | tf_op jit(solution)/shard_map/ppermute | solution.py:350
  86.2 5.8 %collective-permute-start.3 = (bf16[768,768]{1,0:T(8,128)(2,1)S(1)}, bf16[768,768]{1,0:T(8,128)(2,1)S(1)}, u32[]{:S(2)}, u32[]{:S(2)}) collective-permute-start(bf16[768,768]{1,0:T(8,128)(2,1)S(1)} %bitcast.17), channel_id=1, source_target_pairs={{0,32},{32,0},{1,33},{33,1},{2,34},{34,2},{3,35},{35,3},{4,36},{36... | collective-permute-start | bytes 3538952 | tf_op jit(solution)/shard_map/ppermute | solution.py:350
  92.0 1.4 copy-start.15
  118.0 20.9 %collective-permute-start.5 = (bf16[2304,384]{1,0:T(8,128)(2,1)}, bf16[2304,384]{1,0:T(8,128)(2,1)S(1)}, u32[]{:S(2)}, u32[]{:S(2)}) collective-permute-start(bf16[2304,384]{1,0:T(8,128)(2,1)} %all-gather.2.cloned.1.call-done.q_a), channel_id=1, source_target_pairs={{0,32},{32,0},{1,33},{33,1},{2,34},{34,2},{3,35},{35,3},{4,36},{36... | collective-permute-start | bytes 5308424 | tf_op jit(solution)/shard_map/ppermute | solution.py:350
  121.9 17.0 %collective-permute-start.6 = (bf16[128,768]{1,0:T(8,128)(2,1)S(1)}, bf16[128,768]{1,0:T(8,128)(2,1)S(1)}, u32[]{:S(2)}, u32[]{:S(2)}) collective-permute-start(bf16[128,768]{1,0:T(8,128)(2,1)S(1)} %get-tuple-element.53), channel_id=1, source_target_pairs={{0,256},{2,258},{4,260},{6,262},{8,264},{10,266},{12,268},{14,270}... | collective-permute-start | bytes 589832 | tf_op jit(solution)/shard_map/ppermute | solution.py:334
  138.9 1.5 copy-start.1
  140.4 2.8 %copy-start.3 = (bf16[2304,384]{1,0:T(8,128)(2,1)}, bf16[2304,384]{1,0:T(8,128)(2,1)S(1)}, u32[]{:S(2)}) copy-start(bf16[2304,384]{1,0:T(8,128)(2,1)S(1)} %collective-permute-done.5.q_b) | copy-start | bytes 5308420
  143.2 48.0 %copy-start.6 = (bf16[768,192]{1,0:T(8,128)(2,1)}, bf16[768,192]{1,0:T(8,128)(2,1)S(1)}, u32[]{:S(2)}) copy-start(bf16[768,192]{1,0:T(8,128)(2,1)S(1)} %get-tuple-element.66.q) | copy-start | bytes 884740
  156.0 39.6 %copy-start.2 = (bf16[2304,384]{1,0:T(8,128)(2,1)S(1)}, bf16[2304,384]{1,0:T(8,128)(2,1)}, u32[]{:S(2)}) copy-start(bf16[2304,384]{1,0:T(8,128)(2,1)} %all-gather.2.cloned.1.call-done.q_a) | copy-start | bytes 5308420
  156.1 31.5 %collective-permute-start.7 = (bf16[96,768]{1,0:T(8,128)(2,1)S(1)}, bf16[96,768]{1,0:T(8,128)(2,1)S(1)}, u32[]{:S(2)}, u32[]{:S(2)}) collective-permute-start(bf16[96,768]{1,0:T(8,128)(2,1)S(1)} %pack_keys.1), channel_id=1, source_target_pairs={{0,1},{1,0},{2,3},{3,2},{4,5},{5,4},{6,7},{7,6},{8,9},{9,8},{10,11... | collective-permute-start | bytes 442376 | tf_op jit(solution)/shard_map/ppermute | solution.py:313
  168.4 12.7 %collective-permute-start.8 = (bf16[64,768]{1,0:T(8,128)(2,1)S(1)}, bf16[64,768]{1,0:T(8,128)(2,1)S(1)}, u32[]{:S(2)}, u32[]{:S(2)}) collective-permute-start(bf16[64,768]{1,0:T(8,128)(2,1)S(1)} %get-tuple-element.74), channel_id=1, source_target_pairs={{256,1},{258,3},{260,5},{262,7},{264,9},{266,11},{268,13},{270,15}... | collective-permute-start | bytes 294920 | tf_op jit(solution)/shard_map/ppermute | solution.py:346
  170.3 16.6 %collective-permute-start.9 = (bf16[64,768]{1,0:T(8,128)(2,1)S(1)}, bf16[64,768]{1,0:T(8,128)(2,1)S(1)}, u32[]{:S(2)}, u32[]{:S(2)}) collective-permute-start(bf16[64,768]{1,0:T(8,128)(2,1)S(1)} %get-tuple-element.73), channel_id=1, source_target_pairs={{258,1},{260,3},{262,5},{264,7},{266,9},{268,11},{270,13},{272,15}... | collective-permute-start | bytes 294920 | tf_op jit(solution)/shard_map/ppermute | solution.py:346
  181.1 0.6 copy-start.8
  191.2 14.3 %all-to-all-start.3 = ((bf16[16,48,128]{2,1,0:T(8,128)(2,1)}), bf16[16,48,128]{2,1,0:T(8,128)(2,1)}, u32[]{:S(2)}, u32[]{:S(2)}) async-start(bf16[16,48,128]{2,1,0:T(8,128)(2,1)} %far_rest.1), calls=%async_computation.3 | async-start | bytes 393216 | tf_op jit(solution)/shard_map/all_to_all | solution.py:407
  195.6 1.5 copy-start.4
  197.0 1.0 copy-start.7
  198.0 0.9 copy-start.9
  198.9 0.9 copy-start.11
  (1 other events, 0.6 us)
Sparse Core Ops, SparseCore 0:
  53.3 64.6 all-gather.1

commit v6 on v5

--- a/solution.py
+++ b/solution.py
@@ -25,7 +25,7 @@
 BF16 = jnp.bfloat16
 F32 = jnp.float32
 I32 = jnp.int32
-VMEM_LIMIT = 48 * 1024 * 1024
+VMEM_LIMIT = 24 * 1024 * 1024
 
 CORE, HIGH, PLANE_ID, RATE, SEGMENT, START_ME, COUNT_ME = range(7)
 ALL_STARTS = 8
@@ -379,22 +379,20 @@
     w_other = mirrored(w_own)
     p_other = mirrored(p_own)
     q_other = mirrored(q_own)
-    q_pair = in_order(q_own, q_other, high)
+    q_both = copies(in_order(q_own, q_other, high))
     place = jnp.stack([core, high, plane_id]).astype(I32)
     res_split = resid[0].reshape(TILE_DEV, PLANES, 2, W_ROWS).transpose(2, 0, 1, 3).reshape(2, TILE_DEV, D)
     own_ctx, own_res, table = prepare(place, kept_count, dilation, ctx_in, res_split, tissue)
     far = copies(jnp.concatenate([w_other, in_order(p_own, p_other, high)]))
-    far, near_a, own_ctx, own_res, table, q_pair = hold(far, near_a, own_ctx, own_res, table, q_pair)
-    q_a = lax.all_gather(q_pair, PLANE, axis=0, tiled=True)
-    far_a, near_a = hold(over_plane(far), near_a)
-    near_a = near_a.reshape(D, D)
+    far, near_a, own_ctx, own_res, table, q_both = hold(far, near_a, own_ctx, own_res, table, q_both)
+    far_a, q_both, near_a = hold(over_plane(far), q_both, near_a)
+    q_a, far_a, near_a = hold(over_plane(q_both), far_a, near_a)
+    near_a, q_a = near_a.reshape(D, D), q_a.reshape(3 * D, D // 2)
     near_b = other_core(near_a)
     far_b = other_core(far_a)
+    q_b = other_core(q_a)
     embedded, rims = embed(table, own_ctx, own_res, near_a, near_b, far_a, far_b)
     rims = quarter_way(rims)
-    q_a, embedded = hold(q_a, embedded)
-    q_b = other_core(q_a)
-    q_b, rims = hold(q_b, rims)
     payload, q_rows, kv_rows = project(table, embedded, q_a, q_b)
     arrived, rims = hold(lax.all_to_all(payload, PLANE, 0, 0), rims)
     other = across(pack(arrived))

time: 216 us -> 202 us (0.935); the launches traced: 215 us -> 198 us
  waiting for transfers between devices: 73.7 us -> 21.7 us
  blocking collectives: 12.7 us -> 60.2 us
  between operations: 13.7 us -> 0.41 us
  Pallas kernels: 24.4 us -> 21.6 us
    all_to_all x1 -> x2, blocking collectives: 12.7 us -> 60.2 us  [over_plane(): return lax.all_to_all(x, PLANE, 0, 0)]
    all_to_all x2 -> x1, waiting for transfers between devices: 29.3 us -> 0.01 us  [over_plane(): return lax.all_to_all(x, PLANE, 0, 0)]
    all_gather x1 -> x0, waiting for transfers between devices: 18.9 us -> none  [on_device(): q_a = lax.all_gather(q_pair, PLANE, axis=0, tiled=True)]
    all_to_all x2 -> x1, starting transfers between devices: 14.4 us -> 7.72 us  [over_plane(): return lax.all_to_all(x, PLANE, 0, 0)]
    ppermute x2, starting transfers between devices: 3.22 us -> 9.28 us  [to_next(): return lax.ppermute(x, EVERY, pairs)]
    ppermute x1, starting transfers between devices: 12.3 us -> 7.46 us  [across(): return lax.ppermute(x, 'zhi', [(0, 1), (1, 0)])]
    ppermute x1, starting transfers between devices: 8.1 us -> 11.7 us  [quarter_way(): return lax.ppermute(x, EVERY, pairs)]
    all_to_all x0 -> x1, starting transfers between devices: none -> 3.55 us  [on_device(): arrived, rims = hold(lax.all_to_all(payload, PLANE, 0, 0), rims)]
  transfers between devices with their start and end apart: 14 -> 13, of which waited for: 6 -> 3; matrix products, arithmetic and copies ran while one was open for 2% -> 3% of each run, Pallas kernels for 7% -> 7%
where the time goes in v6:
time: 202 us; the launch traced here: 198 us
  starting transfers between devices  73.9 us (37%)
  blocking collectives  60.2 us (30%)
  waiting for transfers between devices  21.7 us (11%)
  Pallas kernels  21.6 us (11%)
  local copies, waits for them, and re-layouts  17.5 us (9%)
  other arithmetic  2.76 us (1%)
    all_to_all x2, blocking collectives, over_plane(): return lax.all_to_all(x, PLANE, 0, 0)  60.2 us
    ppermute x3, starting transfers between devices, mirrored(): return lax.ppermute(x, ('zlo', 'zhi'), pairs)  17.6 us
    ppermute x1, starting transfers between devices, quarter_way(): return lax.ppermute(x, EVERY, pairs)  11.7 us
    unnamed x47, local copies, waits for them, and re-layouts  11.6 us
    ppermute x3, starting transfers between devices, other_core(): return lax.ppermute(x, 'core', [(0, 1), (1, 0)])  11.3 us
    ppermute x2, waiting for transfers between devices, to_next(): return lax.ppermute(x, EVERY, pairs)  9.47 us
    ppermute x2, starting transfers between devices, to_next(): return lax.ppermute(x, EVERY, pairs)  9.28 us
    ppermute x1, waiting for transfers between devices, quarter_way(): return lax.ppermute(x, EVERY, pairs)  8.15 us
  transfers between devices with their start and end apart: 13, of which 3 were waited for; matrix products, arithmetic and copies ran while one was open for 3% of the time, Pallas kernels for 7%

profile of v6, /device:TPU:1, one launch (start us, length us, event | category | flops | bytes accessed | tf_op | source)
XLA Modules:
  0.0 198.0 jit_solution(4936019791345601825)
XLA Ops:
  0.0 0.9 copy-done
  1.6 2.0 %broadcast_in_dim.7 = bf16[16,48,768]{2,1,0:T(8,128)(2,1)} broadcast(bf16[48,768]{1,0:T(8,128)(2,1)} %dynamic-slice_bitcast_fusion), dimensions={1,2} | broadcast | bytes 1253376 | tf_op jit(solution)/shard_map/broadcast_in_dim | solution.py:362
  3.6 7.7 %all-to-all-start = ((bf16[16,48,768]{2,1,0:T(8,128)(2,1)}), bf16[16,48,768]{2,1,0:T(8,128)(2,1)S(1)}, u32[]{:S(2)}, u32[]{:S(2)}) async-start(bf16[16,48,768]{2,1,0:T(8,128)(2,1)} %broadcast_in_dim.7), calls=%async_computation | async-start | bytes 2359296 | tf_op jit(solution)/shard_map/all_to_all | solution.py:354
  11.3 11.1 %collective-permute-start = (bf16[48,768]{1,0:T(8,128)(2,1)}, bf16[48,768]{1,0:T(8,128)(2,1)}, u32[]{:S(2)}, u32[]{:S(2)}) collective-permute-start(bf16[48,768]{1,0:T(8,128)(2,1)} %dynamic-slice_bitcast_fusion), channel_id=1, source_target_pairs={{0,449},{1,448},{64,385},{65,384},{128,321},{129,320},{192,257},{1... | collective-permute-start | bytes 221192 | tf_op jit(solution)/shard_map/ppermute | solution.py:309
  23.4 1.9 collective-permute-start.1
  26.0 4.6 %collective-permute-start.2 = (bf16[72,384]{1,0:T(8,128)(2,1)}, bf16[72,384]{1,0:T(8,128)(2,1)}, u32[]{:S(2)}, u32[]{:S(2)}) collective-permute-start(bf16[72,384]{1,0:T(8,128)(2,1)} %dynamic-slice_bitcast_fusion.1), channel_id=1, source_target_pairs={{0,449},{1,448},{64,385},{65,384},{128,321},{129,320},{192,257},{1... | collective-permute-start | bytes 165896 | tf_op jit(solution)/shard_map/ppermute | solution.py:309
  32.0 1.5 prepare_rows.1
  36.1 0.9 maximum_select_fusion
  38.4 36.0 %all_to_all.25.far_a = bf16[16,96,768]{2,1,0:T(8,128)(2,1)S(1)} all-to-all(bf16[16,96,768]{2,1,0:T(8,128)(2,1)S(1)} %broadcast_in_dim.6), channel_id=1, replica_groups=mesh['zlo'=8,'core'=2,'y'=4,'x'=4,'zhi'=2] {'y','x'}, dimensions={0} | all-to-all | bytes 4718592 | tf_op jit(solution)/shard_map/all_to_all | solution.py:354
  74.4 24.1 %all_to_all.26 = bf16[16,144,384]{2,1,0:T(8,128)(2,1)S(1)} all-to-all(bf16[16,144,384]{2,1,0:T(8,128)(2,1)S(1)} %broadcast_in_dim.8), channel_id=1, replica_groups=mesh['zlo'=8,'core'=2,'y'=4,'x'=4,'zhi'=2] {'y','x'}, dimensions={0} | all-to-all | bytes 3538944 | tf_op jit(solution)/shard_map/all_to_all | solution.py:354
  98.5 6.9 %collective-permute-start.4 = (bf16[16,96,768]{2,1,0:T(8,128)(2,1)S(1)}, bf16[16,96,768]{2,1,0:T(8,128)(2,1)S(1)}, u32[]{:S(2)}, u32[]{:S(2)}) collective-permute-start(bf16[16,96,768]{2,1,0:T(8,128)(2,1)S(1)} %all_to_all.25.far_a), channel_id=1, source_target_pairs={{0,32},{32,0},{1,33},{33,1},{2,34},{34,2},{3,35},{35,3},{4,36},{36... | collective-permute-start | bytes 7077896 | tf_op jit(solution)/shard_map/ppermute | solution.py:350
  105.5 1.9 collective-permute-start.5
  107.4 2.4 %collective-permute-start.3 = (bf16[768,768]{1,0:T(8,128)(2,1)S(1)}, bf16[768,768]{1,0:T(8,128)(2,1)S(1)}, u32[]{:S(2)}, u32[]{:S(2)}) collective-permute-start(bf16[768,768]{1,0:T(8,128)(2,1)S(1)} %bitcast.21), channel_id=1, source_target_pairs={{0,32},{32,0},{1,33},{33,1},{2,34},{34,2},{3,35},{35,3},{4,36},{36... | collective-permute-start | bytes 3538952 | tf_op jit(solution)/shard_map/ppermute | solution.py:350
  109.8 4.0 %collective-permute-done.3.near_b = bf16[768,768]{1,0:T(8,128)(2,1)S(1)} collective-permute-done((bf16[768,768]{1,0:T(8,128)(2,1)S(1)}, bf16[768,768]{1,0:T(8,128)(2,1)S(1)}, u32[]{:S(2)}, u32[]{:S(2)}) %collective-permute-start.3) | collective-permute-done | bytes 1179680 | tf_op jit(solution)/shard_map/ppermute | solution.py:350
  113.8 3.8 %embed_rows.1 = (bf16[192,768]{1,0:T(8,128)(2,1)S(1)}, bf16[128,768]{1,0:T(8,128)(2,1)S(1)}) custom-call(s32[72]{0:T(128)S(1)} %get-tuple-element.42.table, bf16[192,1536]{1,0:T(8,128)(2,1)S(1)} %copy-done.6, bf16[2,192,768]{2,1,0:T(8,128)(2,1)S(1)} %copy-done.8, bf16[768,768]{1,0:T(8,128)(2,1)S(1)} %bitcast.22, ...), custom_call_target="tpu_custom_call" | custom-call | flops 1400000000 | bytes 9000000 | tf_op jit(solution)/shard_map/embed_rows/pallas_call | solution.py:130
  117.7 2.8 %project_rows.1 = (bf16[16,96,128]{2,1,0:T(8,128)(2,1)S(1)}, bf16[768,192]{1,0:T(8,128)(2,1)S(1)}, bf16[1536,192]{1,0:T(8,128)(2,1)S(1)}) custom-call(s32[72]{0:T(128)S(1)} %get-tuple-element.42.table, bf16[192,768]{1,0:T(8,128)(2,1)S(1)} %get-tuple-element.53.own, bf16[2304,384]{1,0:T(8,128)(2,1)S(1)} %bitcast.19, ...), custom_call_target="tpu_custom_call" | custom-call | flops 1000000000 | bytes 5000000 | tf_op jit(solution)/shard_map/project_rows/pallas_call | solution.py:155
  121.2 3.6 %all-to-all-start.3 = ((bf16[16,96,128]{2,1,0:T(8,128)(2,1)}), bf16[16,96,128]{2,1,0:T(8,128)(2,1)S(1)}, u32[]{:S(2)}, u32[]{:S(2)}) async-start(bf16[16,96,128]{2,1,0:T(8,128)(2,1)} %copy-done.10), calls=%async_computation.3 | async-start | bytes 786432 | tf_op jit(solution)/shard_map/all_to_all | solution.py:397
  124.8 11.7 %collective-permute-start.6 = (bf16[128,768]{1,0:T(8,128)(2,1)}, bf16[128,768]{1,0:T(8,128)(2,1)}, u32[]{:S(2)}, u32[]{:S(2)}) collective-permute-start(bf16[128,768]{1,0:T(8,128)(2,1)} %copy-done.19), channel_id=1, source_target_pairs={{0,256},{2,258},{4,260},{6,262},{8,264},{10,266},{12,268},{14,270}... | collective-permute-start | bytes 589832 | tf_op jit(solution)/shard_map/ppermute | solution.py:334
  136.6 8.2 %collective-permute-done.6 = bf16[128,768]{1,0:T(8,128)(2,1)} collective-permute-done((bf16[128,768]{1,0:T(8,128)(2,1)}, bf16[128,768]{1,0:T(8,128)(2,1)}, u32[]{:S(2)}, u32[]{:S(2)}) %collective-permute-start.6) | collective-permute-done | bytes 196640 | tf_op jit(solution)/shard_map/ppermute | solution.py:334
  144.8 7.5 %collective-permute-start.7 = (bf16[96,768]{1,0:T(8,128)(2,1)S(1)}, bf16[96,768]{1,0:T(8,128)(2,1)S(1)}, u32[]{:S(2)}, u32[]{:S(2)}) collective-permute-start(bf16[96,768]{1,0:T(8,128)(2,1)S(1)} %pack_keys.1), channel_id=1, source_target_pairs={{0,1},{1,0},{2,3},{3,2},{4,5},{5,4},{6,7},{7,6},{8,9},{9,8},{10,11... | collective-permute-start | bytes 442376 | tf_op jit(solution)/shard_map/ppermute | solution.py:313
  152.3 1.0 fusion
  153.2 8.0 %collective-permute-start.8 = (bf16[64,768]{1,0:T(8,128)(2,1)S(1)}, bf16[64,768]{1,0:T(8,128)(2,1)S(1)}, u32[]{:S(2)}, u32[]{:S(2)}) collective-permute-start(bf16[64,768]{1,0:T(8,128)(2,1)S(1)} %get-tuple-element.74), channel_id=1, source_target_pairs={{256,1},{258,3},{260,5},{262,7},{264,9},{266,11},{268,13},{270,15}... | collective-permute-start | bytes 294920 | tf_op jit(solution)/shard_map/ppermute | solution.py:346
  161.2 1.3 collective-permute-start.9
  162.5 2.8 %far_own.1 = (f32[48,768]{1,0:T(8,128)S(1)}, f32[1,768]{1,0:T(1,128)S(1)}, f32[1,768]{1,0:T(1,128)S(1)}) custom-call(s32[72]{0:T(128)S(1)} %get-tuple-element.42.table, bf16[16,96,128]{2,1,0:T(8,128)(2,1)S(1)} %all-to-all-done.3.arrived), custom_call_target="tpu_custom_call" | custom-call | flops 300000000 | bytes 700000 | tf_op jit(solution)/shard_map/far_own/pallas_call | solution.py:239
  165.9 9.5 %collective-permute-done.9.after = bf16[64,768]{1,0:T(8,128)(2,1)S(1)} collective-permute-done((bf16[64,768]{1,0:T(8,128)(2,1)S(1)}, bf16[64,768]{1,0:T(8,128)(2,1)S(1)}, u32[]{:S(2)}, u32[]{:S(2)}) %collective-permute-start.9) | collective-permute-done | bytes 98336 | tf_op jit(solution)/shard_map/ppermute | solution.py:346
  176.0 3.0 %far_rest.1 = bf16[16,48,128]{2,1,0:T(8,128)(2,1)S(1)} custom-call(s32[72]{0:T(128)S(1)} %get-tuple-element.42.table, bf16[16,96,128]{2,1,0:T(8,128)(2,1)S(1)} %all-to-all-done.3.arrived, bf16[96,768]{1,0:T(8,128)(2,1)S(1)} %collective-permute-done.7.other, f32[48,768]{1,0:T(8,128)S(1)} %get-tuple-element.62.own_sum, ...), custom_call_target="tpu_custom_call" | custom-call | flops 300000000 | bytes 1000000 | tf_op jit(solution)/shard_map/far_rest/pallas_call | solution.py:269
  179.7 5.3 %all-to-all-start.4 = ((bf16[16,48,128]{2,1,0:T(8,128)(2,1)}), bf16[16,48,128]{2,1,0:T(8,128)(2,1)S(1)}, u32[]{:S(2)}, u32[]{:S(2)}) async-start(bf16[16,48,128]{2,1,0:T(8,128)(2,1)} %copy-done.11), calls=%async_computation.4 | async-start | bytes 393216 | tf_op jit(solution)/shard_map/all_to_all | solution.py:405
  185.0 1.5 copy-done.2
  188.3 5.7 %local_branch.1 = (f32[768,192]{1,0:T(8,128)S(1)}, f32[16,192]{1,0:T(8,128)S(1)}, f32[16,192]{1,0:T(8,128)S(1)}) custom-call(s32[72]{0:T(128)S(1)} %get-tuple-element.42.table, bf16[768,192]{1,0:T(8,128)(2,1)S(1)} %get-tuple-element.66.q, bf16[1536,192]{1,0:T(8,128)(2,1)S(1)} %get-tuple-element.67.kv, bf16[64,768]{1,0:T(8,128)(2,1)S(1)} %copy-done.13, ...), custom_call_target="tpu_custom_call" | custom-call | flops 600000000 | bytes 5000000 | tf_op jit(solution)/shard_map/local_branch/pallas_call | solution.py:202
  193.9 0.9 copy-done.3
  194.9 1.1 copy-done.4
  196.0 2.0 finish_rows.1
  (66 shorter events, 12.0 us)
Async XLA Ops:
  0.0 0.9 copy-start
  1.5 20.9 %copy-start.21 = (bf16[1536,24]{0,1:T(8,128)(2,1)S(1)}, bf16[1536,24]{0,1:T(8,128)(2,1)}, u32[]{:S(2)}) copy-start(bf16[1536,24]{0,1:T(8,128)(2,1)} %param.11) | copy-start | bytes 221188
  3.6 21.8 %copy-start.22 = (bf16[768,72]{0,1:T(8,128)(2,1)S(1)}, bf16[768,72]{0,1:T(8,128)(2,1)}, u32[]{:S(2)}) copy-start(bf16[768,72]{0,1:T(8,128)(2,1)} %param.12) | copy-start | bytes 331780
  3.6 27.1 %copy-start.20 = (bf16[1,192,1536]{2,1,0:T(8,128)(2,1)S(1)}, bf16[1,192,1536]{2,1,0:T(8,128)(2,1)}, u32[]{:S(2)}) copy-start(bf16[1,192,1536]{2,1,0:T(8,128)(2,1)} %param.9) | copy-start | bytes 1769476
  3.6 34.4 %all-to-all-start = ((bf16[16,48,768]{2,1,0:T(8,128)(2,1)}), bf16[16,48,768]{2,1,0:T(8,128)(2,1)S(1)}, u32[]{:S(2)}, u32[]{:S(2)}) async-start(bf16[16,48,768]{2,1,0:T(8,128)(2,1)} %broadcast_in_dim.7), calls=%async_computation | async-start | bytes 2359296 | tf_op jit(solution)/shard_map/all_to_all | solution.py:354
  11.3 25.7 %collective-permute-start = (bf16[48,768]{1,0:T(8,128)(2,1)}, bf16[48,768]{1,0:T(8,128)(2,1)}, u32[]{:S(2)}, u32[]{:S(2)}) collective-permute-start(bf16[48,768]{1,0:T(8,128)(2,1)} %dynamic-slice_bitcast_fusion), channel_id=1, source_target_pairs={{0,449},{1,448},{64,385},{65,384},{128,321},{129,320},{192,257},{1... | collective-permute-start | bytes 221192 | tf_op jit(solution)/shard_map/ppermute | solution.py:309
  23.4 11.8 %collective-permute-start.1 = (bf16[24,768]{1,0:T(8,128)(2,1)S(1)}, bf16[24,768]{1,0:T(8,128)(2,1)}, u32[]{:S(2)}, u32[]{:S(2)}) collective-permute-start(bf16[24,768]{1,0:T(8,128)(2,1)S(1)} %bitcast.25), channel_id=1, source_target_pairs={{0,449},{1,448},{64,385},{65,384},{128,321},{129,320},{192,257},{1... | collective-permute-start | bytes 110600 | tf_op jit(solution)/shard_map/ppermute | solution.py:309
  26.0 10.1 %collective-permute-start.2 = (bf16[72,384]{1,0:T(8,128)(2,1)}, bf16[72,384]{1,0:T(8,128)(2,1)}, u32[]{:S(2)}, u32[]{:S(2)}) collective-permute-start(bf16[72,384]{1,0:T(8,128)(2,1)} %dynamic-slice_bitcast_fusion.1), channel_id=1, source_target_pairs={{0,449},{1,448},{64,385},{65,384},{128,321},{129,320},{192,257},{1... | collective-permute-start | bytes 165896 | tf_op jit(solution)/shard_map/ppermute | solution.py:309
  30.9 1.1 copy-start.9
  31.0 1.1 copy-start.16
  31.0 1.0 copy-start.17
  31.0 1.0 copy-start.18
  33.6 0.8 copy-start.5
  34.4 0.8 copy-start.7
  74.4 39.4 %copy-start.6 = (bf16[192,1536]{1,0:T(8,128)(2,1)S(1)}, bf16[192,1536]{1,0:T(8,128)(2,1)}, u32[]{:S(2)}) copy-start(bf16[192,1536]{1,0:T(8,128)(2,1)} %copy-done.5) | copy-start | bytes 1769476
  74.4 39.4 %copy-start.8 = (bf16[2,192,768]{2,1,0:T(8,128)(2,1)S(1)}, bf16[2,192,768]{2,1,0:T(8,128)(2,1)}, u32[]{:S(2)}) copy-start(bf16[2,192,768]{2,1,0:T(8,128)(2,1)} %copy-done.7) | copy-start | bytes 1769476
  98.5 15.3 %collective-permute-start.4 = (bf16[16,96,768]{2,1,0:T(8,128)(2,1)S(1)}, bf16[16,96,768]{2,1,0:T(8,128)(2,1)S(1)}, u32[]{:S(2)}, u32[]{:S(2)}) collective-permute-start(bf16[16,96,768]{2,1,0:T(8,128)(2,1)S(1)} %all_to_all.25.far_a), channel_id=1, source_target_pairs={{0,32},{32,0},{1,33},{33,1},{2,34},{34,2},{3,35},{35,3},{4,36},{36... | collective-permute-start | bytes 7077896 | tf_op jit(solution)/shard_map/ppermute | solution.py:350
  105.5 12.2 %collective-permute-start.5 = (bf16[2304,384]{1,0:T(8,128)(2,1)S(1)}, bf16[2304,384]{1,0:T(8,128)(2,1)S(1)}, u32[]{:S(2)}, u32[]{:S(2)}) collective-permute-start(bf16[2304,384]{1,0:T(8,128)(2,1)S(1)} %bitcast.18), channel_id=1, source_target_pairs={{0,32},{32,0},{1,33},{33,1},{2,34},{34,2},{3,35},{35,3},{4,36},{36... | collective-permute-start | bytes 5308424 | tf_op jit(solution)/shard_map/ppermute | solution.py:350
  107.4 6.4 %collective-permute-start.3 = (bf16[768,768]{1,0:T(8,128)(2,1)S(1)}, bf16[768,768]{1,0:T(8,128)(2,1)S(1)}, u32[]{:S(2)}, u32[]{:S(2)}) collective-permute-start(bf16[768,768]{1,0:T(8,128)(2,1)S(1)} %bitcast.21), channel_id=1, source_target_pairs={{0,32},{32,0},{1,33},{33,1},{2,34},{34,2},{3,35},{35,3},{4,36},{36... | collective-permute-start | bytes 3538952 | tf_op jit(solution)/shard_map/ppermute | solution.py:350
  117.6 2.8 %copy-start.19 = (bf16[128,768]{1,0:T(8,128)(2,1)}, bf16[128,768]{1,0:T(8,128)(2,1)S(1)}, u32[]{:S(2)}) copy-start(bf16[128,768]{1,0:T(8,128)(2,1)S(1)} %get-tuple-element.57) | copy-start | bytes 589828
  117.7 2.8 %copy-start.1 = (bf16[2304,384]{1,0:T(8,128)(2,1)}, bf16[2304,384]{1,0:T(8,128)(2,1)S(1)}, u32[]{:S(2)}) copy-start(bf16[2304,384]{1,0:T(8,128)(2,1)S(1)} %collective-permute-done.5.q_b) | copy-start | bytes 5308420
  121.2 23.5 %all-to-all-start.3 = ((bf16[16,96,128]{2,1,0:T(8,128)(2,1)}), bf16[16,96,128]{2,1,0:T(8,128)(2,1)S(1)}, u32[]{:S(2)}, u32[]{:S(2)}) async-start(bf16[16,96,128]{2,1,0:T(8,128)(2,1)} %copy-done.10), calls=%async_computation.3 | async-start | bytes 786432 | tf_op jit(solution)/shard_map/all_to_all | solution.py:397
  124.8 19.9 %collective-permute-start.6 = (bf16[128,768]{1,0:T(8,128)(2,1)}, bf16[128,768]{1,0:T(8,128)(2,1)}, u32[]{:S(2)}, u32[]{:S(2)}) collective-permute-start(bf16[128,768]{1,0:T(8,128)(2,1)} %copy-done.19), channel_id=1, source_target_pairs={{0,256},{2,258},{4,260},{6,262},{8,264},{10,266},{12,268},{14,270}... | collective-permute-start | bytes 589832 | tf_op jit(solution)/shard_map/ppermute | solution.py:334
  144.8 31.2 %collective-permute-start.7 = (bf16[96,768]{1,0:T(8,128)(2,1)S(1)}, bf16[96,768]{1,0:T(8,128)(2,1)S(1)}, u32[]{:S(2)}, u32[]{:S(2)}) collective-permute-start(bf16[96,768]{1,0:T(8,128)(2,1)S(1)} %pack_keys.1), channel_id=1, source_target_pairs={{0,1},{1,0},{2,3},{3,2},{4,5},{5,4},{6,7},{7,6},{8,9},{9,8},{10,11... | collective-permute-start | bytes 442376 | tf_op jit(solution)/shard_map/ppermute | solution.py:313
  153.2 12.1 %collective-permute-start.8 = (bf16[64,768]{1,0:T(8,128)(2,1)S(1)}, bf16[64,768]{1,0:T(8,128)(2,1)S(1)}, u32[]{:S(2)}, u32[]{:S(2)}) collective-permute-start(bf16[64,768]{1,0:T(8,128)(2,1)S(1)} %get-tuple-element.74), channel_id=1, source_target_pairs={{256,1},{258,3},{260,5},{262,7},{264,9},{266,11},{268,13},{270,15}... | collective-permute-start | bytes 294920 | tf_op jit(solution)/shard_map/ppermute | solution.py:346
  161.2 14.2 %collective-permute-start.9 = (bf16[64,768]{1,0:T(8,128)(2,1)S(1)}, bf16[64,768]{1,0:T(8,128)(2,1)S(1)}, u32[]{:S(2)}, u32[]{:S(2)}) collective-permute-start(bf16[64,768]{1,0:T(8,128)(2,1)S(1)} %get-tuple-element.73), channel_id=1, source_target_pairs={{258,1},{260,3},{262,5},{264,7},{266,9},{268,11},{270,13},{272,15}... | collective-permute-start | bytes 294920 | tf_op jit(solution)/shard_map/ppermute | solution.py:346
  179.7 15.2 %all-to-all-start.4 = ((bf16[16,48,128]{2,1,0:T(8,128)(2,1)}), bf16[16,48,128]{2,1,0:T(8,128)(2,1)S(1)}, u32[]{:S(2)}, u32[]{:S(2)}) async-start(bf16[16,48,128]{2,1,0:T(8,128)(2,1)} %copy-done.11), calls=%async_computation.4 | async-start | bytes 393216 | tf_op jit(solution)/shard_map/all_to_all | solution.py:405
  185.0 1.5 copy-start.2
  186.5 0.9 copy-start.13
  187.4 0.9 copy-start.15
  193.9 0.9 copy-start.3
  194.9 1.1 copy-start.4
  (4 other events, 2.7 us)

commit v7 on v6

--- a/solution.py
+++ b/solution.py
@@ -18,7 +18,7 @@
 P_ROWS = 24
 PLANES = 16
 PLANE = ("y", "x")
-EVERY = ("zlo", "core", "y", "x", "zhi")
+SEQ = ("y", "x", "zhi")
 NORM_EPS = 1e-06
 BIG_NEGATIVE = -1e30
 SCALE = HEAD_DIM**-0.5
@@ -101,7 +101,7 @@
     return first, second
 
 
-def embed_kernel(table, ctx, res, near_a, near_b, far_a, far_b, out, rims, hidden, normed):
+def embed_kernel(table, ctx, res, near_a, near_b, far_a, far_b, out, tail, head, hidden, normed):
     core, high = table[CORE], table[HIGH]
     first, second = halves(table, ctx, D)
     near = dot_nt(first, near_a[...]) + dot_nt(second, near_b[...]) + res[high].astype(F32)
@@ -120,14 +120,14 @@
     out[...] = total.astype(BF16)
     lane = iota((HALF, TILE_DEV), 1)
     pick = (lane == iota((HALF, TILE_DEV), 0) + (table[COUNT_ME] - HALF)).astype(BF16)
-    rims[:HALF] = dot_nn(pick, out[...]).astype(BF16)
-    rims[HALF:] = out[:HALF]
+    tail[...] = dot_nn(pick, out[...]).astype(BF16)
+    head[...] = out[:HALF]
 
 
 def embed(*args):
     scratch = [pltpu.VMEM((2, TILE_DEV, D), F32), pltpu.VMEM((2, TILE_DEV, D), BF16)]
-    shapes = (((TILE_DEV, D), BF16), ((2 * HALF, D), BF16))
-    return call(embed_kernel, "embed_rows", shapes, "svvvvvv-vv", scratch, 1_400_000_000, 9_000_000)(*args)
+    shapes = (((TILE_DEV, D), BF16), ((HALF, D), BF16), ((HALF, D), BF16))
+    return call(embed_kernel, "embed_rows", shapes, "svvvvvv-vvv", scratch, 1_400_000_000, 9_000_000)(*args)
 
 
 def project_kernel(table, own, q_a, q_b, payload, q_out, kv_out):
@@ -313,39 +313,6 @@
     return lax.ppermute(x, "zhi", [(0, 1), (1, 0)])
 
 
-def rank(z, core, plane):
-    z_low = lax.axis_size("zlo")
-    return ((z % z_low * 2 + core) * PLANES + plane) * 2 + z // z_low
-
-
-def all_places():
-    z_size = 2 * lax.axis_size("zlo")
-    return [(z, core, plane) for z in range(z_size) for core in range(2) for plane in range(PLANES)]
-
-
-def toward(z, core):
-    z_size = 2 * lax.axis_size("zlo")
-    step = z_size // 4
-    return (z + (step if core == 0 else -step)) % z_size
-
-
-def quarter_way(x):
-    pairs = [(rank(z, core, plane), rank(toward(z, core), core, plane)) for z, core, plane in all_places()]
-    return lax.ppermute(x, EVERY, pairs)
-
-
-def to_next(x, sign):
-    pairs = []
-    z_low = lax.axis_size("zlo")
-    for z, core, plane in all_places():
-        half_way = toward(z, core)
-        block = 2 * plane + z // z_low + sign
-        if 0 <= block < 2 * PLANES:
-            target = rank(z % z_low + z_low * (block % 2), core, block // 2)
-            pairs.append((rank(half_way, core, plane), target))
-    return lax.ppermute(x, EVERY, pairs)
-
-
 def other_core(x):
     return lax.ppermute(x, "core", [(0, 1), (1, 0)])
 
@@ -376,32 +343,34 @@
     p_own = lax.dynamic_index_in_dim(p_split, core, 1, keepdims=False).reshape(D, P_ROWS).T
     q_own = lax.dynamic_slice_in_dim(qkv_w, core * (D // 2), D // 2, 0).T
     near_a = over_plane(copies(w_own))
-    w_other = mirrored(w_own)
-    p_other = mirrored(p_own)
+    other_wp = mirrored(jnp.concatenate([w_own, p_own]))
     q_other = mirrored(q_own)
-    q_both = copies(in_order(q_own, q_other, high))
     place = jnp.stack([core, high, plane_id]).astype(I32)
     res_split = resid[0].reshape(TILE_DEV, PLANES, 2, W_ROWS).transpose(2, 0, 1, 3).reshape(2, TILE_DEV, D)
     own_ctx, own_res, table = prepare(place, kept_count, dilation, ctx_in, res_split, tissue)
-    far = copies(jnp.concatenate([w_other, in_order(p_own, p_other, high)]))
-    far, near_a, own_ctx, own_res, table, q_both = hold(far, near_a, own_ctx, own_res, table, q_both)
-    far_a, q_both, near_a = hold(over_plane(far), q_both, near_a)
-    q_a, far_a, near_a = hold(over_plane(q_both), far_a, near_a)
-    near_a, q_a = near_a.reshape(D, D), q_a.reshape(3 * D, D // 2)
+    far = copies(jnp.concatenate([other_wp[:W_ROWS], in_order(p_own, other_wp[W_ROWS:], high)]))
+    far, near_a, own_ctx, own_res, table = hold(far, near_a, own_ctx, own_res, table)
+    far_a = over_plane(far)
+    near_a = near_a.reshape(D, D)
     near_b = other_core(near_a)
+    q_both = copies(in_order(q_own, q_other, high))
+    far_a, near_b, q_both = hold(far_a, near_b, q_both)
+    q_a = over_plane(q_both)
     far_b = other_core(far_a)
+    embedded, tail, head = embed(table, own_ctx, own_res, near_a, near_b, far_a, far_b)
+    blocks = 2 * PLANES
+    before = lax.ppermute(tail, SEQ, [(b, b + 1) for b in range(blocks - 1)])
+    after = lax.ppermute(head, SEQ, [(b + 1, b) for b in range(blocks - 1)])
+    q_a, embedded, before, after = hold(q_a, embedded, before, after)
+    q_a = q_a.reshape(3 * D, D // 2)
     q_b = other_core(q_a)
-    embedded, rims = embed(table, own_ctx, own_res, near_a, near_b, far_a, far_b)
-    rims = quarter_way(rims)
     payload, q_rows, kv_rows = project(table, embedded, q_a, q_b)
-    arrived, rims = hold(lax.all_to_all(payload, PLANE, 0, 0), rims)
+    arrived = lax.all_to_all(payload, PLANE, 0, 0)
     other = across(pack(arrived))
     own_sum, own_best, own_total = far_own(table, arrived)
-    before, after = to_next(rims[:HALF], 1), to_next(rims[HALF:], -1)
-    other, own_sum, before, after = hold(other, own_sum, before, after)
+    local_sum, local_best, local_total = local_branch(table, q_rows, kv_rows, before, after, q_a, q_b)
+    other, own_sum, local_sum = hold(other, own_sum, local_sum)
     answer = far_rest(table, arrived, other, own_sum, own_best, own_total)
-    q_rows, answer = hold(q_rows, answer)
-    local_sum, local_best, local_total = local_branch(table, q_rows, kv_rows, before, after, q_a, q_b)
     answers = lax.all_to_all(answer, PLANE, 0, 0)
     return finish(table, answers, local_sum, local_best, local_total, tissue)
 

time: 202 us -> 189 us (0.936)
  the two profiles are of different devices: /device:TPU:1 before, /device:TPU:64 now
where the time goes in v7:
time: 189 us
  starting transfers between devices  62.4 us (33%)
  waiting for transfers between devices  54.2 us (29%)
  blocking collectives  31.9 us (17%)
  Pallas kernels  24.1 us (13%)
  local copies, waits for them, and re-layouts  15.6 us (8%)
    all_to_all x3, waiting for transfers between devices, over_plane(): return lax.all_to_all(x, PLANE, 0, 0)  30.7 us
    all_to_all x1, blocking collectives, on_device(): arrived = lax.all_to_all(payload, PLANE, 0, 0)  20.3 us
    ppermute x2, starting transfers between devices, mirrored(): return lax.ppermute(x, ('zlo', 'zhi'), pairs)  18.9 us
    all_to_all x3, starting transfers between devices, over_plane(): return lax.all_to_all(x, PLANE, 0, 0)  18.3 us
    all_to_all x1, blocking collectives, on_device(): answers = lax.all_to_all(answer, PLANE, 0, 0)  11.5 us
    ppermute x1, starting transfers between devices, on_device(): before = lax.ppermute(tail, SEQ, [(b, b + 1) for b in range(blocks - 1)])  9.52 us
    ppermute x1, starting transfers between devices, across(): return lax.ppermute(x, 'zhi', [(0, 1), (1, 0)])  8.67 us
    ppermute x1, waiting for transfers between devices, across(): return lax.ppermute(x, 'zhi', [(0, 1), (1, 0)])  7.71 us
  transfers between devices with their start and end apart: 11, of which 7 were waited for; matrix products, arithmetic and copies ran while one was open for 3% of the time, Pallas kernels for 9%

profile of v7, /device:TPU:64, one launch (start us, length us, event | category | flops | bytes accessed | tf_op | source)
XLA Modules:
  0.0 188.6 jit_solution(9630589657145506372)
XLA Ops:
  0.9 1.1 broadcast_in_dim.7
  2.0 7.2 %all-to-all-start = ((bf16[16,48,768]{2,1,0:T(8,128)(2,1)}), bf16[16,48,768]{2,1,0:T(8,128)(2,1)S(1)}, u32[]{:S(2)}, u32[]{:S(2)}) async-start(bf16[16,48,768]{2,1,0:T(8,128)(2,1)} %broadcast_in_dim.7), calls=%async_computation | async-start | bytes 2359296 | tf_op jit(solution)/shard_map/all_to_all | solution.py:321
  10.2 11.4 %collective-permute-start = (bf16[72,768]{1,0:T(8,128)(2,1)S(1)}, bf16[72,768]{1,0:T(8,128)(2,1)}, u32[]{:S(2)}, u32[]{:S(2)}) collective-permute-start(bf16[72,768]{1,0:T(8,128)(2,1)S(1)} %pad_maximum_fusion.1), channel_id=1, source_target_pairs={{0,449},{1,448},{64,385},{65,384},{128,321},{129,320},{192,257},{1... | collective-permute-start | bytes 331784 | tf_op jit(solution)/shard_map/ppermute | solution.py:309
  21.6 1.2 copy.11
  22.8 1.2 copy.12
  24.4 1.5 prepare_rows.1
  29.4 1.7 broadcast_in_dim.6
  31.1 7.4 %all-to-all-start.1 = ((bf16[16,96,768]{2,1,0:T(8,128)(2,1)}), bf16[16,96,768]{2,1,0:T(8,128)(2,1)}, u32[]{:S(2)}, u32[]{:S(2)}) async-start(bf16[16,96,768]{2,1,0:T(8,128)(2,1)} %broadcast_in_dim.6), calls=%async_computation.1 | async-start | bytes 4718592 | tf_op jit(solution)/shard_map/all_to_all | solution.py:321
  38.5 1.9 %collective-permute-start.1 = (bf16[768,768]{1,0:T(8,128)(2,1)S(1)}, bf16[768,768]{1,0:T(8,128)(2,1)S(1)}, u32[]{:S(2)}, u32[]{:S(2)}) collective-permute-start(bf16[768,768]{1,0:T(8,128)(2,1)S(1)} %bitcast.21), channel_id=1, source_target_pairs={{0,32},{32,0},{1,33},{33,1},{2,34},{34,2},{3,35},{35,3},{4,36},{36... | collective-permute-start | bytes 3538952 | tf_op jit(solution)/shard_map/ppermute | solution.py:317
  40.5 7.6 %collective-permute-start.2 = (bf16[72,384]{1,0:T(8,128)(2,1)S(1)}, bf16[72,384]{1,0:T(8,128)(2,1)S(1)}, u32[]{:S(2)}, u32[]{:S(2)}) collective-permute-start(bf16[72,384]{1,0:T(8,128)(2,1)S(1)} %dynamic-slice_bitcast_fusion.1), channel_id=1, source_target_pairs={{0,449},{1,448},{64,385},{65,384},{128,321},{129,320},{192,257},{1... | collective-permute-start | bytes 165896 | tf_op jit(solution)/shard_map/ppermute | solution.py:309
  48.0 3.6 %collective-permute-done.2 = bf16[72,384]{1,0:T(8,128)(2,1)S(1)} collective-permute-done((bf16[72,384]{1,0:T(8,128)(2,1)S(1)}, bf16[72,384]{1,0:T(8,128)(2,1)S(1)}, u32[]{:S(2)}, u32[]{:S(2)}) %collective-permute-start.2) | collective-permute-done | bytes 55328 | tf_op jit(solution)/shard_map/ppermute | solution.py:309
  51.7 20.1 %all-to-all-done.1.far_a = bf16[16,96,768]{2,1,0:T(8,128)(2,1)} async-done(((bf16[16,96,768]{2,1,0:T(8,128)(2,1)}), bf16[16,96,768]{2,1,0:T(8,128)(2,1)}, u32[]{:S(2)}, u32[]{:S(2)}) %all-to-all-start.1) | async-done | bytes 2359328 | tf_op jit(solution)/shard_map/all_to_all | solution.py:321
  71.8 1.4 broadcast_in_dim.8
  73.2 1.9 %collective-permute-start.3 = (bf16[16,96,768]{2,1,0:T(8,128)(2,1)}, bf16[16,96,768]{2,1,0:T(8,128)(2,1)}, u32[]{:S(2)}, u32[]{:S(2)}) collective-permute-start(bf16[16,96,768]{2,1,0:T(8,128)(2,1)} %all-to-all-done.1.far_a), channel_id=1, source_target_pairs={{0,32},{32,0},{1,33},{33,1},{2,34},{34,2},{3,35},{35,3},{4,36},{36... | collective-permute-start | bytes 7077896 | tf_op jit(solution)/shard_map/ppermute | solution.py:317
  75.2 3.7 %all-to-all-start.2 = ((bf16[16,144,384]{2,1,0:T(8,128)(2,1)}), bf16[16,144,384]{2,1,0:T(8,128)(2,1)S(1)}, u32[]{:S(2)}, u32[]{:S(2)}) async-start(bf16[16,144,384]{2,1,0:T(8,128)(2,1)} %broadcast_in_dim.8), calls=%async_computation.2 | async-start | bytes 3538944 | tf_op jit(solution)/shard_map/all_to_all | solution.py:321
  80.0 1.3 copy-done.2
  83.4 6.3 %embed_rows.1 = (bf16[192,768]{1,0:T(8,128)(2,1)S(1)}, bf16[64,768]{1,0:T(8,128)(2,1)}, bf16[64,768]{1,0:T(8,128)(2,1)S(1)}) custom-call(s32[72]{0:T(128)S(1)} %get-tuple-element.38.table, bf16[192,1536]{1,0:T(8,128)(2,1)S(1)} %copy-done.4, bf16[2,192,768]{2,1,0:T(8,128)(2,1)S(1)} %copy-done.6, bf16[768,768]{1,0:T(8,128)(2,1)S(1)} %bitcast.22, ...), custom_call_target="tpu_custom_call" | custom-call | flops 1400000000 | bytes 9000000 | tf_op jit(solution)/shard_map/embed_rows/pallas_call | solution.py:130
  89.7 9.5 %collective-permute-start.4 = (bf16[64,768]{1,0:T(8,128)(2,1)}, bf16[64,768]{1,0:T(8,128)(2,1)S(1)}, u32[]{:S(2)}, u32[]{:S(2)}) collective-permute-start(bf16[64,768]{1,0:T(8,128)(2,1)} %get-tuple-element.47), channel_id=1, source_target_pairs={{0,1},{1,2},{2,3},{3,4},{4,5},{5,6},{6,7},{7,8},{8,9},{9,10},{10,1... | collective-permute-start | bytes 294920 | tf_op jit(solution)/shard_map/ppermute | solution.py:362
  99.2 1.3 collective-permute-start.5
  100.5 10.6 %all-to-all-done.2 = bf16[16,144,384]{2,1,0:T(8,128)(2,1)S(1)} async-done(((bf16[16,144,384]{2,1,0:T(8,128)(2,1)}), bf16[16,144,384]{2,1,0:T(8,128)(2,1)S(1)}, u32[]{:S(2)}, u32[]{:S(2)}) %all-to-all-start.2) | async-done | bytes 1769504 | tf_op jit(solution)/shard_map/all_to_all | solution.py:321
  111.1 7.4 %collective-permute-done.5.after = bf16[64,768]{1,0:T(8,128)(2,1)S(1)} collective-permute-done((bf16[64,768]{1,0:T(8,128)(2,1)S(1)}, bf16[64,768]{1,0:T(8,128)(2,1)S(1)}, u32[]{:S(2)}, u32[]{:S(2)}) %collective-permute-start.5) | collective-permute-done | bytes 98336 | tf_op jit(solution)/shard_map/ppermute | solution.py:363
  118.5 1.9 %collective-permute-start.6 = (bf16[2304,384]{1,0:T(8,128)(2,1)S(1)}, bf16[2304,384]{1,0:T(8,128)(2,1)S(1)}, u32[]{:S(2)}, u32[]{:S(2)}) collective-permute-start(bf16[2304,384]{1,0:T(8,128)(2,1)S(1)} %bitcast.18), channel_id=1, source_target_pairs={{0,32},{32,0},{1,33},{33,1},{2,34},{34,2},{3,35},{35,3},{4,36},{36... | collective-permute-start | bytes 5308424 | tf_op jit(solution)/shard_map/ppermute | solution.py:317
  120.4 3.7 %collective-permute-done.6.q_b = bf16[2304,384]{1,0:T(8,128)(2,1)S(1)} collective-permute-done((bf16[2304,384]{1,0:T(8,128)(2,1)S(1)}, bf16[2304,384]{1,0:T(8,128)(2,1)S(1)}, u32[]{:S(2)}, u32[]{:S(2)}) %collective-permute-start.6) | collective-permute-done | bytes 1769504 | tf_op jit(solution)/shard_map/ppermute | solution.py:317
  124.1 2.8 %project_rows.1 = (bf16[16,96,128]{2,1,0:T(8,128)(2,1)S(1)}, bf16[768,192]{1,0:T(8,128)(2,1)S(1)}, bf16[1536,192]{1,0:T(8,128)(2,1)S(1)}) custom-call(s32[72]{0:T(128)S(1)} %get-tuple-element.38.table, bf16[192,768]{1,0:T(8,128)(2,1)S(1)} %get-tuple-element.49.own, bf16[2304,384]{1,0:T(8,128)(2,1)S(1)} %bitcast.19, ...), custom_call_target="tpu_custom_call" | custom-call | flops 1000000000 | bytes 5000000 | tf_op jit(solution)/shard_map/project_rows/pallas_call | solution.py:155
  126.9 20.3 %all_to_all.25.arrived = bf16[16,96,128]{2,1,0:T(8,128)(2,1)S(1)} all-to-all(bf16[16,96,128]{2,1,0:T(8,128)(2,1)S(1)} %get-tuple-element.51), channel_id=1, replica_groups=mesh['zlo'=8,'core'=2,'y'=4,'x'=4,'zhi'=2] {'y','x'}, dimensions={0} | all-to-all | bytes 786432 | tf_op jit(solution)/shard_map/all_to_all | solution.py:368
  147.3 8.7 %collective-permute-start.7 = (bf16[96,768]{1,0:T(8,128)(2,1)S(1)}, bf16[96,768]{1,0:T(8,128)(2,1)S(1)}, u32[]{:S(2)}, u32[]{:S(2)}) collective-permute-start(bf16[96,768]{1,0:T(8,128)(2,1)S(1)} %pack_keys.1), channel_id=1, source_target_pairs={{0,1},{1,0},{2,3},{3,2},{4,5},{5,4},{6,7},{7,6},{8,9},{9,8},{10,11... | collective-permute-start | bytes 442376 | tf_op jit(solution)/shard_map/ppermute | solution.py:313
  156.0 5.7 %local_branch.1 = (f32[768,192]{1,0:T(8,128)S(1)}, f32[16,192]{1,0:T(8,128)S(1)}, f32[16,192]{1,0:T(8,128)S(1)}) custom-call(s32[72]{0:T(128)S(1)} %get-tuple-element.38.table, bf16[768,192]{1,0:T(8,128)(2,1)S(1)} %get-tuple-element.53.q, bf16[1536,192]{1,0:T(8,128)(2,1)S(1)} %get-tuple-element.54.kv, bf16[64,768]{1,0:T(8,128)(2,1)S(1)} %collective-permute-done.4.before, ...), custom_call_target="tpu_custom_call" | custom-call | flops 600000000 | bytes 5000000 | tf_op jit(solution)/shard_map/local_branch/pallas_call | solution.py:202
  161.7 2.8 %far_own.1 = (f32[48,768]{1,0:T(8,128)S(1)}, f32[1,768]{1,0:T(1,128)S(1)}, f32[1,768]{1,0:T(1,128)S(1)}) custom-call(s32[72]{0:T(128)S(1)} %get-tuple-element.38.table, bf16[16,96,128]{2,1,0:T(8,128)(2,1)S(1)} %all_to_all.25.arrived), custom_call_target="tpu_custom_call" | custom-call | flops 300000000 | bytes 700000 | tf_op jit(solution)/shard_map/far_own/pallas_call | solution.py:239
  164.4 7.7 %collective-permute-done.7.other = bf16[96,768]{1,0:T(8,128)(2,1)S(1)} collective-permute-done((bf16[96,768]{1,0:T(8,128)(2,1)S(1)}, bf16[96,768]{1,0:T(8,128)(2,1)S(1)}, u32[]{:S(2)}, u32[]{:S(2)}) %collective-permute-start.7) | collective-permute-done | bytes 147488 | tf_op jit(solution)/shard_map/ppermute | solution.py:313
  172.1 3.0 %far_rest.1 = bf16[16,48,128]{2,1,0:T(8,128)(2,1)S(1)} custom-call(s32[72]{0:T(128)S(1)} %get-tuple-element.38.table, bf16[16,96,128]{2,1,0:T(8,128)(2,1)S(1)} %all_to_all.25.arrived, bf16[96,768]{1,0:T(8,128)(2,1)S(1)} %collective-permute-done.7.other, f32[48,768]{1,0:T(8,128)S(1)} %get-tuple-element.59.own_sum, f32[1,768]{1,0:T(1,128)S(1)} %get-tuple-element.60.own_best, ...), custom_call_target="tpu_custom_call" | custom-call | flops 300000000 | bytes 1000000 | tf_op jit(solution)/shard_map/far_rest/pallas_call | solution.py:269
  175.1 11.5 %all_to_all.26.answers = bf16[16,48,128]{2,1,0:T(8,128)(2,1)S(1)} all-to-all(bf16[16,48,128]{2,1,0:T(8,128)(2,1)S(1)} %far_rest.1), channel_id=1, replica_groups=mesh['zlo'=8,'core'=2,'y'=4,'x'=4,'zhi'=2] {'y','x'}, dimensions={0} | all-to-all | bytes 393216 | tf_op jit(solution)/shard_map/all_to_all | solution.py:374
  186.6 2.0 %finish_rows.1 = bf16[1,192,768]{2,1,0:T(8,128)(2,1)} custom-call(s32[72]{0:T(128)S(1)} %get-tuple-element.38.table, bf16[16,48,128]{2,1,0:T(8,128)(2,1)S(1)} %all_to_all.26.answers, f32[768,192]{1,0:T(8,128)S(1)} %get-tuple-element.62.local_sum, f32[16,192]{1,0:T(8,128)S(1)} %get-tuple-element.63.local_best, f32[16,192]{1,0:T(8,128)S(1)} %get-tuple-element.64.local_total, ...), custom_call_target="tpu_custom_call" | custom-call | flops 100000000 | bytes 1500000 | tf_op jit(solution)/shard_map/finish_rows/pallas_call | solution.py:299
  (46 shorter events, 9.1 us)
Async XLA Ops:
  0.0 0.9 copy-start
  0.9 8.3 %copy-start.12 = (bf16[1536,24]{0,1:T(8,128)(2,1)S(1)}, bf16[1536,24]{0,1:T(8,128)(2,1)}, u32[]{:S(2)}) copy-start(bf16[1536,24]{0,1:T(8,128)(2,1)} %param.11) | copy-start | bytes 221188
  2.0 19.6 %copy-start.11 = (bf16[1,192,1536]{2,1,0:T(8,128)(2,1)S(1)}, bf16[1,192,1536]{2,1,0:T(8,128)(2,1)}, u32[]{:S(2)}) copy-start(bf16[1,192,1536]{2,1,0:T(8,128)(2,1)} %param.9) | copy-start | bytes 1769476
  2.0 27.4 %all-to-all-start = ((bf16[16,48,768]{2,1,0:T(8,128)(2,1)}), bf16[16,48,768]{2,1,0:T(8,128)(2,1)S(1)}, u32[]{:S(2)}, u32[]{:S(2)}) async-start(bf16[16,48,768]{2,1,0:T(8,128)(2,1)} %broadcast_in_dim.7), calls=%async_computation | async-start | bytes 2359296 | tf_op jit(solution)/shard_map/all_to_all | solution.py:321
  10.2 17.5 %collective-permute-start = (bf16[72,768]{1,0:T(8,128)(2,1)S(1)}, bf16[72,768]{1,0:T(8,128)(2,1)}, u32[]{:S(2)}, u32[]{:S(2)}) collective-permute-start(bf16[72,768]{1,0:T(8,128)(2,1)S(1)} %pad_maximum_fusion.1), channel_id=1, source_target_pairs={{0,449},{1,448},{64,385},{65,384},{128,321},{129,320},{192,257},{1... | collective-permute-start | bytes 331784 | tf_op jit(solution)/shard_map/ppermute | solution.py:309
  22.8 1.6 copy-start.7
  22.8 1.6 copy-start.8
  22.8 1.6 copy-start.9
  22.8 1.6 copy-start.10
  26.0 0.9 copy-start.3
  26.8 0.9 copy-start.5
  31.1 9.3 %copy-start.13 = (bf16[768,72]{0,1:T(8,128)(2,1)S(1)}, bf16[768,72]{0,1:T(8,128)(2,1)}, u32[]{:S(2)}) copy-start(bf16[768,72]{0,1:T(8,128)(2,1)} %param.12) | copy-start | bytes 331780
  31.1 40.7 %all-to-all-start.1 = ((bf16[16,96,768]{2,1,0:T(8,128)(2,1)}), bf16[16,96,768]{2,1,0:T(8,128)(2,1)}, u32[]{:S(2)}, u32[]{:S(2)}) async-start(bf16[16,96,768]{2,1,0:T(8,128)(2,1)} %broadcast_in_dim.6), calls=%async_computation.1 | async-start | bytes 4718592 | tf_op jit(solution)/shard_map/all_to_all | solution.py:321
  38.5 13.2 %collective-permute-start.1 = (bf16[768,768]{1,0:T(8,128)(2,1)S(1)}, bf16[768,768]{1,0:T(8,128)(2,1)S(1)}, u32[]{:S(2)}, u32[]{:S(2)}) collective-permute-start(bf16[768,768]{1,0:T(8,128)(2,1)S(1)} %bitcast.21), channel_id=1, source_target_pairs={{0,32},{32,0},{1,33},{33,1},{2,34},{34,2},{3,35},{35,3},{4,36},{36... | collective-permute-start | bytes 3538952 | tf_op jit(solution)/shard_map/ppermute | solution.py:317
  40.5 11.2 %collective-permute-start.2 = (bf16[72,384]{1,0:T(8,128)(2,1)S(1)}, bf16[72,384]{1,0:T(8,128)(2,1)S(1)}, u32[]{:S(2)}, u32[]{:S(2)}) collective-permute-start(bf16[72,384]{1,0:T(8,128)(2,1)S(1)} %dynamic-slice_bitcast_fusion.1), channel_id=1, source_target_pairs={{0,449},{1,448},{64,385},{65,384},{128,321},{129,320},{192,257},{1... | collective-permute-start | bytes 165896 | tf_op jit(solution)/shard_map/ppermute | solution.py:309
  51.7 23.4 %copy-start.1 = (bf16[768,768]{1,0:T(8,128)(2,1)}, bf16[768,768]{1,0:T(8,128)(2,1)S(1)}, u32[]{:S(2)}) copy-start(bf16[768,768]{1,0:T(8,128)(2,1)S(1)} %collective-permute-done.1.near_b) | copy-start | bytes 3538948
  73.2 6.8 %collective-permute-start.3 = (bf16[16,96,768]{2,1,0:T(8,128)(2,1)}, bf16[16,96,768]{2,1,0:T(8,128)(2,1)}, u32[]{:S(2)}, u32[]{:S(2)}) collective-permute-start(bf16[16,96,768]{2,1,0:T(8,128)(2,1)} %all-to-all-done.1.far_a), channel_id=1, source_target_pairs={{0,32},{32,0},{1,33},{33,1},{2,34},{34,2},{3,35},{35,3},{4,36},{36... | collective-permute-start | bytes 7077896 | tf_op jit(solution)/shard_map/ppermute | solution.py:317
  75.2 36.0 %all-to-all-start.2 = ((bf16[16,144,384]{2,1,0:T(8,128)(2,1)}), bf16[16,144,384]{2,1,0:T(8,128)(2,1)S(1)}, u32[]{:S(2)}, u32[]{:S(2)}) async-start(bf16[16,144,384]{2,1,0:T(8,128)(2,1)} %broadcast_in_dim.8), calls=%async_computation.2 | async-start | bytes 3538944 | tf_op jit(solution)/shard_map/all_to_all | solution.py:321
  80.0 1.3 copy-start.2
  81.3 1.1 copy-start.4
  82.3 1.1 copy-start.6
  89.7 21.4 %collective-permute-start.4 = (bf16[64,768]{1,0:T(8,128)(2,1)}, bf16[64,768]{1,0:T(8,128)(2,1)S(1)}, u32[]{:S(2)}, u32[]{:S(2)}) collective-permute-start(bf16[64,768]{1,0:T(8,128)(2,1)} %get-tuple-element.47), channel_id=1, source_target_pairs={{0,1},{1,2},{2,3},{3,4},{4,5},{5,6},{6,7},{7,8},{8,9},{9,10},{10,1... | collective-permute-start | bytes 294920 | tf_op jit(solution)/shard_map/ppermute | solution.py:362
  99.2 19.3 %collective-permute-start.5 = (bf16[64,768]{1,0:T(8,128)(2,1)S(1)}, bf16[64,768]{1,0:T(8,128)(2,1)S(1)}, u32[]{:S(2)}, u32[]{:S(2)}) collective-permute-start(bf16[64,768]{1,0:T(8,128)(2,1)S(1)} %get-tuple-element.48), channel_id=1, source_target_pairs={{1,0},{2,1},{3,2},{4,3},{5,4},{6,5},{7,6},{8,7},{9,8},{10,9},{11,1... | collective-permute-start | bytes 294920 | tf_op jit(solution)/shard_map/ppermute | solution.py:363
  118.5 5.6 %collective-permute-start.6 = (bf16[2304,384]{1,0:T(8,128)(2,1)S(1)}, bf16[2304,384]{1,0:T(8,128)(2,1)S(1)}, u32[]{:S(2)}, u32[]{:S(2)}) collective-permute-start(bf16[2304,384]{1,0:T(8,128)(2,1)S(1)} %bitcast.18), channel_id=1, source_target_pairs={{0,32},{32,0},{1,33},{33,1},{2,34},{34,2},{3,35},{35,3},{4,36},{36... | collective-permute-start | bytes 5308424 | tf_op jit(solution)/shard_map/ppermute | solution.py:317
  147.3 24.8 %collective-permute-start.7 = (bf16[96,768]{1,0:T(8,128)(2,1)S(1)}, bf16[96,768]{1,0:T(8,128)(2,1)S(1)}, u32[]{:S(2)}, u32[]{:S(2)}) collective-permute-start(bf16[96,768]{1,0:T(8,128)(2,1)S(1)} %pack_keys.1), channel_id=1, source_target_pairs={{0,1},{1,0},{2,3},{3,2},{4,5},{5,4},{6,7},{7,6},{8,9},{9,8},{10,11... | collective-permute-start | bytes 442376 | tf_op jit(solution)/shard_map/ppermute | solution.py:313

commit v8 on v7

--- a/solution.py
+++ b/solution.py
@@ -19,6 +19,7 @@
 PLANES = 16
 PLANE = ("y", "x")
 SEQ = ("y", "x", "zhi")
+EVERY = ("zlo", "core", "y", "x", "zhi")
 NORM_EPS = 1e-06
 BIG_NEGATIVE = -1e30
 SCALE = HEAD_DIM**-0.5
@@ -85,12 +86,12 @@
         start = start + count
     order = (iota((TILE_DEV, TILE_DEV), 0) == listing[0]).astype(BF16)
     own_ctx[...] = dot_tn(order, ctx[0]).astype(BF16)
-    for z in range(2):
-        own_res[z] = dot_tn(order, res[z]).astype(BF16)
+    own_res[...] = dot_tn(order, res[0]).astype(BF16)
 
 
 def prepare(*args):
-    shapes = (((TILE_DEV, D_ENC), BF16), ((2, TILE_DEV, D), BF16), ((ALL_COUNTS + BLOCKS,), I32))
+    rows = ((TILE_DEV, D_ENC), BF16)
+    shapes = (rows, rows, ((ALL_COUNTS + BLOCKS,), I32))
     return call(prepare_kernel, "prepare_rows", shapes, "sssvvv-vvs", [], 250_000_000, 2_400_000)(*args)
 
 
@@ -101,23 +102,29 @@
     return first, second
 
 
-def embed_kernel(table, ctx, res, near_a, near_b, far_a, far_b, out, tail, head, hidden, normed):
-    core, high = table[CORE], table[HIGH]
-    first, second = halves(table, ctx, D)
-    near = dot_nt(first, near_a[...]) + dot_nt(second, near_b[...]) + res[high].astype(F32)
-    hidden[0] = near
-    far = dot_nt(first, far_a[:, :W_ROWS].reshape(D, D)) + dot_nt(second, far_b[:, :W_ROWS].reshape(D, D))
-    far += res[1 - high].astype(F32)
-    hidden[1] = far
-    mean = (jnp.sum(near, axis=1, keepdims=True) + jnp.sum(far, axis=1, keepdims=True)) / D_ENC
-    near, far = hidden[0] - mean, hidden[1] - mean
-    spread = (jnp.sum(near * near, axis=1, keepdims=True) + jnp.sum(far * far, axis=1, keepdims=True)) / D_ENC
-    scale = lax.rsqrt(spread + NORM_EPS)
-    normed[high] = (near * scale).astype(BF16)
-    normed[1 - high] = (far * scale).astype(BF16)
-    total = dot_nt(normed[core], far_a[:, W_ROWS:].reshape(D, D))
-    total += dot_nt(normed[1 - core], far_b[:, W_ROWS:].reshape(D, D))
-    out[...] = total.astype(BF16)
+def embed_kernel(table, ctx, res, own, other, out, tail, head, w, p, hidden, normed):
+    core = table[CORE]
+    for block in range(PLANES):
+        turned = block % 4 * 4 + block // 4
+        at_own = jnp.where(core == 0, block, turned)
+        at_other = jnp.where(core == 0, turned, block)
+        w_rows = slice(block * 2 * W_ROWS, (block + 1) * 2 * W_ROWS)
+        p_rows = slice(block * 2 * P_ROWS, (block + 1) * 2 * P_ROWS)
+        w[core, w_rows] = own[at_own, : 2 * W_ROWS]
+        p[core, p_rows] = own[at_own, 2 * W_ROWS :]
+        w[1 - core, w_rows] = other[at_other, : 2 * W_ROWS]
+        p[1 - core, p_rows] = other[at_other, 2 * W_ROWS :]
+    total = jnp.zeros((TILE_DEV, 1), F32)
+    width = D // 2
+    for n in range(4):
+        columns = slice(n * width, (n + 1) * width)
+        part = res[:, columns].astype(F32) + dot_nt(ctx[:, :D], w[0, columns]) + dot_nt(ctx[:, D:], w[1, columns])
+        hidden[:, columns] = part
+        total += jnp.sum(part, axis=1, keepdims=True)
+    center = hidden[...] - total / D_ENC
+    spread = jnp.sum(center * center, axis=1, keepdims=True) / D_ENC
+    normed[...] = (center * lax.rsqrt(spread + NORM_EPS)).astype(BF16)
+    out[...] = (dot_nt(normed[:, :D], p[0]) + dot_nt(normed[:, D:], p[1])).astype(BF16)
     lane = iota((HALF, TILE_DEV), 1)
     pick = (lane == iota((HALF, TILE_DEV), 0) + (table[COUNT_ME] - HALF)).astype(BF16)
     tail[...] = dot_nn(pick, out[...]).astype(BF16)
@@ -125,9 +132,14 @@
 
 
 def embed(*args):
-    scratch = [pltpu.VMEM((2, TILE_DEV, D), F32), pltpu.VMEM((2, TILE_DEV, D), BF16)]
+    scratch = [
+        pltpu.VMEM((2, D_ENC, D), BF16),
+        pltpu.VMEM((2, D, D), BF16),
+        pltpu.VMEM((TILE_DEV, D_ENC), F32),
+        pltpu.VMEM((TILE_DEV, D_ENC), BF16),
+    ]
     shapes = (((TILE_DEV, D), BF16), ((HALF, D), BF16), ((HALF, D), BF16))
-    return call(embed_kernel, "embed_rows", shapes, "svvvvvv-vvv", scratch, 1_400_000_000, 9_000_000)(*args)
+    return call(embed_kernel, "embed_rows", shapes, "svvvv-vvv", scratch, 1_400_000_000, 9_000_000)(*args)
 
 
 def project_kernel(table, own, q_a, q_b, payload, q_out, kv_out):
@@ -329,6 +341,19 @@
     return jnp.broadcast_to(x[None], (PLANES,) + x.shape)
 
 
+def along_lines(x, stage):
+    groups = []
+    for low in range(lax.axis_size("zlo")):
+        for core in range(2):
+            for high in range(2):
+                for line in range(4):
+                    across_x = (core == 0) == (stage == 0)
+                    plane = [line * 4 + k if across_x else k * 4 + line for k in range(4)]
+                    groups.append([((low * 2 + core) * PLANES + p) * 2 + high for p in plane])
+    spread = jnp.broadcast_to(x[None], (4,) + x.shape)
+    return lax.all_to_all(spread, EVERY, 0, 0, axis_index_groups=groups)
+
+
 def in_order(own, other, high):
     return jnp.where(high == 0, jnp.concatenate([own, other]), jnp.concatenate([other, own]))
 
@@ -339,25 +364,20 @@
     plane_id = lax.axis_index("y") * lax.axis_size("x") + lax.axis_index("x")
 
     w_own = lax.dynamic_slice_in_dim(enc_out_w, core * D, D, 0).T
-    p_split = slide_proj.reshape(PLANES, 2, W_ROWS, P_ROWS)
-    p_own = lax.dynamic_index_in_dim(p_split, core, 1, keepdims=False).reshape(D, P_ROWS).T
+    p_own = lax.dynamic_slice_in_dim(slide_proj, core * D, D, 0).T
     q_own = lax.dynamic_slice_in_dim(qkv_w, core * (D // 2), D // 2, 0).T
-    near_a = over_plane(copies(w_own))
     other_wp = mirrored(jnp.concatenate([w_own, p_own]))
     q_other = mirrored(q_own)
     place = jnp.stack([core, high, plane_id]).astype(I32)
-    res_split = resid[0].reshape(TILE_DEV, PLANES, 2, W_ROWS).transpose(2, 0, 1, 3).reshape(2, TILE_DEV, D)
-    own_ctx, own_res, table = prepare(place, kept_count, dilation, ctx_in, res_split, tissue)
-    far = copies(jnp.concatenate([other_wp[:W_ROWS], in_order(p_own, other_wp[W_ROWS:], high)]))
-    far, near_a, own_ctx, own_res, table = hold(far, near_a, own_ctx, own_res, table)
-    far_a = over_plane(far)
-    near_a = near_a.reshape(D, D)
-    near_b = other_core(near_a)
+    own_ctx, own_res, table = prepare(place, kept_count, dilation, ctx_in, resid, tissue)
+    wp = jnp.concatenate(
+        [in_order(w_own, other_wp[:W_ROWS], high), in_order(p_own, other_wp[W_ROWS:], high)]
+    )
+    wp = along_lines(along_lines(wp, 0).reshape(-1, D), 1).reshape(PLANES, -1, D)
     q_both = copies(in_order(q_own, q_other, high))
-    far_a, near_b, q_both = hold(far_a, near_b, q_both)
+    wp, q_both = hold(wp, q_both)
     q_a = over_plane(q_both)
-    far_b = other_core(far_a)
-    embedded, tail, head = embed(table, own_ctx, own_res, near_a, near_b, far_a, far_b)
+    embedded, tail, head = embed(table, own_ctx, own_res, wp, other_core(wp))
     blocks = 2 * PLANES
     before = lax.ppermute(tail, SEQ, [(b, b + 1) for b in range(blocks - 1)])
     after = lax.ppermute(head, SEQ, [(b + 1, b) for b in range(blocks - 1)])

time: 189 us -> 180 us (0.952)
  the two profiles are of different devices: /device:TPU:64 before, /device:TPU:1 now
where the time goes in v8:
time: 180 us
  waiting for transfers between devices  58.3 us (32%)
  starting transfers between devices  46.5 us (26%)
  blocking collectives  45.7 us (25%)
  Pallas kernels  24.4 us (14%)
  local copies, waits for them, and re-layouts  4.52 us (3%)
    all_to_all x1, blocking collectives, on_device(): arrived = lax.all_to_all(payload, PLANE, 0, 0)  22.4 us
    ppermute x2, waiting for transfers between devices, mirrored(): return lax.ppermute(x, ('zlo', 'zhi'), pairs)  15.9 us
    all_to_all x1, waiting for transfers between devices, along_lines(): return lax.all_to_all(spread, EVERY, 0, 0, axis_index_groups=groups)  15.5 us
    ppermute x2, starting transfers between devices, mirrored(): return lax.ppermute(x, ('zlo', 'zhi'), pairs)  14 us
    all_to_all x1, blocking collectives, along_lines(): return lax.all_to_all(spread, EVERY, 0, 0, axis_index_groups=groups)  13.1 us
    all_to_all x1, waiting for transfers between devices, over_plane(): return lax.all_to_all(x, PLANE, 0, 0)  11.7 us
    all_to_all x1, blocking collectives, on_device(): answers = lax.all_to_all(answer, PLANE, 0, 0)  10.1 us
    ppermute x1, waiting for transfers between devices, across(): return lax.ppermute(x, 'zhi', [(0, 1), (1, 0)])  9.97 us
  transfers between devices with their start and end apart: 9, of which 8 were waited for; matrix products, arithmetic and copies ran while one was open for 0% of the time, Pallas kernels for 9%

profile of v8, /device:TPU:1, one launch (start us, length us, event | category | flops | bytes accessed | tf_op | source)
XLA Modules:
  0.0 179.9 jit_solution(7627480483228952537)
XLA Ops:
  0.0 0.8 dynamic-slice_bitcast_fusion.2
  0.8 0.1 copy-done
  0.9 12.0 %collective-permute-start = (bf16[72,768]{1,0:T(8,128)(2,1)S(1)}, bf16[72,768]{1,0:T(8,128)(2,1)S(1)}, u32[]{:S(2)}, u32[]{:S(2)}) collective-permute-start(bf16[72,768]{1,0:T(8,128)(2,1)S(1)} %pad_maximum_fusion.1), channel_id=1, source_target_pairs={{0,449},{1,448},{64,385},{65,384},{128,321},{129,320},{192,257},{1... | collective-permute-start | bytes 331784 | tf_op jit(solution)/shard_map/ppermute | solution.py:321
  12.9 10.2 %collective-permute-done = bf16[72,768]{1,0:T(8,128)(2,1)S(1)} collective-permute-done((bf16[72,768]{1,0:T(8,128)(2,1)S(1)}, bf16[72,768]{1,0:T(8,128)(2,1)S(1)}, u32[]{:S(2)}, u32[]{:S(2)}) %collective-permute-start) | collective-permute-done | bytes 110624 | tf_op jit(solution)/shard_map/ppermute | solution.py:321
  23.3 13.1 %all_to_all.25 = bf16[4,144,768]{2,1,0:T(8,128)(2,1)S(1)} all-to-all(bf16[4,144,768]{2,1,0:T(8,128)(2,1)S(1)} %broadcast_in_dim.8), channel_id=1, replica_groups={{0,2,4,6},{8,10,12,14},{16,18,20,22},{24,26,28,30},{1,3,5,7},{9,11,13,1..., dimensions={0} | all-to-all | bytes 1769472 | tf_op jit(solution)/shard_map/all_to_all | solution.py:354
  36.4 2.0 %broadcast_in_dim.10 = bf16[4,576,768]{2,1,0:T(8,128)(2,1)} broadcast(bf16[576,768]{1,0:T(8,128)(2,1)S(1)} %bitcast.15), dimensions={1,2} | broadcast | bytes 4423680 | tf_op jit(solution)/shard_map/broadcast_in_dim | solution.py:353
  38.4 4.9 %all-to-all-start.1 = ((bf16[4,576,768]{2,1,0:T(8,128)(2,1)}), bf16[4,576,768]{2,1,0:T(8,128)(2,1)}, u32[]{:S(2)}, u32[]{:S(2)}) async-start(bf16[4,576,768]{2,1,0:T(8,128)(2,1)} %broadcast_in_dim.10), calls=%async_computation.1 | async-start | bytes 7077888 | tf_op jit(solution)/shard_map/all_to_all | solution.py:354
  43.4 2.1 %collective-permute-start.1 = (bf16[72,384]{1,0:T(8,128)(2,1)S(1)}, bf16[72,384]{1,0:T(8,128)(2,1)S(1)}, u32[]{:S(2)}, u32[]{:S(2)}) collective-permute-start(bf16[72,384]{1,0:T(8,128)(2,1)S(1)} %dynamic-slice_bitcast_fusion.1), channel_id=1, source_target_pairs={{0,449},{1,448},{64,385},{65,384},{128,321},{129,320},{192,257},{1... | collective-permute-start | bytes 165896 | tf_op jit(solution)/shard_map/ppermute | solution.py:321
  45.5 5.8 %collective-permute-done.1 = bf16[72,384]{1,0:T(8,128)(2,1)S(1)} collective-permute-done((bf16[72,384]{1,0:T(8,128)(2,1)S(1)}, bf16[72,384]{1,0:T(8,128)(2,1)S(1)}, u32[]{:S(2)}, u32[]{:S(2)}) %collective-permute-start.1) | collective-permute-done | bytes 55328 | tf_op jit(solution)/shard_map/ppermute | solution.py:321
  51.2 15.5 %all-to-all-done.1 = bf16[4,576,768]{2,1,0:T(8,128)(2,1)} async-done(((bf16[4,576,768]{2,1,0:T(8,128)(2,1)}), bf16[4,576,768]{2,1,0:T(8,128)(2,1)}, u32[]{:S(2)}, u32[]{:S(2)}) %all-to-all-start.1) | async-done | bytes 3538976 | tf_op jit(solution)/shard_map/all_to_all | solution.py:354
  66.7 1.4 broadcast_in_dim.22
  68.2 4.6 %collective-permute-start.2 = (bf16[16,144,768]{2,1,0:T(8,128)(2,1)}, bf16[16,144,768]{2,1,0:T(8,128)(2,1)}, u32[]{:S(2)}, u32[]{:S(2)}) collective-permute-start(bf16[16,144,768]{2,1,0:T(8,128)(2,1)} %bitcast.6.own), channel_id=1, source_target_pairs={{0,32},{32,0},{1,33},{33,1},{2,34},{34,2},{3,35},{35,3},{4,36},{36... | collective-permute-start | bytes 10616840 | tf_op jit(solution)/shard_map/ppermute | solution.py:329
  72.8 3.7 %all-to-all-start.2 = ((bf16[16,144,384]{2,1,0:T(8,128)(2,1)}), bf16[16,144,384]{2,1,0:T(8,128)(2,1)S(1)}, u32[]{:S(2)}, u32[]{:S(2)}) async-start(bf16[16,144,384]{2,1,0:T(8,128)(2,1)} %broadcast_in_dim.22), calls=%async_computation.2 | async-start | bytes 3538944 | tf_op jit(solution)/shard_map/all_to_all | solution.py:333
  76.7 1.5 prepare_rows.1
  78.2 0.8 collective-permute-done.2.other
  79.0 6.7 %embed_rows.1 = (bf16[192,768]{1,0:T(8,128)(2,1)S(1)}, bf16[64,768]{1,0:T(8,128)(2,1)S(1)}, bf16[64,768]{1,0:T(8,128)(2,1)S(1)}) custom-call(s32[72]{0:T(128)S(1)} %get-tuple-element.29.table, bf16[192,1536]{1,0:T(8,128)(2,1)S(1)} %get-tuple-element.31.ctx, bf16[192,1536]{1,0:T(8,128)(2,1)S(1)} %get-tuple-element.32.res, bf16[16,144,768]{2,1,0:T(8,128)(2,1)} %bitcast.6.own, ...), custom_call_target="tpu_custom_call" | custom-call | flops 1400000000 | bytes 9000000 | tf_op jit(solution)/shard_map/embed_rows/pallas_call | solution.py:142
  85.7 8.9 %collective-permute-start.3 = (bf16[64,768]{1,0:T(8,128)(2,1)S(1)}, bf16[64,768]{1,0:T(8,128)(2,1)S(1)}, u32[]{:S(2)}, u32[]{:S(2)}) collective-permute-start(bf16[64,768]{1,0:T(8,128)(2,1)S(1)} %get-tuple-element.35), channel_id=1, source_target_pairs={{0,1},{1,2},{2,3},{3,4},{4,5},{5,6},{6,7},{7,8},{8,9},{9,10},{10,1... | collective-permute-start | bytes 294920 | tf_op jit(solution)/shard_map/ppermute | solution.py:382
  94.6 1.3 collective-permute-start.4
  95.9 11.7 %all-to-all-done.2 = bf16[16,144,384]{2,1,0:T(8,128)(2,1)S(1)} async-done(((bf16[16,144,384]{2,1,0:T(8,128)(2,1)}), bf16[16,144,384]{2,1,0:T(8,128)(2,1)S(1)}, u32[]{:S(2)}, u32[]{:S(2)}) %all-to-all-start.2) | async-done | bytes 1769504 | tf_op jit(solution)/shard_map/all_to_all | solution.py:333
  107.6 1.1 collective-permute-done.4.after
  108.7 3.7 %collective-permute-start.5 = (bf16[2304,384]{1,0:T(8,128)(2,1)S(1)}, bf16[2304,384]{1,0:T(8,128)(2,1)S(1)}, u32[]{:S(2)}, u32[]{:S(2)}) collective-permute-start(bf16[2304,384]{1,0:T(8,128)(2,1)S(1)} %bitcast.12), channel_id=1, source_target_pairs={{0,32},{32,0},{1,33},{33,1},{2,34},{34,2},{3,35},{35,3},{4,36},{36... | collective-permute-start | bytes 5308424 | tf_op jit(solution)/shard_map/ppermute | solution.py:329
  112.4 3.3 %collective-permute-done.5.q_b = bf16[2304,384]{1,0:T(8,128)(2,1)S(1)} collective-permute-done((bf16[2304,384]{1,0:T(8,128)(2,1)S(1)}, bf16[2304,384]{1,0:T(8,128)(2,1)S(1)}, u32[]{:S(2)}, u32[]{:S(2)}) %collective-permute-start.5) | collective-permute-done | bytes 1769504 | tf_op jit(solution)/shard_map/ppermute | solution.py:329
  115.7 2.8 %project_rows.1 = (bf16[16,96,128]{2,1,0:T(8,128)(2,1)S(1)}, bf16[768,192]{1,0:T(8,128)(2,1)S(1)}, bf16[1536,192]{1,0:T(8,128)(2,1)S(1)}) custom-call(s32[72]{0:T(128)S(1)} %get-tuple-element.29.table, bf16[192,768]{1,0:T(8,128)(2,1)S(1)} %get-tuple-element.37.own, bf16[2304,384]{1,0:T(8,128)(2,1)S(1)} %bitcast.13, ...), custom_call_target="tpu_custom_call" | custom-call | flops 1000000000 | bytes 5000000 | tf_op jit(solution)/shard_map/project_rows/pallas_call | solution.py:167
  118.5 22.4 %all_to_all.26.arrived = bf16[16,96,128]{2,1,0:T(8,128)(2,1)S(1)} all-to-all(bf16[16,96,128]{2,1,0:T(8,128)(2,1)S(1)} %get-tuple-element.39), channel_id=1, replica_groups=mesh['zlo'=8,'core'=2,'y'=4,'x'=4,'zhi'=2] {'y','x'}, dimensions={0} | all-to-all | bytes 786432 | tf_op jit(solution)/shard_map/all_to_all | solution.py:388
  140.9 0.1 pack_keys.1
  141.0 5.5 %collective-permute-start.6 = (bf16[96,768]{1,0:T(8,128)(2,1)S(1)}, bf16[96,768]{1,0:T(8,128)(2,1)S(1)}, u32[]{:S(2)}, u32[]{:S(2)}) collective-permute-start(bf16[96,768]{1,0:T(8,128)(2,1)S(1)} %pack_keys.1), channel_id=1, source_target_pairs={{0,1},{1,0},{2,3},{3,2},{4,5},{5,4},{6,7},{7,6},{8,9},{9,8},{10,11... | collective-permute-start | bytes 442376 | tf_op jit(solution)/shard_map/ppermute | solution.py:325
  146.5 5.6 %local_branch.1 = (f32[768,192]{1,0:T(8,128)S(1)}, f32[16,192]{1,0:T(8,128)S(1)}, f32[16,192]{1,0:T(8,128)S(1)}) custom-call(s32[72]{0:T(128)S(1)} %get-tuple-element.29.table, bf16[768,192]{1,0:T(8,128)(2,1)S(1)} %get-tuple-element.41.q, bf16[1536,192]{1,0:T(8,128)(2,1)S(1)} %get-tuple-element.42.kv, bf16[64,768]{1,0:T(8,128)(2,1)S(1)} %collective-permute-done.3.before, ...), custom_call_target="tpu_custom_call" | custom-call | flops 600000000 | bytes 5000000 | tf_op jit(solution)/shard_map/local_branch/pallas_call | solution.py:214
  152.1 2.8 %far_own.1 = (f32[48,768]{1,0:T(8,128)S(1)}, f32[1,768]{1,0:T(1,128)S(1)}, f32[1,768]{1,0:T(1,128)S(1)}) custom-call(s32[72]{0:T(128)S(1)} %get-tuple-element.29.table, bf16[16,96,128]{2,1,0:T(8,128)(2,1)S(1)} %all_to_all.26.arrived), custom_call_target="tpu_custom_call" | custom-call | flops 300000000 | bytes 700000 | tf_op jit(solution)/shard_map/far_own/pallas_call | solution.py:251
  154.9 10.0 %collective-permute-done.6.other = bf16[96,768]{1,0:T(8,128)(2,1)S(1)} collective-permute-done((bf16[96,768]{1,0:T(8,128)(2,1)S(1)}, bf16[96,768]{1,0:T(8,128)(2,1)S(1)}, u32[]{:S(2)}, u32[]{:S(2)}) %collective-permute-start.6) | collective-permute-done | bytes 147488 | tf_op jit(solution)/shard_map/ppermute | solution.py:325
  164.9 3.0 %far_rest.1 = bf16[16,48,128]{2,1,0:T(8,128)(2,1)S(1)} custom-call(s32[72]{0:T(128)S(1)} %get-tuple-element.29.table, bf16[16,96,128]{2,1,0:T(8,128)(2,1)S(1)} %all_to_all.26.arrived, bf16[96,768]{1,0:T(8,128)(2,1)S(1)} %collective-permute-done.6.other, f32[48,768]{1,0:T(8,128)S(1)} %get-tuple-element.47.own_sum, f32[1,768]{1,0:T(1,128)S(1)} %get-tuple-element.48.own_best, ...), custom_call_target="tpu_custom_call" | custom-call | flops 300000000 | bytes 1000000 | tf_op jit(solution)/shard_map/far_rest/pallas_call | solution.py:281
  167.8 10.1 %all_to_all.27.answers = bf16[16,48,128]{2,1,0:T(8,128)(2,1)S(1)} all-to-all(bf16[16,48,128]{2,1,0:T(8,128)(2,1)S(1)} %far_rest.1), channel_id=1, replica_groups=mesh['zlo'=8,'core'=2,'y'=4,'x'=4,'zhi'=2] {'y','x'}, dimensions={0} | all-to-all | bytes 393216 | tf_op jit(solution)/shard_map/all_to_all | solution.py:394
  177.9 2.0 %finish_rows.1 = bf16[1,192,768]{2,1,0:T(8,128)(2,1)} custom-call(s32[72]{0:T(128)S(1)} %get-tuple-element.29.table, bf16[16,48,128]{2,1,0:T(8,128)(2,1)S(1)} %all_to_all.27.answers, f32[768,192]{1,0:T(8,128)S(1)} %get-tuple-element.50.local_sum, f32[16,192]{1,0:T(8,128)S(1)} %get-tuple-element.51.local_best, f32[16,192]{1,0:T(8,128)S(1)} %get-tuple-element.52.local_total, ...), custom_call_target="tpu_custom_call" | custom-call | flops 100000000 | bytes 1500000 | tf_op jit(solution)/shard_map/finish_rows/pallas_call | solution.py:311
  (25 shorter events, 0.3 us)
Async XLA Ops:
  0.0 0.9 copy-start
  0.9 22.2 %collective-permute-start = (bf16[72,768]{1,0:T(8,128)(2,1)S(1)}, bf16[72,768]{1,0:T(8,128)(2,1)S(1)}, u32[]{:S(2)}, u32[]{:S(2)}) collective-permute-start(bf16[72,768]{1,0:T(8,128)(2,1)S(1)} %pad_maximum_fusion.1), channel_id=1, source_target_pairs={{0,449},{1,448},{64,385},{65,384},{128,321},{129,320},{192,257},{1... | collective-permute-start | bytes 331784 | tf_op jit(solution)/shard_map/ppermute | solution.py:321
  38.4 4.9 %copy-start.6 = (bf16[768,72]{0,1:T(8,128)(2,1)S(1)}, bf16[768,72]{0,1:T(8,128)(2,1)}, u32[]{:S(2)}) copy-start(bf16[768,72]{0,1:T(8,128)(2,1)} %param.12) | copy-start | bytes 331780
  38.4 28.3 %all-to-all-start.1 = ((bf16[4,576,768]{2,1,0:T(8,128)(2,1)}), bf16[4,576,768]{2,1,0:T(8,128)(2,1)}, u32[]{:S(2)}, u32[]{:S(2)}) async-start(bf16[4,576,768]{2,1,0:T(8,128)(2,1)} %broadcast_in_dim.10), calls=%async_computation.1 | async-start | bytes 7077888 | tf_op jit(solution)/shard_map/all_to_all | solution.py:354
  43.3 33.3 %copy-start.1 = (bf16[1,192,1536]{2,1,0:T(8,128)(2,1)S(1)}, bf16[1,192,1536]{2,1,0:T(8,128)(2,1)}, u32[]{:S(2)}) copy-start(bf16[1,192,1536]{2,1,0:T(8,128)(2,1)} %ctx.1) | copy-start | bytes 1769476
  43.3 33.3 %copy-start.2 = (bf16[1,192,1536]{2,1,0:T(8,128)(2,1)S(1)}, bf16[1,192,1536]{2,1,0:T(8,128)(2,1)}, u32[]{:S(2)}) copy-start(bf16[1,192,1536]{2,1,0:T(8,128)(2,1)} %res.1) | copy-start | bytes 1769476
  43.3 33.3 %copy-start.3 = (s32[1,1,192]{2,1,0:T(1,128)S(1)}, s32[1,1,192]{2,1,0:T(1,128)}, u32[]{:S(2)}) copy-start(s32[1,1,192]{2,1,0:T(1,128)} %listing.3) | copy-start | bytes 2308
  43.3 33.3 %copy-start.4 = (s32[1,32]{1,0:T(1,128)S(1)}, s32[1,32]{1,0:T(1,128)}, u32[]{:S(2)}) copy-start(s32[1,32]{1,0:T(1,128)} %counts.1) | copy-start | bytes 388
  43.3 33.3 %copy-start.5 = (s32[1,2]{1,0:T(1,128)S(1)}, s32[1,2]{1,0:T(1,128)}, u32[]{:S(2)}) copy-start(s32[1,2]{1,0:T(1,128)} %dilation.1) | copy-start | bytes 28
  43.4 7.8 %collective-permute-start.1 = (bf16[72,384]{1,0:T(8,128)(2,1)S(1)}, bf16[72,384]{1,0:T(8,128)(2,1)S(1)}, u32[]{:S(2)}, u32[]{:S(2)}) collective-permute-start(bf16[72,384]{1,0:T(8,128)(2,1)S(1)} %dynamic-slice_bitcast_fusion.1), channel_id=1, source_target_pairs={{0,449},{1,448},{64,385},{65,384},{128,321},{129,320},{192,257},{1... | collective-permute-start | bytes 165896 | tf_op jit(solution)/shard_map/ppermute | solution.py:321
  68.2 10.8 %collective-permute-start.2 = (bf16[16,144,768]{2,1,0:T(8,128)(2,1)}, bf16[16,144,768]{2,1,0:T(8,128)(2,1)}, u32[]{:S(2)}, u32[]{:S(2)}) collective-permute-start(bf16[16,144,768]{2,1,0:T(8,128)(2,1)} %bitcast.6.own), channel_id=1, source_target_pairs={{0,32},{32,0},{1,33},{33,1},{2,34},{34,2},{3,35},{35,3},{4,36},{36... | collective-permute-start | bytes 10616840 | tf_op jit(solution)/shard_map/ppermute | solution.py:329
  72.8 34.8 %all-to-all-start.2 = ((bf16[16,144,384]{2,1,0:T(8,128)(2,1)}), bf16[16,144,384]{2,1,0:T(8,128)(2,1)S(1)}, u32[]{:S(2)}, u32[]{:S(2)}) async-start(bf16[16,144,384]{2,1,0:T(8,128)(2,1)} %broadcast_in_dim.22), calls=%async_computation.2 | async-start | bytes 3538944 | tf_op jit(solution)/shard_map/all_to_all | solution.py:333
  85.7 21.9 %collective-permute-start.3 = (bf16[64,768]{1,0:T(8,128)(2,1)S(1)}, bf16[64,768]{1,0:T(8,128)(2,1)S(1)}, u32[]{:S(2)}, u32[]{:S(2)}) collective-permute-start(bf16[64,768]{1,0:T(8,128)(2,1)S(1)} %get-tuple-element.35), channel_id=1, source_target_pairs={{0,1},{1,2},{2,3},{3,4},{4,5},{5,6},{6,7},{7,8},{8,9},{9,10},{10,1... | collective-permute-start | bytes 294920 | tf_op jit(solution)/shard_map/ppermute | solution.py:382
  94.6 14.1 %collective-permute-start.4 = (bf16[64,768]{1,0:T(8,128)(2,1)S(1)}, bf16[64,768]{1,0:T(8,128)(2,1)S(1)}, u32[]{:S(2)}, u32[]{:S(2)}) collective-permute-start(bf16[64,768]{1,0:T(8,128)(2,1)S(1)} %get-tuple-element.36), channel_id=1, source_target_pairs={{1,0},{2,1},{3,2},{4,3},{5,4},{6,5},{7,6},{8,7},{9,8},{10,9},{11,1... | collective-permute-start | bytes 294920 | tf_op jit(solution)/shard_map/ppermute | solution.py:383
  108.7 7.0 %collective-permute-start.5 = (bf16[2304,384]{1,0:T(8,128)(2,1)S(1)}, bf16[2304,384]{1,0:T(8,128)(2,1)S(1)}, u32[]{:S(2)}, u32[]{:S(2)}) collective-permute-start(bf16[2304,384]{1,0:T(8,128)(2,1)S(1)} %bitcast.12), channel_id=1, source_target_pairs={{0,32},{32,0},{1,33},{33,1},{2,34},{34,2},{3,35},{35,3},{4,36},{36... | collective-permute-start | bytes 5308424 | tf_op jit(solution)/shard_map/ppermute | solution.py:329
  141.0 23.8 %collective-permute-start.6 = (bf16[96,768]{1,0:T(8,128)(2,1)S(1)}, bf16[96,768]{1,0:T(8,128)(2,1)S(1)}, u32[]{:S(2)}, u32[]{:S(2)}) collective-permute-start(bf16[96,768]{1,0:T(8,128)(2,1)S(1)} %pack_keys.1), channel_id=1, source_target_pairs={{0,1},{1,0},{2,3},{3,2},{4,5},{5,4},{6,7},{7,6},{8,9},{9,8},{10,11... | collective-permute-start | bytes 442376 | tf_op jit(solution)/shard_map/ppermute | solution.py:325

commit v9 on v8

--- a/solution.py
+++ b/solution.py
@@ -12,6 +12,8 @@
 HALF = 64
 TILE_DEV = 192
 SEQ_LEN = 4096
+WINDOW = 320
+KEY_SLOTS = 80
 SLOTS = 48
 LANES = 128
 W_ROWS = 48
@@ -28,10 +30,10 @@
 I32 = jnp.int32
 VMEM_LIMIT = 24 * 1024 * 1024
 
-CORE, HIGH, PLANE_ID, RATE, SEGMENT, START_ME, COUNT_ME = range(7)
-ALL_STARTS = 8
-ALL_COUNTS = 40
-BLOCKS = 32
+CORE, HIGH, PLANE_ID, RATE, SEGMENT = range(5)
+START_ME, COUNT_ME, START_OTHER, COUNT_OTHER, PAIR_START, PAIR_COUNT = range(5, 11)
+ALL_STARTS = 16
+ALL_COUNTS = 32
 
 
 def dot_nn(a, b):
@@ -71,19 +73,23 @@
 def prepare_kernel(place, counts, dilation, ctx, res, listing, own_ctx, own_res, table):
     table[CORE], table[HIGH], table[PLANE_ID] = place[0], place[1], place[2]
     table[RATE], table[SEGMENT] = dilation[0, 1], dilation[0, 0]
-    me = place[2] * 2 + place[1]
+    high = place[1]
     start = jnp.int32(0)
-    for b in range(BLOCKS):
-        count = counts[0, b]
-        table[ALL_STARTS + b] = start
-        table[ALL_COUNTS + b] = count
-
-        @pl.when(me == b)
-        def _(start=start, count=count):
-            table[START_ME] = start
-            table[COUNT_ME] = count
-
-        start = start + count
+    for p in range(PLANES):
+        first, second = counts[0, 2 * p], counts[0, 2 * p + 1]
+        table[ALL_STARTS + p] = start
+        table[ALL_COUNTS + p] = first + second
+
+        @pl.when(place[2] == p)
+        def _(first=first, second=second, start=start):
+            table[PAIR_START] = start
+            table[PAIR_COUNT] = first + second
+            table[COUNT_ME] = jnp.where(high == 0, first, second)
+            table[COUNT_OTHER] = jnp.where(high == 0, second, first)
+            table[START_ME] = jnp.where(high == 0, start, start + first)
+            table[START_OTHER] = jnp.where(high == 0, start + first, start)
+
+        start = start + first + second
     order = (iota((TILE_DEV, TILE_DEV), 0) == listing[0]).astype(BF16)
     own_ctx[...] = dot_tn(order, ctx[0]).astype(BF16)
     own_res[...] = dot_tn(order, res[0]).astype(BF16)
@@ -91,7 +97,7 @@
 
 def prepare(*args):
     rows = ((TILE_DEV, D_ENC), BF16)
-    shapes = (rows, rows, ((ALL_COUNTS + BLOCKS,), I32))
+    shapes = (rows, rows, ((ALL_COUNTS + PLANES,), I32))
     return call(prepare_kernel, "prepare_rows", shapes, "sssvvv-vvs", [], 250_000_000, 2_400_000)(*args)
 
 
@@ -102,7 +108,7 @@
     return first, second
 
 
-def embed_kernel(table, ctx, res, own, other, out, tail, head, w, p, hidden, normed):
+def embed_kernel(table, ctx, res, own, other, out, w, p, hidden, normed):
     core = table[CORE]
     for block in range(PLANES):
         turned = block % 4 * 4 + block // 4
@@ -125,10 +131,6 @@
     spread = jnp.sum(center * center, axis=1, keepdims=True) / D_ENC
     normed[...] = (center * lax.rsqrt(spread + NORM_EPS)).astype(BF16)
     out[...] = (dot_nt(normed[:, :D], p[0]) + dot_nt(normed[:, D:], p[1])).astype(BF16)
-    lane = iota((HALF, TILE_DEV), 1)
-    pick = (lane == iota((HALF, TILE_DEV), 0) + (table[COUNT_ME] - HALF)).astype(BF16)
-    tail[...] = dot_nn(pick, out[...]).astype(BF16)
-    head[...] = out[:HALF]
 
 
 def embed(*args):
@@ -138,61 +140,70 @@
         pltpu.VMEM((TILE_DEV, D_ENC), F32),
         pltpu.VMEM((TILE_DEV, D_ENC), BF16),
     ]
-    shapes = (((TILE_DEV, D), BF16), ((HALF, D), BF16), ((HALF, D), BF16))
-    return call(embed_kernel, "embed_rows", shapes, "svvvv-vvv", scratch, 1_400_000_000, 9_000_000)(*args)
-
-
-def project_kernel(table, own, q_a, q_b, payload, q_out, kv_out):
-    rate, start_me = table[RATE], table[START_ME]
-    first, second = halves(table, own, D // 2)
-    q_out[...] = (dot_nt(q_a[:D], first) + dot_nt(q_b[:D], second)).astype(BF16)
+    shapes = (((TILE_DEV, D), BF16),)
+    return call(embed_kernel, "embed_rows", shapes, "svvvv-v", scratch, 1_400_000_000, 9_000_000)(*args)[0]
+
+
+def project_kernel(table, own, partner, qa, qb, payload, q_out, kv_out, spanned):
+    core, rate, base = table[CORE], table[RATE], table[PAIR_START]
+
+    def placed(first, count, length):
+        lane = iota((WINDOW, length), 1)
+        hit = (iota((WINDOW, length), 0) == lane + first) & (lane < count)
+        return hit.astype(BF16)
+
+    spread = dot_nn(placed(table[START_ME] - base, table[COUNT_ME], TILE_DEV), own[...])
+    spread += dot_nn(placed(table[START_OTHER] - base, table[COUNT_OTHER], TILE_DEV), partner[...])
+    spanned[...] = spread.astype(BF16)
+    half = D // 2
+    lanes_a = pl.ds(pl.multiple_of(core * half, LANES), half)
+    lanes_b = pl.ds(pl.multiple_of((1 - core) * half, LANES), half)
+    own_a, own_b = own[:, lanes_a], own[:, lanes_b]
+    q_out[...] = (dot_nt(qa[:D], own_a) + dot_nt(qb[:D], own_b)).astype(BF16)
+    span_a, span_b = spanned[:, lanes_a], spanned[:, lanes_b]
     for n in range(2):
         rows = slice((n + 1) * D, (n + 2) * D)
-        kv_out[n * D : (n + 1) * D] = (dot_nt(q_a[rows], first) + dot_nt(q_b[rows], second)).astype(BF16)
-    slot = iota((SLOTS, TILE_DEV), 0) * rate
-    lane = iota((SLOTS, TILE_DEV), 1)
-    key_rest = jnp.zeros((LANES - 2 * HEAD_DIM, TILE_DEV), BF16)
+        kv_out[n * D : (n + 1) * D] = (dot_nt(qa[rows], span_a) + dot_nt(qb[rows], span_b)).astype(BF16)
+    key_slot = iota((KEY_SLOTS, WINDOW), 0) * rate
+    key_lane = iota((KEY_SLOTS, WINDOW), 1)
+    query_slot = iota((SLOTS, TILE_DEV), 0) * rate
+    query_lane = iota((SLOTS, TILE_DEV), 1)
+    key_rest = jnp.zeros((LANES - 2 * HEAD_DIM, WINDOW), BF16)
     query_rest = jnp.zeros((LANES - HEAD_DIM, TILE_DEV), BF16)
     for h in range(HEADS):
         rows = slice(h * HEAD_DIM, (h + 1) * HEAD_DIM)
-        pick = (lane == slot + ((h - start_me) & (rate - 1))).astype(BF16)
+        key_first = (h - base) & (rate - 1)
+        key_pick = (key_lane == key_slot + key_first).astype(BF16)
         both = jnp.concatenate([kv_out[rows], kv_out[D + h * HEAD_DIM : D + (h + 1) * HEAD_DIM], key_rest], axis=0)
+        payload[h, :KEY_SLOTS] = dot_nt(key_pick, both).astype(BF16)
+        query_first = (h - table[START_ME]) & (rate - 1)
+        query_pick = (query_lane == query_slot + query_first).astype(BF16)
         ask = jnp.concatenate([q_out[rows], query_rest], axis=0)
-        payload[h, :SLOTS] = dot_nt(pick, both).astype(BF16)
-        payload[h, SLOTS:] = dot_nt(pick, ask).astype(BF16)
+        payload[h, KEY_SLOTS:] = dot_nt(query_pick, ask).astype(BF16)
 
 
 def project(*args):
-    shapes = (((HEADS, 2 * SLOTS, LANES), BF16), ((D, TILE_DEV), BF16), ((2 * D, TILE_DEV), BF16))
-    return call(project_kernel, "project_rows", shapes, "svvv-vvv", [], 1_000_000_000, 5_000_000)(*args)
-
-
-def pack_kernel(arrived, out):
-    rows = arrived[:, :SLOTS].reshape(PLANES * SLOTS, LANES)
-    out[...] = rows.T[: 2 * HEAD_DIM]
-
-
-def pack(*args):
-    shapes = (((2 * HEAD_DIM, PLANES * SLOTS), BF16),)
-    return call(pack_kernel, "pack_keys", shapes, "v-v", [], 1_000_000, 500_000)(*args)[0]
-
-
-def local_kernel(table, q, kv, before, after, q_a, q_b, out_sum, out_best, out_total, rims, rim):
-    start_me, count_me = table[START_ME], table[COUNT_ME]
-    rims[:HALF] = before[...]
-    rims[HALF:] = after[...]
-    first, second = halves(table, rims, D // 2)
-    rim[...] = (dot_nt(q_a[D:], first) + dot_nt(q_b[D:], second)).astype(BF16)
+    shapes = (((HEADS, KEY_SLOTS + SLOTS, LANES), BF16), ((D, TILE_DEV), BF16), ((2 * D, WINDOW), BF16))
+    scratch = [pltpu.VMEM((WINDOW, D), BF16)]
+    return call(project_kernel, "project_rows", shapes, "svvvv-vvv", scratch, 1_500_000_000, 5_000_000)(*args)
+
+
+def local_kernel(table, q, kv, halo, qa, qb, out_sum, out_best, out_total, rim):
+    core, high, start_me = table[CORE], table[HIGH], table[START_ME]
+    half = D // 2
+    halo_a = halo[:, pl.ds(pl.multiple_of(core * half, LANES), half)]
+    halo_b = halo[:, pl.ds(pl.multiple_of((1 - core) * half, LANES), half)]
+    rim[...] = (dot_nt(qa[D:], halo_a) + dot_nt(qb[D:], halo_b)).astype(BF16)
     length = jnp.full((1, 1), table[SEGMENT], I32).astype(F32)
 
     def segment(position):
         return jnp.floor((position.astype(F32) + 0.5) / length)
 
     query_seg = segment(start_me + iota((1, TILE_DEV), 1))
-    key_at = iota((TILE_DEV, 1), 0)
-    key_seg = jnp.where(key_at < count_me, segment(start_me + key_at), -1.0)
-    rim_id = iota((2 * HALF, 1), 0)
-    rim_at = start_me + jnp.where(rim_id < HALF, rim_id - HALF, rim_id - HALF + count_me)
+    key_at = iota((WINDOW, 1), 0)
+    key_seg = jnp.where(key_at < table[PAIR_COUNT], segment(table[PAIR_START] + key_at), -1.0)
+    rim_first = table[PAIR_START] + jnp.where(high == 0, -HALF, table[PAIR_COUNT])
+    rim_at = rim_first + iota((HALF, 1), 0)
     rim_seg = jnp.where((rim_at >= 0) & (rim_at < SEQ_LEN), segment(rim_at), -1.0)
     key_ok, rim_ok = key_seg == query_seg, rim_seg == query_seg
     for h in range(HEADS):
@@ -210,75 +221,43 @@
 def local_branch(*args):
     stat = ((HEADS, TILE_DEV), F32)
     shapes = (((D, TILE_DEV), F32), stat, stat)
-    scratch = [pltpu.VMEM((2 * HALF, D), BF16), pltpu.VMEM((2 * D, 2 * HALF), BF16)]
-    return call(local_kernel, "local_branch", shapes, "svvvvvv-vvv", scratch, 600_000_000, 5_000_000, 1_000_000)(*args)
-
-
-def far_scores(table, high, keys, asks, scores):
+    scratch = [pltpu.VMEM((2 * D, HALF), BF16)]
+    return call(local_kernel, "local_branch", shapes, "svvvvv-vvv", scratch, 600_000_000, 5_000_000, 1_000_000)(*args)
+
+
+def far_kernel(table, arrived, answer, scores):
     rate = table[RATE]
-    slot = iota((SLOTS, asks.shape[0]), 0) * rate
-    best = jnp.full((1, asks.shape[0]), BIG_NEGATIVE, F32)
-    for p in range(PLANES):
-        block = 2 * p + high
-        phase = (table[PLANE_ID] - table[ALL_STARTS + block]) & (rate - 1)
-        piece = dot_nt(keys[p * SLOTS : (p + 1) * SLOTS], asks) * SCALE
-        piece = jnp.where(slot + phase < table[ALL_COUNTS + block], piece, BIG_NEGATIVE)
-        scores[p * SLOTS : (p + 1) * SLOTS] = piece
-        best = jnp.maximum(best, jnp.max(piece, axis=0, keepdims=True))
-    return best
-
-
-FAR_GROUP = 8
-FAR_WIDTH = FAR_GROUP * SLOTS
-
-
-def far_own_kernel(table, arrived, out_sum, out_best, out_total, scores):
-    keys = arrived[:, :SLOTS].reshape(PLANES * SLOTS, LANES)
-    for n in range(PLANES // FAR_GROUP):
-        lanes = slice(n * FAR_WIDTH, (n + 1) * FAR_WIDTH)
-        asks = arrived[n * FAR_GROUP : (n + 1) * FAR_GROUP, SLOTS:].reshape(FAR_WIDTH, LANES)
-        best = far_scores(table, table[HIGH], keys, asks, scores)
+    kv = arrived[:, :KEY_SLOTS].reshape(PLANES * KEY_SLOTS, LANES)
+    group = 8
+    width = group * SLOTS
+    slot = iota((KEY_SLOTS, width), 0) * rate
+    for n in range(PLANES // group):
+        asks = arrived[n * group : (n + 1) * group, KEY_SLOTS:].reshape(width, LANES)
+        best = jnp.full((1, width), BIG_NEGATIVE, F32)
+        for p in range(PLANES):
+            phase = (table[PLANE_ID] - table[ALL_STARTS + p]) & (rate - 1)
+            piece = dot_nt(arrived[p, :KEY_SLOTS], asks) * SCALE
+            piece = jnp.where(slot + phase < table[ALL_COUNTS + p], piece, BIG_NEGATIVE)
+            scores[p * KEY_SLOTS : (p + 1) * KEY_SLOTS] = piece
+            best = jnp.maximum(best, jnp.max(piece, axis=0, keepdims=True))
         weights = jnp.exp(scores[...] - best)
-        out_best[:, lanes] = best
-        out_total[:, lanes] = jnp.sum(weights, axis=0, keepdims=True)
-        out_sum[:, lanes] = dot_tn(keys, weights.astype(BF16))[HEAD_DIM : 2 * HEAD_DIM]
-
-
-def far_own(*args):
-    width = PLANES * SLOTS
-    shapes = (((HEAD_DIM, width), F32), ((1, width), F32), ((1, width), F32))
-    scratch = [pltpu.VMEM((width, FAR_WIDTH), F32)]
-    return call(far_own_kernel, "far_own", shapes, "sv-vvv", scratch, 300_000_000, 700_000, 600_000)(*args)
-
-
-def far_rest_kernel(table, arrived, other, own_sum, own_best, own_total, answer, scores):
-    other_t = other[...]
-    keys = other_t.T
-    values = other_t[HEAD_DIM:]
-    for n in range(PLANES // FAR_GROUP):
-        lanes = slice(n * FAR_WIDTH, (n + 1) * FAR_WIDTH)
-        asks = arrived[n * FAR_GROUP : (n + 1) * FAR_GROUP, SLOTS:].reshape(FAR_WIDTH, LANES)[:, : 2 * HEAD_DIM]
-        best_o = own_best[:, lanes]
-        best = jnp.maximum(best_o, far_scores(table, 1 - table[HIGH], keys, asks, scores))
-        weights = jnp.exp(scores[...] - best)
-        scale_o = jnp.exp(best_o - best)
-        total = jnp.sum(weights, axis=0, keepdims=True) + scale_o * own_total[:, lanes]
-        summed = dot_nn(values, weights.astype(BF16)) + scale_o * own_sum[:, lanes]
-        shared = summed / total
+        total = jnp.sum(weights, axis=0, keepdims=True)
+        summed = dot_tn(kv, weights.astype(BF16))
+        shared = summed[HEAD_DIM : 2 * HEAD_DIM] / total
         log_all = best + jnp.log(total)
         log_a = log_all.astype(BF16).astype(F32)
         log_b = (log_all - log_a).astype(BF16).astype(F32)
         log_c = log_all - log_a - log_b
-        row = iota((LANES - HEAD_DIM, FAR_WIDTH), 0)
+        row = iota((LANES - HEAD_DIM, width), 0)
         tail = jnp.where(row == 0, log_a, jnp.where(row == 1, log_b, jnp.where(row == 2, log_c, 0.0)))
         block = jnp.concatenate([shared, tail], axis=0)
-        answer[n * FAR_GROUP : (n + 1) * FAR_GROUP] = block.T.astype(BF16).reshape(FAR_GROUP, SLOTS, LANES)
-
-
-def far_rest(*args):
+        answer[n * group : (n + 1) * group] = block.T.astype(BF16).reshape(group, SLOTS, LANES)
+
+
+def far_branch(*args):
     shapes = (((PLANES, SLOTS, LANES), BF16),)
-    scratch = [pltpu.VMEM((PLANES * SLOTS, FAR_WIDTH), F32)]
-    return call(far_rest_kernel, "far_rest", shapes, "svvvvv-v", scratch, 300_000_000, 1_000_000, 600_000)(*args)[0]
+    scratch = [pltpu.VMEM((PLANES * KEY_SLOTS, PLANES // 2 * SLOTS), F32)]
+    return call(far_kernel, "far_branch", shapes, "sv-v", scratch, 500_000_000, 1_000_000, 1_000_000)(*args)[0]
 
 
 def finish_kernel(table, answers, local_sum, local_best, local_total, listing, out, attended):
@@ -321,8 +300,18 @@
     return lax.ppermute(x, ("zlo", "zhi"), pairs)
 
 
-def across(x):
-    return lax.ppermute(x, "zhi", [(0, 1), (1, 0)])
+def quarter_way(x):
+    z_low = lax.axis_size("zlo")
+
+    def rank(z, core):
+        return (z % z_low * 2 + core) * 2 + z // z_low
+
+    pairs = []
+    for z in range(2 * z_low):
+        for core in range(2):
+            step = z_low // 2 if core == 0 else -(z_low // 2)
+            pairs.append((rank(z, core), rank((z + step) % (2 * z_low), core)))
+    return lax.ppermute(x, ("zlo", "core", "zhi"), pairs)
 
 
 def other_core(x):
@@ -377,20 +366,20 @@
     q_both = copies(in_order(q_own, q_other, high))
     wp, q_both = hold(wp, q_both)
     q_a = over_plane(q_both)
-    embedded, tail, head = embed(table, own_ctx, own_res, wp, other_core(wp))
-    blocks = 2 * PLANES
-    before = lax.ppermute(tail, SEQ, [(b, b + 1) for b in range(blocks - 1)])
-    after = lax.ppermute(head, SEQ, [(b + 1, b) for b in range(blocks - 1)])
-    q_a, embedded, before, after = hold(q_a, embedded, before, after)
+    embedded = embed(table, own_ctx, own_res, wp, other_core(wp))
+    q_a, embedded, on_way = hold(q_a, embedded, quarter_way(embedded))
     q_a = q_a.reshape(3 * D, D // 2)
-    q_b = other_core(q_a)
-    payload, q_rows, kv_rows = project(table, embedded, q_a, q_b)
+    q_b, partner = hold(other_core(q_a), quarter_way(on_way))
+    rim_from = jnp.where(high == 0, table[COUNT_OTHER] - HALF, 0)
+    rim = lax.dynamic_slice_in_dim(partner, rim_from, HALF, 0)
+    halo_pairs = [(p * 2, p * 2 + 2) for p in range(PLANES - 1)]
+    halo_pairs += [(p * 2 + 1, p * 2 - 1) for p in range(1, PLANES)]
+    halo = lax.ppermute(rim, SEQ, halo_pairs)
+    payload, q_rows, kv_rows = project(table, embedded, partner, q_a, q_b)
     arrived = lax.all_to_all(payload, PLANE, 0, 0)
-    other = across(pack(arrived))
-    own_sum, own_best, own_total = far_own(table, arrived)
-    local_sum, local_best, local_total = local_branch(table, q_rows, kv_rows, before, after, q_a, q_b)
-    other, own_sum, local_sum = hold(other, own_sum, local_sum)
-    answer = far_rest(table, arrived, other, own_sum, own_best, own_total)
+    local_sum, local_best, local_total = local_branch(table, q_rows, kv_rows, halo, q_a, q_b)
+    arrived, local_sum = hold(arrived, local_sum)
+    answer = far_branch(table, arrived)
     answers = lax.all_to_all(answer, PLANE, 0, 0)
     return finish(table, answers, local_sum, local_best, local_total, tissue)
 

time: 180 us -> 177 us (0.983)
  blocking collectives: 45.7 us -> 27.8 us
  local copies, waits for them, and re-layouts: 4.52 us -> 11 us
  waiting for transfers between devices: 58.3 us -> 63.2 us
    all_to_all x1 -> x0, blocking collectives: 22.4 us -> none  [on_device(): arrived = lax.all_to_all(payload, PLANE, 0, 0)]
    unnamed x14 -> x30, local copies, waits for them, and re-layouts: 0.15 us -> 5.12 us
    ppermute x3, waiting for transfers between devices: 11.1 us -> 15.7 us  [the longest x2 13.9 us: quarter_way(): return lax.ppermute(x, ('zlo', 'core', 'zhi'), pairs)]
    all_to_all x1, blocking collectives: 10.1 us -> 14.6 us  [on_device(): answers = lax.all_to_all(answer, PLANE, 0, 0)]
    all_to_all x0 -> x1, starting transfers between devices: none -> 4.25 us  [on_device(): arrived = lax.all_to_all(payload, PLANE, 0, 0)]
    all_to_all x1, waiting for transfers between devices: 11.7 us -> 15.2 us  [over_plane(): return lax.all_to_all(x, PLANE, 0, 0)]
    ppermute x2, waiting for transfers between devices: 4.07 us -> 0.67 us  [other_core(): return lax.ppermute(x, 'core', [(0, 1), (1, 0)])]
    ppermute x3, starting transfers between devices: 15.6 us -> 13.3 us  [the longest x2 10 us: quarter_way(): return lax.ppermute(x, ('zlo', 'core', 'zhi'), pairs)]
  transfers between devices with their start and end apart: 9 -> 10, of which waited for: 8 -> 7; matrix products, arithmetic and copies ran while one was open for 0% -> 1% of each run, Pallas kernels for 9% -> 9%
where the time goes in v9:
time: 177 us; the launch traced here: 175 us
  waiting for transfers between devices  63.2 us (36%)
  starting transfers between devices  47.5 us (27%)
  blocking collectives  27.8 us (16%)
  Pallas kernels  24.7 us (14%)
  local copies, waits for them, and re-layouts  11 us (6%)
    ppermute x2, waiting for transfers between devices, mirrored(): return lax.ppermute(x, ('zlo', 'zhi'), pairs)  15.9 us
    all_to_all x1, waiting for transfers between devices, along_lines(): return lax.all_to_all(spread, EVERY, 0, 0, axis_index_groups=groups)  15.7 us
    all_to_all x1, waiting for transfers between devices, over_plane(): return lax.all_to_all(x, PLANE, 0, 0)  15.2 us
    all_to_all x1, blocking collectives, on_device(): answers = lax.all_to_all(answer, PLANE, 0, 0)  14.6 us
    ppermute x2, waiting for transfers between devices, quarter_way(): return lax.ppermute(x, ('zlo', 'core', 'zhi'), pairs)  13.9 us
    ppermute x2, starting transfers between devices, mirrored(): return lax.ppermute(x, ('zlo', 'zhi'), pairs)  13.9 us
    all_to_all x1, blocking collectives, along_lines(): return lax.all_to_all(spread, EVERY, 0, 0, axis_index_groups=groups)  13.1 us
    ppermute x2, starting transfers between devices, quarter_way(): return lax.ppermute(x, ('zlo', 'core', 'zhi'), pairs)  10 us
  transfers between devices with their start and end apart: 10, of which 7 were waited for; matrix products, arithmetic and copies ran while one was open for 1% of the time, Pallas kernels for 9%

profile of v9, /device:TPU:1, one launch (start us, length us, event | category | flops | bytes accessed | tf_op | source)
XLA Modules:
  0.0 175.3 jit_solution(17136258312317972704)
XLA Ops:
  0.0 0.8 dynamic-slice_bitcast_fusion.2
  0.9 12.0 %collective-permute-start = (bf16[72,768]{1,0:T(8,128)(2,1)S(1)}, bf16[72,768]{1,0:T(8,128)(2,1)S(1)}, u32[]{:S(2)}, u32[]{:S(2)}) collective-permute-start(bf16[72,768]{1,0:T(8,128)(2,1)S(1)} %pad_maximum_fusion.1), channel_id=1, source_target_pairs={{0,449},{1,448},{64,385},{65,384},{128,321},{129,320},{192,257},{1... | collective-permute-start | bytes 331784 | tf_op jit(solution)/shard_map/ppermute | solution.py:300
  12.9 10.2 %collective-permute-done = bf16[72,768]{1,0:T(8,128)(2,1)S(1)} collective-permute-done((bf16[72,768]{1,0:T(8,128)(2,1)S(1)}, bf16[72,768]{1,0:T(8,128)(2,1)S(1)}, u32[]{:S(2)}, u32[]{:S(2)}) %collective-permute-start) | collective-permute-done | bytes 110624 | tf_op jit(solution)/shard_map/ppermute | solution.py:300
  23.3 13.1 %all_to_all.25 = bf16[4,144,768]{2,1,0:T(8,128)(2,1)S(1)} all-to-all(bf16[4,144,768]{2,1,0:T(8,128)(2,1)S(1)} %broadcast_in_dim.8), channel_id=1, replica_groups={{0,2,4,6},{8,10,12,14},{16,18,20,22},{24,26,28,30},{1,3,5,7},{9,11,13,1..., dimensions={0} | all-to-all | bytes 1769472 | tf_op jit(solution)/shard_map/all_to_all | solution.py:343
  36.4 2.0 %broadcast_in_dim.10 = bf16[4,576,768]{2,1,0:T(8,128)(2,1)} broadcast(bf16[576,768]{1,0:T(8,128)(2,1)S(1)} %bitcast.16), dimensions={1,2} | broadcast | bytes 4423680 | tf_op jit(solution)/shard_map/broadcast_in_dim | solution.py:342
  38.4 4.9 %all-to-all-start.1 = ((bf16[4,576,768]{2,1,0:T(8,128)(2,1)}), bf16[4,576,768]{2,1,0:T(8,128)(2,1)}, u32[]{:S(2)}, u32[]{:S(2)}) async-start(bf16[4,576,768]{2,1,0:T(8,128)(2,1)} %broadcast_in_dim.10), calls=%async_computation.1 | async-start | bytes 7077888 | tf_op jit(solution)/shard_map/all_to_all | solution.py:343
  43.4 1.9 %collective-permute-start.1 = (bf16[72,384]{1,0:T(8,128)(2,1)S(1)}, bf16[72,384]{1,0:T(8,128)(2,1)S(1)}, u32[]{:S(2)}, u32[]{:S(2)}) collective-permute-start(bf16[72,384]{1,0:T(8,128)(2,1)S(1)} %dynamic-slice_bitcast_fusion.1), channel_id=1, source_target_pairs={{0,449},{1,448},{64,385},{65,384},{128,321},{129,320},{192,257},{1... | collective-permute-start | bytes 165896 | tf_op jit(solution)/shard_map/ppermute | solution.py:300
  45.3 5.8 %collective-permute-done.1 = bf16[72,384]{1,0:T(8,128)(2,1)S(1)} collective-permute-done((bf16[72,384]{1,0:T(8,128)(2,1)S(1)}, bf16[72,384]{1,0:T(8,128)(2,1)S(1)}, u32[]{:S(2)}, u32[]{:S(2)}) %collective-permute-start.1) | collective-permute-done | bytes 55328 | tf_op jit(solution)/shard_map/ppermute | solution.py:300
  51.1 15.7 %all-to-all-done.1 = bf16[4,576,768]{2,1,0:T(8,128)(2,1)} async-done(((bf16[4,576,768]{2,1,0:T(8,128)(2,1)}), bf16[4,576,768]{2,1,0:T(8,128)(2,1)}, u32[]{:S(2)}, u32[]{:S(2)}) %all-to-all-start.1) | async-done | bytes 3538976 | tf_op jit(solution)/shard_map/all_to_all | solution.py:343
  66.8 1.4 broadcast_in_dim.22
  68.2 4.8 %collective-permute-start.2 = (bf16[16,144,768]{2,1,0:T(8,128)(2,1)}, bf16[16,144,768]{2,1,0:T(8,128)(2,1)}, u32[]{:S(2)}, u32[]{:S(2)}) collective-permute-start(bf16[16,144,768]{2,1,0:T(8,128)(2,1)} %bitcast.6.own), channel_id=1, source_target_pairs={{0,32},{32,0},{1,33},{33,1},{2,34},{34,2},{3,35},{35,3},{4,36},{36... | collective-permute-start | bytes 10616840 | tf_op jit(solution)/shard_map/ppermute | solution.py:318
  73.0 3.7 %all-to-all-start.2 = ((bf16[16,144,384]{2,1,0:T(8,128)(2,1)}), bf16[16,144,384]{2,1,0:T(8,128)(2,1)S(1)}, u32[]{:S(2)}, u32[]{:S(2)}) async-start(bf16[16,144,384]{2,1,0:T(8,128)(2,1)} %broadcast_in_dim.22), calls=%async_computation.2 | async-start | bytes 3538944 | tf_op jit(solution)/shard_map/all_to_all | solution.py:322
  76.8 1.6 prepare_rows.1
  79.2 6.6 %embed_rows.1.own = bf16[192,768]{1,0:T(8,128)(2,1)S(1)} custom-call(s32[48]{0:T(128)S(1)} %get-tuple-element.23.table, bf16[192,1536]{1,0:T(8,128)(2,1)S(1)} %get-tuple-element.25.ctx, bf16[192,1536]{1,0:T(8,128)(2,1)S(1)} %get-tuple-element.26.res, bf16[16,144,768]{2,1,0:T(8,128)(2,1)} %bitcast.6.own, bf16[16,144,768]{2,1,0:T(8,128)(2,1)} %collective-permute-done.2.other), custom_call_target="tpu_custom_call" | custom-call | flops 1400000000 | bytes 9000000 | tf_op jit(solution)/shard_map/embed_rows/pallas_call | solution.py:144
  85.7 4.4 %collective-permute-start.3 = (bf16[192,768]{1,0:T(8,128)(2,1)S(1)}, bf16[192,768]{1,0:T(8,128)(2,1)S(1)}, u32[]{:S(2)}, u32[]{:S(2)}) collective-permute-start(bf16[192,768]{1,0:T(8,128)(2,1)S(1)} %embed_rows.1.own), channel_id=1, source_target_pairs={{0,256},{32,289},{64,320},{96,353},{128,384},{160,417},{192,448},{... | collective-permute-start | bytes 884744 | tf_op jit(solution)/shard_map/ppermute | solution.py:314
  90.8 15.2 %all-to-all-done.2 = bf16[16,144,384]{2,1,0:T(8,128)(2,1)S(1)} async-done(((bf16[16,144,384]{2,1,0:T(8,128)(2,1)}), bf16[16,144,384]{2,1,0:T(8,128)(2,1)S(1)}, u32[]{:S(2)}, u32[]{:S(2)}) %all-to-all-start.2) | async-done | bytes 1769504 | tf_op jit(solution)/shard_map/all_to_all | solution.py:322
  106.1 2.7 %collective-permute-start.4 = (bf16[2304,384]{1,0:T(8,128)(2,1)S(1)}, bf16[2304,384]{1,0:T(8,128)(2,1)S(1)}, u32[]{:S(2)}, u32[]{:S(2)}) collective-permute-start(bf16[2304,384]{1,0:T(8,128)(2,1)S(1)} %bitcast.13), channel_id=1, source_target_pairs={{0,32},{32,0},{1,33},{33,1},{2,34},{34,2},{3,35},{35,3},{4,36},{36... | collective-permute-start | bytes 5308424 | tf_op jit(solution)/shard_map/ppermute | solution.py:318
  108.8 5.7 %collective-permute-start.5 = (bf16[192,768]{1,0:T(8,128)(2,1)S(1)}, bf16[192,768]{1,0:T(8,128)(2,1)S(1)}, u32[]{:S(2)}, u32[]{:S(2)}) collective-permute-start(bf16[192,768]{1,0:T(8,128)(2,1)S(1)} %collective-permute-done.3), channel_id=1, source_target_pairs={{0,256},{32,289},{64,320},{96,353},{128,384},{160,417},{192,448},{... | collective-permute-start | bytes 884744 | tf_op jit(solution)/shard_map/ppermute | solution.py:314
  114.4 13.9 %collective-permute-done.5.partner = bf16[192,768]{1,0:T(8,128)(2,1)S(1)} collective-permute-done((bf16[192,768]{1,0:T(8,128)(2,1)S(1)}, bf16[192,768]{1,0:T(8,128)(2,1)S(1)}, u32[]{:S(2)}, u32[]{:S(2)}) %collective-permute-start.5) | collective-permute-done | bytes 294944 | tf_op jit(solution)/shard_map/ppermute | solution.py:314
  128.3 1.1 copy-done.9
  129.4 3.7 %project_rows.1 = (bf16[16,128,128]{2,1,0:T(8,128)(2,1)S(1)}, bf16[768,192]{1,0:T(8,128)(2,1)S(1)}, bf16[1536,320]{1,0:T(8,128)(2,1)S(1)}) custom-call(s32[48]{0:T(128)S(1)} %get-tuple-element.23.table, bf16[192,768]{1,0:T(8,128)(2,1)S(1)} %copy-done.9, bf16[192,768]{1,0:T(8,128)(2,1)S(1)} %collective-permute-done.5.partner, bf16[2304,384]{1,0:T(8,128)(2,1)S(1)} %bitcast.14, ...), custom_call_target="tpu_custom_call" | custom-call | flops 1500000000 | bytes 5000000 | tf_op jit(solution)/shard_map/project_rows/pallas_call | solution.py:188
  133.1 0.8 copy-done.7
  133.9 4.2 %all-to-all-start.3 = ((bf16[16,128,128]{2,1,0:T(8,128)(2,1)}), bf16[16,128,128]{2,1,0:T(8,128)(2,1)}, u32[]{:S(2)}, u32[]{:S(2)}) async-start(bf16[16,128,128]{2,1,0:T(8,128)(2,1)} %copy-done.7), calls=%async_computation.3 | async-start | bytes 1048576 | tf_op jit(solution)/shard_map/all_to_all | solution.py:379
  139.4 0.9 constant_dynamic-slice_fusion
  140.3 3.3 %collective-permute-start.6 = (bf16[64,768]{1,0:T(8,128)(2,1)S(1)}, bf16[64,768]{1,0:T(8,128)(2,1)S(1)}, u32[]{:S(2)}, u32[]{:S(2)}) collective-permute-start(bf16[64,768]{1,0:T(8,128)(2,1)S(1)} %constant_dynamic-slice_fusion), channel_id=1, source_target_pairs={{0,2},{2,4},{4,6},{6,8},{8,10},{10,12},{12,14},{14,16},{16,18},{18... | collective-permute-start | bytes 294920 | tf_op jit(solution)/shard_map/ppermute | solution.py:377
  143.6 1.8 %collective-permute-done.6.halo = bf16[64,768]{1,0:T(8,128)(2,1)S(1)} collective-permute-done((bf16[64,768]{1,0:T(8,128)(2,1)S(1)}, bf16[64,768]{1,0:T(8,128)(2,1)S(1)}, u32[]{:S(2)}, u32[]{:S(2)}) %collective-permute-start.6) | collective-permute-done | bytes 98336 | tf_op jit(solution)/shard_map/ppermute | solution.py:377
  145.4 1.5 copy-done.2
  146.9 7.0 %local_branch.1 = (f32[768,192]{1,0:T(8,128)S(1)}, f32[16,192]{1,0:T(8,128)S(1)}, f32[16,192]{1,0:T(8,128)S(1)}) custom-call(s32[48]{0:T(128)S(1)} %get-tuple-element.23.table, bf16[768,192]{1,0:T(8,128)(2,1)S(1)} %get-tuple-element.34.q, bf16[1536,320]{1,0:T(8,128)(2,1)S(1)} %get-tuple-element.35.kv, bf16[64,768]{1,0:T(8,128)(2,1)S(1)} %collective-permute-done.6.halo, ...), custom_call_target="tpu_custom_call" | custom-call | flops 600000000 | bytes 5000000 | tf_op jit(solution)/shard_map/local_branch/pallas_call | solution.py:225
  153.9 0.9 copy-done.3
  154.8 3.9 %far_branch.1 = bf16[16,48,128]{2,1,0:T(8,128)(2,1)S(1)} custom-call(s32[48]{0:T(128)S(1)} %get-tuple-element.23.table, bf16[16,128,128]{2,1,0:T(8,128)(2,1)} %all-to-all-done.3.arrived), custom_call_target="tpu_custom_call" | custom-call | flops 500000000 | bytes 1000000 | tf_op jit(solution)/shard_map/far_branch/pallas_call | solution.py:260
  158.7 14.6 %all_to_all.26.answers = bf16[16,48,128]{2,1,0:T(8,128)(2,1)S(1)} all-to-all(bf16[16,48,128]{2,1,0:T(8,128)(2,1)S(1)} %far_branch.1), channel_id=1, replica_groups=mesh['zlo'=8,'core'=2,'y'=4,'x'=4,'zhi'=2] {'y','x'}, dimensions={0} | all-to-all | bytes 393216 | tf_op jit(solution)/shard_map/all_to_all | solution.py:383
  173.3 2.0 %finish_rows.1 = bf16[1,192,768]{2,1,0:T(8,128)(2,1)} custom-call(s32[48]{0:T(128)S(1)} %get-tuple-element.23.table, bf16[16,48,128]{2,1,0:T(8,128)(2,1)S(1)} %all_to_all.26.answers, f32[768,192]{1,0:T(8,128)S(1)} %copy-done.4, f32[16,192]{1,0:T(8,128)S(1)} %get-tuple-element.39.local_best, f32[16,192]{1,0:T(8,128)S(1)} %get-tuple-element.40.local_total, ...), custom_call_target="tpu_custom_call" | custom-call | flops 100000000 | bytes 1500000 | tf_op jit(solution)/shard_map/finish_rows/pallas_call | solution.py:290
  (42 shorter events, 2.4 us)
Async XLA Ops:
  0.0 0.9 copy-start
  0.9 22.2 %collective-permute-start = (bf16[72,768]{1,0:T(8,128)(2,1)S(1)}, bf16[72,768]{1,0:T(8,128)(2,1)S(1)}, u32[]{:S(2)}, u32[]{:S(2)}) collective-permute-start(bf16[72,768]{1,0:T(8,128)(2,1)S(1)} %pad_maximum_fusion.1), channel_id=1, source_target_pairs={{0,449},{1,448},{64,385},{65,384},{128,321},{129,320},{192,257},{1... | collective-permute-start | bytes 331784 | tf_op jit(solution)/shard_map/ppermute | solution.py:300
  38.4 4.9 %copy-start.14 = (bf16[768,72]{0,1:T(8,128)(2,1)S(1)}, bf16[768,72]{0,1:T(8,128)(2,1)}, u32[]{:S(2)}) copy-start(bf16[768,72]{0,1:T(8,128)(2,1)} %param.12) | copy-start | bytes 331780
  38.4 28.3 %all-to-all-start.1 = ((bf16[4,576,768]{2,1,0:T(8,128)(2,1)}), bf16[4,576,768]{2,1,0:T(8,128)(2,1)}, u32[]{:S(2)}, u32[]{:S(2)}) async-start(bf16[4,576,768]{2,1,0:T(8,128)(2,1)} %broadcast_in_dim.10), calls=%async_computation.1 | async-start | bytes 7077888 | tf_op jit(solution)/shard_map/all_to_all | solution.py:343
  43.4 7.7 %collective-permute-start.1 = (bf16[72,384]{1,0:T(8,128)(2,1)S(1)}, bf16[72,384]{1,0:T(8,128)(2,1)S(1)}, u32[]{:S(2)}, u32[]{:S(2)}) collective-permute-start(bf16[72,384]{1,0:T(8,128)(2,1)S(1)} %dynamic-slice_bitcast_fusion.1), channel_id=1, source_target_pairs={{0,449},{1,448},{64,385},{65,384},{128,321},{129,320},{192,257},{1... | collective-permute-start | bytes 165896 | tf_op jit(solution)/shard_map/ppermute | solution.py:300
  68.2 8.6 %copy-start.5 = (bf16[1,192,1536]{2,1,0:T(8,128)(2,1)S(1)}, bf16[1,192,1536]{2,1,0:T(8,128)(2,1)}, u32[]{:S(2)}) copy-start(bf16[1,192,1536]{2,1,0:T(8,128)(2,1)} %ctx.1) | copy-start | bytes 1769476
  68.2 8.6 %copy-start.6 = (bf16[1,192,1536]{2,1,0:T(8,128)(2,1)S(1)}, bf16[1,192,1536]{2,1,0:T(8,128)(2,1)}, u32[]{:S(2)}) copy-start(bf16[1,192,1536]{2,1,0:T(8,128)(2,1)} %res.1) | copy-start | bytes 1769476
  68.2 8.6 %copy-start.11 = (s32[1,1,192]{2,1,0:T(1,128)S(1)}, s32[1,1,192]{2,1,0:T(1,128)}, u32[]{:S(2)}) copy-start(s32[1,1,192]{2,1,0:T(1,128)} %listing.3) | copy-start | bytes 2308
  68.2 8.6 %copy-start.12 = (s32[1,32]{1,0:T(1,128)S(1)}, s32[1,32]{1,0:T(1,128)}, u32[]{:S(2)}) copy-start(s32[1,32]{1,0:T(1,128)} %counts.1) | copy-start | bytes 388
  68.2 8.6 %copy-start.13 = (s32[1,2]{1,0:T(1,128)S(1)}, s32[1,2]{1,0:T(1,128)}, u32[]{:S(2)}) copy-start(s32[1,2]{1,0:T(1,128)} %dilation.1) | copy-start | bytes 28
  68.2 11.0 %collective-permute-start.2 = (bf16[16,144,768]{2,1,0:T(8,128)(2,1)}, bf16[16,144,768]{2,1,0:T(8,128)(2,1)}, u32[]{:S(2)}, u32[]{:S(2)}) collective-permute-start(bf16[16,144,768]{2,1,0:T(8,128)(2,1)} %bitcast.6.own), channel_id=1, source_target_pairs={{0,32},{32,0},{1,33},{33,1},{2,34},{34,2},{3,35},{35,3},{4,36},{36... | collective-permute-start | bytes 10616840 | tf_op jit(solution)/shard_map/ppermute | solution.py:318
  73.0 33.1 %all-to-all-start.2 = ((bf16[16,144,384]{2,1,0:T(8,128)(2,1)}), bf16[16,144,384]{2,1,0:T(8,128)(2,1)S(1)}, u32[]{:S(2)}, u32[]{:S(2)}) async-start(bf16[16,144,384]{2,1,0:T(8,128)(2,1)} %broadcast_in_dim.22), calls=%async_computation.2 | async-start | bytes 3538944 | tf_op jit(solution)/shard_map/all_to_all | solution.py:322
  85.7 20.3 %collective-permute-start.3 = (bf16[192,768]{1,0:T(8,128)(2,1)S(1)}, bf16[192,768]{1,0:T(8,128)(2,1)S(1)}, u32[]{:S(2)}, u32[]{:S(2)}) collective-permute-start(bf16[192,768]{1,0:T(8,128)(2,1)S(1)} %embed_rows.1.own), channel_id=1, source_target_pairs={{0,256},{32,289},{64,320},{96,353},{128,384},{160,417},{192,448},{... | collective-permute-start | bytes 884744 | tf_op jit(solution)/shard_map/ppermute | solution.py:314
  90.1 0.7 copy-start.8
  106.1 22.3 %collective-permute-start.4 = (bf16[2304,384]{1,0:T(8,128)(2,1)S(1)}, bf16[2304,384]{1,0:T(8,128)(2,1)S(1)}, u32[]{:S(2)}, u32[]{:S(2)}) collective-permute-start(bf16[2304,384]{1,0:T(8,128)(2,1)S(1)} %bitcast.13), channel_id=1, source_target_pairs={{0,32},{32,0},{1,33},{33,1},{2,34},{34,2},{3,35},{35,3},{4,36},{36... | collective-permute-start | bytes 5308424 | tf_op jit(solution)/shard_map/ppermute | solution.py:318
  108.8 19.6 %collective-permute-start.5 = (bf16[192,768]{1,0:T(8,128)(2,1)S(1)}, bf16[192,768]{1,0:T(8,128)(2,1)S(1)}, u32[]{:S(2)}, u32[]{:S(2)}) collective-permute-start(bf16[192,768]{1,0:T(8,128)(2,1)S(1)} %collective-permute-done.3), channel_id=1, source_target_pairs={{0,256},{32,289},{64,320},{96,353},{128,384},{160,417},{192,448},{... | collective-permute-start | bytes 884744 | tf_op jit(solution)/shard_map/ppermute | solution.py:314
  128.3 4.8 %copy-start.10 = (bf16[192,768]{1,0:T(8,128)(2,1)}, bf16[192,768]{1,0:T(8,128)(2,1)S(1)}, u32[]{:S(2)}) copy-start(bf16[192,768]{1,0:T(8,128)(2,1)S(1)} %collective-permute-done.5.partner) | copy-start | bytes 884740
  128.3 1.1 copy-start.9
  129.4 3.7 %copy-start.1 = (bf16[2304,384]{1,0:T(8,128)(2,1)}, bf16[2304,384]{1,0:T(8,128)(2,1)S(1)}, u32[]{:S(2)}) copy-start(bf16[2304,384]{1,0:T(8,128)(2,1)S(1)} %collective-permute-done.4.qb) | copy-start | bytes 5308420
  133.1 0.8 copy-start.7
  133.9 20.9 %all-to-all-start.3 = ((bf16[16,128,128]{2,1,0:T(8,128)(2,1)}), bf16[16,128,128]{2,1,0:T(8,128)(2,1)}, u32[]{:S(2)}, u32[]{:S(2)}) async-start(bf16[16,128,128]{2,1,0:T(8,128)(2,1)} %copy-done.7), calls=%async_computation.3 | async-start | bytes 1048576 | tf_op jit(solution)/shard_map/all_to_all | solution.py:379
  140.3 5.0 %collective-permute-start.6 = (bf16[64,768]{1,0:T(8,128)(2,1)S(1)}, bf16[64,768]{1,0:T(8,128)(2,1)S(1)}, u32[]{:S(2)}, u32[]{:S(2)}) collective-permute-start(bf16[64,768]{1,0:T(8,128)(2,1)S(1)} %constant_dynamic-slice_fusion), channel_id=1, source_target_pairs={{0,2},{2,4},{4,6},{6,8},{8,10},{10,12},{12,14},{14,16},{16,18},{18... | collective-permute-start | bytes 294920 | tf_op jit(solution)/shard_map/ppermute | solution.py:377
  145.4 1.5 copy-start.2
  153.9 0.9 copy-start.3
  154.8 18.6 %copy-start.4 = (f32[768,192]{1,0:T(8,128)S(1)}, f32[768,192]{1,0:T(8,128)}, u32[]{:S(2)}) copy-start(f32[768,192]{1,0:T(8,128)} %copy-done.3) | copy-start | bytes 1769476

commit v10 on v9

--- a/solution.py
+++ b/solution.py
@@ -144,85 +144,110 @@
     return call(embed_kernel, "embed_rows", shapes, "svvvv-v", scratch, 1_400_000_000, 9_000_000)(*args)[0]
 
 
-def project_kernel(table, own, partner, qa, qb, payload, q_out, kv_out, spanned):
-    core, rate, base = table[CORE], table[RATE], table[PAIR_START]
-
-    def placed(first, count, length):
-        lane = iota((WINDOW, length), 1)
-        hit = (iota((WINDOW, length), 0) == lane + first) & (lane < count)
-        return hit.astype(BF16)
-
-    spread = dot_nn(placed(table[START_ME] - base, table[COUNT_ME], TILE_DEV), own[...])
-    spread += dot_nn(placed(table[START_OTHER] - base, table[COUNT_OTHER], TILE_DEV), partner[...])
-    spanned[...] = spread.astype(BF16)
-    half = D // 2
-    lanes_a = pl.ds(pl.multiple_of(core * half, LANES), half)
-    lanes_b = pl.ds(pl.multiple_of((1 - core) * half, LANES), half)
-    own_a, own_b = own[:, lanes_a], own[:, lanes_b]
-    q_out[...] = (dot_nt(qa[:D], own_a) + dot_nt(qb[:D], own_b)).astype(BF16)
-    span_a, span_b = spanned[:, lanes_a], spanned[:, lanes_b]
-    for n in range(2):
-        rows = slice((n + 1) * D, (n + 2) * D)
-        kv_out[n * D : (n + 1) * D] = (dot_nt(qa[rows], span_a) + dot_nt(qb[rows], span_b)).astype(BF16)
-    key_slot = iota((KEY_SLOTS, WINDOW), 0) * rate
-    key_lane = iota((KEY_SLOTS, WINDOW), 1)
-    query_slot = iota((SLOTS, TILE_DEV), 0) * rate
-    query_lane = iota((SLOTS, TILE_DEV), 1)
-    key_rest = jnp.zeros((LANES - 2 * HEAD_DIM, WINDOW), BF16)
-    query_rest = jnp.zeros((LANES - HEAD_DIM, TILE_DEV), BF16)
+def key_picks(table, h, first, count):
+    rate, base = table[RATE], table[PAIR_START]
+    lane = iota((KEY_SLOTS, TILE_DEV), 1)
+    place = iota((KEY_SLOTS, TILE_DEV), 0) * rate + ((h - base) & (rate - 1)) + (base - first)
+    return ((lane == place) & (lane < count)).astype(BF16)
+
+
+def key_rows(kv, h):
+    rest = jnp.zeros((LANES - 2 * HEAD_DIM, TILE_DEV), BF16)
+    return jnp.concatenate([kv[head_rows(h)], kv[head_rows(HEADS + h)], rest], axis=0)
+
+
+def head_rows(h):
+    return slice(h * HEAD_DIM, (h + 1) * HEAD_DIM)
+
+
+def segments(table, position):
+    length = jnp.full((1, 1), table[SEGMENT], I32).astype(F32)
+    return jnp.floor((position.astype(F32) + 0.5) / length)
+
+
+def own_kernel(table, own, q_a, q_b, payload, q_out, kv_out, out_sum, out_best, out_total):
+    rate, start_me, count_me = table[RATE], table[START_ME], table[COUNT_ME]
+    first, second = halves(table, own, D // 2)
+    q_out[...] = (dot_nt(q_a[:D], first) + dot_nt(q_b[:D], second)).astype(BF16)
+    kv_out[...] = (dot_nt(q_a[D:], first) + dot_nt(q_b[D:], second)).astype(BF16)
+    slot = iota((SLOTS, TILE_DEV), 0) * rate
+    lane = iota((SLOTS, TILE_DEV), 1)
+    rest = jnp.zeros((LANES - HEAD_DIM, TILE_DEV), BF16)
     for h in range(HEADS):
-        rows = slice(h * HEAD_DIM, (h + 1) * HEAD_DIM)
-        key_first = (h - base) & (rate - 1)
-        key_pick = (key_lane == key_slot + key_first).astype(BF16)
-        both = jnp.concatenate([kv_out[rows], kv_out[D + h * HEAD_DIM : D + (h + 1) * HEAD_DIM], key_rest], axis=0)
-        payload[h, :KEY_SLOTS] = dot_nt(key_pick, both).astype(BF16)
-        query_first = (h - table[START_ME]) & (rate - 1)
-        query_pick = (query_lane == query_slot + query_first).astype(BF16)
-        ask = jnp.concatenate([q_out[rows], query_rest], axis=0)
-        payload[h, KEY_SLOTS:] = dot_nt(query_pick, ask).astype(BF16)
-
-
-def project(*args):
-    shapes = (((HEADS, KEY_SLOTS + SLOTS, LANES), BF16), ((D, TILE_DEV), BF16), ((2 * D, WINDOW), BF16))
-    scratch = [pltpu.VMEM((WINDOW, D), BF16)]
-    return call(project_kernel, "project_rows", shapes, "svvvv-vvv", scratch, 1_500_000_000, 5_000_000)(*args)
-
-
-def local_kernel(table, q, kv, halo, qa, qb, out_sum, out_best, out_total, rim):
-    core, high, start_me = table[CORE], table[HIGH], table[START_ME]
-    half = D // 2
-    halo_a = halo[:, pl.ds(pl.multiple_of(core * half, LANES), half)]
-    halo_b = halo[:, pl.ds(pl.multiple_of((1 - core) * half, LANES), half)]
-    rim[...] = (dot_nt(qa[D:], halo_a) + dot_nt(qb[D:], halo_b)).astype(BF16)
-    length = jnp.full((1, 1), table[SEGMENT], I32).astype(F32)
-
-    def segment(position):
-        return jnp.floor((position.astype(F32) + 0.5) / length)
-
-    query_seg = segment(start_me + iota((1, TILE_DEV), 1))
-    key_at = iota((WINDOW, 1), 0)
-    key_seg = jnp.where(key_at < table[PAIR_COUNT], segment(table[PAIR_START] + key_at), -1.0)
-    rim_first = table[PAIR_START] + jnp.where(high == 0, -HALF, table[PAIR_COUNT])
-    rim_at = rim_first + iota((HALF, 1), 0)
-    rim_seg = jnp.where((rim_at >= 0) & (rim_at < SEQ_LEN), segment(rim_at), -1.0)
-    key_ok, rim_ok = key_seg == query_seg, rim_seg == query_seg
+        payload[h, :KEY_SLOTS] = dot_nt(key_picks(table, h, start_me, count_me), key_rows(kv_out, h)).astype(BF16)
+        pick = (lane == slot + ((h - start_me) & (rate - 1))).astype(BF16)
+        ask = jnp.concatenate([q_out[head_rows(h)], rest], axis=0)
+        payload[h, KEY_SLOTS:] = dot_nt(pick, ask).astype(BF16)
+    key_at = iota((TILE_DEV, 1), 0)
+    key_seg = jnp.where(key_at < count_me, segments(table, start_me + key_at), -1.0)
+    allowed = key_seg == segments(table, start_me + iota((1, TILE_DEV), 1))
     for h in range(HEADS):
-        rows = slice(h * HEAD_DIM, (h + 1) * HEAD_DIM)
-        v_rows = slice(D + h * HEAD_DIM, D + (h + 1) * HEAD_DIM)
-        scores = jnp.where(key_ok, dot_tn(kv[rows], q[rows]) * SCALE, BIG_NEGATIVE)
-        rim_scores = jnp.where(rim_ok, dot_tn(rim[rows], q[rows]) * SCALE, BIG_NEGATIVE)
-        best = jnp.maximum(jnp.max(scores, axis=0, keepdims=True), jnp.max(rim_scores, axis=0, keepdims=True))
-        weights, rim_weights = jnp.exp(scores - best), jnp.exp(rim_scores - best)
+        rows = head_rows(h)
+        scores = jnp.where(allowed, dot_tn(kv_out[rows], q_out[rows]) * SCALE, BIG_NEGATIVE)
+        best = jnp.max(scores, axis=0, keepdims=True)
+        weights = jnp.exp(scores - best)
         out_best[h : h + 1] = best
-        out_total[h : h + 1] = jnp.sum(weights, axis=0, keepdims=True) + jnp.sum(rim_weights, axis=0, keepdims=True)
-        out_sum[rows] = dot_nn(kv[v_rows], weights.astype(BF16)) + dot_nn(rim[v_rows], rim_weights.astype(BF16))
-
-
-def local_branch(*args):
+        out_total[h : h + 1] = jnp.sum(weights, axis=0, keepdims=True)
+        out_sum[rows] = dot_nn(kv_out[head_rows(HEADS + h)], weights.astype(BF16))
+
+
+def own_rows(*args):
+    stat = ((HEADS, TILE_DEV), F32)
+    pay = ((HEADS, KEY_SLOTS + SLOTS, LANES), BF16)
+    shapes = (pay, ((D, TILE_DEV), BF16), ((2 * D, TILE_DEV), BF16), ((D, TILE_DEV), F32), stat, stat)
+    return call(own_kernel, "own_rows", shapes, "svvv-vvvvvv", [], 1_000_000_000, 5_000_000, 600_000)(*args)
+
+
+def pair_kernel(table, partner, q_a, q_b, own_payload, payload, rim, kv):
+    first, second = halves(table, partner, D // 2)
+    kv[...] = (dot_nt(q_a[D:], first) + dot_nt(q_b[D:], second)).astype(BF16)
+    for h in range(HEADS):
+        picks = key_picks(table, h, table[START_OTHER], table[COUNT_OTHER])
+        both = dot_nt(picks, key_rows(kv, h)) + own_payload[h, :KEY_SLOTS].astype(F32)
+        payload[h, :KEY_SLOTS] = both.astype(BF16)
+        payload[h, KEY_SLOTS:] = own_payload[h, KEY_SLOTS:]
+    rim_first = jnp.where(table[HIGH] == 0, 0, table[COUNT_OTHER] - HALF)
+    pick = (iota((TILE_DEV, HALF), 0) == iota((TILE_DEV, HALF), 1) + rim_first).astype(BF16)
+    rim[...] = dot_nn(kv[...], pick).astype(BF16)
+
+
+def pair_rows(*args):
+    shapes = (((HEADS, KEY_SLOTS + SLOTS, LANES), BF16), ((2 * D, HALF), BF16))
+    scratch = [pltpu.VMEM((2 * D, TILE_DEV), BF16)]
+    return call(pair_kernel, "pair_rows", shapes, "svvvv-vv", scratch, 700_000_000, 4_000_000)(*args)
+
+
+def rim_kernel(table, q, near_rim, halo, q_a, q_b, own_sum, own_best, own_total, out_sum, out_best, out_total, far_rim):
+    start_me, end_me = table[START_ME], table[START_ME] + table[COUNT_ME]
+    first, second = halves(table, halo, D // 2)
+    far_rim[...] = (dot_nt(q_a[D:], first) + dot_nt(q_b[D:], second)).astype(BF16)
+    query_seg = segments(table, start_me + iota((1, TILE_DEV), 1))
+
+    def allowed(begin):
+        at = begin + iota((HALF, 1), 0)
+        return jnp.where((at >= 0) & (at < SEQ_LEN), segments(table, at), -1.0) == query_seg
+
+    upper = table[HIGH] == 0
+    near_ok = allowed(jnp.where(upper, end_me, start_me - HALF))
+    far_ok = allowed(jnp.where(upper, start_me - HALF, end_me))
+    for h in range(HEADS):
+        rows, v_rows = head_rows(h), head_rows(HEADS + h)
+        near = jnp.where(near_ok, dot_tn(near_rim[rows], q[rows]) * SCALE, BIG_NEGATIVE)
+        far = jnp.where(far_ok, dot_tn(far_rim[rows], q[rows]) * SCALE, BIG_NEGATIVE)
+        best_o = own_best[h : h + 1]
+        best = jnp.maximum(jnp.max(jnp.maximum(near, far), axis=0, keepdims=True), best_o)
+        near, far, scale = jnp.exp(near - best), jnp.exp(far - best), jnp.exp(best_o - best)
+        out_best[h : h + 1] = best
+        out_total[h : h + 1] = jnp.sum(near + far, axis=0, keepdims=True) + scale * own_total[h : h + 1]
+        summed = dot_nn(near_rim[v_rows], near.astype(BF16)) + dot_nn(far_rim[v_rows], far.astype(BF16))
+        out_sum[rows] = summed + scale * own_sum[rows]
+
+
+def rim_rows(*args):
     stat = ((HEADS, TILE_DEV), F32)
     shapes = (((D, TILE_DEV), F32), stat, stat)
     scratch = [pltpu.VMEM((2 * D, HALF), BF16)]
-    return call(local_kernel, "local_branch", shapes, "svvvvv-vvv", scratch, 600_000_000, 5_000_000, 1_000_000)(*args)
+    return call(rim_kernel, "rim_rows", shapes, "svvvvvvvv-vvv", scratch, 400_000_000, 5_000_000, 400_000)(*args)
 
 
 def far_kernel(table, arrived, answer, scores):
@@ -300,16 +325,17 @@
     return lax.ppermute(x, ("zlo", "zhi"), pairs)
 
 
-def quarter_way(x):
+def along_z(x, part):
     z_low = lax.axis_size("zlo")
 
     def rank(z, core):
         return (z % z_low * 2 + core) * 2 + z // z_low
 
+    half = z_low // 2 if part == 0 else z_low - z_low // 2
     pairs = []
     for z in range(2 * z_low):
         for core in range(2):
-            step = z_low // 2 if core == 0 else -(z_low // 2)
+            step = half if core == 0 else -half
             pairs.append((rank(z, core), rank((z + step) % (2 * z_low), core)))
     return lax.ppermute(x, ("zlo", "core", "zhi"), pairs)
 
@@ -367,17 +393,23 @@
     wp, q_both = hold(wp, q_both)
     q_a = over_plane(q_both)
     embedded = embed(table, own_ctx, own_res, wp, other_core(wp))
-    q_a, embedded, on_way = hold(q_a, embedded, quarter_way(embedded))
+    on_way = along_z(embedded, 0)
+    q_a, embedded, on_way = hold(q_a, embedded, on_way)
     q_a = q_a.reshape(3 * D, D // 2)
-    q_b, partner = hold(other_core(q_a), quarter_way(on_way))
+    q_b = other_core(q_a)
+    partner = along_z(on_way, 1)
+    own_payload, q_rows, _, own_sum, own_best, own_total = own_rows(table, embedded, q_a, q_b)
+    partner, own_payload = hold(partner, own_payload)
     rim_from = jnp.where(high == 0, table[COUNT_OTHER] - HALF, 0)
     rim = lax.dynamic_slice_in_dim(partner, rim_from, HALF, 0)
     halo_pairs = [(p * 2, p * 2 + 2) for p in range(PLANES - 1)]
     halo_pairs += [(p * 2 + 1, p * 2 - 1) for p in range(1, PLANES)]
     halo = lax.ppermute(rim, SEQ, halo_pairs)
-    payload, q_rows, kv_rows = project(table, embedded, partner, q_a, q_b)
+    payload, near_rim = pair_rows(table, partner, q_a, q_b, own_payload)
     arrived = lax.all_to_all(payload, PLANE, 0, 0)
-    local_sum, local_best, local_total = local_branch(table, q_rows, kv_rows, halo, q_a, q_b)
+    local_sum, local_best, local_total = rim_rows(
+        table, q_rows, near_rim, halo, q_a, q_b, own_sum, own_best, own_total
+    )
     arrived, local_sum = hold(arrived, local_sum)
     answer = far_branch(table, arrived)
     answers = lax.all_to_all(answer, PLANE, 0, 0)

time: 177 us -> 176 us (level)
  waiting for transfers between devices: 63.2 us -> 56.3 us
  Pallas kernels: 24.7 us -> 29.2 us
    ppermute x2, waiting for transfers between devices: 13.9 us -> 5.83 us  [along_z(): return lax.ppermute(x, ('zlo', 'core', 'zhi'), pairs)]
    pallas_call x2 -> x3, Pallas kernels: 10.7 us -> 15.2 us  [the longest x1 7.4 us: own_rows(): call(own_kernel, 'own_rows', shapes, 'svvv-vvvvvv', [], 1000000000, 50000...]
    unnamed x30 -> x34, local copies, waits for them, and re-layouts: 5.12 us -> 7.13 us
  transfers between devices with their start and end apart: 10 -> 10, of which waited for: 7 -> 7; matrix products, arithmetic and copies ran while one was open for 1% -> 0% of each run, Pallas kernels for 9% -> 11%
where the time goes in v10:
time: 176 us; the launch traced here: 174 us
  waiting for transfers between devices  56.3 us (32%)
  starting transfers between devices  47.6 us (27%)
  Pallas kernels  29.2 us (17%)
  blocking collectives  27.7 us (16%)
  local copies, waits for them, and re-layouts  12.1 us (7%)
    ppermute x2, waiting for transfers between devices, mirrored(): return lax.ppermute(x, ('zlo', 'zhi'), pairs)  15.9 us
    all_to_all x1, waiting for transfers between devices, over_plane(): return lax.all_to_all(x, PLANE, 0, 0)  15.9 us
    all_to_all x1, waiting for transfers between devices, along_lines(): return lax.all_to_all(spread, EVERY, 0, 0, axis_index_groups=groups)  15.5 us
    all_to_all x1, blocking collectives, on_device(): answers = lax.all_to_all(answer, PLANE, 0, 0)  14.6 us
    ppermute x2, starting transfers between devices, mirrored(): return lax.ppermute(x, ('zlo', 'zhi'), pairs)  14 us
    all_to_all x1, blocking collectives, along_lines(): return lax.all_to_all(spread, EVERY, 0, 0, axis_index_groups=groups)  13.1 us
    ppermute x2, starting transfers between devices, along_z(): return lax.ppermute(x, ('zlo', 'core', 'zhi'), pairs)  10.2 us
    pallas_call x1, Pallas kernels, own_rows(): call(own_kernel, 'own_rows', shapes, 'svvv-vvvvvv', [], 1000000000, 50000...  7.4 us
  transfers between devices with their start and end apart: 10, of which 7 were waited for; matrix products, arithmetic and copies ran while one was open for 0% of the time, Pallas kernels for 11%

profile of v10, /device:TPU:1, one launch (start us, length us, event | category | flops | bytes accessed | tf_op | source)
XLA Modules:
  0.0 174.1 jit_solution(16655138239227300702)
XLA Ops:
  0.0 0.8 dynamic-slice_bitcast_fusion.2
  0.9 12.0 %collective-permute-start = (bf16[72,768]{1,0:T(8,128)(2,1)S(1)}, bf16[72,768]{1,0:T(8,128)(2,1)S(1)}, u32[]{:S(2)}, u32[]{:S(2)}) collective-permute-start(bf16[72,768]{1,0:T(8,128)(2,1)S(1)} %pad_maximum_fusion.1), channel_id=1, source_target_pairs={{0,449},{1,448},{64,385},{65,384},{128,321},{129,320},{192,257},{1... | collective-permute-start | bytes 331784 | tf_op jit(solution)/shard_map/ppermute | solution.py:325
  12.9 10.2 %collective-permute-done = bf16[72,768]{1,0:T(8,128)(2,1)S(1)} collective-permute-done((bf16[72,768]{1,0:T(8,128)(2,1)S(1)}, bf16[72,768]{1,0:T(8,128)(2,1)S(1)}, u32[]{:S(2)}, u32[]{:S(2)}) %collective-permute-start) | collective-permute-done | bytes 110624 | tf_op jit(solution)/shard_map/ppermute | solution.py:325
  23.3 13.1 %all_to_all.25 = bf16[4,144,768]{2,1,0:T(8,128)(2,1)S(1)} all-to-all(bf16[4,144,768]{2,1,0:T(8,128)(2,1)S(1)} %broadcast_in_dim.8), channel_id=1, replica_groups={{0,2,4,6},{8,10,12,14},{16,18,20,22},{24,26,28,30},{1,3,5,7},{9,11,13,1..., dimensions={0} | all-to-all | bytes 1769472 | tf_op jit(solution)/shard_map/all_to_all | solution.py:369
  36.4 2.0 %broadcast_in_dim.10 = bf16[4,576,768]{2,1,0:T(8,128)(2,1)} broadcast(bf16[576,768]{1,0:T(8,128)(2,1)S(1)} %bitcast.17), dimensions={1,2} | broadcast | bytes 4423680 | tf_op jit(solution)/shard_map/broadcast_in_dim | solution.py:368
  38.5 4.8 %all-to-all-start.1 = ((bf16[4,576,768]{2,1,0:T(8,128)(2,1)}), bf16[4,576,768]{2,1,0:T(8,128)(2,1)}, u32[]{:S(2)}, u32[]{:S(2)}) async-start(bf16[4,576,768]{2,1,0:T(8,128)(2,1)} %broadcast_in_dim.10), calls=%async_computation.1 | async-start | bytes 7077888 | tf_op jit(solution)/shard_map/all_to_all | solution.py:369
  43.4 2.1 %collective-permute-start.1 = (bf16[72,384]{1,0:T(8,128)(2,1)S(1)}, bf16[72,384]{1,0:T(8,128)(2,1)S(1)}, u32[]{:S(2)}, u32[]{:S(2)}) collective-permute-start(bf16[72,384]{1,0:T(8,128)(2,1)S(1)} %dynamic-slice_bitcast_fusion.1), channel_id=1, source_target_pairs={{0,449},{1,448},{64,385},{65,384},{128,321},{129,320},{192,257},{1... | collective-permute-start | bytes 165896 | tf_op jit(solution)/shard_map/ppermute | solution.py:325
  45.5 5.8 %collective-permute-done.1 = bf16[72,384]{1,0:T(8,128)(2,1)S(1)} collective-permute-done((bf16[72,384]{1,0:T(8,128)(2,1)S(1)}, bf16[72,384]{1,0:T(8,128)(2,1)S(1)}, u32[]{:S(2)}, u32[]{:S(2)}) %collective-permute-start.1) | collective-permute-done | bytes 55328 | tf_op jit(solution)/shard_map/ppermute | solution.py:325
  51.2 15.5 %all-to-all-done.1 = bf16[4,576,768]{2,1,0:T(8,128)(2,1)} async-done(((bf16[4,576,768]{2,1,0:T(8,128)(2,1)}), bf16[4,576,768]{2,1,0:T(8,128)(2,1)}, u32[]{:S(2)}, u32[]{:S(2)}) %all-to-all-start.1) | async-done | bytes 3538976 | tf_op jit(solution)/shard_map/all_to_all | solution.py:369
  66.7 1.4 broadcast_in_dim.22
  68.2 4.6 %collective-permute-start.2 = (bf16[16,144,768]{2,1,0:T(8,128)(2,1)}, bf16[16,144,768]{2,1,0:T(8,128)(2,1)}, u32[]{:S(2)}, u32[]{:S(2)}) collective-permute-start(bf16[16,144,768]{2,1,0:T(8,128)(2,1)} %bitcast.6.own), channel_id=1, source_target_pairs={{0,32},{32,0},{1,33},{33,1},{2,34},{34,2},{3,35},{35,3},{4,36},{36... | collective-permute-start | bytes 10616840 | tf_op jit(solution)/shard_map/ppermute | solution.py:344
  72.8 3.7 %all-to-all-start.2 = ((bf16[16,144,384]{2,1,0:T(8,128)(2,1)}), bf16[16,144,384]{2,1,0:T(8,128)(2,1)S(1)}, u32[]{:S(2)}, u32[]{:S(2)}) async-start(bf16[16,144,384]{2,1,0:T(8,128)(2,1)} %broadcast_in_dim.22), calls=%async_computation.2 | async-start | bytes 3538944 | tf_op jit(solution)/shard_map/all_to_all | solution.py:348
  76.7 1.6 prepare_rows.1
  79.0 6.6 %embed_rows.1.own = bf16[192,768]{1,0:T(8,128)(2,1)S(1)} custom-call(s32[48]{0:T(128)S(1)} %get-tuple-element.27.table, bf16[192,1536]{1,0:T(8,128)(2,1)S(1)} %get-tuple-element.29.ctx, bf16[192,1536]{1,0:T(8,128)(2,1)S(1)} %get-tuple-element.30.res, bf16[16,144,768]{2,1,0:T(8,128)(2,1)} %bitcast.6.own, bf16[16,144,768]{2,1,0:T(8,128)(2,1)} %collective-permute-done.2.other), custom_call_target="tpu_custom_call" | custom-call | flops 1400000000 | bytes 9000000 | tf_op jit(solution)/shard_map/embed_rows/pallas_call | solution.py:144
  85.6 4.4 %collective-permute-start.3 = (bf16[192,768]{1,0:T(8,128)(2,1)S(1)}, bf16[192,768]{1,0:T(8,128)(2,1)}, u32[]{:S(2)}, u32[]{:S(2)}) collective-permute-start(bf16[192,768]{1,0:T(8,128)(2,1)S(1)} %embed_rows.1.own), channel_id=1, source_target_pairs={{0,256},{32,289},{64,320},{96,353},{128,384},{160,417},{192,448},{... | collective-permute-start | bytes 884744 | tf_op jit(solution)/shard_map/ppermute | solution.py:340
  90.0 15.9 %all-to-all-done.2 = bf16[16,144,384]{2,1,0:T(8,128)(2,1)S(1)} async-done(((bf16[16,144,384]{2,1,0:T(8,128)(2,1)}), bf16[16,144,384]{2,1,0:T(8,128)(2,1)S(1)}, u32[]{:S(2)}, u32[]{:S(2)}) %all-to-all-start.2) | async-done | bytes 1769504 | tf_op jit(solution)/shard_map/all_to_all | solution.py:348
  105.9 2.7 %collective-permute-start.5 = (bf16[2304,384]{1,0:T(8,128)(2,1)S(1)}, bf16[2304,384]{1,0:T(8,128)(2,1)S(1)}, u32[]{:S(2)}, u32[]{:S(2)}) collective-permute-start(bf16[2304,384]{1,0:T(8,128)(2,1)S(1)} %bitcast.13), channel_id=1, source_target_pairs={{0,32},{32,0},{1,33},{33,1},{2,34},{34,2},{3,35},{35,3},{4,36},{36... | collective-permute-start | bytes 5308424 | tf_op jit(solution)/shard_map/ppermute | solution.py:344
  108.6 5.8 %collective-permute-start.4 = (bf16[192,768]{1,0:T(8,128)(2,1)}, bf16[192,768]{1,0:T(8,128)(2,1)S(1)}, u32[]{:S(2)}, u32[]{:S(2)}) collective-permute-start(bf16[192,768]{1,0:T(8,128)(2,1)} %collective-permute-done.3), channel_id=1, source_target_pairs={{0,256},{32,289},{64,320},{96,353},{128,384},{160,417},{192,448},{... | collective-permute-start | bytes 884744 | tf_op jit(solution)/shard_map/ppermute | solution.py:340
  114.4 7.4 %own_rows.1 = (bf16[16,128,128]{2,1,0:T(8,128)(2,1)S(1)}, bf16[768,192]{1,0:T(8,128)(2,1)S(1)}, bf16[1536,192]{1,0:T(8,128)(2,1)}, f32[768,192]{1,0:T(8,128)S(1)...) custom-call(s32[48]{0:T(128)S(1)} %get-tuple-element.27.table, bf16[192,768]{1,0:T(8,128)(2,1)S(1)} %embed_rows.1.own, ...), custom_call_target="tpu_custom_call" | custom-call | flops 1000000000 | bytes 5000000 | tf_op jit(solution)/shard_map/own_rows/pallas_call | solution.py:198
  122.5 5.8 %collective-permute-done.4.partner = bf16[192,768]{1,0:T(8,128)(2,1)S(1)} collective-permute-done((bf16[192,768]{1,0:T(8,128)(2,1)}, bf16[192,768]{1,0:T(8,128)(2,1)S(1)}, u32[]{:S(2)}, u32[]{:S(2)}) %collective-permute-start.4) | collective-permute-done | bytes 294944 | tf_op jit(solution)/shard_map/ppermute | solution.py:340
  128.4 3.5 %pair_rows.1 = (bf16[16,128,128]{2,1,0:T(8,128)(2,1)}, bf16[1536,64]{1,0:T(8,128)(2,1)S(1)}) custom-call(s32[48]{0:T(128)S(1)} %get-tuple-element.27.table, bf16[192,768]{1,0:T(8,128)(2,1)S(1)} %collective-permute-done.4.partner, bf16[2304,384]{1,0:T(8,128)(2,1)S(1)} %bitcast.15, bf16[2304,384]{1,0:T(8,128)(2,1)S(1)} %collective-permute-done.5.q_b, ...), custom_call_target="tpu_custom_call" | custom-call | flops 700000000 | bytes 4000000 | tf_op jit(solution)/shard_map/pair_rows/pallas_call | solution.py:217
  131.8 0.8 copy-done.7
  132.6 4.2 %all-to-all-start.3 = ((bf16[16,128,128]{2,1,0:T(8,128)(2,1)}), bf16[16,128,128]{2,1,0:T(8,128)(2,1)}, u32[]{:S(2)}, u32[]{:S(2)}) async-start(bf16[16,128,128]{2,1,0:T(8,128)(2,1)} %get-tuple-element.38), calls=%async_computation.3 | async-start | bytes 1048576 | tf_op jit(solution)/shard_map/all_to_all | solution.py:409
  138.1 3.3 %collective-permute-start.6 = (bf16[64,768]{1,0:T(8,128)(2,1)S(1)}, bf16[64,768]{1,0:T(8,128)(2,1)S(1)}, u32[]{:S(2)}, u32[]{:S(2)}) collective-permute-start(bf16[64,768]{1,0:T(8,128)(2,1)S(1)} %constant_dynamic-slice_fusion), channel_id=1, source_target_pairs={{0,2},{2,4},{4,6},{6,8},{8,10},{10,12},{12,14},{14,16},{16,18},{18... | collective-permute-start | bytes 294920 | tf_op jit(solution)/shard_map/ppermute | solution.py:407
  141.4 2.5 %collective-permute-done.6.halo = bf16[64,768]{1,0:T(8,128)(2,1)S(1)} collective-permute-done((bf16[64,768]{1,0:T(8,128)(2,1)S(1)}, bf16[64,768]{1,0:T(8,128)(2,1)S(1)}, u32[]{:S(2)}, u32[]{:S(2)}) %collective-permute-start.6) | collective-permute-done | bytes 98336 | tf_op jit(solution)/shard_map/ppermute | solution.py:407
  143.9 1.5 copy-done.2
  145.4 1.0 copy-done.6
  146.4 1.0 copy-done.8
  148.0 4.4 %rim_rows.1 = (f32[768,192]{1,0:T(8,128)S(1)}, f32[16,192]{1,0:T(8,128)S(1)}, f32[16,192]{1,0:T(8,128)S(1)}) custom-call(s32[48]{0:T(128)S(1)} %copy-done.10, bf16[768,192]{1,0:T(8,128)(2,1)S(1)} %copy-done.6, bf16[1536,64]{1,0:T(8,128)(2,1)S(1)} %copy-done.8, bf16[64,768]{1,0:T(8,128)(2,1)S(1)} %collective-permute-done.6.halo, ...), custom_call_target="tpu_custom_call" | custom-call | flops 400000000 | bytes 5000000 | tf_op jit(solution)/shard_map/rim_rows/pallas_call | solution.py:250
  153.1 3.8 %far_branch.1 = bf16[16,48,128]{2,1,0:T(8,128)(2,1)S(1)} custom-call(s32[48]{0:T(128)S(1)} %copy-done.11, bf16[16,128,128]{2,1,0:T(8,128)(2,1)} %all-to-all-done.3.arrived), custom_call_target="tpu_custom_call" | custom-call | flops 500000000 | bytes 1000000 | tf_op jit(solution)/shard_map/far_branch/pallas_call | solution.py:285
  156.9 14.6 %all_to_all.26.answers = bf16[16,48,128]{2,1,0:T(8,128)(2,1)S(1)} all-to-all(bf16[16,48,128]{2,1,0:T(8,128)(2,1)S(1)} %far_branch.1), channel_id=1, replica_groups=mesh['zlo'=8,'core'=2,'y'=4,'x'=4,'zhi'=2] {'y','x'}, dimensions={0} | all-to-all | bytes 393216 | tf_op jit(solution)/shard_map/all_to_all | solution.py:415
  172.2 2.0 %finish_rows.1 = bf16[1,192,768]{2,1,0:T(8,128)(2,1)} custom-call(s32[48]{0:T(128)S(1)} %copy-done.11, bf16[16,48,128]{2,1,0:T(8,128)(2,1)S(1)} %all_to_all.26.answers, f32[768,192]{1,0:T(8,128)S(1)} %get-tuple-element.46.local_sum, f32[16,192]{1,0:T(8,128)S(1)} %get-tuple-element.47.local_best, f32[16,192]{1,0:T(8,128)S(1)} %get-tuple-element.48.local_total, ...), custom_call_target="tpu_custom_call" | custom-call | flops 100000000 | bytes 1500000 | tf_op jit(solution)/shard_map/finish_rows/pallas_call | solution.py:315
  (47 shorter events, 4.5 us)
Async XLA Ops:
  0.0 0.9 copy-start
  0.9 22.2 %collective-permute-start = (bf16[72,768]{1,0:T(8,128)(2,1)S(1)}, bf16[72,768]{1,0:T(8,128)(2,1)S(1)}, u32[]{:S(2)}, u32[]{:S(2)}) collective-permute-start(bf16[72,768]{1,0:T(8,128)(2,1)S(1)} %pad_maximum_fusion.1), channel_id=1, source_target_pairs={{0,449},{1,448},{64,385},{65,384},{128,321},{129,320},{192,257},{1... | collective-permute-start | bytes 331784 | tf_op jit(solution)/shard_map/ppermute | solution.py:325
  38.5 4.9 %copy-start.16 = (bf16[768,72]{0,1:T(8,128)(2,1)S(1)}, bf16[768,72]{0,1:T(8,128)(2,1)}, u32[]{:S(2)}) copy-start(bf16[768,72]{0,1:T(8,128)(2,1)} %param.12) | copy-start | bytes 331780
  38.5 28.3 %all-to-all-start.1 = ((bf16[4,576,768]{2,1,0:T(8,128)(2,1)}), bf16[4,576,768]{2,1,0:T(8,128)(2,1)}, u32[]{:S(2)}, u32[]{:S(2)}) async-start(bf16[4,576,768]{2,1,0:T(8,128)(2,1)} %broadcast_in_dim.10), calls=%async_computation.1 | async-start | bytes 7077888 | tf_op jit(solution)/shard_map/all_to_all | solution.py:369
  43.3 33.3 %copy-start.3 = (bf16[1,192,1536]{2,1,0:T(8,128)(2,1)S(1)}, bf16[1,192,1536]{2,1,0:T(8,128)(2,1)}, u32[]{:S(2)}) copy-start(bf16[1,192,1536]{2,1,0:T(8,128)(2,1)} %ctx.1) | copy-start | bytes 1769476
  43.3 33.3 %copy-start.4 = (bf16[1,192,1536]{2,1,0:T(8,128)(2,1)S(1)}, bf16[1,192,1536]{2,1,0:T(8,128)(2,1)}, u32[]{:S(2)}) copy-start(bf16[1,192,1536]{2,1,0:T(8,128)(2,1)} %res.1) | copy-start | bytes 1769476
  43.3 33.3 %copy-start.12 = (s32[1,1,192]{2,1,0:T(1,128)S(1)}, s32[1,1,192]{2,1,0:T(1,128)}, u32[]{:S(2)}) copy-start(s32[1,1,192]{2,1,0:T(1,128)} %listing.3) | copy-start | bytes 2308
  43.3 33.3 %copy-start.14 = (s32[1,32]{1,0:T(1,128)S(1)}, s32[1,32]{1,0:T(1,128)}, u32[]{:S(2)}) copy-start(s32[1,32]{1,0:T(1,128)} %counts.1) | copy-start | bytes 388
  43.4 33.3 %copy-start.15 = (s32[1,2]{1,0:T(1,128)S(1)}, s32[1,2]{1,0:T(1,128)}, u32[]{:S(2)}) copy-start(s32[1,2]{1,0:T(1,128)} %dilation.1) | copy-start | bytes 28
  43.4 7.8 %collective-permute-start.1 = (bf16[72,384]{1,0:T(8,128)(2,1)S(1)}, bf16[72,384]{1,0:T(8,128)(2,1)S(1)}, u32[]{:S(2)}, u32[]{:S(2)}) collective-permute-start(bf16[72,384]{1,0:T(8,128)(2,1)S(1)} %dynamic-slice_bitcast_fusion.1), channel_id=1, source_target_pairs={{0,449},{1,448},{64,385},{65,384},{128,321},{129,320},{192,257},{1... | collective-permute-start | bytes 165896 | tf_op jit(solution)/shard_map/ppermute | solution.py:325
  68.2 10.8 %collective-permute-start.2 = (bf16[16,144,768]{2,1,0:T(8,128)(2,1)}, bf16[16,144,768]{2,1,0:T(8,128)(2,1)}, u32[]{:S(2)}, u32[]{:S(2)}) collective-permute-start(bf16[16,144,768]{2,1,0:T(8,128)(2,1)} %bitcast.6.own), channel_id=1, source_target_pairs={{0,32},{32,0},{1,33},{33,1},{2,34},{34,2},{3,35},{35,3},{4,36},{36... | collective-permute-start | bytes 10616840 | tf_op jit(solution)/shard_map/ppermute | solution.py:344
  72.8 33.1 %all-to-all-start.2 = ((bf16[16,144,384]{2,1,0:T(8,128)(2,1)}), bf16[16,144,384]{2,1,0:T(8,128)(2,1)S(1)}, u32[]{:S(2)}, u32[]{:S(2)}) async-start(bf16[16,144,384]{2,1,0:T(8,128)(2,1)} %broadcast_in_dim.22), calls=%async_computation.2 | async-start | bytes 3538944 | tf_op jit(solution)/shard_map/all_to_all | solution.py:348
  78.3 58.5 %copy-start.9 = (s32[48]{0:T(128)}, s32[48]{0:T(128)S(1)}, u32[]{:S(2)}) copy-start(s32[48]{0:T(128)S(1)} %get-tuple-element.27.table) | copy-start | bytes 580
  85.6 20.3 %collective-permute-start.3 = (bf16[192,768]{1,0:T(8,128)(2,1)S(1)}, bf16[192,768]{1,0:T(8,128)(2,1)}, u32[]{:S(2)}, u32[]{:S(2)}) collective-permute-start(bf16[192,768]{1,0:T(8,128)(2,1)S(1)} %embed_rows.1.own), channel_id=1, source_target_pairs={{0,256},{32,289},{64,320},{96,353},{128,384},{160,417},{192,448},{... | collective-permute-start | bytes 884744 | tf_op jit(solution)/shard_map/ppermute | solution.py:340
  105.9 8.5 %collective-permute-start.5 = (bf16[2304,384]{1,0:T(8,128)(2,1)S(1)}, bf16[2304,384]{1,0:T(8,128)(2,1)S(1)}, u32[]{:S(2)}, u32[]{:S(2)}) collective-permute-start(bf16[2304,384]{1,0:T(8,128)(2,1)S(1)} %bitcast.13), channel_id=1, source_target_pairs={{0,32},{32,0},{1,33},{33,1},{2,34},{34,2},{3,35},{35,3},{4,36},{36... | collective-permute-start | bytes 5308424 | tf_op jit(solution)/shard_map/ppermute | solution.py:344
  108.6 19.8 %collective-permute-start.4 = (bf16[192,768]{1,0:T(8,128)(2,1)}, bf16[192,768]{1,0:T(8,128)(2,1)S(1)}, u32[]{:S(2)}, u32[]{:S(2)}) collective-permute-start(bf16[192,768]{1,0:T(8,128)(2,1)} %collective-permute-done.3), channel_id=1, source_target_pairs={{0,256},{32,289},{64,320},{96,353},{128,384},{160,417},{192,448},{... | collective-permute-start | bytes 884744 | tf_op jit(solution)/shard_map/ppermute | solution.py:340
  114.4 17.5 %copy-start.1 = (bf16[2304,384]{1,0:T(8,128)(2,1)}, bf16[2304,384]{1,0:T(8,128)(2,1)S(1)}, u32[]{:S(2)}) copy-start(bf16[2304,384]{1,0:T(8,128)(2,1)S(1)} %collective-permute-done.5.q_b) | copy-start | bytes 5308420
  121.8 0.8 copy-start.5
  131.8 0.8 copy-start.7
  132.6 19.8 %all-to-all-start.3 = ((bf16[16,128,128]{2,1,0:T(8,128)(2,1)}), bf16[16,128,128]{2,1,0:T(8,128)(2,1)}, u32[]{:S(2)}, u32[]{:S(2)}) async-start(bf16[16,128,128]{2,1,0:T(8,128)(2,1)} %get-tuple-element.38), calls=%async_computation.3 | async-start | bytes 1048576 | tf_op jit(solution)/shard_map/all_to_all | solution.py:409
  138.1 5.8 %collective-permute-start.6 = (bf16[64,768]{1,0:T(8,128)(2,1)S(1)}, bf16[64,768]{1,0:T(8,128)(2,1)S(1)}, u32[]{:S(2)}, u32[]{:S(2)}) collective-permute-start(bf16[64,768]{1,0:T(8,128)(2,1)S(1)} %constant_dynamic-slice_fusion), channel_id=1, source_target_pairs={{0,2},{2,4},{4,6},{6,8},{8,10},{10,12},{12,14},{14,16},{16,18},{18... | collective-permute-start | bytes 294920 | tf_op jit(solution)/shard_map/ppermute | solution.py:407
  143.9 1.5 copy-start.2
  145.4 1.0 copy-start.6
  146.4 1.0 copy-start.8
  147.4 0.7 copy-start.10
  152.4 0.7 copy-start.11
  171.5 0.7 copy-start.13

commit v11 on v10

--- a/solution.py
+++ b/solution.py
@@ -11,6 +11,7 @@
 D_ENC = 1536
 HALF = 64
 TILE_DEV = 192
+CHUNK = 96
 SEQ_LEN = 4096
 WINDOW = 320
 KEY_SLOTS = 80
@@ -108,7 +109,7 @@
     return first, second
 
 
-def embed_kernel(table, ctx, res, own, other, out, w, p, hidden, normed):
+def embed_kernel(table, ctx, res, own, other, out, lower, upper, w, p, hidden, normed):
     core = table[CORE]
     for block in range(PLANES):
         turned = block % 4 * 4 + block // 4
@@ -131,6 +132,8 @@
     spread = jnp.sum(center * center, axis=1, keepdims=True) / D_ENC
     normed[...] = (center * lax.rsqrt(spread + NORM_EPS)).astype(BF16)
     out[...] = (dot_nt(normed[:, :D], p[0]) + dot_nt(normed[:, D:], p[1])).astype(BF16)
+    lower[...] = out[:CHUNK]
+    upper[...] = out[CHUNK:]
 
 
 def embed(*args):
@@ -140,8 +143,8 @@
         pltpu.VMEM((TILE_DEV, D_ENC), F32),
         pltpu.VMEM((TILE_DEV, D_ENC), BF16),
     ]
-    shapes = (((TILE_DEV, D), BF16),)
-    return call(embed_kernel, "embed_rows", shapes, "svvvv-v", scratch, 1_400_000_000, 9_000_000)(*args)[0]
+    shapes = (((TILE_DEV, D), BF16), ((CHUNK, D), BF16), ((CHUNK, D), BF16))
+    return call(embed_kernel, "embed_rows", shapes, "svvvv-vvv", scratch, 1_400_000_000, 9_000_000)(*args)
 
 
 def key_picks(table, h, first, count):
@@ -198,7 +201,9 @@
     return call(own_kernel, "own_rows", shapes, "svvv-vvvvvv", [], 1_000_000_000, 5_000_000, 600_000)(*args)
 
 
-def pair_kernel(table, partner, q_a, q_b, own_payload, payload, rim, kv):
+def pair_kernel(table, lower, upper, q_a, q_b, own_payload, payload, rim, kv, partner):
+    partner[:CHUNK] = lower[...]
+    partner[CHUNK:] = upper[...]
     first, second = halves(table, partner, D // 2)
     kv[...] = (dot_nt(q_a[D:], first) + dot_nt(q_b[D:], second)).astype(BF16)
     for h in range(HEADS):
@@ -213,8 +218,8 @@
 
 def pair_rows(*args):
     shapes = (((HEADS, KEY_SLOTS + SLOTS, LANES), BF16), ((2 * D, HALF), BF16))
-    scratch = [pltpu.VMEM((2 * D, TILE_DEV), BF16)]
-    return call(pair_kernel, "pair_rows", shapes, "svvvv-vv", scratch, 700_000_000, 4_000_000)(*args)
+    scratch = [pltpu.VMEM((2 * D, TILE_DEV), BF16), pltpu.VMEM((TILE_DEV, D), BF16)]
+    return call(pair_kernel, "pair_rows", shapes, "svvvvv-vv", scratch, 700_000_000, 4_000_000)(*args)
 
 
 def rim_kernel(table, q, near_rim, halo, q_a, q_b, own_sum, own_best, own_total, out_sum, out_best, out_total, far_rim):
@@ -392,25 +397,25 @@
     q_both = copies(in_order(q_own, q_other, high))
     wp, q_both = hold(wp, q_both)
     q_a = over_plane(q_both)
-    embedded = embed(table, own_ctx, own_res, wp, other_core(wp))
-    on_way = along_z(embedded, 0)
-    q_a, embedded, on_way = hold(q_a, embedded, on_way)
+    embedded, lower, upper = embed(table, own_ctx, own_res, wp, other_core(wp))
+    lower = along_z(along_z(lower, 0), 1)
+    upper = along_z(upper, 0)
+    q_a, embedded, lower, upper = hold(q_a, embedded, lower, upper)
     q_a = q_a.reshape(3 * D, D // 2)
     q_b = other_core(q_a)
-    partner = along_z(on_way, 1)
+    upper = along_z(upper, 1)
     own_payload, q_rows, _, own_sum, own_best, own_total = own_rows(table, embedded, q_a, q_b)
-    partner, own_payload = hold(partner, own_payload)
+    upper, own_payload = hold(upper, own_payload)
     rim_from = jnp.where(high == 0, table[COUNT_OTHER] - HALF, 0)
-    rim = lax.dynamic_slice_in_dim(partner, rim_from, HALF, 0)
+    rim = lax.dynamic_slice_in_dim(jnp.concatenate([lower, upper]), rim_from, HALF, 0)
     halo_pairs = [(p * 2, p * 2 + 2) for p in range(PLANES - 1)]
     halo_pairs += [(p * 2 + 1, p * 2 - 1) for p in range(1, PLANES)]
     halo = lax.ppermute(rim, SEQ, halo_pairs)
-    payload, near_rim = pair_rows(table, partner, q_a, q_b, own_payload)
-    arrived = lax.all_to_all(payload, PLANE, 0, 0)
+    payload, near_rim = pair_rows(table, lower, upper, q_a, q_b, own_payload)
+    arrived, halo = hold(lax.all_to_all(payload, PLANE, 0, 0), halo)
     local_sum, local_best, local_total = rim_rows(
         table, q_rows, near_rim, halo, q_a, q_b, own_sum, own_best, own_total
     )
-    arrived, local_sum = hold(arrived, local_sum)
     answer = far_branch(table, arrived)
     answers = lax.all_to_all(answer, PLANE, 0, 0)
     return finish(table, answers, local_sum, local_best, local_total, tissue)

time: 176 us -> 174 us (0.989)
  starting transfers between devices: 47.6 us -> 66.8 us
  blocking collectives: 27.7 us -> 13.1 us
  waiting for transfers between devices: 56.3 us -> 52 us
    all_to_all x1 -> x0, blocking collectives: 14.6 us -> none  [on_device(): answers = lax.all_to_all(answer, PLANE, 0, 0)]
    all_to_all x1, waiting for transfers between devices: 15.9 us -> 2.23 us  [over_plane(): return lax.all_to_all(x, PLANE, 0, 0)]
    ppermute x2 -> x4, starting transfers between devices: 10.2 us -> 23.5 us  [along_z(): return lax.ppermute(x, ('zlo', 'core', 'zhi'), pairs)]
    all_to_all x1 -> x2, starting transfers between devices: 4.24 us -> 10.7 us  [the longest x1 5.86 us: on_device(): arrived, halo = hold(lax.all_to_all(payload, PLANE, 0, 0), halo)]
    ppermute x2 -> x4, waiting for transfers between devices: 5.83 us -> 11.1 us  [along_z(): return lax.ppermute(x, ('zlo', 'core', 'zhi'), pairs)]
    all_to_all x1 -> x2, waiting for transfers between devices: 0.01 us -> 3.28 us  [the longest x1 3.28 us: on_device(): arrived, halo = hold(lax.all_to_all(payload, PLANE, 0, 0), halo)]
    unnamed x34 -> x26, local copies, waits for them, and re-layouts: 7.13 us -> 5.41 us
  transfers between devices with their start and end apart: 10 -> 13, of which waited for: 7 -> 9; matrix products, arithmetic and copies ran while one was open for 0% -> 0% of each run, Pallas kernels for 11% -> 12%
where the time goes in v11:
time: 174 us; the launch traced here: 173 us
  starting transfers between devices  66.8 us (38%)
  waiting for transfers between devices  52 us (30%)
  Pallas kernels  29.5 us (17%)
  blocking collectives  13.1 us (8%)
  local copies, waits for them, and re-layouts  10.4 us (6%)
    ppermute x4, starting transfers between devices, along_z(): return lax.ppermute(x, ('zlo', 'core', 'zhi'), pairs)  23.5 us
    ppermute x2, waiting for transfers between devices, mirrored(): return lax.ppermute(x, ('zlo', 'zhi'), pairs)  15.9 us
    all_to_all x1, waiting for transfers between devices, along_lines(): return lax.all_to_all(spread, EVERY, 0, 0, axis_index_groups=groups)  15.5 us
    ppermute x2, starting transfers between devices, mirrored(): return lax.ppermute(x, ('zlo', 'zhi'), pairs)  14 us
    all_to_all x1, blocking collectives, along_lines(): return lax.all_to_all(spread, EVERY, 0, 0, axis_index_groups=groups)  13.1 us
    ppermute x4, waiting for transfers between devices, along_z(): return lax.ppermute(x, ('zlo', 'core', 'zhi'), pairs)  11.1 us
    pallas_call x1, Pallas kernels, own_rows(): call(own_kernel, 'own_rows', shapes, 'svvv-vvvvvv', [], 1000000000, 50000...  7.42 us
    pallas_call x1, Pallas kernels, embed(): call(embed_kernel, 'embed_rows', shapes, 'svvvv-vvv', scratch, 1400000000...  6.57 us
  transfers between devices with their start and end apart: 13, of which 9 were waited for; matrix products, arithmetic and copies ran while one was open for 0% of the time, Pallas kernels for 12%

profile of v11, /device:TPU:1, one launch (start us, length us, event | category | flops | bytes accessed | tf_op | source)
XLA Modules:
  0.0 173.1 jit_solution(10276872724564732871)
XLA Ops:
  0.9 12.0 %collective-permute-start = (bf16[72,768]{1,0:T(8,128)(2,1)S(1)}, bf16[72,768]{1,0:T(8,128)(2,1)S(1)}, u32[]{:S(2)}, u32[]{:S(2)}) collective-permute-start(bf16[72,768]{1,0:T(8,128)(2,1)S(1)} %pad_maximum_fusion.1), channel_id=1, source_target_pairs={{0,449},{1,448},{64,385},{65,384},{128,321},{129,320},{192,257},{1... | collective-permute-start | bytes 331784 | tf_op jit(solution)/shard_map/ppermute | solution.py:330
  12.9 10.2 %collective-permute-done = bf16[72,768]{1,0:T(8,128)(2,1)S(1)} collective-permute-done((bf16[72,768]{1,0:T(8,128)(2,1)S(1)}, bf16[72,768]{1,0:T(8,128)(2,1)S(1)}, u32[]{:S(2)}, u32[]{:S(2)}) %collective-permute-start) | collective-permute-done | bytes 110624 | tf_op jit(solution)/shard_map/ppermute | solution.py:330
  23.3 13.1 %all_to_all.25 = bf16[4,144,768]{2,1,0:T(8,128)(2,1)S(1)} all-to-all(bf16[4,144,768]{2,1,0:T(8,128)(2,1)S(1)} %broadcast_in_dim.8), channel_id=1, replica_groups={{0,2,4,6},{8,10,12,14},{16,18,20,22},{24,26,28,30},{1,3,5,7},{9,11,13,1..., dimensions={0} | all-to-all | bytes 1769472 | tf_op jit(solution)/shard_map/all_to_all | solution.py:374
  36.4 2.0 %broadcast_in_dim.10 = bf16[4,576,768]{2,1,0:T(8,128)(2,1)} broadcast(bf16[576,768]{1,0:T(8,128)(2,1)S(1)} %bitcast.17), dimensions={1,2} | broadcast | bytes 4423680 | tf_op jit(solution)/shard_map/broadcast_in_dim | solution.py:373
  38.4 4.9 %all-to-all-start.1 = ((bf16[4,576,768]{2,1,0:T(8,128)(2,1)}), bf16[4,576,768]{2,1,0:T(8,128)(2,1)}, u32[]{:S(2)}, u32[]{:S(2)}) async-start(bf16[4,576,768]{2,1,0:T(8,128)(2,1)} %broadcast_in_dim.10), calls=%async_computation.1 | async-start | bytes 7077888 | tf_op jit(solution)/shard_map/all_to_all | solution.py:374
  43.4 2.1 %collective-permute-start.1 = (bf16[72,384]{1,0:T(8,128)(2,1)S(1)}, bf16[72,384]{1,0:T(8,128)(2,1)S(1)}, u32[]{:S(2)}, u32[]{:S(2)}) collective-permute-start(bf16[72,384]{1,0:T(8,128)(2,1)S(1)} %dynamic-slice_bitcast_fusion.1), channel_id=1, source_target_pairs={{0,449},{1,448},{64,385},{65,384},{128,321},{129,320},{192,257},{1... | collective-permute-start | bytes 165896 | tf_op jit(solution)/shard_map/ppermute | solution.py:330
  45.5 5.8 %collective-permute-done.1 = bf16[72,384]{1,0:T(8,128)(2,1)S(1)} collective-permute-done((bf16[72,384]{1,0:T(8,128)(2,1)S(1)}, bf16[72,384]{1,0:T(8,128)(2,1)S(1)}, u32[]{:S(2)}, u32[]{:S(2)}) %collective-permute-start.1) | collective-permute-done | bytes 55328 | tf_op jit(solution)/shard_map/ppermute | solution.py:330
  51.2 15.5 %all-to-all-done.1 = bf16[4,576,768]{2,1,0:T(8,128)(2,1)} async-done(((bf16[4,576,768]{2,1,0:T(8,128)(2,1)}), bf16[4,576,768]{2,1,0:T(8,128)(2,1)}, u32[]{:S(2)}, u32[]{:S(2)}) %all-to-all-start.1) | async-done | bytes 3538976 | tf_op jit(solution)/shard_map/all_to_all | solution.py:374
  66.7 1.4 broadcast_in_dim.22
  68.2 4.6 %collective-permute-start.2 = (bf16[16,144,768]{2,1,0:T(8,128)(2,1)}, bf16[16,144,768]{2,1,0:T(8,128)(2,1)}, u32[]{:S(2)}, u32[]{:S(2)}) collective-permute-start(bf16[16,144,768]{2,1,0:T(8,128)(2,1)} %bitcast.6.own), channel_id=1, source_target_pairs={{0,32},{32,0},{1,33},{33,1},{2,34},{34,2},{3,35},{35,3},{4,36},{36... | collective-permute-start | bytes 10616840 | tf_op jit(solution)/shard_map/ppermute | solution.py:349
  72.8 3.7 %all-to-all-start.2 = ((bf16[16,144,384]{2,1,0:T(8,128)(2,1)}), bf16[16,144,384]{2,1,0:T(8,128)(2,1)S(1)}, u32[]{:S(2)}, u32[]{:S(2)}) async-start(bf16[16,144,384]{2,1,0:T(8,128)(2,1)} %broadcast_in_dim.22), calls=%async_computation.2 | async-start | bytes 3538944 | tf_op jit(solution)/shard_map/all_to_all | solution.py:353
  76.7 1.7 prepare_rows.1
  79.0 6.6 %embed_rows.1 = (bf16[192,768]{1,0:T(8,128)(2,1)S(1)}, bf16[96,768]{1,0:T(8,128)(2,1)S(1)}, bf16[96,768]{1,0:T(8,128)(2,1)S(1)}) custom-call(s32[48]{0:T(128)S(1)} %get-tuple-element.31.table, bf16[192,1536]{1,0:T(8,128)(2,1)S(1)} %get-tuple-element.33.ctx, bf16[192,1536]{1,0:T(8,128)(2,1)S(1)} %get-tuple-element.34.res, bf16[16,144,768]{2,1,0:T(8,128)(2,1)} %bitcast.6.own, ...), custom_call_target="tpu_custom_call" | custom-call | flops 1400000000 | bytes 9000000 | tf_op jit(solution)/shard_map/embed_rows/pallas_call | solution.py:147
  85.6 4.4 %collective-permute-start.3 = (bf16[96,768]{1,0:T(8,128)(2,1)S(1)}, bf16[96,768]{1,0:T(8,128)(2,1)S(1)}, u32[]{:S(2)}, u32[]{:S(2)}) collective-permute-start(bf16[96,768]{1,0:T(8,128)(2,1)S(1)} %get-tuple-element.37), channel_id=1, source_target_pairs={{0,256},{32,289},{64,320},{96,353},{128,384},{160,417},{192,448},{... | collective-permute-start | bytes 442376 | tf_op jit(solution)/shard_map/ppermute | solution.py:345
  90.0 6.7 %collective-permute-start.5 = (bf16[96,768]{1,0:T(8,128)(2,1)S(1)}, bf16[96,768]{1,0:T(8,128)(2,1)S(1)}, u32[]{:S(2)}, u32[]{:S(2)}) collective-permute-start(bf16[96,768]{1,0:T(8,128)(2,1)S(1)} %get-tuple-element.38), channel_id=1, source_target_pairs={{0,256},{32,289},{64,320},{96,353},{128,384},{160,417},{192,448},{... | collective-permute-start | bytes 442376 | tf_op jit(solution)/shard_map/ppermute | solution.py:345
  96.7 1.9 %collective-permute-done.3 = bf16[96,768]{1,0:T(8,128)(2,1)S(1)} collective-permute-done((bf16[96,768]{1,0:T(8,128)(2,1)S(1)}, bf16[96,768]{1,0:T(8,128)(2,1)S(1)}, u32[]{:S(2)}, u32[]{:S(2)}) %collective-permute-start.3) | collective-permute-done | bytes 147488 | tf_op jit(solution)/shard_map/ppermute | solution.py:345
  98.6 5.1 %collective-permute-start.4 = (bf16[96,768]{1,0:T(8,128)(2,1)S(1)}, bf16[96,768]{1,0:T(8,128)(2,1)S(1)}, u32[]{:S(2)}, u32[]{:S(2)}) collective-permute-start(bf16[96,768]{1,0:T(8,128)(2,1)S(1)} %collective-permute-done.3), channel_id=1, source_target_pairs={{0,256},{32,289},{64,320},{96,353},{128,384},{160,417},{192,448},{... | collective-permute-start | bytes 442376 | tf_op jit(solution)/shard_map/ppermute | solution.py:345
  103.7 2.2 %all-to-all-done.2 = bf16[16,144,384]{2,1,0:T(8,128)(2,1)S(1)} async-done(((bf16[16,144,384]{2,1,0:T(8,128)(2,1)}), bf16[16,144,384]{2,1,0:T(8,128)(2,1)S(1)}, u32[]{:S(2)}, u32[]{:S(2)}) %all-to-all-start.2) | async-done | bytes 1769504 | tf_op jit(solution)/shard_map/all_to_all | solution.py:353
  105.9 9.2 %collective-permute-done.4.lower = bf16[96,768]{1,0:T(8,128)(2,1)S(1)} collective-permute-done((bf16[96,768]{1,0:T(8,128)(2,1)S(1)}, bf16[96,768]{1,0:T(8,128)(2,1)S(1)}, u32[]{:S(2)}, u32[]{:S(2)}) %collective-permute-start.4) | collective-permute-done | bytes 147488 | tf_op jit(solution)/shard_map/ppermute | solution.py:345
  115.1 1.9 %collective-permute-start.7 = (bf16[2304,384]{1,0:T(8,128)(2,1)S(1)}, bf16[2304,384]{1,0:T(8,128)(2,1)S(1)}, u32[]{:S(2)}, u32[]{:S(2)}) collective-permute-start(bf16[2304,384]{1,0:T(8,128)(2,1)S(1)} %bitcast.13), channel_id=1, source_target_pairs={{0,32},{32,0},{1,33},{33,1},{2,34},{34,2},{3,35},{35,3},{4,36},{36... | collective-permute-start | bytes 5308424 | tf_op jit(solution)/shard_map/ppermute | solution.py:349
  117.0 7.3 %collective-permute-start.6 = (bf16[96,768]{1,0:T(8,128)(2,1)S(1)}, bf16[96,768]{1,0:T(8,128)(2,1)S(1)}, u32[]{:S(2)}, u32[]{:S(2)}) collective-permute-start(bf16[96,768]{1,0:T(8,128)(2,1)S(1)} %collective-permute-done.5), channel_id=1, source_target_pairs={{0,256},{32,289},{64,320},{96,353},{128,384},{160,417},{192,448},{... | collective-permute-start | bytes 442376 | tf_op jit(solution)/shard_map/ppermute | solution.py:345
  124.4 7.4 %own_rows.1 = (bf16[16,128,128]{2,1,0:T(8,128)(2,1)S(1)}, bf16[768,192]{1,0:T(8,128)(2,1)S(1)}, bf16[1536,192]{1,0:T(8,128)(2,1)}, f32[768,192]{1,0:T(8,128)S(1)...) custom-call(s32[48]{0:T(128)S(1)} %get-tuple-element.31.table, bf16[192,768]{1,0:T(8,128)(2,1)S(1)} %get-tuple-element.41.own, ...), custom_call_target="tpu_custom_call" | custom-call | flops 1000000000 | bytes 5000000 | tf_op jit(solution)/shard_map/own_rows/pallas_call | solution.py:201
  132.7 3.5 %pair_rows.1 = (bf16[16,128,128]{2,1,0:T(8,128)(2,1)}, bf16[1536,64]{1,0:T(8,128)(2,1)S(1)}) custom-call(s32[48]{0:T(128)S(1)} %get-tuple-element.31.table, bf16[96,768]{1,0:T(8,128)(2,1)S(1)} %collective-permute-done.4.lower, bf16[96,768]{1,0:T(8,128)(2,1)S(1)} %collective-permute-done.6.upper, bf16[2304,384]{1,0:T(8,128)(2,1)S(1)} %bitcast.15, ...), custom_call_target="tpu_custom_call" | custom-call | flops 700000000 | bytes 4000000 | tf_op jit(solution)/shard_map/pair_rows/pallas_call | solution.py:222
  136.9 5.9 %all-to-all-start.3 = ((bf16[16,128,128]{2,1,0:T(8,128)(2,1)}), bf16[16,128,128]{2,1,0:T(8,128)(2,1)S(1)}, u32[]{:S(2)}, u32[]{:S(2)}) async-start(bf16[16,128,128]{2,1,0:T(8,128)(2,1)} %get-tuple-element.46), calls=%async_computation.3 | async-start | bytes 1048576 | tf_op jit(solution)/shard_map/all_to_all | solution.py:415
  144.2 3.5 %collective-permute-start.8 = (bf16[64,768]{1,0:T(8,128)(2,1)S(1)}, bf16[64,768]{1,0:T(8,128)(2,1)S(1)}, u32[]{:S(2)}, u32[]{:S(2)}) collective-permute-start(bf16[64,768]{1,0:T(8,128)(2,1)S(1)} %fusion), channel_id=1, source_target_pairs={{0,2},{2,4},{4,6},{6,8},{8,10},{10,12},{12,14},{14,16},{16,18},{18... | collective-permute-start | bytes 294920 | tf_op jit(solution)/shard_map/ppermute | solution.py:413
  147.6 3.2 %collective-permute-done.8.halo = bf16[64,768]{1,0:T(8,128)(2,1)S(1)} collective-permute-done((bf16[64,768]{1,0:T(8,128)(2,1)S(1)}, bf16[64,768]{1,0:T(8,128)(2,1)S(1)}, u32[]{:S(2)}, u32[]{:S(2)}) %collective-permute-start.8) | collective-permute-done | bytes 98336 | tf_op jit(solution)/shard_map/ppermute | solution.py:413
  150.9 3.3 %all-to-all-done.3.arrived = bf16[16,128,128]{2,1,0:T(8,128)(2,1)S(1)} async-done(((bf16[16,128,128]{2,1,0:T(8,128)(2,1)}), bf16[16,128,128]{2,1,0:T(8,128)(2,1)S(1)}, u32[]{:S(2)}, u32[]{:S(2)}) %all-to-all-start.3) | async-done | bytes 524320 | tf_op jit(solution)/shard_map/all_to_all | solution.py:415
  154.2 4.0 %far_branch.1 = bf16[16,48,128]{2,1,0:T(8,128)(2,1)} custom-call(s32[48]{0:T(128)S(1)} %get-tuple-element.31.table, bf16[16,128,128]{2,1,0:T(8,128)(2,1)S(1)} %all-to-all-done.3.arrived), custom_call_target="tpu_custom_call" | custom-call | flops 500000000 | bytes 1000000 | tf_op jit(solution)/shard_map/far_branch/pallas_call | solution.py:290
  158.2 4.9 %all-to-all-start.4 = ((bf16[16,48,128]{2,1,0:T(8,128)(2,1)}), bf16[16,48,128]{2,1,0:T(8,128)(2,1)S(1)}, u32[]{:S(2)}, u32[]{:S(2)}) async-start(bf16[16,48,128]{2,1,0:T(8,128)(2,1)} %far_branch.1), calls=%async_computation.4 | async-start | bytes 393216 | tf_op jit(solution)/shard_map/all_to_all | solution.py:420
  163.1 1.5 copy-done.2
  166.7 4.4 %rim_rows.1 = (f32[768,192]{1,0:T(8,128)S(1)}, f32[16,192]{1,0:T(8,128)S(1)}, f32[16,192]{1,0:T(8,128)S(1)}) custom-call(s32[48]{0:T(128)S(1)} %get-tuple-element.31.table, bf16[768,192]{1,0:T(8,128)(2,1)S(1)} %get-tuple-element.48.q, bf16[1536,64]{1,0:T(8,128)(2,1)S(1)} %copy-done.8, bf16[64,768]{1,0:T(8,128)(2,1)S(1)} %collective-permute-done.8.halo, ...), custom_call_target="tpu_custom_call" | custom-call | flops 400000000 | bytes 5000000 | tf_op jit(solution)/shard_map/rim_rows/pallas_call | solution.py:255
  171.1 2.0 %finish_rows.1 = bf16[1,192,768]{2,1,0:T(8,128)(2,1)} custom-call(s32[48]{0:T(128)S(1)} %get-tuple-element.31.table, bf16[16,48,128]{2,1,0:T(8,128)(2,1)S(1)} %all-to-all-done.4.answers, f32[768,192]{1,0:T(8,128)S(1)} %get-tuple-element.54.local_sum, f32[16,192]{1,0:T(8,128)S(1)} %get-tuple-element.55.local_best, ...), custom_call_target="tpu_custom_call" | custom-call | flops 100000000 | bytes 1500000 | tf_op jit(solution)/shard_map/finish_rows/pallas_call | solution.py:320
  (44 shorter events, 6.4 us)
Async XLA Ops:
  0.0 0.9 copy-start
  0.9 22.2 %collective-permute-start = (bf16[72,768]{1,0:T(8,128)(2,1)S(1)}, bf16[72,768]{1,0:T(8,128)(2,1)S(1)}, u32[]{:S(2)}, u32[]{:S(2)}) collective-permute-start(bf16[72,768]{1,0:T(8,128)(2,1)S(1)} %pad_maximum_fusion.1), channel_id=1, source_target_pairs={{0,449},{1,448},{64,385},{65,384},{128,321},{129,320},{192,257},{1... | collective-permute-start | bytes 331784 | tf_op jit(solution)/shard_map/ppermute | solution.py:330
  38.4 4.9 %copy-start.12 = (bf16[768,72]{0,1:T(8,128)(2,1)S(1)}, bf16[768,72]{0,1:T(8,128)(2,1)}, u32[]{:S(2)}) copy-start(bf16[768,72]{0,1:T(8,128)(2,1)} %param.12) | copy-start | bytes 331780
  38.4 28.3 %all-to-all-start.1 = ((bf16[4,576,768]{2,1,0:T(8,128)(2,1)}), bf16[4,576,768]{2,1,0:T(8,128)(2,1)}, u32[]{:S(2)}, u32[]{:S(2)}) async-start(bf16[4,576,768]{2,1,0:T(8,128)(2,1)} %broadcast_in_dim.10), calls=%async_computation.1 | async-start | bytes 7077888 | tf_op jit(solution)/shard_map/all_to_all | solution.py:374
  43.3 33.3 %copy-start.5 = (bf16[1,192,1536]{2,1,0:T(8,128)(2,1)S(1)}, bf16[1,192,1536]{2,1,0:T(8,128)(2,1)}, u32[]{:S(2)}) copy-start(bf16[1,192,1536]{2,1,0:T(8,128)(2,1)} %ctx.1) | copy-start | bytes 1769476
  43.3 33.3 %copy-start.6 = (bf16[1,192,1536]{2,1,0:T(8,128)(2,1)S(1)}, bf16[1,192,1536]{2,1,0:T(8,128)(2,1)}, u32[]{:S(2)}) copy-start(bf16[1,192,1536]{2,1,0:T(8,128)(2,1)} %res.1) | copy-start | bytes 1769476
  43.3 33.3 %copy-start.9 = (s32[1,1,192]{2,1,0:T(1,128)S(1)}, s32[1,1,192]{2,1,0:T(1,128)}, u32[]{:S(2)}) copy-start(s32[1,1,192]{2,1,0:T(1,128)} %listing.3) | copy-start | bytes 2308
  43.3 33.3 %copy-start.10 = (s32[1,32]{1,0:T(1,128)S(1)}, s32[1,32]{1,0:T(1,128)}, u32[]{:S(2)}) copy-start(s32[1,32]{1,0:T(1,128)} %counts.1) | copy-start | bytes 388
  43.4 33.3 %copy-start.11 = (s32[1,2]{1,0:T(1,128)S(1)}, s32[1,2]{1,0:T(1,128)}, u32[]{:S(2)}) copy-start(s32[1,2]{1,0:T(1,128)} %dilation.1) | copy-start | bytes 28
  43.4 7.8 %collective-permute-start.1 = (bf16[72,384]{1,0:T(8,128)(2,1)S(1)}, bf16[72,384]{1,0:T(8,128)(2,1)S(1)}, u32[]{:S(2)}, u32[]{:S(2)}) collective-permute-start(bf16[72,384]{1,0:T(8,128)(2,1)S(1)} %dynamic-slice_bitcast_fusion.1), channel_id=1, source_target_pairs={{0,449},{1,448},{64,385},{65,384},{128,321},{129,320},{192,257},{1... | collective-permute-start | bytes 165896 | tf_op jit(solution)/shard_map/ppermute | solution.py:330
  68.2 10.8 %collective-permute-start.2 = (bf16[16,144,768]{2,1,0:T(8,128)(2,1)}, bf16[16,144,768]{2,1,0:T(8,128)(2,1)}, u32[]{:S(2)}, u32[]{:S(2)}) collective-permute-start(bf16[16,144,768]{2,1,0:T(8,128)(2,1)} %bitcast.6.own), channel_id=1, source_target_pairs={{0,32},{32,0},{1,33},{33,1},{2,34},{34,2},{3,35},{35,3},{4,36},{36... | collective-permute-start | bytes 10616840 | tf_op jit(solution)/shard_map/ppermute | solution.py:349
  72.8 33.1 %all-to-all-start.2 = ((bf16[16,144,384]{2,1,0:T(8,128)(2,1)}), bf16[16,144,384]{2,1,0:T(8,128)(2,1)S(1)}, u32[]{:S(2)}, u32[]{:S(2)}) async-start(bf16[16,144,384]{2,1,0:T(8,128)(2,1)} %broadcast_in_dim.22), calls=%async_computation.2 | async-start | bytes 3538944 | tf_op jit(solution)/shard_map/all_to_all | solution.py:353
  85.6 13.0 %collective-permute-start.3 = (bf16[96,768]{1,0:T(8,128)(2,1)S(1)}, bf16[96,768]{1,0:T(8,128)(2,1)S(1)}, u32[]{:S(2)}, u32[]{:S(2)}) collective-permute-start(bf16[96,768]{1,0:T(8,128)(2,1)S(1)} %get-tuple-element.37), channel_id=1, source_target_pairs={{0,256},{32,289},{64,320},{96,353},{128,384},{160,417},{192,448},{... | collective-permute-start | bytes 442376 | tf_op jit(solution)/shard_map/ppermute | solution.py:345
  90.0 15.9 %collective-permute-start.5 = (bf16[96,768]{1,0:T(8,128)(2,1)S(1)}, bf16[96,768]{1,0:T(8,128)(2,1)S(1)}, u32[]{:S(2)}, u32[]{:S(2)}) collective-permute-start(bf16[96,768]{1,0:T(8,128)(2,1)S(1)} %get-tuple-element.38), channel_id=1, source_target_pairs={{0,256},{32,289},{64,320},{96,353},{128,384},{160,417},{192,448},{... | collective-permute-start | bytes 442376 | tf_op jit(solution)/shard_map/ppermute | solution.py:345
  98.6 16.5 %collective-permute-start.4 = (bf16[96,768]{1,0:T(8,128)(2,1)S(1)}, bf16[96,768]{1,0:T(8,128)(2,1)S(1)}, u32[]{:S(2)}, u32[]{:S(2)}) collective-permute-start(bf16[96,768]{1,0:T(8,128)(2,1)S(1)} %collective-permute-done.3), channel_id=1, source_target_pairs={{0,256},{32,289},{64,320},{96,353},{128,384},{160,417},{192,448},{... | collective-permute-start | bytes 442376 | tf_op jit(solution)/shard_map/ppermute | solution.py:345
  115.1 9.3 %collective-permute-start.7 = (bf16[2304,384]{1,0:T(8,128)(2,1)S(1)}, bf16[2304,384]{1,0:T(8,128)(2,1)S(1)}, u32[]{:S(2)}, u32[]{:S(2)}) collective-permute-start(bf16[2304,384]{1,0:T(8,128)(2,1)S(1)} %bitcast.13), channel_id=1, source_target_pairs={{0,32},{32,0},{1,33},{33,1},{2,34},{34,2},{3,35},{35,3},{4,36},{36... | collective-permute-start | bytes 5308424 | tf_op jit(solution)/shard_map/ppermute | solution.py:349
  117.0 15.7 %collective-permute-start.6 = (bf16[96,768]{1,0:T(8,128)(2,1)S(1)}, bf16[96,768]{1,0:T(8,128)(2,1)S(1)}, u32[]{:S(2)}, u32[]{:S(2)}) collective-permute-start(bf16[96,768]{1,0:T(8,128)(2,1)S(1)} %collective-permute-done.5), channel_id=1, source_target_pairs={{0,256},{32,289},{64,320},{96,353},{128,384},{160,417},{192,448},{... | collective-permute-start | bytes 442376 | tf_op jit(solution)/shard_map/ppermute | solution.py:345
  124.4 11.8 %copy-start.1 = (bf16[2304,384]{1,0:T(8,128)(2,1)}, bf16[2304,384]{1,0:T(8,128)(2,1)S(1)}, u32[]{:S(2)}) copy-start(bf16[2304,384]{1,0:T(8,128)(2,1)S(1)} %collective-permute-done.7.q_b) | copy-start | bytes 5308420
  131.8 0.9 copy-start.3
  136.2 0.8 copy-start.7
  136.9 17.2 %all-to-all-start.3 = ((bf16[16,128,128]{2,1,0:T(8,128)(2,1)}), bf16[16,128,128]{2,1,0:T(8,128)(2,1)S(1)}, u32[]{:S(2)}, u32[]{:S(2)}) async-start(bf16[16,128,128]{2,1,0:T(8,128)(2,1)} %get-tuple-element.46), calls=%async_computation.3 | async-start | bytes 1048576 | tf_op jit(solution)/shard_map/all_to_all | solution.py:415
  144.2 6.7 %collective-permute-start.8 = (bf16[64,768]{1,0:T(8,128)(2,1)S(1)}, bf16[64,768]{1,0:T(8,128)(2,1)S(1)}, u32[]{:S(2)}, u32[]{:S(2)}) collective-permute-start(bf16[64,768]{1,0:T(8,128)(2,1)S(1)} %fusion), channel_id=1, source_target_pairs={{0,2},{2,4},{4,6},{6,8},{8,10},{10,12},{12,14},{14,16},{16,18},{18... | collective-permute-start | bytes 294920 | tf_op jit(solution)/shard_map/ppermute | solution.py:413
  158.2 12.9 %all-to-all-start.4 = ((bf16[16,48,128]{2,1,0:T(8,128)(2,1)}), bf16[16,48,128]{2,1,0:T(8,128)(2,1)S(1)}, u32[]{:S(2)}, u32[]{:S(2)}) async-start(bf16[16,48,128]{2,1,0:T(8,128)(2,1)} %far_branch.1), calls=%async_computation.4 | async-start | bytes 393216 | tf_op jit(solution)/shard_map/all_to_all | solution.py:420
  163.1 1.5 copy-start.2
  164.5 1.1 copy-start.4
  165.7 1.0 copy-start.8

commit v12 on v11

--- a/solution.py
+++ b/solution.py
@@ -11,7 +11,7 @@
 D_ENC = 1536
 HALF = 64
 TILE_DEV = 192
-CHUNK = 96
+CHUNK = 64
 SEQ_LEN = 4096
 WINDOW = 320
 KEY_SLOTS = 80
@@ -109,42 +109,55 @@
     return first, second
 
 
-def embed_kernel(table, ctx, res, own, other, out, lower, upper, w, p, hidden, normed):
+def embed_kernel(table, ctx, res, own, other, out, lower, upper, w, p, hidden, normed, sems):
     core = table[CORE]
+    w_loads, p_loads = [], []
     for block in range(PLANES):
         turned = block % 4 * 4 + block // 4
         at_own = jnp.where(core == 0, block, turned)
         at_other = jnp.where(core == 0, turned, block)
-        w_rows = slice(block * 2 * W_ROWS, (block + 1) * 2 * W_ROWS)
-        p_rows = slice(block * 2 * P_ROWS, (block + 1) * 2 * P_ROWS)
-        w[core, w_rows] = own[at_own, : 2 * W_ROWS]
-        p[core, p_rows] = own[at_own, 2 * W_ROWS :]
-        w[1 - core, w_rows] = other[at_other, : 2 * W_ROWS]
-        p[1 - core, p_rows] = other[at_other, 2 * W_ROWS :]
+        for n, (source, half, at) in enumerate(((own, core, at_own), (other, 1 - core, at_other))):
+            w_loads.append(
+                pltpu.make_async_copy(source.at[at, : 2 * W_ROWS], w.at[half, block], sems.at[0, n, block])
+            )
+            p_loads.append(
+                pltpu.make_async_copy(source.at[at, 2 * W_ROWS :], p.at[half, block], sems.at[1, n, block])
+            )
+    for load in w_loads + p_loads:
+        load.start()
     total = jnp.zeros((TILE_DEV, 1), F32)
     width = D // 2
+    group = PLANES // 4
     for n in range(4):
+        for load in w_loads[2 * group * n : 2 * group * (n + 1)]:
+            load.wait()
         columns = slice(n * width, (n + 1) * width)
-        part = res[:, columns].astype(F32) + dot_nt(ctx[:, :D], w[0, columns]) + dot_nt(ctx[:, D:], w[1, columns])
+        part = res[:, columns].astype(F32)
+        for half in range(2):
+            rows = w[half, n * group : (n + 1) * group].reshape(width, D)
+            part += dot_nt(ctx[:, half * D : (half + 1) * D], rows)
         hidden[:, columns] = part
         total += jnp.sum(part, axis=1, keepdims=True)
     center = hidden[...] - total / D_ENC
     spread = jnp.sum(center * center, axis=1, keepdims=True) / D_ENC
     normed[...] = (center * lax.rsqrt(spread + NORM_EPS)).astype(BF16)
-    out[...] = (dot_nt(normed[:, :D], p[0]) + dot_nt(normed[:, D:], p[1])).astype(BF16)
+    for load in p_loads:
+        load.wait()
+    out[...] = (dot_nt(normed[:, :D], p[0].reshape(D, D)) + dot_nt(normed[:, D:], p[1].reshape(D, D))).astype(BF16)
     lower[...] = out[:CHUNK]
     upper[...] = out[CHUNK:]
 
 
 def embed(*args):
     scratch = [
-        pltpu.VMEM((2, D_ENC, D), BF16),
-        pltpu.VMEM((2, D, D), BF16),
+        pltpu.VMEM((2, PLANES, 2 * W_ROWS, D), BF16),
+        pltpu.VMEM((2, PLANES, 2 * P_ROWS, D), BF16),
         pltpu.VMEM((TILE_DEV, D_ENC), F32),
         pltpu.VMEM((TILE_DEV, D_ENC), BF16),
+        pltpu.SemaphoreType.DMA((2, 2, PLANES)),
     ]
-    shapes = (((TILE_DEV, D), BF16), ((CHUNK, D), BF16), ((CHUNK, D), BF16))
-    return call(embed_kernel, "embed_rows", shapes, "svvvv-vvv", scratch, 1_400_000_000, 9_000_000)(*args)
+    shapes = (((TILE_DEV, D), BF16), ((CHUNK, D), BF16), ((TILE_DEV - CHUNK, D), BF16))
+    return call(embed_kernel, "embed_rows", shapes, "svvhh-vvv", scratch, 1_400_000_000, 9_000_000)(*args)
 
 
 def key_picks(table, h, first, count):

time: 174 us -> 173 us (level)
    ppermute x4, waiting for transfers between devices: 11.1 us -> 5.97 us  [along_z(): return lax.ppermute(x, ('zlo', 'core', 'zhi'), pairs)]
    ppermute x2, starting transfers between devices: 6.54 us -> 10.9 us  [other_core(): return lax.ppermute(x, 'core', [(0, 1), (1, 0)])]
    ppermute x4, starting transfers between devices: 23.5 us -> 19.2 us  [along_z(): return lax.ppermute(x, ('zlo', 'core', 'zhi'), pairs)]
    all_to_all x1, waiting for transfers between devices: 2.23 us -> 6.36 us  [over_plane(): return lax.all_to_all(x, PLANE, 0, 0)]
where the time goes in v12:
time: 173 us; the launch traced here: 172 us
  starting transfers between devices  66.3 us (38%)
  waiting for transfers between devices  51.9 us (30%)
  Pallas kernels  29.5 us (17%)
  blocking collectives  13.1 us (8%)
  local copies, waits for them, and re-layouts  10.4 us (6%)
    ppermute x4, starting transfers between devices, along_z(): return lax.ppermute(x, ('zlo', 'core', 'zhi'), pairs)  19.2 us
    ppermute x2, waiting for transfers between devices, mirrored(): return lax.ppermute(x, ('zlo', 'zhi'), pairs)  15.9 us
    all_to_all x1, waiting for transfers between devices, along_lines(): return lax.all_to_all(spread, EVERY, 0, 0, axis_index_groups=groups)  15.5 us
    ppermute x2, starting transfers between devices, mirrored(): return lax.ppermute(x, ('zlo', 'zhi'), pairs)  14 us
    all_to_all x1, blocking collectives, along_lines(): return lax.all_to_all(spread, EVERY, 0, 0, axis_index_groups=groups)  13.1 us
    ppermute x2, starting transfers between devices, other_core(): return lax.ppermute(x, 'core', [(0, 1), (1, 0)])  10.9 us
    pallas_call x1, Pallas kernels, own_rows(): call(own_kernel, 'own_rows', shapes, 'svvv-vvvvvv', [], 1000000000, 50000...  7.43 us
    pallas_call x1, Pallas kernels, embed(): call(embed_kernel, 'embed_rows', shapes, 'svvhh-vvv', scratch, 1400000000...  6.56 us
  transfers between devices with their start and end apart: 13, of which 9 were waited for; matrix products, arithmetic and copies ran while one was open for 0% of the time, Pallas kernels for 12%

profile of v12, /device:TPU:1, one launch (start us, length us, event | category | flops | bytes accessed | tf_op | source)
XLA Modules:
  0.0 172.4 jit_solution(169488392491235302)
XLA Ops:
  0.9 12.0 %collective-permute-start = (bf16[72,768]{1,0:T(8,128)(2,1)S(1)}, bf16[72,768]{1,0:T(8,128)(2,1)S(1)}, u32[]{:S(2)}, u32[]{:S(2)}) collective-permute-start(bf16[72,768]{1,0:T(8,128)(2,1)S(1)} %pad_maximum_fusion.1), channel_id=1, source_target_pairs={{0,449},{1,448},{64,385},{65,384},{128,321},{129,320},{192,257},{1... | collective-permute-start | bytes 331784 | tf_op jit(solution)/shard_map/ppermute | solution.py:343
  12.9 10.2 %collective-permute-done = bf16[72,768]{1,0:T(8,128)(2,1)S(1)} collective-permute-done((bf16[72,768]{1,0:T(8,128)(2,1)S(1)}, bf16[72,768]{1,0:T(8,128)(2,1)S(1)}, u32[]{:S(2)}, u32[]{:S(2)}) %collective-permute-start) | collective-permute-done | bytes 110624 | tf_op jit(solution)/shard_map/ppermute | solution.py:343
  23.3 13.1 %all_to_all.25 = bf16[4,144,768]{2,1,0:T(8,128)(2,1)S(1)} all-to-all(bf16[4,144,768]{2,1,0:T(8,128)(2,1)S(1)} %broadcast_in_dim.8), channel_id=1, replica_groups={{0,2,4,6},{8,10,12,14},{16,18,20,22},{24,26,28,30},{1,3,5,7},{9,11,13,1..., dimensions={0} | all-to-all | bytes 1769472 | tf_op jit(solution)/shard_map/all_to_all | solution.py:387
  36.4 2.0 %broadcast_in_dim.10 = bf16[4,576,768]{2,1,0:T(8,128)(2,1)} broadcast(bf16[576,768]{1,0:T(8,128)(2,1)S(1)} %bitcast.17), dimensions={1,2} | broadcast | bytes 4423680 | tf_op jit(solution)/shard_map/broadcast_in_dim | solution.py:386
  38.4 4.9 %all-to-all-start.1 = ((bf16[4,576,768]{2,1,0:T(8,128)(2,1)}), bf16[4,576,768]{2,1,0:T(8,128)(2,1)}, u32[]{:S(2)}, u32[]{:S(2)}) async-start(bf16[4,576,768]{2,1,0:T(8,128)(2,1)} %broadcast_in_dim.10), calls=%async_computation.1 | async-start | bytes 7077888 | tf_op jit(solution)/shard_map/all_to_all | solution.py:387
  43.4 2.1 %collective-permute-start.1 = (bf16[72,384]{1,0:T(8,128)(2,1)S(1)}, bf16[72,384]{1,0:T(8,128)(2,1)S(1)}, u32[]{:S(2)}, u32[]{:S(2)}) collective-permute-start(bf16[72,384]{1,0:T(8,128)(2,1)S(1)} %dynamic-slice_bitcast_fusion.1), channel_id=1, source_target_pairs={{0,449},{1,448},{64,385},{65,384},{128,321},{129,320},{192,257},{1... | collective-permute-start | bytes 165896 | tf_op jit(solution)/shard_map/ppermute | solution.py:343
  45.5 5.8 %collective-permute-done.1 = bf16[72,384]{1,0:T(8,128)(2,1)S(1)} collective-permute-done((bf16[72,384]{1,0:T(8,128)(2,1)S(1)}, bf16[72,384]{1,0:T(8,128)(2,1)S(1)}, u32[]{:S(2)}, u32[]{:S(2)}) %collective-permute-start.1) | collective-permute-done | bytes 55328 | tf_op jit(solution)/shard_map/ppermute | solution.py:343
  51.2 15.5 %all-to-all-done.1 = bf16[4,576,768]{2,1,0:T(8,128)(2,1)} async-done(((bf16[4,576,768]{2,1,0:T(8,128)(2,1)}), bf16[4,576,768]{2,1,0:T(8,128)(2,1)}, u32[]{:S(2)}, u32[]{:S(2)}) %all-to-all-start.1) | async-done | bytes 3538976 | tf_op jit(solution)/shard_map/all_to_all | solution.py:387
  66.7 1.4 broadcast_in_dim.22
  68.2 4.6 %collective-permute-start.2 = (bf16[16,144,768]{2,1,0:T(8,128)(2,1)}, bf16[16,144,768]{2,1,0:T(8,128)(2,1)}, u32[]{:S(2)}, u32[]{:S(2)}) collective-permute-start(bf16[16,144,768]{2,1,0:T(8,128)(2,1)} %bitcast.6.own), channel_id=1, source_target_pairs={{0,32},{32,0},{1,33},{33,1},{2,34},{34,2},{3,35},{35,3},{4,36},{36... | collective-permute-start | bytes 10616840 | tf_op jit(solution)/shard_map/ppermute | solution.py:362
  72.8 3.7 %all-to-all-start.2 = ((bf16[16,144,384]{2,1,0:T(8,128)(2,1)}), bf16[16,144,384]{2,1,0:T(8,128)(2,1)S(1)}, u32[]{:S(2)}, u32[]{:S(2)}) async-start(bf16[16,144,384]{2,1,0:T(8,128)(2,1)} %broadcast_in_dim.22), calls=%async_computation.2 | async-start | bytes 3538944 | tf_op jit(solution)/shard_map/all_to_all | solution.py:366
  76.7 1.7 prepare_rows.1
  79.0 6.6 %embed_rows.1 = (bf16[192,768]{1,0:T(8,128)(2,1)S(1)}, bf16[64,768]{1,0:T(8,128)(2,1)S(1)}, bf16[128,768]{1,0:T(8,128)(2,1)S(1)}) custom-call(s32[48]{0:T(128)S(1)} %get-tuple-element.31.table, bf16[192,1536]{1,0:T(8,128)(2,1)S(1)} %get-tuple-element.33.ctx, bf16[192,1536]{1,0:T(8,128)(2,1)S(1)} %get-tuple-element.34.res, bf16[16,144,768]{2,1,0:T(8,128)(2,1)} %bitcast.6.own, ...), custom_call_target="tpu_custom_call" | custom-call | flops 1400000000 | bytes 9000000 | tf_op jit(solution)/shard_map/embed_rows/pallas_call | solution.py:160
  85.6 4.4 %collective-permute-start.3 = (bf16[64,768]{1,0:T(8,128)(2,1)S(1)}, bf16[64,768]{1,0:T(8,128)(2,1)S(1)}, u32[]{:S(2)}, u32[]{:S(2)}) collective-permute-start(bf16[64,768]{1,0:T(8,128)(2,1)S(1)} %get-tuple-element.37), channel_id=1, source_target_pairs={{0,256},{32,289},{64,320},{96,353},{128,384},{160,417},{192,448},{... | collective-permute-start | bytes 294920 | tf_op jit(solution)/shard_map/ppermute | solution.py:358
  90.0 6.7 %collective-permute-start.5 = (bf16[128,768]{1,0:T(8,128)(2,1)S(1)}, bf16[128,768]{1,0:T(8,128)(2,1)S(1)}, u32[]{:S(2)}, u32[]{:S(2)}) collective-permute-start(bf16[128,768]{1,0:T(8,128)(2,1)S(1)} %get-tuple-element.38), channel_id=1, source_target_pairs={{0,256},{32,289},{64,320},{96,353},{128,384},{160,417},{192,448},{... | collective-permute-start | bytes 589832 | tf_op jit(solution)/shard_map/ppermute | solution.py:358
  96.7 2.9 %collective-permute-start.4 = (bf16[64,768]{1,0:T(8,128)(2,1)S(1)}, bf16[64,768]{1,0:T(8,128)(2,1)S(1)}, u32[]{:S(2)}, u32[]{:S(2)}) collective-permute-start(bf16[64,768]{1,0:T(8,128)(2,1)S(1)} %collective-permute-done.3), channel_id=1, source_target_pairs={{0,256},{32,289},{64,320},{96,353},{128,384},{160,417},{192,448},{... | collective-permute-start | bytes 294920 | tf_op jit(solution)/shard_map/ppermute | solution.py:358
  99.5 6.4 %all-to-all-done.2 = bf16[16,144,384]{2,1,0:T(8,128)(2,1)S(1)} async-done(((bf16[16,144,384]{2,1,0:T(8,128)(2,1)}), bf16[16,144,384]{2,1,0:T(8,128)(2,1)S(1)}, u32[]{:S(2)}, u32[]{:S(2)}) %all-to-all-start.2) | async-done | bytes 1769504 | tf_op jit(solution)/shard_map/all_to_all | solution.py:366
  105.9 3.1 %collective-permute-done.4.lower = bf16[64,768]{1,0:T(8,128)(2,1)S(1)} collective-permute-done((bf16[64,768]{1,0:T(8,128)(2,1)S(1)}, bf16[64,768]{1,0:T(8,128)(2,1)S(1)}, u32[]{:S(2)}, u32[]{:S(2)}) %collective-permute-start.4) | collective-permute-done | bytes 98336 | tf_op jit(solution)/shard_map/ppermute | solution.py:358
  109.0 6.3 %collective-permute-start.7 = (bf16[2304,384]{1,0:T(8,128)(2,1)S(1)}, bf16[2304,384]{1,0:T(8,128)(2,1)S(1)}, u32[]{:S(2)}, u32[]{:S(2)}) collective-permute-start(bf16[2304,384]{1,0:T(8,128)(2,1)S(1)} %bitcast.13), channel_id=1, source_target_pairs={{0,32},{32,0},{1,33},{33,1},{2,34},{34,2},{3,35},{35,3},{4,36},{36... | collective-permute-start | bytes 5308424 | tf_op jit(solution)/shard_map/ppermute | solution.py:362
  115.3 5.2 %collective-permute-start.6 = (bf16[128,768]{1,0:T(8,128)(2,1)S(1)}, bf16[128,768]{1,0:T(8,128)(2,1)S(1)}, u32[]{:S(2)}, u32[]{:S(2)}) collective-permute-start(bf16[128,768]{1,0:T(8,128)(2,1)S(1)} %collective-permute-done.5), channel_id=1, source_target_pairs={{0,256},{32,289},{64,320},{96,353},{128,384},{160,417},{192,448},{... | collective-permute-start | bytes 589832 | tf_op jit(solution)/shard_map/ppermute | solution.py:358
  120.6 7.4 %own_rows.1 = (bf16[16,128,128]{2,1,0:T(8,128)(2,1)S(1)}, bf16[768,192]{1,0:T(8,128)(2,1)S(1)}, bf16[1536,192]{1,0:T(8,128)(2,1)}, f32[768,192]{1,0:T(8,128)S(1)...) custom-call(s32[48]{0:T(128)S(1)} %get-tuple-element.31.table, bf16[192,768]{1,0:T(8,128)(2,1)S(1)} %get-tuple-element.41.own, ...), custom_call_target="tpu_custom_call" | custom-call | flops 1000000000 | bytes 5000000 | tf_op jit(solution)/shard_map/own_rows/pallas_call | solution.py:214
  128.9 2.8 %collective-permute-done.6.upper = bf16[128,768]{1,0:T(8,128)(2,1)S(1)} collective-permute-done((bf16[128,768]{1,0:T(8,128)(2,1)S(1)}, bf16[128,768]{1,0:T(8,128)(2,1)S(1)}, u32[]{:S(2)}, u32[]{:S(2)}) %collective-permute-start.6) | collective-permute-done | bytes 196640 | tf_op jit(solution)/shard_map/ppermute | solution.py:358
  131.7 3.5 %pair_rows.1 = (bf16[16,128,128]{2,1,0:T(8,128)(2,1)}, bf16[1536,64]{1,0:T(8,128)(2,1)S(1)}) custom-call(s32[48]{0:T(128)S(1)} %get-tuple-element.31.table, bf16[64,768]{1,0:T(8,128)(2,1)S(1)} %collective-permute-done.4.lower, bf16[128,768]{1,0:T(8,128)(2,1)S(1)} %collective-permute-done.6.upper, bf16[2304,384]{1,0:T(8,128)(2,1)S(1)} %bitcast.15, ...), custom_call_target="tpu_custom_call" | custom-call | flops 700000000 | bytes 4000000 | tf_op jit(solution)/shard_map/pair_rows/pallas_call | solution.py:235
  136.0 5.9 %all-to-all-start.3 = ((bf16[16,128,128]{2,1,0:T(8,128)(2,1)}), bf16[16,128,128]{2,1,0:T(8,128)(2,1)S(1)}, u32[]{:S(2)}, u32[]{:S(2)}) async-start(bf16[16,128,128]{2,1,0:T(8,128)(2,1)} %get-tuple-element.46), calls=%async_computation.3 | async-start | bytes 1048576 | tf_op jit(solution)/shard_map/all_to_all | solution.py:428
  143.2 3.5 %collective-permute-start.8 = (bf16[64,768]{1,0:T(8,128)(2,1)S(1)}, bf16[64,768]{1,0:T(8,128)(2,1)S(1)}, u32[]{:S(2)}, u32[]{:S(2)}) collective-permute-start(bf16[64,768]{1,0:T(8,128)(2,1)S(1)} %fusion), channel_id=1, source_target_pairs={{0,2},{2,4},{4,6},{6,8},{8,10},{10,12},{12,14},{14,16},{16,18},{18... | collective-permute-start | bytes 294920 | tf_op jit(solution)/shard_map/ppermute | solution.py:426
  146.7 3.5 %collective-permute-done.8.halo = bf16[64,768]{1,0:T(8,128)(2,1)S(1)} collective-permute-done((bf16[64,768]{1,0:T(8,128)(2,1)S(1)}, bf16[64,768]{1,0:T(8,128)(2,1)S(1)}, u32[]{:S(2)}, u32[]{:S(2)}) %collective-permute-start.8) | collective-permute-done | bytes 98336 | tf_op jit(solution)/shard_map/ppermute | solution.py:426
  150.1 4.0 %all-to-all-done.3.arrived = bf16[16,128,128]{2,1,0:T(8,128)(2,1)S(1)} async-done(((bf16[16,128,128]{2,1,0:T(8,128)(2,1)}), bf16[16,128,128]{2,1,0:T(8,128)(2,1)S(1)}, u32[]{:S(2)}, u32[]{:S(2)}) %all-to-all-start.3) | async-done | bytes 524320 | tf_op jit(solution)/shard_map/all_to_all | solution.py:428
  154.1 4.0 %far_branch.1 = bf16[16,48,128]{2,1,0:T(8,128)(2,1)} custom-call(s32[48]{0:T(128)S(1)} %get-tuple-element.31.table, bf16[16,128,128]{2,1,0:T(8,128)(2,1)S(1)} %all-to-all-done.3.arrived), custom_call_target="tpu_custom_call" | custom-call | flops 500000000 | bytes 1000000 | tf_op jit(solution)/shard_map/far_branch/pallas_call | solution.py:303
  158.1 4.3 %all-to-all-start.4 = ((bf16[16,48,128]{2,1,0:T(8,128)(2,1)}), bf16[16,48,128]{2,1,0:T(8,128)(2,1)S(1)}, u32[]{:S(2)}, u32[]{:S(2)}) async-start(bf16[16,48,128]{2,1,0:T(8,128)(2,1)} %far_branch.1), calls=%async_computation.4 | async-start | bytes 393216 | tf_op jit(solution)/shard_map/all_to_all | solution.py:433
  162.4 1.5 copy-done.2
  166.0 4.4 %rim_rows.1 = (f32[768,192]{1,0:T(8,128)S(1)}, f32[16,192]{1,0:T(8,128)S(1)}, f32[16,192]{1,0:T(8,128)S(1)}) custom-call(s32[48]{0:T(128)S(1)} %get-tuple-element.31.table, bf16[768,192]{1,0:T(8,128)(2,1)S(1)} %get-tuple-element.48.q, bf16[1536,64]{1,0:T(8,128)(2,1)S(1)} %copy-done.8, bf16[64,768]{1,0:T(8,128)(2,1)S(1)} %collective-permute-done.8.halo, ...), custom_call_target="tpu_custom_call" | custom-call | flops 400000000 | bytes 5000000 | tf_op jit(solution)/shard_map/rim_rows/pallas_call | solution.py:268
  170.5 2.0 %finish_rows.1 = bf16[1,192,768]{2,1,0:T(8,128)(2,1)} custom-call(s32[48]{0:T(128)S(1)} %get-tuple-element.31.table, bf16[16,48,128]{2,1,0:T(8,128)(2,1)S(1)} %all-to-all-done.4.answers, f32[768,192]{1,0:T(8,128)S(1)} %get-tuple-element.54.local_sum, f32[16,192]{1,0:T(8,128)S(1)} %get-tuple-element.55.local_best, ...), custom_call_target="tpu_custom_call" | custom-call | flops 100000000 | bytes 1500000 | tf_op jit(solution)/shard_map/finish_rows/pallas_call | solution.py:333
  (44 shorter events, 6.4 us)
Async XLA Ops:
  0.0 0.9 copy-start
  0.9 22.2 %collective-permute-start = (bf16[72,768]{1,0:T(8,128)(2,1)S(1)}, bf16[72,768]{1,0:T(8,128)(2,1)S(1)}, u32[]{:S(2)}, u32[]{:S(2)}) collective-permute-start(bf16[72,768]{1,0:T(8,128)(2,1)S(1)} %pad_maximum_fusion.1), channel_id=1, source_target_pairs={{0,449},{1,448},{64,385},{65,384},{128,321},{129,320},{192,257},{1... | collective-permute-start | bytes 331784 | tf_op jit(solution)/shard_map/ppermute | solution.py:343
  38.4 4.9 %copy-start.12 = (bf16[768,72]{0,1:T(8,128)(2,1)S(1)}, bf16[768,72]{0,1:T(8,128)(2,1)}, u32[]{:S(2)}) copy-start(bf16[768,72]{0,1:T(8,128)(2,1)} %param.12) | copy-start | bytes 331780
  38.4 28.3 %all-to-all-start.1 = ((bf16[4,576,768]{2,1,0:T(8,128)(2,1)}), bf16[4,576,768]{2,1,0:T(8,128)(2,1)}, u32[]{:S(2)}, u32[]{:S(2)}) async-start(bf16[4,576,768]{2,1,0:T(8,128)(2,1)} %broadcast_in_dim.10), calls=%async_computation.1 | async-start | bytes 7077888 | tf_op jit(solution)/shard_map/all_to_all | solution.py:387
  43.3 33.3 %copy-start.5 = (bf16[1,192,1536]{2,1,0:T(8,128)(2,1)S(1)}, bf16[1,192,1536]{2,1,0:T(8,128)(2,1)}, u32[]{:S(2)}) copy-start(bf16[1,192,1536]{2,1,0:T(8,128)(2,1)} %ctx.1) | copy-start | bytes 1769476
  43.3 33.3 %copy-start.6 = (bf16[1,192,1536]{2,1,0:T(8,128)(2,1)S(1)}, bf16[1,192,1536]{2,1,0:T(8,128)(2,1)}, u32[]{:S(2)}) copy-start(bf16[1,192,1536]{2,1,0:T(8,128)(2,1)} %res.1) | copy-start | bytes 1769476
  43.3 33.3 %copy-start.9 = (s32[1,1,192]{2,1,0:T(1,128)S(1)}, s32[1,1,192]{2,1,0:T(1,128)}, u32[]{:S(2)}) copy-start(s32[1,1,192]{2,1,0:T(1,128)} %listing.3) | copy-start | bytes 2308
  43.3 33.3 %copy-start.10 = (s32[1,32]{1,0:T(1,128)S(1)}, s32[1,32]{1,0:T(1,128)}, u32[]{:S(2)}) copy-start(s32[1,32]{1,0:T(1,128)} %counts.1) | copy-start | bytes 388
  43.4 33.3 %copy-start.11 = (s32[1,2]{1,0:T(1,128)S(1)}, s32[1,2]{1,0:T(1,128)}, u32[]{:S(2)}) copy-start(s32[1,2]{1,0:T(1,128)} %dilation.1) | copy-start | bytes 28
  43.4 7.8 %collective-permute-start.1 = (bf16[72,384]{1,0:T(8,128)(2,1)S(1)}, bf16[72,384]{1,0:T(8,128)(2,1)S(1)}, u32[]{:S(2)}, u32[]{:S(2)}) collective-permute-start(bf16[72,384]{1,0:T(8,128)(2,1)S(1)} %dynamic-slice_bitcast_fusion.1), channel_id=1, source_target_pairs={{0,449},{1,448},{64,385},{65,384},{128,321},{129,320},{192,257},{1... | collective-permute-start | bytes 165896 | tf_op jit(solution)/shard_map/ppermute | solution.py:343
  68.2 10.8 %collective-permute-start.2 = (bf16[16,144,768]{2,1,0:T(8,128)(2,1)}, bf16[16,144,768]{2,1,0:T(8,128)(2,1)}, u32[]{:S(2)}, u32[]{:S(2)}) collective-permute-start(bf16[16,144,768]{2,1,0:T(8,128)(2,1)} %bitcast.6.own), channel_id=1, source_target_pairs={{0,32},{32,0},{1,33},{33,1},{2,34},{34,2},{3,35},{35,3},{4,36},{36... | collective-permute-start | bytes 10616840 | tf_op jit(solution)/shard_map/ppermute | solution.py:362
  72.8 33.1 %all-to-all-start.2 = ((bf16[16,144,384]{2,1,0:T(8,128)(2,1)}), bf16[16,144,384]{2,1,0:T(8,128)(2,1)S(1)}, u32[]{:S(2)}, u32[]{:S(2)}) async-start(bf16[16,144,384]{2,1,0:T(8,128)(2,1)} %broadcast_in_dim.22), calls=%async_computation.2 | async-start | bytes 3538944 | tf_op jit(solution)/shard_map/all_to_all | solution.py:366
  85.6 11.1 %collective-permute-start.3 = (bf16[64,768]{1,0:T(8,128)(2,1)S(1)}, bf16[64,768]{1,0:T(8,128)(2,1)S(1)}, u32[]{:S(2)}, u32[]{:S(2)}) collective-permute-start(bf16[64,768]{1,0:T(8,128)(2,1)S(1)} %get-tuple-element.37), channel_id=1, source_target_pairs={{0,256},{32,289},{64,320},{96,353},{128,384},{160,417},{192,448},{... | collective-permute-start | bytes 294920 | tf_op jit(solution)/shard_map/ppermute | solution.py:358
  90.0 19.1 %collective-permute-start.5 = (bf16[128,768]{1,0:T(8,128)(2,1)S(1)}, bf16[128,768]{1,0:T(8,128)(2,1)S(1)}, u32[]{:S(2)}, u32[]{:S(2)}) collective-permute-start(bf16[128,768]{1,0:T(8,128)(2,1)S(1)} %get-tuple-element.38), channel_id=1, source_target_pairs={{0,256},{32,289},{64,320},{96,353},{128,384},{160,417},{192,448},{... | collective-permute-start | bytes 589832 | tf_op jit(solution)/shard_map/ppermute | solution.py:358
  96.7 12.4 %collective-permute-start.4 = (bf16[64,768]{1,0:T(8,128)(2,1)S(1)}, bf16[64,768]{1,0:T(8,128)(2,1)S(1)}, u32[]{:S(2)}, u32[]{:S(2)}) collective-permute-start(bf16[64,768]{1,0:T(8,128)(2,1)S(1)} %collective-permute-done.3), channel_id=1, source_target_pairs={{0,256},{32,289},{64,320},{96,353},{128,384},{160,417},{192,448},{... | collective-permute-start | bytes 294920 | tf_op jit(solution)/shard_map/ppermute | solution.py:358
  109.0 11.5 %collective-permute-start.7 = (bf16[2304,384]{1,0:T(8,128)(2,1)S(1)}, bf16[2304,384]{1,0:T(8,128)(2,1)S(1)}, u32[]{:S(2)}, u32[]{:S(2)}) collective-permute-start(bf16[2304,384]{1,0:T(8,128)(2,1)S(1)} %bitcast.13), channel_id=1, source_target_pairs={{0,32},{32,0},{1,33},{33,1},{2,34},{34,2},{3,35},{35,3},{4,36},{36... | collective-permute-start | bytes 5308424 | tf_op jit(solution)/shard_map/ppermute | solution.py:362
  115.3 16.4 %collective-permute-start.6 = (bf16[128,768]{1,0:T(8,128)(2,1)S(1)}, bf16[128,768]{1,0:T(8,128)(2,1)S(1)}, u32[]{:S(2)}, u32[]{:S(2)}) collective-permute-start(bf16[128,768]{1,0:T(8,128)(2,1)S(1)} %collective-permute-done.5), channel_id=1, source_target_pairs={{0,256},{32,289},{64,320},{96,353},{128,384},{160,417},{192,448},{... | collective-permute-start | bytes 589832 | tf_op jit(solution)/shard_map/ppermute | solution.py:358
  120.6 14.6 %copy-start.1 = (bf16[2304,384]{1,0:T(8,128)(2,1)}, bf16[2304,384]{1,0:T(8,128)(2,1)S(1)}, u32[]{:S(2)}) copy-start(bf16[2304,384]{1,0:T(8,128)(2,1)S(1)} %collective-permute-done.7.q_b) | copy-start | bytes 5308420
  128.0 0.9 copy-start.3
  135.2 0.8 copy-start.7
  136.0 18.1 %all-to-all-start.3 = ((bf16[16,128,128]{2,1,0:T(8,128)(2,1)}), bf16[16,128,128]{2,1,0:T(8,128)(2,1)S(1)}, u32[]{:S(2)}, u32[]{:S(2)}) async-start(bf16[16,128,128]{2,1,0:T(8,128)(2,1)} %get-tuple-element.46), calls=%async_computation.3 | async-start | bytes 1048576 | tf_op jit(solution)/shard_map/all_to_all | solution.py:428
  143.2 6.9 %collective-permute-start.8 = (bf16[64,768]{1,0:T(8,128)(2,1)S(1)}, bf16[64,768]{1,0:T(8,128)(2,1)S(1)}, u32[]{:S(2)}, u32[]{:S(2)}) collective-permute-start(bf16[64,768]{1,0:T(8,128)(2,1)S(1)} %fusion), channel_id=1, source_target_pairs={{0,2},{2,4},{4,6},{6,8},{8,10},{10,12},{12,14},{14,16},{16,18},{18... | collective-permute-start | bytes 294920 | tf_op jit(solution)/shard_map/ppermute | solution.py:426
  158.1 12.3 %all-to-all-start.4 = ((bf16[16,48,128]{2,1,0:T(8,128)(2,1)}), bf16[16,48,128]{2,1,0:T(8,128)(2,1)S(1)}, u32[]{:S(2)}, u32[]{:S(2)}) async-start(bf16[16,48,128]{2,1,0:T(8,128)(2,1)} %far_branch.1), calls=%async_computation.4 | async-start | bytes 393216 | tf_op jit(solution)/shard_map/all_to_all | solution.py:433
  162.4 1.5 copy-start.2
  163.9 1.1 copy-start.4
  165.1 1.0 copy-start.8

commit v13 on v12

--- a/solution.py
+++ b/solution.py
@@ -109,27 +109,26 @@
     return first, second
 
 
-def embed_kernel(table, ctx, res, own, other, out, lower, upper, w, p, hidden, normed, sems):
-    core = table[CORE]
-    w_loads, p_loads = [], []
+def block_loads(core, own, other, to, sems):
+    loads = []
     for block in range(PLANES):
         turned = block % 4 * 4 + block // 4
         at_own = jnp.where(core == 0, block, turned)
         at_other = jnp.where(core == 0, turned, block)
         for n, (source, half, at) in enumerate(((own, core, at_own), (other, 1 - core, at_other))):
-            w_loads.append(
-                pltpu.make_async_copy(source.at[at, : 2 * W_ROWS], w.at[half, block], sems.at[0, n, block])
-            )
-            p_loads.append(
-                pltpu.make_async_copy(source.at[at, 2 * W_ROWS :], p.at[half, block], sems.at[1, n, block])
-            )
-    for load in w_loads + p_loads:
+            loads.append(pltpu.make_async_copy(source.at[at], to.at[half, block], sems.at[n, block]))
+    for load in loads:
         load.start()
+    return loads
+
+
+def hidden_kernel(table, ctx, res, own, other, normed, w, hidden, sems):
+    loads = block_loads(table[CORE], own, other, w, sems)
     total = jnp.zeros((TILE_DEV, 1), F32)
     width = D // 2
     group = PLANES // 4
     for n in range(4):
-        for load in w_loads[2 * group * n : 2 * group * (n + 1)]:
+        for load in loads[2 * group * n : 2 * group * (n + 1)]:
             load.wait()
         columns = slice(n * width, (n + 1) * width)
         part = res[:, columns].astype(F32)
@@ -141,7 +140,20 @@
     center = hidden[...] - total / D_ENC
     spread = jnp.sum(center * center, axis=1, keepdims=True) / D_ENC
     normed[...] = (center * lax.rsqrt(spread + NORM_EPS)).astype(BF16)
-    for load in p_loads:
+
+
+def hidden_rows(*args):
+    scratch = [
+        pltpu.VMEM((2, PLANES, 2 * W_ROWS, D), BF16),
+        pltpu.VMEM((TILE_DEV, D_ENC), F32),
+        pltpu.SemaphoreType.DMA((2, PLANES)),
+    ]
+    shapes = (((TILE_DEV, D_ENC), BF16),)
+    return call(hidden_kernel, "hidden_rows", shapes, "svvhh-v", scratch, 900_000_000, 6_000_000)(*args)[0]
+
+
+def embed_kernel(table, normed, own, other, out, lower, upper, p, sems):
+    for load in block_loads(table[CORE], own, other, p, sems):
         load.wait()
     out[...] = (dot_nt(normed[:, :D], p[0].reshape(D, D)) + dot_nt(normed[:, D:], p[1].reshape(D, D))).astype(BF16)
     lower[...] = out[:CHUNK]
@@ -149,15 +161,9 @@
 
 
 def embed(*args):
-    scratch = [
-        pltpu.VMEM((2, PLANES, 2 * W_ROWS, D), BF16),
-        pltpu.VMEM((2, PLANES, 2 * P_ROWS, D), BF16),
-        pltpu.VMEM((TILE_DEV, D_ENC), F32),
-        pltpu.VMEM((TILE_DEV, D_ENC), BF16),
-        pltpu.SemaphoreType.DMA((2, 2, PLANES)),
-    ]
+    scratch = [pltpu.VMEM((2, PLANES, 2 * P_ROWS, D), BF16), pltpu.SemaphoreType.DMA((2, PLANES))]
     shapes = (((TILE_DEV, D), BF16), ((CHUNK, D), BF16), ((TILE_DEV - CHUNK, D), BF16))
-    return call(embed_kernel, "embed_rows", shapes, "svvhh-vvv", scratch, 1_400_000_000, 9_000_000)(*args)
+    return call(embed_kernel, "embed_rows", shapes, "svhh-vvv", scratch, 500_000_000, 3_000_000)(*args)
 
 
 def key_picks(table, h, first, count):
@@ -406,11 +412,15 @@
     wp = jnp.concatenate(
         [in_order(w_own, other_wp[:W_ROWS], high), in_order(p_own, other_wp[W_ROWS:], high)]
     )
-    wp = along_lines(along_lines(wp, 0).reshape(-1, D), 1).reshape(PLANES, -1, D)
-    q_both = copies(in_order(q_own, q_other, high))
-    wp, q_both = hold(wp, q_both)
+    lines = along_lines(wp, 0)
+    w_lines, p_lines = lines[:, : 2 * W_ROWS].reshape(-1, D), lines[:, 2 * W_ROWS :].reshape(-1, D)
+    w_all = along_lines(w_lines, 1).reshape(PLANES, -1, D)
+    w_all, p_lines = hold(w_all, p_lines)
+    p_all = along_lines(p_lines, 1).reshape(PLANES, -1, D)
+    normed = hidden_rows(table, own_ctx, own_res, w_all, other_core(w_all))
+    p_all, normed, q_both = hold(p_all, normed, copies(in_order(q_own, q_other, high)))
     q_a = over_plane(q_both)
-    embedded, lower, upper = embed(table, own_ctx, own_res, wp, other_core(wp))
+    embedded, lower, upper = embed(table, normed, p_all, other_core(p_all))
     lower = along_z(along_z(lower, 0), 1)
     upper = along_z(upper, 0)
     q_a, embedded, lower, upper = hold(q_a, embedded, lower, upper)

time: 173 us -> 191 us (1.10)
  starting transfers between devices: 66.3 us -> 80.4 us
  waiting for transfers between devices: 51.9 us -> 47 us
  Pallas kernels: 29.5 us -> 33.9 us
  local copies, waits for them, and re-layouts: 10.4 us -> 13.6 us
    ppermute x4, starting transfers between devices: 19.2 us -> 25.7 us  [along_z(): return lax.ppermute(x, ('zlo', 'core', 'zhi'), pairs)]
    all_to_all x1, waiting for transfers between devices: 6.36 us -> 0.01 us  [over_plane(): return lax.all_to_all(x, PLANE, 0, 0)]
    pallas_call x1 -> x2, Pallas kernels: 6.56 us -> 11 us  [the longest x1 6.81 us: hidden_rows(): call(hidden_kernel, 'hidden_rows', shapes, 'svvhh-v', scratch, 900000000,...]
    all_to_all x1 -> x2, starting transfers between devices: 4.85 us -> 8 us  [along_lines(): return lax.all_to_all(spread, EVERY, 0, 0, axis_index_groups=groups)]
    ppermute x4, waiting for transfers between devices: 5.97 us -> 9.07 us  [along_z(): return lax.ppermute(x, ('zlo', 'core', 'zhi'), pairs)]
    ppermute x2, waiting for transfers between devices: 15.9 us -> 13.3 us  [mirrored(): return lax.ppermute(x, ('zlo', 'zhi'), pairs)]
    ppermute x2, starting transfers between devices: 14 us -> 16.5 us  [mirrored(): return lax.ppermute(x, ('zlo', 'zhi'), pairs)]
    ppermute x2 -> x3, waiting for transfers between devices: 0.66 us -> 2.67 us  [other_core(): return lax.ppermute(x, 'core', [(0, 1), (1, 0)])]
  transfers between devices with their start and end apart: 13 -> 15, of which waited for: 9 -> 9; matrix products, arithmetic and copies ran while one was open for 0% -> 2% of each run, Pallas kernels for 12% -> 13%
where the time goes in v13:
time: 191 us; the launch traced here: 189 us
  starting transfers between devices  80.4 us (42%)
  waiting for transfers between devices  47 us (25%)
  Pallas kernels  33.9 us (18%)
  local copies, waits for them, and re-layouts  13.6 us (7%)
  blocking collectives  13.1 us (7%)
    ppermute x4, starting transfers between devices, along_z(): return lax.ppermute(x, ('zlo', 'core', 'zhi'), pairs)  25.7 us
    ppermute x2, starting transfers between devices, mirrored(): return lax.ppermute(x, ('zlo', 'zhi'), pairs)  16.5 us
    all_to_all x2, waiting for transfers between devices, along_lines(): return lax.all_to_all(spread, EVERY, 0, 0, axis_index_groups=groups)  16.3 us
    ppermute x2, waiting for transfers between devices, mirrored(): return lax.ppermute(x, ('zlo', 'zhi'), pairs)  13.3 us
    all_to_all x1, blocking collectives, along_lines(): return lax.all_to_all(spread, EVERY, 0, 0, axis_index_groups=groups)  13.1 us
    ppermute x3, starting transfers between devices, other_core(): return lax.ppermute(x, 'core', [(0, 1), (1, 0)])  10 us
    ppermute x4, waiting for transfers between devices, along_z(): return lax.ppermute(x, ('zlo', 'core', 'zhi'), pairs)  9.07 us
    all_to_all x2, starting transfers between devices, along_lines(): return lax.all_to_all(spread, EVERY, 0, 0, axis_index_groups=groups)  8 us
  transfers between devices with their start and end apart: 15, of which 9 were waited for; matrix products, arithmetic and copies ran while one was open for 2% of the time, Pallas kernels for 13%

profile of v13, /device:TPU:1, one launch (start us, length us, event | category | flops | bytes accessed | tf_op | source)
XLA Modules:
  0.0 189.3 jit_solution(44715017809603313)
XLA Ops:
  1.7 12.0 %collective-permute-start = (bf16[72,768]{1,0:T(8,128)(2,1)S(1)}, bf16[72,768]{1,0:T(8,128)(2,1)S(1)}, u32[]{:S(2)}, u32[]{:S(2)}) collective-permute-start(bf16[72,768]{1,0:T(8,128)(2,1)S(1)} %pad_maximum_fusion.1), channel_id=1, source_target_pairs={{0,449},{1,448},{64,385},{65,384},{128,321},{129,320},{192,257},{1... | collective-permute-start | bytes 331784 | tf_op jit(solution)/shard_map/ppermute | solution.py:349
  13.7 10.2 %collective-permute-done = bf16[72,768]{1,0:T(8,128)(2,1)S(1)} collective-permute-done((bf16[72,768]{1,0:T(8,128)(2,1)S(1)}, bf16[72,768]{1,0:T(8,128)(2,1)S(1)}, u32[]{:S(2)}, u32[]{:S(2)}) %collective-permute-start) | collective-permute-done | bytes 110624 | tf_op jit(solution)/shard_map/ppermute | solution.py:349
  24.0 13.1 %all_to_all.30 = bf16[4,144,768]{2,1,0:T(8,128)(2,1)S(1)} all-to-all(bf16[4,144,768]{2,1,0:T(8,128)(2,1)S(1)} %broadcast_in_dim.10), channel_id=1, replica_groups={{0,2,4,6},{8,10,12,14},{16,18,20,22},{24,26,28,30},{1,3,5,7},{9,11,13,1..., dimensions={0} | all-to-all | bytes 1769472 | tf_op jit(solution)/shard_map/all_to_all | solution.py:393
  38.8 3.7 %all-to-all-start.1 = ((bf16[4,384,768]{2,1,0:T(8,128)(2,1)}), bf16[4,384,768]{2,1,0:T(8,128)(2,1)S(1)}, u32[]{:S(2)}, u32[]{:S(2)}) async-start(bf16[4,384,768]{2,1,0:T(8,128)(2,1)} %broadcast_in_dim.12), calls=%async_computation.1 | async-start | bytes 4718592 | tf_op jit(solution)/shard_map/all_to_all | solution.py:393
  43.2 16.3 %all-to-all-done.1 = bf16[4,384,768]{2,1,0:T(8,128)(2,1)S(1)} async-done(((bf16[4,384,768]{2,1,0:T(8,128)(2,1)}), bf16[4,384,768]{2,1,0:T(8,128)(2,1)S(1)}, u32[]{:S(2)}, u32[]{:S(2)}) %all-to-all-start.1) | async-done | bytes 2359328 | tf_op jit(solution)/shard_map/all_to_all | solution.py:393
  59.6 5.5 %collective-permute-start.1 = (bf16[16,96,768]{2,1,0:T(8,128)(2,1)S(1)}, bf16[16,96,768]{2,1,0:T(8,128)(2,1)}, u32[]{:S(2)}, u32[]{:S(2)}) collective-permute-start(bf16[16,96,768]{2,1,0:T(8,128)(2,1)S(1)} %bitcast.19), channel_id=1, source_target_pairs={{0,32},{32,0},{1,33},{33,1},{2,34},{34,2},{3,35},{35,3},{4,36},{36... | collective-permute-start | bytes 7077896 | tf_op jit(solution)/shard_map/ppermute | solution.py:368
  65.1 2.1 %broadcast_in_dim.13 = bf16[4,192,768]{2,1,0:T(8,128)(2,1)} broadcast(bf16[192,768]{1,0:T(8,128)(2,1)} %bitcast.22), dimensions={1,2} | broadcast | bytes 1474560 | tf_op jit(solution)/shard_map/broadcast_in_dim | solution.py:392
  67.2 4.3 %all-to-all-start.2 = ((bf16[4,192,768]{2,1,0:T(8,128)(2,1)}), bf16[4,192,768]{2,1,0:T(8,128)(2,1)}, u32[]{:S(2)}, u32[]{:S(2)}) async-start(bf16[4,192,768]{2,1,0:T(8,128)(2,1)} %broadcast_in_dim.13), calls=%async_computation.2 | async-start | bytes 2359296 | tf_op jit(solution)/shard_map/all_to_all | solution.py:393
  71.5 4.6 %collective-permute-start.2 = (bf16[72,384]{1,0:T(8,128)(2,1)S(1)}, bf16[72,384]{1,0:T(8,128)(2,1)S(1)}, u32[]{:S(2)}, u32[]{:S(2)}) collective-permute-start(bf16[72,384]{1,0:T(8,128)(2,1)S(1)} %dynamic-slice_bitcast_fusion.1), channel_id=1, source_target_pairs={{0,449},{1,448},{64,385},{65,384},{128,321},{129,320},{192,257},{1... | collective-permute-start | bytes 165896 | tf_op jit(solution)/shard_map/ppermute | solution.py:349
  77.2 1.7 prepare_rows.1
  78.9 3.1 %collective-permute-done.2 = bf16[72,384]{1,0:T(8,128)(2,1)S(1)} collective-permute-done((bf16[72,384]{1,0:T(8,128)(2,1)S(1)}, bf16[72,384]{1,0:T(8,128)(2,1)S(1)}, u32[]{:S(2)}, u32[]{:S(2)}) %collective-permute-start.2) | collective-permute-done | bytes 55328 | tf_op jit(solution)/shard_map/ppermute | solution.py:349
  82.0 6.8 %hidden_rows.1.normed = bf16[192,1536]{1,0:T(8,128)(2,1)S(1)} custom-call(s32[48]{0:T(128)S(1)} %get-tuple-element.34.table, bf16[192,1536]{1,0:T(8,128)(2,1)S(1)} %get-tuple-element.36.ctx, bf16[192,1536]{1,0:T(8,128)(2,1)S(1)} %get-tuple-element.37.res, bf16[16,96,768]{2,1,0:T(8,128)(2,1)S(1)} %bitcast.20, bf16[16,96,768]{2,1,0:T(8,128)(2,1)} %collective-permute-done.1.other), custom_call_target="tpu_custom_call" | custom-call | flops 900000000 | bytes 6000000 | tf_op jit(solution)/shard_map/hidden_rows/pallas_call | solution.py:152
  90.3 4.8 %all-to-all-start.3 = ((bf16[16,144,384]{2,1,0:T(8,128)(2,1)}), bf16[16,144,384]{2,1,0:T(8,128)(2,1)S(1)}, u32[]{:S(2)}, u32[]{:S(2)}) async-start(bf16[16,144,384]{2,1,0:T(8,128)(2,1)} %broadcast_in_dim.14), calls=%async_computation.3 | async-start | bytes 3538944 | tf_op jit(solution)/shard_map/all_to_all | solution.py:372
  95.1 2.6 %collective-permute-start.3 = (bf16[16,48,768]{2,1,0:T(8,128)(2,1)}, bf16[16,48,768]{2,1,0:T(8,128)(2,1)S(1)}, u32[]{:S(2)}, u32[]{:S(2)}) collective-permute-start(bf16[16,48,768]{2,1,0:T(8,128)(2,1)} %bitcast.8.own), channel_id=1, source_target_pairs={{0,32},{32,0},{1,33},{33,1},{2,34},{34,2},{3,35},{35,3},{4,36},{36... | collective-permute-start | bytes 3538952 | tf_op jit(solution)/shard_map/ppermute | solution.py:368
  97.7 2.7 %collective-permute-done.3.other = bf16[16,48,768]{2,1,0:T(8,128)(2,1)S(1)} collective-permute-done((bf16[16,48,768]{2,1,0:T(8,128)(2,1)}, bf16[16,48,768]{2,1,0:T(8,128)(2,1)S(1)}, u32[]{:S(2)}, u32[]{:S(2)}) %collective-permute-start.3) | collective-permute-done | bytes 1179680 | tf_op jit(solution)/shard_map/ppermute | solution.py:368
  100.4 4.1 %embed_rows.1 = (bf16[192,768]{1,0:T(8,128)(2,1)S(1)}, bf16[64,768]{1,0:T(8,128)(2,1)S(1)}, bf16[128,768]{1,0:T(8,128)(2,1)S(1)}) custom-call(s32[48]{0:T(128)S(1)} %get-tuple-element.34.table, bf16[192,1536]{1,0:T(8,128)(2,1)S(1)} %hidden_rows.1.normed, bf16[16,48,768]{2,1,0:T(8,128)(2,1)} %bitcast.8.own, bf16[16,48,768]{2,1,0:T(8,128)(2,1)S(1)} %collective-permute-done.3.other), custom_call_target="tpu_custom_call" | custom-call | flops 500000000 | bytes 3000000 | tf_op jit(solution)/shard_map/embed_rows/pallas_call | solution.py:166
  104.5 6.6 %collective-permute-start.4 = (bf16[64,768]{1,0:T(8,128)(2,1)S(1)}, bf16[64,768]{1,0:T(8,128)(2,1)S(1)}, u32[]{:S(2)}, u32[]{:S(2)}) collective-permute-start(bf16[64,768]{1,0:T(8,128)(2,1)S(1)} %get-tuple-element.43), channel_id=1, source_target_pairs={{0,256},{32,289},{64,320},{96,353},{128,384},{160,417},{192,448},{... | collective-permute-start | bytes 294920 | tf_op jit(solution)/shard_map/ppermute | solution.py:364
  111.1 4.5 %collective-permute-start.6 = (bf16[128,768]{1,0:T(8,128)(2,1)S(1)}, bf16[128,768]{1,0:T(8,128)(2,1)S(1)}, u32[]{:S(2)}, u32[]{:S(2)}) collective-permute-start(bf16[128,768]{1,0:T(8,128)(2,1)S(1)} %get-tuple-element.44), channel_id=1, source_target_pairs={{0,256},{32,289},{64,320},{96,353},{128,384},{160,417},{192,448},{... | collective-permute-start | bytes 589832 | tf_op jit(solution)/shard_map/ppermute | solution.py:364
  116.6 5.9 %collective-permute-start.5 = (bf16[64,768]{1,0:T(8,128)(2,1)S(1)}, bf16[64,768]{1,0:T(8,128)(2,1)S(1)}, u32[]{:S(2)}, u32[]{:S(2)}) collective-permute-start(bf16[64,768]{1,0:T(8,128)(2,1)S(1)} %collective-permute-done.4), channel_id=1, source_target_pairs={{0,256},{32,289},{64,320},{96,353},{128,384},{160,417},{192,448},{... | collective-permute-start | bytes 294920 | tf_op jit(solution)/shard_map/ppermute | solution.py:364
  122.5 7.8 %collective-permute-done.5.lower = bf16[64,768]{1,0:T(8,128)(2,1)S(1)} collective-permute-done((bf16[64,768]{1,0:T(8,128)(2,1)S(1)}, bf16[64,768]{1,0:T(8,128)(2,1)S(1)}, u32[]{:S(2)}, u32[]{:S(2)}) %collective-permute-start.5) | collective-permute-done | bytes 98336 | tf_op jit(solution)/shard_map/ppermute | solution.py:364
  130.3 1.9 %collective-permute-start.8 = (bf16[2304,384]{1,0:T(8,128)(2,1)S(1)}, bf16[2304,384]{1,0:T(8,128)(2,1)S(1)}, u32[]{:S(2)}, u32[]{:S(2)}) collective-permute-start(bf16[2304,384]{1,0:T(8,128)(2,1)S(1)} %bitcast.15), channel_id=1, source_target_pairs={{0,32},{32,0},{1,33},{33,1},{2,34},{34,2},{3,35},{35,3},{4,36},{36... | collective-permute-start | bytes 5308424 | tf_op jit(solution)/shard_map/ppermute | solution.py:368
  132.2 8.6 %collective-permute-start.7 = (bf16[128,768]{1,0:T(8,128)(2,1)S(1)}, bf16[128,768]{1,0:T(8,128)(2,1)S(1)}, u32[]{:S(2)}, u32[]{:S(2)}) collective-permute-start(bf16[128,768]{1,0:T(8,128)(2,1)S(1)} %collective-permute-done.6), channel_id=1, source_target_pairs={{0,256},{32,289},{64,320},{96,353},{128,384},{160,417},{192,448},{... | collective-permute-start | bytes 589832 | tf_op jit(solution)/shard_map/ppermute | solution.py:364
  140.8 7.4 %own_rows.1 = (bf16[16,128,128]{2,1,0:T(8,128)(2,1)S(1)}, bf16[768,192]{1,0:T(8,128)(2,1)S(1)}, bf16[1536,192]{1,0:T(8,128)(2,1)}, f32[768,192]{1,0:T(8,128)S(1)...) custom-call(s32[48]{0:T(128)S(1)} %get-tuple-element.34.table, bf16[192,768]{1,0:T(8,128)(2,1)S(1)} %get-tuple-element.47.own, ...), custom_call_target="tpu_custom_call" | custom-call | flops 1000000000 | bytes 5000000 | tf_op jit(solution)/shard_map/own_rows/pallas_call | solution.py:220
  148.7 3.5 %pair_rows.1 = (bf16[16,128,128]{2,1,0:T(8,128)(2,1)}, bf16[1536,64]{1,0:T(8,128)(2,1)S(1)}) custom-call(s32[48]{0:T(128)S(1)} %get-tuple-element.34.table, bf16[64,768]{1,0:T(8,128)(2,1)S(1)} %collective-permute-done.5.lower, bf16[128,768]{1,0:T(8,128)(2,1)S(1)} %collective-permute-done.7.upper, bf16[2304,384]{1,0:T(8,128)(2,1)S(1)} %bitcast.17, ...), custom_call_target="tpu_custom_call" | custom-call | flops 700000000 | bytes 4000000 | tf_op jit(solution)/shard_map/pair_rows/pallas_call | solution.py:241
  152.9 6.9 %all-to-all-start.4 = ((bf16[16,128,128]{2,1,0:T(8,128)(2,1)}), bf16[16,128,128]{2,1,0:T(8,128)(2,1)S(1)}, u32[]{:S(2)}, u32[]{:S(2)}) async-start(bf16[16,128,128]{2,1,0:T(8,128)(2,1)} %get-tuple-element.52), calls=%async_computation.4 | async-start | bytes 1048576 | tf_op jit(solution)/shard_map/all_to_all | solution.py:438
  161.1 3.5 %collective-permute-start.9 = (bf16[64,768]{1,0:T(8,128)(2,1)S(1)}, bf16[64,768]{1,0:T(8,128)(2,1)S(1)}, u32[]{:S(2)}, u32[]{:S(2)}) collective-permute-start(bf16[64,768]{1,0:T(8,128)(2,1)S(1)} %fusion), channel_id=1, source_target_pairs={{0,2},{2,4},{4,6},{6,8},{8,10},{10,12},{12,14},{14,16},{16,18},{18... | collective-permute-start | bytes 294920 | tf_op jit(solution)/shard_map/ppermute | solution.py:436
  164.6 2.4 %collective-permute-done.9.halo = bf16[64,768]{1,0:T(8,128)(2,1)S(1)} collective-permute-done((bf16[64,768]{1,0:T(8,128)(2,1)S(1)}, bf16[64,768]{1,0:T(8,128)(2,1)S(1)}, u32[]{:S(2)}, u32[]{:S(2)}) %collective-permute-start.9) | collective-permute-done | bytes 98336 | tf_op jit(solution)/shard_map/ppermute | solution.py:436
  167.0 3.2 %all-to-all-done.4.arrived = bf16[16,128,128]{2,1,0:T(8,128)(2,1)S(1)} async-done(((bf16[16,128,128]{2,1,0:T(8,128)(2,1)}), bf16[16,128,128]{2,1,0:T(8,128)(2,1)S(1)}, u32[]{:S(2)}, u32[]{:S(2)}) %all-to-all-start.4) | async-done | bytes 524320 | tf_op jit(solution)/shard_map/all_to_all | solution.py:438
  170.2 4.0 %far_branch.1 = bf16[16,48,128]{2,1,0:T(8,128)(2,1)} custom-call(s32[48]{0:T(128)S(1)} %get-tuple-element.34.table, bf16[16,128,128]{2,1,0:T(8,128)(2,1)S(1)} %all-to-all-done.4.arrived), custom_call_target="tpu_custom_call" | custom-call | flops 500000000 | bytes 1000000 | tf_op jit(solution)/shard_map/far_branch/pallas_call | solution.py:309
  174.3 5.0 %all-to-all-start.5 = ((bf16[16,48,128]{2,1,0:T(8,128)(2,1)}), bf16[16,48,128]{2,1,0:T(8,128)(2,1)S(1)}, u32[]{:S(2)}, u32[]{:S(2)}) async-start(bf16[16,48,128]{2,1,0:T(8,128)(2,1)} %far_branch.1), calls=%async_computation.5 | async-start | bytes 393216 | tf_op jit(solution)/shard_map/all_to_all | solution.py:443
  182.9 4.4 %rim_rows.1 = (f32[768,192]{1,0:T(8,128)S(1)}, f32[16,192]{1,0:T(8,128)S(1)}, f32[16,192]{1,0:T(8,128)S(1)}) custom-call(s32[48]{0:T(128)S(1)} %get-tuple-element.34.table, bf16[768,192]{1,0:T(8,128)(2,1)S(1)} %get-tuple-element.54.q, bf16[1536,64]{1,0:T(8,128)(2,1)S(1)} %copy-done.8, bf16[64,768]{1,0:T(8,128)(2,1)S(1)} %collective-permute-done.9.halo, ...), custom_call_target="tpu_custom_call" | custom-call | flops 400000000 | bytes 5000000 | tf_op jit(solution)/shard_map/rim_rows/pallas_call | solution.py:274
  187.3 2.0 %finish_rows.1 = bf16[1,192,768]{2,1,0:T(8,128)(2,1)} custom-call(s32[48]{0:T(128)S(1)} %get-tuple-element.34.table, bf16[16,48,128]{2,1,0:T(8,128)(2,1)S(1)} %all-to-all-done.5.answers, f32[768,192]{1,0:T(8,128)S(1)} %get-tuple-element.60.local_sum, f32[16,192]{1,0:T(8,128)S(1)} %get-tuple-element.61.local_best, ...), custom_call_target="tpu_custom_call" | custom-call | flops 100000000 | bytes 1500000 | tf_op jit(solution)/shard_map/finish_rows/pallas_call | solution.py:339
  (52 shorter events, 13.0 us)
Async XLA Ops:
  0.0 0.9 copy-start
  1.7 22.2 %collective-permute-start = (bf16[72,768]{1,0:T(8,128)(2,1)S(1)}, bf16[72,768]{1,0:T(8,128)(2,1)S(1)}, u32[]{:S(2)}, u32[]{:S(2)}) collective-permute-start(bf16[72,768]{1,0:T(8,128)(2,1)S(1)} %pad_maximum_fusion.1), channel_id=1, source_target_pairs={{0,449},{1,448},{64,385},{65,384},{128,321},{129,320},{192,257},{1... | collective-permute-start | bytes 331784 | tf_op jit(solution)/shard_map/ppermute | solution.py:349
  38.8 20.8 %all-to-all-start.1 = ((bf16[4,384,768]{2,1,0:T(8,128)(2,1)}), bf16[4,384,768]{2,1,0:T(8,128)(2,1)S(1)}, u32[]{:S(2)}, u32[]{:S(2)}) async-start(bf16[4,384,768]{2,1,0:T(8,128)(2,1)} %broadcast_in_dim.12), calls=%async_computation.1 | async-start | bytes 4718592 | tf_op jit(solution)/shard_map/all_to_all | solution.py:393
  59.5 11.9 %copy-start.12 = (bf16[768,72]{0,1:T(8,128)(2,1)S(1)}, bf16[768,72]{0,1:T(8,128)(2,1)}, u32[]{:S(2)}) copy-start(bf16[768,72]{0,1:T(8,128)(2,1)} %param.12) | copy-start | bytes 331780
  59.5 16.6 %copy-start.5 = (bf16[1,192,1536]{2,1,0:T(8,128)(2,1)S(1)}, bf16[1,192,1536]{2,1,0:T(8,128)(2,1)}, u32[]{:S(2)}) copy-start(bf16[1,192,1536]{2,1,0:T(8,128)(2,1)} %ctx.1) | copy-start | bytes 1769476
  59.6 16.6 %copy-start.9 = (s32[1,1,192]{2,1,0:T(1,128)S(1)}, s32[1,1,192]{2,1,0:T(1,128)}, u32[]{:S(2)}) copy-start(s32[1,1,192]{2,1,0:T(1,128)} %listing.3) | copy-start | bytes 2308
  59.6 16.6 %copy-start.10 = (s32[1,32]{1,0:T(1,128)S(1)}, s32[1,32]{1,0:T(1,128)}, u32[]{:S(2)}) copy-start(s32[1,32]{1,0:T(1,128)} %counts.1) | copy-start | bytes 388
  59.6 16.6 %copy-start.11 = (s32[1,2]{1,0:T(1,128)S(1)}, s32[1,2]{1,0:T(1,128)}, u32[]{:S(2)}) copy-start(s32[1,2]{1,0:T(1,128)} %dilation.1) | copy-start | bytes 28
  59.6 22.5 %collective-permute-start.1 = (bf16[16,96,768]{2,1,0:T(8,128)(2,1)S(1)}, bf16[16,96,768]{2,1,0:T(8,128)(2,1)}, u32[]{:S(2)}, u32[]{:S(2)}) collective-permute-start(bf16[16,96,768]{2,1,0:T(8,128)(2,1)S(1)} %bitcast.19), channel_id=1, source_target_pairs={{0,32},{32,0},{1,33},{33,1},{2,34},{34,2},{3,35},{35,3},{4,36},{36... | collective-permute-start | bytes 7077896 | tf_op jit(solution)/shard_map/ppermute | solution.py:368
  67.2 21.7 %all-to-all-start.2 = ((bf16[4,192,768]{2,1,0:T(8,128)(2,1)}), bf16[4,192,768]{2,1,0:T(8,128)(2,1)}, u32[]{:S(2)}, u32[]{:S(2)}) async-start(bf16[4,192,768]{2,1,0:T(8,128)(2,1)} %broadcast_in_dim.13), calls=%async_computation.2 | async-start | bytes 2359296 | tf_op jit(solution)/shard_map/all_to_all | solution.py:393
  71.5 10.5 %collective-permute-start.2 = (bf16[72,384]{1,0:T(8,128)(2,1)S(1)}, bf16[72,384]{1,0:T(8,128)(2,1)S(1)}, u32[]{:S(2)}, u32[]{:S(2)}) collective-permute-start(bf16[72,384]{1,0:T(8,128)(2,1)S(1)} %dynamic-slice_bitcast_fusion.1), channel_id=1, source_target_pairs={{0,449},{1,448},{64,385},{65,384},{128,321},{129,320},{192,257},{1... | collective-permute-start | bytes 165896 | tf_op jit(solution)/shard_map/ppermute | solution.py:349
  76.2 1.1 copy-start.6
  90.3 40.0 %all-to-all-start.3 = ((bf16[16,144,384]{2,1,0:T(8,128)(2,1)}), bf16[16,144,384]{2,1,0:T(8,128)(2,1)S(1)}, u32[]{:S(2)}, u32[]{:S(2)}) async-start(bf16[16,144,384]{2,1,0:T(8,128)(2,1)} %broadcast_in_dim.14), calls=%async_computation.3 | async-start | bytes 3538944 | tf_op jit(solution)/shard_map/all_to_all | solution.py:372
  95.1 5.3 %collective-permute-start.3 = (bf16[16,48,768]{2,1,0:T(8,128)(2,1)}, bf16[16,48,768]{2,1,0:T(8,128)(2,1)S(1)}, u32[]{:S(2)}, u32[]{:S(2)}) collective-permute-start(bf16[16,48,768]{2,1,0:T(8,128)(2,1)} %bitcast.8.own), channel_id=1, source_target_pairs={{0,32},{32,0},{1,33},{33,1},{2,34},{34,2},{3,35},{35,3},{4,36},{36... | collective-permute-start | bytes 3538952 | tf_op jit(solution)/shard_map/ppermute | solution.py:368
  104.5 12.0 %collective-permute-start.4 = (bf16[64,768]{1,0:T(8,128)(2,1)S(1)}, bf16[64,768]{1,0:T(8,128)(2,1)S(1)}, u32[]{:S(2)}, u32[]{:S(2)}) collective-permute-start(bf16[64,768]{1,0:T(8,128)(2,1)S(1)} %get-tuple-element.43), channel_id=1, source_target_pairs={{0,256},{32,289},{64,320},{96,353},{128,384},{160,417},{192,448},{... | collective-permute-start | bytes 294920 | tf_op jit(solution)/shard_map/ppermute | solution.py:364
  111.1 19.1 %collective-permute-start.6 = (bf16[128,768]{1,0:T(8,128)(2,1)S(1)}, bf16[128,768]{1,0:T(8,128)(2,1)S(1)}, u32[]{:S(2)}, u32[]{:S(2)}) collective-permute-start(bf16[128,768]{1,0:T(8,128)(2,1)S(1)} %get-tuple-element.44), channel_id=1, source_target_pairs={{0,256},{32,289},{64,320},{96,353},{128,384},{160,417},{192,448},{... | collective-permute-start | bytes 589832 | tf_op jit(solution)/shard_map/ppermute | solution.py:364
  116.6 13.7 %collective-permute-start.5 = (bf16[64,768]{1,0:T(8,128)(2,1)S(1)}, bf16[64,768]{1,0:T(8,128)(2,1)S(1)}, u32[]{:S(2)}, u32[]{:S(2)}) collective-permute-start(bf16[64,768]{1,0:T(8,128)(2,1)S(1)} %collective-permute-done.4), channel_id=1, source_target_pairs={{0,256},{32,289},{64,320},{96,353},{128,384},{160,417},{192,448},{... | collective-permute-start | bytes 294920 | tf_op jit(solution)/shard_map/ppermute | solution.py:364
  130.3 10.6 %collective-permute-start.8 = (bf16[2304,384]{1,0:T(8,128)(2,1)S(1)}, bf16[2304,384]{1,0:T(8,128)(2,1)S(1)}, u32[]{:S(2)}, u32[]{:S(2)}) collective-permute-start(bf16[2304,384]{1,0:T(8,128)(2,1)S(1)} %bitcast.15), channel_id=1, source_target_pairs={{0,32},{32,0},{1,33},{33,1},{2,34},{34,2},{3,35},{35,3},{4,36},{36... | collective-permute-start | bytes 5308424 | tf_op jit(solution)/shard_map/ppermute | solution.py:368
  132.2 16.5 %collective-permute-start.7 = (bf16[128,768]{1,0:T(8,128)(2,1)S(1)}, bf16[128,768]{1,0:T(8,128)(2,1)S(1)}, u32[]{:S(2)}, u32[]{:S(2)}) collective-permute-start(bf16[128,768]{1,0:T(8,128)(2,1)S(1)} %collective-permute-done.6), channel_id=1, source_target_pairs={{0,256},{32,289},{64,320},{96,353},{128,384},{160,417},{192,448},{... | collective-permute-start | bytes 589832 | tf_op jit(solution)/shard_map/ppermute | solution.py:364
  140.8 7.8 %copy-start.1 = (bf16[2304,384]{1,0:T(8,128)(2,1)}, bf16[2304,384]{1,0:T(8,128)(2,1)S(1)}, u32[]{:S(2)}) copy-start(bf16[2304,384]{1,0:T(8,128)(2,1)S(1)} %collective-permute-done.8.q_b) | copy-start | bytes 5308420
  148.3 3.9 %copy-start.3 = (f32[768,192]{1,0:T(8,128)}, f32[768,192]{1,0:T(8,128)S(1)}, u32[]{:S(2)}) copy-start(f32[768,192]{1,0:T(8,128)S(1)} %get-tuple-element.57.own_sum) | copy-start | bytes 1769476
  152.1 0.7 copy-start.7
  152.9 17.4 %all-to-all-start.4 = ((bf16[16,128,128]{2,1,0:T(8,128)(2,1)}), bf16[16,128,128]{2,1,0:T(8,128)(2,1)S(1)}, u32[]{:S(2)}, u32[]{:S(2)}) async-start(bf16[16,128,128]{2,1,0:T(8,128)(2,1)} %get-tuple-element.52), calls=%async_computation.4 | async-start | bytes 1048576 | tf_op jit(solution)/shard_map/all_to_all | solution.py:438
  161.1 5.9 %collective-permute-start.9 = (bf16[64,768]{1,0:T(8,128)(2,1)S(1)}, bf16[64,768]{1,0:T(8,128)(2,1)S(1)}, u32[]{:S(2)}, u32[]{:S(2)}) collective-permute-start(bf16[64,768]{1,0:T(8,128)(2,1)S(1)} %fusion), channel_id=1, source_target_pairs={{0,2},{2,4},{4,6},{6,8},{8,10},{10,12},{12,14},{14,16},{16,18},{18... | collective-permute-start | bytes 294920 | tf_op jit(solution)/shard_map/ppermute | solution.py:436
  174.3 13.0 %all-to-all-start.5 = ((bf16[16,48,128]{2,1,0:T(8,128)(2,1)}), bf16[16,48,128]{2,1,0:T(8,128)(2,1)S(1)}, u32[]{:S(2)}, u32[]{:S(2)}) async-start(bf16[16,48,128]{2,1,0:T(8,128)(2,1)} %far_branch.1), calls=%async_computation.5 | async-start | bytes 393216 | tf_op jit(solution)/shard_map/all_to_all | solution.py:443
  179.3 1.5 copy-start.2
  180.8 1.1 copy-start.4
  181.9 1.0 copy-start.8

commit v14 on v12

--- a/solution.py
+++ b/solution.py
@@ -144,8 +144,17 @@
     for load in p_loads:
         load.wait()
     out[...] = (dot_nt(normed[:, :D], p[0].reshape(D, D)) + dot_nt(normed[:, D:], p[1].reshape(D, D))).astype(BF16)
-    lower[...] = out[:CHUNK]
-    upper[...] = out[CHUNK:]
+    pass_first = jnp.where(table[HIGH] == 0, 0, table[COUNT_ME] - CHUNK)
+    pick = (iota((CHUNK, TILE_DEV), 1) == iota((CHUNK, TILE_DEV), 0) + pass_first).astype(BF16)
+    lower[...] = dot_nn(pick, out[...]).astype(BF16)
+
+    @pl.when(table[HIGH] == 0)
+    def _():
+        upper[...] = out[CHUNK:]
+
+    @pl.when(table[HIGH] != 0)
+    def _():
+        upper[...] = out[: TILE_DEV - CHUNK]
 
 
 def embed(*args):
@@ -160,11 +169,14 @@
     return call(embed_kernel, "embed_rows", shapes, "svvhh-vvv", scratch, 1_400_000_000, 9_000_000)(*args)
 
 
-def key_picks(table, h, first, count):
+def key_picks(table, h, first, block_rows):
     rate, base = table[RATE], table[PAIR_START]
-    lane = iota((KEY_SLOTS, TILE_DEV), 1)
     place = iota((KEY_SLOTS, TILE_DEV), 0) * rate + ((h - base) & (rate - 1)) + (base - first)
-    return ((lane == place) & (lane < count)).astype(BF16)
+    return (block_rows == place).astype(BF16)
+
+
+def live_rows(rows, lane, count):
+    return jnp.where(lane < count, rows, -SEQ_LEN)
 
 
 def key_rows(kv, h):
@@ -189,8 +201,10 @@
     slot = iota((SLOTS, TILE_DEV), 0) * rate
     lane = iota((SLOTS, TILE_DEV), 1)
     rest = jnp.zeros((LANES - HEAD_DIM, TILE_DEV), BF16)
+    wide_lane = iota((KEY_SLOTS, TILE_DEV), 1)
+    block_rows = live_rows(wide_lane, wide_lane, count_me)
     for h in range(HEADS):
-        payload[h, :KEY_SLOTS] = dot_nt(key_picks(table, h, start_me, count_me), key_rows(kv_out, h)).astype(BF16)
+        payload[h, :KEY_SLOTS] = dot_nt(key_picks(table, h, start_me, block_rows), key_rows(kv_out, h)).astype(BF16)
         pick = (lane == slot + ((h - start_me) & (rate - 1))).astype(BF16)
         ask = jnp.concatenate([q_out[head_rows(h)], rest], axis=0)
         payload[h, KEY_SLOTS:] = dot_nt(pick, ask).astype(BF16)
@@ -219,12 +233,16 @@
     partner[CHUNK:] = upper[...]
     first, second = halves(table, partner, D // 2)
     kv[...] = (dot_nt(q_a[D:], first) + dot_nt(q_b[D:], second)).astype(BF16)
+    count, upward = table[COUNT_OTHER], table[HIGH] == 0
+    lane = iota((KEY_SLOTS, TILE_DEV), 1)
+    turned = jnp.where(lane < CHUNK, lane + (count - CHUNK), lane - CHUNK)
+    block_rows = live_rows(jnp.where(upward, turned, lane), lane, count)
     for h in range(HEADS):
-        picks = key_picks(table, h, table[START_OTHER], table[COUNT_OTHER])
+        picks = key_picks(table, h, table[START_OTHER], block_rows)
         both = dot_nt(picks, key_rows(kv, h)) + own_payload[h, :KEY_SLOTS].astype(F32)
         payload[h, :KEY_SLOTS] = both.astype(BF16)
         payload[h, KEY_SLOTS:] = own_payload[h, KEY_SLOTS:]
-    rim_first = jnp.where(table[HIGH] == 0, 0, table[COUNT_OTHER] - HALF)
+    rim_first = jnp.where(upward, CHUNK, count - HALF)
     pick = (iota((TILE_DEV, HALF), 0) == iota((TILE_DEV, HALF), 1) + rim_first).astype(BF16)
     rim[...] = dot_nn(kv[...], pick).astype(BF16)
 
@@ -418,14 +436,12 @@
     q_b = other_core(q_a)
     upper = along_z(upper, 1)
     own_payload, q_rows, _, own_sum, own_best, own_total = own_rows(table, embedded, q_a, q_b)
-    upper, own_payload = hold(upper, own_payload)
-    rim_from = jnp.where(high == 0, table[COUNT_OTHER] - HALF, 0)
-    rim = lax.dynamic_slice_in_dim(jnp.concatenate([lower, upper]), rim_from, HALF, 0)
     halo_pairs = [(p * 2, p * 2 + 2) for p in range(PLANES - 1)]
     halo_pairs += [(p * 2 + 1, p * 2 - 1) for p in range(1, PLANES)]
-    halo = lax.ppermute(rim, SEQ, halo_pairs)
+    halo = lax.ppermute(lower, SEQ, halo_pairs)
+    upper, own_payload, halo = hold(upper, own_payload, halo)
     payload, near_rim = pair_rows(table, lower, upper, q_a, q_b, own_payload)
-    arrived, halo = hold(lax.all_to_all(payload, PLANE, 0, 0), halo)
+    arrived = lax.all_to_all(payload, PLANE, 0, 0)
     local_sum, local_best, local_total = rim_rows(
         table, q_rows, near_rim, halo, q_a, q_b, own_sum, own_best, own_total
     )

time: 173 us -> 170 us (0.983)
  blocking collectives: 13.1 us -> 30.3 us
  waiting for transfers between devices: 51.9 us -> 42.9 us
  starting transfers between devices: 66.3 us -> 58.6 us
  local copies, waits for them, and re-layouts: 10.4 us -> 8.11 us
    all_to_all x0 -> x1, blocking collectives: none -> 17.2 us  [on_device(): arrived = lax.all_to_all(payload, PLANE, 0, 0)]
    all_to_all x1 -> x0, starting transfers between devices: 5.9 us -> none  [on_device(): arrived, halo = hold(lax.all_to_all(payload, PLANE, 0, 0), halo)]
    all_to_all x1 -> x0, waiting for transfers between devices: 3.98 us -> none  [on_device(): arrived, halo = hold(lax.all_to_all(payload, PLANE, 0, 0), halo)]
    ppermute x1, waiting for transfers between devices: 3.46 us -> 0.01 us  [on_device(): halo = lax.ppermute(lower, SEQ, halo_pairs)]
  transfers between devices with their start and end apart: 13 -> 12, of which waited for: 9 -> 7; matrix products, arithmetic and copies ran while one was open for 0% -> 0% of each run, Pallas kernels for 12% -> 12%
where the time goes in v14:
time: 170 us; the launch traced here: 169 us
  starting transfers between devices  58.6 us (34%)
  waiting for transfers between devices  42.9 us (25%)
  blocking collectives  30.3 us (18%)
  Pallas kernels  28.9 us (17%)
  local copies, waits for them, and re-layouts  8.11 us (5%)
    ppermute x4, starting transfers between devices, along_z(): return lax.ppermute(x, ('zlo', 'core', 'zhi'), pairs)  19.2 us
    all_to_all x1, blocking collectives, on_device(): arrived = lax.all_to_all(payload, PLANE, 0, 0)  17.2 us
    ppermute x2, waiting for transfers between devices, mirrored(): return lax.ppermute(x, ('zlo', 'zhi'), pairs)  15.9 us
    all_to_all x1, waiting for transfers between devices, along_lines(): return lax.all_to_all(spread, EVERY, 0, 0, axis_index_groups=groups)  15.5 us
    ppermute x2, starting transfers between devices, mirrored(): return lax.ppermute(x, ('zlo', 'zhi'), pairs)  14 us
    all_to_all x1, blocking collectives, along_lines(): return lax.all_to_all(spread, EVERY, 0, 0, axis_index_groups=groups)  13.1 us
    ppermute x2, starting transfers between devices, other_core(): return lax.ppermute(x, 'core', [(0, 1), (1, 0)])  10.9 us
    pallas_call x1, Pallas kernels, own_rows(): call(own_kernel, 'own_rows', shapes, 'svvv-vvvvvv', [], 1000000000, 50000...  7.4 us
  transfers between devices with their start and end apart: 12, of which 7 were waited for; matrix products, arithmetic and copies ran while one was open for 0% of the time, Pallas kernels for 12%

profile of v14, /device:TPU:1, one launch (start us, length us, event | category | flops | bytes accessed | tf_op | source)
XLA Modules:
  0.0 169.3 jit_solution(5001686679820885519)
XLA Ops:
  0.9 12.0 %collective-permute-start = (bf16[72,768]{1,0:T(8,128)(2,1)S(1)}, bf16[72,768]{1,0:T(8,128)(2,1)S(1)}, u32[]{:S(2)}, u32[]{:S(2)}) collective-permute-start(bf16[72,768]{1,0:T(8,128)(2,1)S(1)} %pad_maximum_fusion.1), channel_id=1, source_target_pairs={{0,449},{1,448},{64,385},{65,384},{128,321},{129,320},{192,257},{1... | collective-permute-start | bytes 331784 | tf_op jit(solution)/shard_map/ppermute | solution.py:361
  12.9 10.2 %collective-permute-done = bf16[72,768]{1,0:T(8,128)(2,1)S(1)} collective-permute-done((bf16[72,768]{1,0:T(8,128)(2,1)S(1)}, bf16[72,768]{1,0:T(8,128)(2,1)S(1)}, u32[]{:S(2)}, u32[]{:S(2)}) %collective-permute-start) | collective-permute-done | bytes 110624 | tf_op jit(solution)/shard_map/ppermute | solution.py:361
  23.3 13.1 %all_to_all.25 = bf16[4,144,768]{2,1,0:T(8,128)(2,1)S(1)} all-to-all(bf16[4,144,768]{2,1,0:T(8,128)(2,1)S(1)} %broadcast_in_dim.8), channel_id=1, replica_groups={{0,2,4,6},{8,10,12,14},{16,18,20,22},{24,26,28,30},{1,3,5,7},{9,11,13,1..., dimensions={0} | all-to-all | bytes 1769472 | tf_op jit(solution)/shard_map/all_to_all | solution.py:405
  36.4 2.0 %broadcast_in_dim.10 = bf16[4,576,768]{2,1,0:T(8,128)(2,1)} broadcast(bf16[576,768]{1,0:T(8,128)(2,1)S(1)} %bitcast.16), dimensions={1,2} | broadcast | bytes 4423680 | tf_op jit(solution)/shard_map/broadcast_in_dim | solution.py:404
  38.4 4.9 %all-to-all-start.1 = ((bf16[4,576,768]{2,1,0:T(8,128)(2,1)}), bf16[4,576,768]{2,1,0:T(8,128)(2,1)}, u32[]{:S(2)}, u32[]{:S(2)}) async-start(bf16[4,576,768]{2,1,0:T(8,128)(2,1)} %broadcast_in_dim.10), calls=%async_computation.1 | async-start | bytes 7077888 | tf_op jit(solution)/shard_map/all_to_all | solution.py:405
  43.4 2.1 %collective-permute-start.1 = (bf16[72,384]{1,0:T(8,128)(2,1)S(1)}, bf16[72,384]{1,0:T(8,128)(2,1)S(1)}, u32[]{:S(2)}, u32[]{:S(2)}) collective-permute-start(bf16[72,384]{1,0:T(8,128)(2,1)S(1)} %dynamic-slice_bitcast_fusion.1), channel_id=1, source_target_pairs={{0,449},{1,448},{64,385},{65,384},{128,321},{129,320},{192,257},{1... | collective-permute-start | bytes 165896 | tf_op jit(solution)/shard_map/ppermute | solution.py:361
  45.5 5.8 %collective-permute-done.1 = bf16[72,384]{1,0:T(8,128)(2,1)S(1)} collective-permute-done((bf16[72,384]{1,0:T(8,128)(2,1)S(1)}, bf16[72,384]{1,0:T(8,128)(2,1)S(1)}, u32[]{:S(2)}, u32[]{:S(2)}) %collective-permute-start.1) | collective-permute-done | bytes 55328 | tf_op jit(solution)/shard_map/ppermute | solution.py:361
  51.2 15.5 %all-to-all-done.1 = bf16[4,576,768]{2,1,0:T(8,128)(2,1)} async-done(((bf16[4,576,768]{2,1,0:T(8,128)(2,1)}), bf16[4,576,768]{2,1,0:T(8,128)(2,1)}, u32[]{:S(2)}, u32[]{:S(2)}) %all-to-all-start.1) | async-done | bytes 3538976 | tf_op jit(solution)/shard_map/all_to_all | solution.py:405
  66.8 1.4 broadcast_in_dim.22
  68.2 4.6 %collective-permute-start.2 = (bf16[16,144,768]{2,1,0:T(8,128)(2,1)}, bf16[16,144,768]{2,1,0:T(8,128)(2,1)}, u32[]{:S(2)}, u32[]{:S(2)}) collective-permute-start(bf16[16,144,768]{2,1,0:T(8,128)(2,1)} %bitcast.6.own), channel_id=1, source_target_pairs={{0,32},{32,0},{1,33},{33,1},{2,34},{34,2},{3,35},{35,3},{4,36},{36... | collective-permute-start | bytes 10616840 | tf_op jit(solution)/shard_map/ppermute | solution.py:380
  72.8 3.7 %all-to-all-start.2 = ((bf16[16,144,384]{2,1,0:T(8,128)(2,1)}), bf16[16,144,384]{2,1,0:T(8,128)(2,1)S(1)}, u32[]{:S(2)}, u32[]{:S(2)}) async-start(bf16[16,144,384]{2,1,0:T(8,128)(2,1)} %broadcast_in_dim.22), calls=%async_computation.2 | async-start | bytes 3538944 | tf_op jit(solution)/shard_map/all_to_all | solution.py:384
  76.7 1.6 prepare_rows.1
  79.0 6.7 %embed_rows.1 = (bf16[192,768]{1,0:T(8,128)(2,1)S(1)}, bf16[64,768]{1,0:T(8,128)(2,1)S(1)}, bf16[128,768]{1,0:T(8,128)(2,1)S(1)}) custom-call(s32[48]{0:T(128)S(1)} %get-tuple-element.30.table, bf16[192,1536]{1,0:T(8,128)(2,1)S(1)} %get-tuple-element.32.ctx, bf16[192,1536]{1,0:T(8,128)(2,1)S(1)} %get-tuple-element.33.res, bf16[16,144,768]{2,1,0:T(8,128)(2,1)} %bitcast.6.own, ...), custom_call_target="tpu_custom_call" | custom-call | flops 1400000000 | bytes 9000000 | tf_op jit(solution)/shard_map/embed_rows/pallas_call | solution.py:169
  85.7 4.4 %collective-permute-start.3 = (bf16[64,768]{1,0:T(8,128)(2,1)S(1)}, bf16[64,768]{1,0:T(8,128)(2,1)S(1)}, u32[]{:S(2)}, u32[]{:S(2)}) collective-permute-start(bf16[64,768]{1,0:T(8,128)(2,1)S(1)} %get-tuple-element.36), channel_id=1, source_target_pairs={{0,256},{32,289},{64,320},{96,353},{128,384},{160,417},{192,448},{... | collective-permute-start | bytes 294920 | tf_op jit(solution)/shard_map/ppermute | solution.py:376
  90.1 6.7 %collective-permute-start.5 = (bf16[128,768]{1,0:T(8,128)(2,1)S(1)}, bf16[128,768]{1,0:T(8,128)(2,1)S(1)}, u32[]{:S(2)}, u32[]{:S(2)}) collective-permute-start(bf16[128,768]{1,0:T(8,128)(2,1)S(1)} %get-tuple-element.37), channel_id=1, source_target_pairs={{0,256},{32,289},{64,320},{96,353},{128,384},{160,417},{192,448},{... | collective-permute-start | bytes 589832 | tf_op jit(solution)/shard_map/ppermute | solution.py:376
  96.8 2.9 %collective-permute-start.4 = (bf16[64,768]{1,0:T(8,128)(2,1)S(1)}, bf16[64,768]{1,0:T(8,128)(2,1)S(1)}, u32[]{:S(2)}, u32[]{:S(2)}) collective-permute-start(bf16[64,768]{1,0:T(8,128)(2,1)S(1)} %collective-permute-done.3), channel_id=1, source_target_pairs={{0,256},{32,289},{64,320},{96,353},{128,384},{160,417},{192,448},{... | collective-permute-start | bytes 294920 | tf_op jit(solution)/shard_map/ppermute | solution.py:376
  99.6 6.2 %all-to-all-done.2 = bf16[16,144,384]{2,1,0:T(8,128)(2,1)S(1)} async-done(((bf16[16,144,384]{2,1,0:T(8,128)(2,1)}), bf16[16,144,384]{2,1,0:T(8,128)(2,1)S(1)}, u32[]{:S(2)}, u32[]{:S(2)}) %all-to-all-start.2) | async-done | bytes 1769504 | tf_op jit(solution)/shard_map/all_to_all | solution.py:384
  105.9 3.3 %collective-permute-done.4.lower = bf16[64,768]{1,0:T(8,128)(2,1)S(1)} collective-permute-done((bf16[64,768]{1,0:T(8,128)(2,1)S(1)}, bf16[64,768]{1,0:T(8,128)(2,1)S(1)}, u32[]{:S(2)}, u32[]{:S(2)}) %collective-permute-start.4) | collective-permute-done | bytes 98336 | tf_op jit(solution)/shard_map/ppermute | solution.py:376
  109.1 6.3 %collective-permute-start.7 = (bf16[2304,384]{1,0:T(8,128)(2,1)S(1)}, bf16[2304,384]{1,0:T(8,128)(2,1)S(1)}, u32[]{:S(2)}, u32[]{:S(2)}) collective-permute-start(bf16[2304,384]{1,0:T(8,128)(2,1)S(1)} %bitcast.12), channel_id=1, source_target_pairs={{0,32},{32,0},{1,33},{33,1},{2,34},{34,2},{3,35},{35,3},{4,36},{36... | collective-permute-start | bytes 5308424 | tf_op jit(solution)/shard_map/ppermute | solution.py:380
  115.4 5.3 %collective-permute-start.6 = (bf16[128,768]{1,0:T(8,128)(2,1)S(1)}, bf16[128,768]{1,0:T(8,128)(2,1)S(1)}, u32[]{:S(2)}, u32[]{:S(2)}) collective-permute-start(bf16[128,768]{1,0:T(8,128)(2,1)S(1)} %collective-permute-done.5), channel_id=1, source_target_pairs={{0,256},{32,289},{64,320},{96,353},{128,384},{160,417},{192,448},{... | collective-permute-start | bytes 589832 | tf_op jit(solution)/shard_map/ppermute | solution.py:376
  120.7 2.3 %collective-permute-start.8 = (bf16[64,768]{1,0:T(8,128)(2,1)S(1)}, bf16[64,768]{1,0:T(8,128)(2,1)S(1)}, u32[]{:S(2)}, u32[]{:S(2)}) collective-permute-start(bf16[64,768]{1,0:T(8,128)(2,1)S(1)} %collective-permute-done.4.lower), channel_id=1, source_target_pairs={{0,2},{2,4},{4,6},{6,8},{8,10},{10,12},{12,14},{14,16},{16,18},{18... | collective-permute-start | bytes 294920 | tf_op jit(solution)/shard_map/ppermute | solution.py:441
  123.1 7.4 %own_rows.1 = (bf16[16,128,128]{2,1,0:T(8,128)(2,1)S(1)}, bf16[768,192]{1,0:T(8,128)(2,1)S(1)}, bf16[1536,192]{1,0:T(8,128)(2,1)}, f32[768,192]{1,0:T(8,128)S(1)...) custom-call(s32[48]{0:T(128)S(1)} %get-tuple-element.30.table, bf16[192,768]{1,0:T(8,128)(2,1)S(1)} %get-tuple-element.40.own, ...), custom_call_target="tpu_custom_call" | custom-call | flops 1000000000 | bytes 5000000 | tf_op jit(solution)/shard_map/own_rows/pallas_call | solution.py:228
  130.5 1.3 collective-permute-done.6.upper
  131.8 2.7 %pair_rows.1 = (bf16[16,128,128]{2,1,0:T(8,128)(2,1)S(1)}, bf16[1536,64]{1,0:T(8,128)(2,1)S(1)}) custom-call(s32[48]{0:T(128)S(1)} %get-tuple-element.30.table, bf16[64,768]{1,0:T(8,128)(2,1)S(1)} %collective-permute-done.4.lower, bf16[128,768]{1,0:T(8,128)(2,1)S(1)} %collective-permute-done.6.upper, bf16[2304,384]{1,0:T(8,128)(2,1)S(1)} %bitcast.14, ...), custom_call_target="tpu_custom_call" | custom-call | flops 700000000 | bytes 4000000 | tf_op jit(solution)/shard_map/pair_rows/pallas_call | solution.py:253
  134.6 17.2 %all_to_all.26.arrived = bf16[16,128,128]{2,1,0:T(8,128)(2,1)S(1)} all-to-all(bf16[16,128,128]{2,1,0:T(8,128)(2,1)S(1)} %get-tuple-element.45), channel_id=1, replica_groups=mesh['zlo'=8,'core'=2,'y'=4,'x'=4,'zhi'=2] {'y','x'}, dimensions={0} | all-to-all | bytes 1048576 | tf_op jit(solution)/shard_map/all_to_all | solution.py:444
  151.8 4.0 %far_branch.1 = bf16[16,48,128]{2,1,0:T(8,128)(2,1)} custom-call(s32[48]{0:T(128)S(1)} %get-tuple-element.30.table, bf16[16,128,128]{2,1,0:T(8,128)(2,1)S(1)} %all_to_all.26.arrived), custom_call_target="tpu_custom_call" | custom-call | flops 500000000 | bytes 1000000 | tf_op jit(solution)/shard_map/far_branch/pallas_call | solution.py:321
  155.8 3.5 %all-to-all-start.4 = ((bf16[16,48,128]{2,1,0:T(8,128)(2,1)}), bf16[16,48,128]{2,1,0:T(8,128)(2,1)S(1)}, u32[]{:S(2)}, u32[]{:S(2)}) async-start(bf16[16,48,128]{2,1,0:T(8,128)(2,1)} %far_branch.1), calls=%async_computation.4 | async-start | bytes 393216 | tf_op jit(solution)/shard_map/all_to_all | solution.py:449
  159.3 1.5 copy-done.2
  160.8 1.1 copy-done.4
  161.9 1.0 copy-done.8
  162.9 4.4 %rim_rows.1 = (f32[768,192]{1,0:T(8,128)S(1)}, f32[16,192]{1,0:T(8,128)S(1)}, f32[16,192]{1,0:T(8,128)S(1)}) custom-call(s32[48]{0:T(128)S(1)} %get-tuple-element.30.table, bf16[768,192]{1,0:T(8,128)(2,1)S(1)} %get-tuple-element.46.q, bf16[1536,64]{1,0:T(8,128)(2,1)S(1)} %copy-done.8, bf16[64,768]{1,0:T(8,128)(2,1)S(1)} %collective-permute-done.8.halo, ...), custom_call_target="tpu_custom_call" | custom-call | flops 400000000 | bytes 5000000 | tf_op jit(solution)/shard_map/rim_rows/pallas_call | solution.py:286
  167.3 2.0 %finish_rows.1 = bf16[1,192,768]{2,1,0:T(8,128)(2,1)} custom-call(s32[48]{0:T(128)S(1)} %get-tuple-element.30.table, bf16[16,48,128]{2,1,0:T(8,128)(2,1)S(1)} %all-to-all-done.4.answers, f32[768,192]{1,0:T(8,128)S(1)} %get-tuple-element.52.local_sum, f32[16,192]{1,0:T(8,128)S(1)} %get-tuple-element.53.local_best, ...), custom_call_target="tpu_custom_call" | custom-call | flops 100000000 | bytes 1500000 | tf_op jit(solution)/shard_map/finish_rows/pallas_call | solution.py:351
  (41 shorter events, 1.9 us)
Async XLA Ops:
  0.0 0.9 copy-start
  0.9 22.2 %collective-permute-start = (bf16[72,768]{1,0:T(8,128)(2,1)S(1)}, bf16[72,768]{1,0:T(8,128)(2,1)S(1)}, u32[]{:S(2)}, u32[]{:S(2)}) collective-permute-start(bf16[72,768]{1,0:T(8,128)(2,1)S(1)} %pad_maximum_fusion.1), channel_id=1, source_target_pairs={{0,449},{1,448},{64,385},{65,384},{128,321},{129,320},{192,257},{1... | collective-permute-start | bytes 331784 | tf_op jit(solution)/shard_map/ppermute | solution.py:361
  38.4 4.9 %copy-start.12 = (bf16[768,72]{0,1:T(8,128)(2,1)S(1)}, bf16[768,72]{0,1:T(8,128)(2,1)}, u32[]{:S(2)}) copy-start(bf16[768,72]{0,1:T(8,128)(2,1)} %param.12) | copy-start | bytes 331780
  38.4 28.3 %all-to-all-start.1 = ((bf16[4,576,768]{2,1,0:T(8,128)(2,1)}), bf16[4,576,768]{2,1,0:T(8,128)(2,1)}, u32[]{:S(2)}, u32[]{:S(2)}) async-start(bf16[4,576,768]{2,1,0:T(8,128)(2,1)} %broadcast_in_dim.10), calls=%async_computation.1 | async-start | bytes 7077888 | tf_op jit(solution)/shard_map/all_to_all | solution.py:405
  43.3 33.3 %copy-start.5 = (bf16[1,192,1536]{2,1,0:T(8,128)(2,1)S(1)}, bf16[1,192,1536]{2,1,0:T(8,128)(2,1)}, u32[]{:S(2)}) copy-start(bf16[1,192,1536]{2,1,0:T(8,128)(2,1)} %ctx.1) | copy-start | bytes 1769476
  43.3 33.3 %copy-start.6 = (bf16[1,192,1536]{2,1,0:T(8,128)(2,1)S(1)}, bf16[1,192,1536]{2,1,0:T(8,128)(2,1)}, u32[]{:S(2)}) copy-start(bf16[1,192,1536]{2,1,0:T(8,128)(2,1)} %res.1) | copy-start | bytes 1769476
  43.3 33.3 %copy-start.9 = (s32[1,1,192]{2,1,0:T(1,128)S(1)}, s32[1,1,192]{2,1,0:T(1,128)}, u32[]{:S(2)}) copy-start(s32[1,1,192]{2,1,0:T(1,128)} %listing.3) | copy-start | bytes 2308
  43.4 33.3 %copy-start.10 = (s32[1,32]{1,0:T(1,128)S(1)}, s32[1,32]{1,0:T(1,128)}, u32[]{:S(2)}) copy-start(s32[1,32]{1,0:T(1,128)} %counts.1) | copy-start | bytes 388
  43.4 33.3 %copy-start.11 = (s32[1,2]{1,0:T(1,128)S(1)}, s32[1,2]{1,0:T(1,128)}, u32[]{:S(2)}) copy-start(s32[1,2]{1,0:T(1,128)} %dilation.1) | copy-start | bytes 28
  43.4 7.8 %collective-permute-start.1 = (bf16[72,384]{1,0:T(8,128)(2,1)S(1)}, bf16[72,384]{1,0:T(8,128)(2,1)S(1)}, u32[]{:S(2)}, u32[]{:S(2)}) collective-permute-start(bf16[72,384]{1,0:T(8,128)(2,1)S(1)} %dynamic-slice_bitcast_fusion.1), channel_id=1, source_target_pairs={{0,449},{1,448},{64,385},{65,384},{128,321},{129,320},{192,257},{1... | collective-permute-start | bytes 165896 | tf_op jit(solution)/shard_map/ppermute | solution.py:361
  68.2 10.8 %collective-permute-start.2 = (bf16[16,144,768]{2,1,0:T(8,128)(2,1)}, bf16[16,144,768]{2,1,0:T(8,128)(2,1)}, u32[]{:S(2)}, u32[]{:S(2)}) collective-permute-start(bf16[16,144,768]{2,1,0:T(8,128)(2,1)} %bitcast.6.own), channel_id=1, source_target_pairs={{0,32},{32,0},{1,33},{33,1},{2,34},{34,2},{3,35},{35,3},{4,36},{36... | collective-permute-start | bytes 10616840 | tf_op jit(solution)/shard_map/ppermute | solution.py:380
  72.8 33.1 %all-to-all-start.2 = ((bf16[16,144,384]{2,1,0:T(8,128)(2,1)}), bf16[16,144,384]{2,1,0:T(8,128)(2,1)S(1)}, u32[]{:S(2)}, u32[]{:S(2)}) async-start(bf16[16,144,384]{2,1,0:T(8,128)(2,1)} %broadcast_in_dim.22), calls=%async_computation.2 | async-start | bytes 3538944 | tf_op jit(solution)/shard_map/all_to_all | solution.py:384
  85.7 11.1 %collective-permute-start.3 = (bf16[64,768]{1,0:T(8,128)(2,1)S(1)}, bf16[64,768]{1,0:T(8,128)(2,1)S(1)}, u32[]{:S(2)}, u32[]{:S(2)}) collective-permute-start(bf16[64,768]{1,0:T(8,128)(2,1)S(1)} %get-tuple-element.36), channel_id=1, source_target_pairs={{0,256},{32,289},{64,320},{96,353},{128,384},{160,417},{192,448},{... | collective-permute-start | bytes 294920 | tf_op jit(solution)/shard_map/ppermute | solution.py:376
  90.1 19.1 %collective-permute-start.5 = (bf16[128,768]{1,0:T(8,128)(2,1)S(1)}, bf16[128,768]{1,0:T(8,128)(2,1)S(1)}, u32[]{:S(2)}, u32[]{:S(2)}) collective-permute-start(bf16[128,768]{1,0:T(8,128)(2,1)S(1)} %get-tuple-element.37), channel_id=1, source_target_pairs={{0,256},{32,289},{64,320},{96,353},{128,384},{160,417},{192,448},{... | collective-permute-start | bytes 589832 | tf_op jit(solution)/shard_map/ppermute | solution.py:376
  96.8 12.3 %collective-permute-start.4 = (bf16[64,768]{1,0:T(8,128)(2,1)S(1)}, bf16[64,768]{1,0:T(8,128)(2,1)S(1)}, u32[]{:S(2)}, u32[]{:S(2)}) collective-permute-start(bf16[64,768]{1,0:T(8,128)(2,1)S(1)} %collective-permute-done.3), channel_id=1, source_target_pairs={{0,256},{32,289},{64,320},{96,353},{128,384},{160,417},{192,448},{... | collective-permute-start | bytes 294920 | tf_op jit(solution)/shard_map/ppermute | solution.py:376
  109.1 13.9 %collective-permute-start.7 = (bf16[2304,384]{1,0:T(8,128)(2,1)S(1)}, bf16[2304,384]{1,0:T(8,128)(2,1)S(1)}, u32[]{:S(2)}, u32[]{:S(2)}) collective-permute-start(bf16[2304,384]{1,0:T(8,128)(2,1)S(1)} %bitcast.12), channel_id=1, source_target_pairs={{0,32},{32,0},{1,33},{33,1},{2,34},{34,2},{3,35},{35,3},{4,36},{36... | collective-permute-start | bytes 5308424 | tf_op jit(solution)/shard_map/ppermute | solution.py:380
  115.4 16.4 %collective-permute-start.6 = (bf16[128,768]{1,0:T(8,128)(2,1)S(1)}, bf16[128,768]{1,0:T(8,128)(2,1)S(1)}, u32[]{:S(2)}, u32[]{:S(2)}) collective-permute-start(bf16[128,768]{1,0:T(8,128)(2,1)S(1)} %collective-permute-done.5), channel_id=1, source_target_pairs={{0,256},{32,289},{64,320},{96,353},{128,384},{160,417},{192,448},{... | collective-permute-start | bytes 589832 | tf_op jit(solution)/shard_map/ppermute | solution.py:376
  120.7 9.8 %collective-permute-start.8 = (bf16[64,768]{1,0:T(8,128)(2,1)S(1)}, bf16[64,768]{1,0:T(8,128)(2,1)S(1)}, u32[]{:S(2)}, u32[]{:S(2)}) collective-permute-start(bf16[64,768]{1,0:T(8,128)(2,1)S(1)} %collective-permute-done.4.lower), channel_id=1, source_target_pairs={{0,2},{2,4},{4,6},{6,8},{8,10},{10,12},{12,14},{14,16},{16,18},{18... | collective-permute-start | bytes 294920 | tf_op jit(solution)/shard_map/ppermute | solution.py:441
  123.1 11.5 %copy-start.1 = (bf16[2304,384]{1,0:T(8,128)(2,1)}, bf16[2304,384]{1,0:T(8,128)(2,1)S(1)}, u32[]{:S(2)}) copy-start(bf16[2304,384]{1,0:T(8,128)(2,1)S(1)} %collective-permute-done.7.q_b) | copy-start | bytes 5308420
  130.5 4.1 %copy-start.3 = (f32[768,192]{1,0:T(8,128)}, f32[768,192]{1,0:T(8,128)S(1)}, u32[]{:S(2)}) copy-start(f32[768,192]{1,0:T(8,128)S(1)} %get-tuple-element.49.own_sum) | copy-start | bytes 1769476
  134.6 17.2 %copy-start.7 = (bf16[1536,64]{1,0:T(8,128)(2,1)}, bf16[1536,64]{1,0:T(8,128)(2,1)S(1)}, u32[]{:S(2)}) copy-start(bf16[1536,64]{1,0:T(8,128)(2,1)S(1)} %get-tuple-element.47.near_rim) | copy-start | bytes 589828
  155.8 11.5 %all-to-all-start.4 = ((bf16[16,48,128]{2,1,0:T(8,128)(2,1)}), bf16[16,48,128]{2,1,0:T(8,128)(2,1)S(1)}, u32[]{:S(2)}, u32[]{:S(2)}) async-start(bf16[16,48,128]{2,1,0:T(8,128)(2,1)} %far_branch.1), calls=%async_computation.4 | async-start | bytes 393216 | tf_op jit(solution)/shard_map/all_to_all | solution.py:449
  159.3 1.5 copy-start.2
  160.8 1.1 copy-start.4
  161.9 1.0 copy-start.8

commit v15 on v14

--- a/solution.py
+++ b/solution.py
@@ -228,7 +228,7 @@
     return call(own_kernel, "own_rows", shapes, "svvv-vvvvvv", [], 1_000_000_000, 5_000_000, 600_000)(*args)
 
 
-def pair_kernel(table, lower, upper, q_a, q_b, own_payload, payload, rim, kv, partner):
+def pair_kernel(table, lower, upper, halo, q_a, q_b, own_payload, payload, rim, far_rim, kv, partner):
     partner[:CHUNK] = lower[...]
     partner[CHUNK:] = upper[...]
     first, second = halves(table, partner, D // 2)
@@ -245,18 +245,19 @@
     rim_first = jnp.where(upward, CHUNK, count - HALF)
     pick = (iota((TILE_DEV, HALF), 0) == iota((TILE_DEV, HALF), 1) + rim_first).astype(BF16)
     rim[...] = dot_nn(kv[...], pick).astype(BF16)
-
-
-def pair_rows(*args):
-    shapes = (((HEADS, KEY_SLOTS + SLOTS, LANES), BF16), ((2 * D, HALF), BF16))
-    scratch = [pltpu.VMEM((2 * D, TILE_DEV), BF16), pltpu.VMEM((TILE_DEV, D), BF16)]
-    return call(pair_kernel, "pair_rows", shapes, "svvvvv-vv", scratch, 700_000_000, 4_000_000)(*args)
-
-
-def rim_kernel(table, q, near_rim, halo, q_a, q_b, own_sum, own_best, own_total, out_sum, out_best, out_total, far_rim):
-    start_me, end_me = table[START_ME], table[START_ME] + table[COUNT_ME]
     first, second = halves(table, halo, D // 2)
     far_rim[...] = (dot_nt(q_a[D:], first) + dot_nt(q_b[D:], second)).astype(BF16)
+
+
+def pair_rows(*args):
+    rim = ((2 * D, HALF), BF16)
+    shapes = (((HEADS, KEY_SLOTS + SLOTS, LANES), BF16), rim, rim)
+    scratch = [pltpu.VMEM((2 * D, TILE_DEV), BF16), pltpu.VMEM((TILE_DEV, D), BF16)]
+    return call(pair_kernel, "pair_rows", shapes, "svvvvvv-vvv", scratch, 700_000_000, 4_000_000)(*args)
+
+
+def rim_kernel(table, q, near_rim, far_rim, own_sum, own_best, own_total, out_sum, out_best, out_total):
+    start_me, end_me = table[START_ME], table[START_ME] + table[COUNT_ME]
     query_seg = segments(table, start_me + iota((1, TILE_DEV), 1))
 
     def allowed(begin):
@@ -282,8 +283,7 @@
 def rim_rows(*args):
     stat = ((HEADS, TILE_DEV), F32)
     shapes = (((D, TILE_DEV), F32), stat, stat)
-    scratch = [pltpu.VMEM((2 * D, HALF), BF16)]
-    return call(rim_kernel, "rim_rows", shapes, "svvvvvvvv-vvv", scratch, 400_000_000, 5_000_000, 400_000)(*args)
+    return call(rim_kernel, "rim_rows", shapes, "svvvvvv-vvv", [], 200_000_000, 2_500_000, 400_000)(*args)
 
 
 def far_kernel(table, arrived, answer, scores):
@@ -440,10 +440,10 @@
     halo_pairs += [(p * 2 + 1, p * 2 - 1) for p in range(1, PLANES)]
     halo = lax.ppermute(lower, SEQ, halo_pairs)
     upper, own_payload, halo = hold(upper, own_payload, halo)
-    payload, near_rim = pair_rows(table, lower, upper, q_a, q_b, own_payload)
+    payload, near_rim, far_rim = pair_rows(table, lower, upper, halo, q_a, q_b, own_payload)
     arrived = lax.all_to_all(payload, PLANE, 0, 0)
     local_sum, local_best, local_total = rim_rows(
-        table, q_rows, near_rim, halo, q_a, q_b, own_sum, own_best, own_total
+        table, q_rows, near_rim, far_rim, own_sum, own_best, own_total
     )
     answer = far_branch(table, arrived)
     answers = lax.all_to_all(answer, PLANE, 0, 0)

time: 170 us -> 172 us (1.012)
  waiting for transfers between devices: 42.9 us -> 45.8 us
    all_to_all x1, waiting for transfers between devices: 0.01 us -> 2.84 us  [on_device(): answers = lax.all_to_all(answer, PLANE, 0, 0)]
    unnamed x26 -> x22, local copies, waits for them, and re-layouts: 3.76 us -> 2.04 us
  transfers between devices with their start and end apart: 12 -> 12, of which waited for: 7 -> 8; matrix products, arithmetic and copies ran while one was open for 0% -> 0% of each run, Pallas kernels for 12% -> 11%
where the time goes in v15:
time: 172 us; the launch traced here: 171 us
  starting transfers between devices  58.8 us (34%)
  waiting for transfers between devices  45.8 us (27%)
  blocking collectives  30.2 us (18%)
  Pallas kernels  29.7 us (17%)
  local copies, waits for them, and re-layouts  6.4 us (4%)
    ppermute x4, starting transfers between devices, along_z(): return lax.ppermute(x, ('zlo', 'core', 'zhi'), pairs)  19.2 us
    all_to_all x1, blocking collectives, on_device(): arrived = lax.all_to_all(payload, PLANE, 0, 0)  17.1 us
    ppermute x2, waiting for transfers between devices, mirrored(): return lax.ppermute(x, ('zlo', 'zhi'), pairs)  15.9 us
    all_to_all x1, waiting for transfers between devices, along_lines(): return lax.all_to_all(spread, EVERY, 0, 0, axis_index_groups=groups)  15.5 us
    ppermute x2, starting transfers between devices, mirrored(): return lax.ppermute(x, ('zlo', 'zhi'), pairs)  14 us
    all_to_all x1, blocking collectives, along_lines(): return lax.all_to_all(spread, EVERY, 0, 0, axis_index_groups=groups)  13.1 us
    ppermute x2, starting transfers between devices, other_core(): return lax.ppermute(x, 'core', [(0, 1), (1, 0)])  10.9 us
    pallas_call x1, Pallas kernels, own_rows(): call(own_kernel, 'own_rows', shapes, 'svvv-vvvvvv', [], 1000000000, 50000...  7.42 us
  transfers between devices with their start and end apart: 12, of which 8 were waited for; matrix products, arithmetic and copies ran while one was open for 0% of the time, Pallas kernels for 11%

profile of v15, /device:TPU:1, one launch (start us, length us, event | category | flops | bytes accessed | tf_op | source)
XLA Modules:
  0.0 171.3 jit_solution(3213157684961572659)
XLA Ops:
  0.9 12.0 %collective-permute-start = (bf16[72,768]{1,0:T(8,128)(2,1)S(1)}, bf16[72,768]{1,0:T(8,128)(2,1)S(1)}, u32[]{:S(2)}, u32[]{:S(2)}) collective-permute-start(bf16[72,768]{1,0:T(8,128)(2,1)S(1)} %pad_maximum_fusion.1), channel_id=1, source_target_pairs={{0,449},{1,448},{64,385},{65,384},{128,321},{129,320},{192,257},{1... | collective-permute-start | bytes 331784 | tf_op jit(solution)/shard_map/ppermute | solution.py:361
  12.9 10.2 %collective-permute-done = bf16[72,768]{1,0:T(8,128)(2,1)S(1)} collective-permute-done((bf16[72,768]{1,0:T(8,128)(2,1)S(1)}, bf16[72,768]{1,0:T(8,128)(2,1)S(1)}, u32[]{:S(2)}, u32[]{:S(2)}) %collective-permute-start) | collective-permute-done | bytes 110624 | tf_op jit(solution)/shard_map/ppermute | solution.py:361
  23.3 13.1 %all_to_all.25 = bf16[4,144,768]{2,1,0:T(8,128)(2,1)S(1)} all-to-all(bf16[4,144,768]{2,1,0:T(8,128)(2,1)S(1)} %broadcast_in_dim.8), channel_id=1, replica_groups={{0,2,4,6},{8,10,12,14},{16,18,20,22},{24,26,28,30},{1,3,5,7},{9,11,13,1..., dimensions={0} | all-to-all | bytes 1769472 | tf_op jit(solution)/shard_map/all_to_all | solution.py:405
  36.4 2.0 %broadcast_in_dim.10 = bf16[4,576,768]{2,1,0:T(8,128)(2,1)} broadcast(bf16[576,768]{1,0:T(8,128)(2,1)S(1)} %bitcast.15), dimensions={1,2} | broadcast | bytes 4423680 | tf_op jit(solution)/shard_map/broadcast_in_dim | solution.py:404
  38.4 4.9 %all-to-all-start.1 = ((bf16[4,576,768]{2,1,0:T(8,128)(2,1)}), bf16[4,576,768]{2,1,0:T(8,128)(2,1)}, u32[]{:S(2)}, u32[]{:S(2)}) async-start(bf16[4,576,768]{2,1,0:T(8,128)(2,1)} %broadcast_in_dim.10), calls=%async_computation.1 | async-start | bytes 7077888 | tf_op jit(solution)/shard_map/all_to_all | solution.py:405
  43.4 2.1 %collective-permute-start.1 = (bf16[72,384]{1,0:T(8,128)(2,1)S(1)}, bf16[72,384]{1,0:T(8,128)(2,1)S(1)}, u32[]{:S(2)}, u32[]{:S(2)}) collective-permute-start(bf16[72,384]{1,0:T(8,128)(2,1)S(1)} %dynamic-slice_bitcast_fusion.1), channel_id=1, source_target_pairs={{0,449},{1,448},{64,385},{65,384},{128,321},{129,320},{192,257},{1... | collective-permute-start | bytes 165896 | tf_op jit(solution)/shard_map/ppermute | solution.py:361
  45.5 5.8 %collective-permute-done.1 = bf16[72,384]{1,0:T(8,128)(2,1)S(1)} collective-permute-done((bf16[72,384]{1,0:T(8,128)(2,1)S(1)}, bf16[72,384]{1,0:T(8,128)(2,1)S(1)}, u32[]{:S(2)}, u32[]{:S(2)}) %collective-permute-start.1) | collective-permute-done | bytes 55328 | tf_op jit(solution)/shard_map/ppermute | solution.py:361
  51.3 15.5 %all-to-all-done.1 = bf16[4,576,768]{2,1,0:T(8,128)(2,1)} async-done(((bf16[4,576,768]{2,1,0:T(8,128)(2,1)}), bf16[4,576,768]{2,1,0:T(8,128)(2,1)}, u32[]{:S(2)}, u32[]{:S(2)}) %all-to-all-start.1) | async-done | bytes 3538976 | tf_op jit(solution)/shard_map/all_to_all | solution.py:405
  66.8 1.4 broadcast_in_dim.22
  68.2 4.6 %collective-permute-start.2 = (bf16[16,144,768]{2,1,0:T(8,128)(2,1)}, bf16[16,144,768]{2,1,0:T(8,128)(2,1)}, u32[]{:S(2)}, u32[]{:S(2)}) collective-permute-start(bf16[16,144,768]{2,1,0:T(8,128)(2,1)} %bitcast.6.own), channel_id=1, source_target_pairs={{0,32},{32,0},{1,33},{33,1},{2,34},{34,2},{3,35},{35,3},{4,36},{36... | collective-permute-start | bytes 10616840 | tf_op jit(solution)/shard_map/ppermute | solution.py:380
  72.8 3.7 %all-to-all-start.2 = ((bf16[16,144,384]{2,1,0:T(8,128)(2,1)}), bf16[16,144,384]{2,1,0:T(8,128)(2,1)S(1)}, u32[]{:S(2)}, u32[]{:S(2)}) async-start(bf16[16,144,384]{2,1,0:T(8,128)(2,1)} %broadcast_in_dim.22), calls=%async_computation.2 | async-start | bytes 3538944 | tf_op jit(solution)/shard_map/all_to_all | solution.py:384
  76.7 1.6 prepare_rows.1
  79.0 6.7 %embed_rows.1 = (bf16[192,768]{1,0:T(8,128)(2,1)S(1)}, bf16[64,768]{1,0:T(8,128)(2,1)S(1)}, bf16[128,768]{1,0:T(8,128)(2,1)S(1)}) custom-call(s32[48]{0:T(128)S(1)} %get-tuple-element.31.table, bf16[192,1536]{1,0:T(8,128)(2,1)S(1)} %get-tuple-element.33.ctx, bf16[192,1536]{1,0:T(8,128)(2,1)S(1)} %get-tuple-element.34.res, bf16[16,144,768]{2,1,0:T(8,128)(2,1)} %bitcast.6.own, ...), custom_call_target="tpu_custom_call" | custom-call | flops 1400000000 | bytes 9000000 | tf_op jit(solution)/shard_map/embed_rows/pallas_call | solution.py:169
  85.7 4.4 %collective-permute-start.3 = (bf16[64,768]{1,0:T(8,128)(2,1)S(1)}, bf16[64,768]{1,0:T(8,128)(2,1)S(1)}, u32[]{:S(2)}, u32[]{:S(2)}) collective-permute-start(bf16[64,768]{1,0:T(8,128)(2,1)S(1)} %get-tuple-element.37), channel_id=1, source_target_pairs={{0,256},{32,289},{64,320},{96,353},{128,384},{160,417},{192,448},{... | collective-permute-start | bytes 294920 | tf_op jit(solution)/shard_map/ppermute | solution.py:376
  90.1 6.7 %collective-permute-start.5 = (bf16[128,768]{1,0:T(8,128)(2,1)S(1)}, bf16[128,768]{1,0:T(8,128)(2,1)}, u32[]{:S(2)}, u32[]{:S(2)}) collective-permute-start(bf16[128,768]{1,0:T(8,128)(2,1)S(1)} %get-tuple-element.38), channel_id=1, source_target_pairs={{0,256},{32,289},{64,320},{96,353},{128,384},{160,417},{192,448},{... | collective-permute-start | bytes 589832 | tf_op jit(solution)/shard_map/ppermute | solution.py:376
  96.8 2.9 %collective-permute-start.4 = (bf16[64,768]{1,0:T(8,128)(2,1)S(1)}, bf16[64,768]{1,0:T(8,128)(2,1)S(1)}, u32[]{:S(2)}, u32[]{:S(2)}) collective-permute-start(bf16[64,768]{1,0:T(8,128)(2,1)S(1)} %collective-permute-done.3), channel_id=1, source_target_pairs={{0,256},{32,289},{64,320},{96,353},{128,384},{160,417},{192,448},{... | collective-permute-start | bytes 294920 | tf_op jit(solution)/shard_map/ppermute | solution.py:376
  99.7 6.2 %all-to-all-done.2 = bf16[16,144,384]{2,1,0:T(8,128)(2,1)S(1)} async-done(((bf16[16,144,384]{2,1,0:T(8,128)(2,1)}), bf16[16,144,384]{2,1,0:T(8,128)(2,1)S(1)}, u32[]{:S(2)}, u32[]{:S(2)}) %all-to-all-start.2) | async-done | bytes 1769504 | tf_op jit(solution)/shard_map/all_to_all | solution.py:384
  105.9 3.3 %collective-permute-done.4.lower = bf16[64,768]{1,0:T(8,128)(2,1)S(1)} collective-permute-done((bf16[64,768]{1,0:T(8,128)(2,1)S(1)}, bf16[64,768]{1,0:T(8,128)(2,1)S(1)}, u32[]{:S(2)}, u32[]{:S(2)}) %collective-permute-start.4) | collective-permute-done | bytes 98336 | tf_op jit(solution)/shard_map/ppermute | solution.py:376
  109.1 6.3 %collective-permute-start.7 = (bf16[2304,384]{1,0:T(8,128)(2,1)S(1)}, bf16[2304,384]{1,0:T(8,128)(2,1)S(1)}, u32[]{:S(2)}, u32[]{:S(2)}) collective-permute-start(bf16[2304,384]{1,0:T(8,128)(2,1)S(1)} %bitcast.12), channel_id=1, source_target_pairs={{0,32},{32,0},{1,33},{33,1},{2,34},{34,2},{3,35},{35,3},{4,36},{36... | collective-permute-start | bytes 5308424 | tf_op jit(solution)/shard_map/ppermute | solution.py:380
  115.4 5.3 %collective-permute-start.6 = (bf16[128,768]{1,0:T(8,128)(2,1)}, bf16[128,768]{1,0:T(8,128)(2,1)S(1)}, u32[]{:S(2)}, u32[]{:S(2)}) collective-permute-start(bf16[128,768]{1,0:T(8,128)(2,1)} %collective-permute-done.5), channel_id=1, source_target_pairs={{0,256},{32,289},{64,320},{96,353},{128,384},{160,417},{192,448},{... | collective-permute-start | bytes 589832 | tf_op jit(solution)/shard_map/ppermute | solution.py:376
  120.8 2.5 %collective-permute-start.8 = (bf16[64,768]{1,0:T(8,128)(2,1)S(1)}, bf16[64,768]{1,0:T(8,128)(2,1)S(1)}, u32[]{:S(2)}, u32[]{:S(2)}) collective-permute-start(bf16[64,768]{1,0:T(8,128)(2,1)S(1)} %collective-permute-done.4.lower), channel_id=1, source_target_pairs={{0,2},{2,4},{4,6},{6,8},{8,10},{10,12},{12,14},{14,16},{16,18},{18... | collective-permute-start | bytes 294920 | tf_op jit(solution)/shard_map/ppermute | solution.py:441
  123.3 7.4 %own_rows.1 = (bf16[16,128,128]{2,1,0:T(8,128)(2,1)S(1)}, bf16[768,192]{1,0:T(8,128)(2,1)S(1)}, bf16[1536,192]{1,0:T(8,128)(2,1)}, f32[768,192]{1,0:T(8,128)S(1)...) custom-call(s32[48]{0:T(128)S(1)} %get-tuple-element.31.table, bf16[192,768]{1,0:T(8,128)(2,1)S(1)} %get-tuple-element.41.own, ...), custom_call_target="tpu_custom_call" | custom-call | flops 1000000000 | bytes 5000000 | tf_op jit(solution)/shard_map/own_rows/pallas_call | solution.py:228
  130.7 1.3 collective-permute-done.6.upper
  132.0 0.9 copy-done.6
  132.9 4.2 %pair_rows.1 = (bf16[16,128,128]{2,1,0:T(8,128)(2,1)S(1)}, bf16[1536,64]{1,0:T(8,128)(2,1)S(1)}, bf16[1536,64]{1,0:T(8,128)(2,1)S(1)}) custom-call(s32[48]{0:T(128)S(1)} %get-tuple-element.31.table, bf16[64,768]{1,0:T(8,128)(2,1)S(1)} %copy-done.6, bf16[128,768]{1,0:T(8,128)(2,1)S(1)} %collective-permute-done.6.upper, ...), custom_call_target="tpu_custom_call" | custom-call | flops 700000000 | bytes 4000000 | tf_op jit(solution)/shard_map/pair_rows/pallas_call | solution.py:256
  137.1 17.1 %all_to_all.26.arrived = bf16[16,128,128]{2,1,0:T(8,128)(2,1)S(1)} all-to-all(bf16[16,128,128]{2,1,0:T(8,128)(2,1)S(1)} %get-tuple-element.47), channel_id=1, replica_groups=mesh['zlo'=8,'core'=2,'y'=4,'x'=4,'zhi'=2] {'y','x'}, dimensions={0} | all-to-all | bytes 1048576 | tf_op jit(solution)/shard_map/all_to_all | solution.py:444
  154.2 4.0 %far_branch.1 = bf16[16,48,128]{2,1,0:T(8,128)(2,1)} custom-call(s32[48]{0:T(128)S(1)} %get-tuple-element.31.table, bf16[16,128,128]{2,1,0:T(8,128)(2,1)S(1)} %all_to_all.26.arrived), custom_call_target="tpu_custom_call" | custom-call | flops 500000000 | bytes 1000000 | tf_op jit(solution)/shard_map/far_branch/pallas_call | solution.py:321
  158.2 3.5 %all-to-all-start.4 = ((bf16[16,48,128]{2,1,0:T(8,128)(2,1)}), bf16[16,48,128]{2,1,0:T(8,128)(2,1)S(1)}, u32[]{:S(2)}, u32[]{:S(2)}) async-start(bf16[16,48,128]{2,1,0:T(8,128)(2,1)} %far_branch.1), calls=%async_computation.4 | async-start | bytes 393216 | tf_op jit(solution)/shard_map/all_to_all | solution.py:449
  161.8 1.0 copy-done.4
  162.8 3.8 %rim_rows.1 = (f32[768,192]{1,0:T(8,128)S(1)}, f32[16,192]{1,0:T(8,128)S(1)}, f32[16,192]{1,0:T(8,128)S(1)}) custom-call(s32[48]{0:T(128)S(1)} %get-tuple-element.31.table, bf16[768,192]{1,0:T(8,128)(2,1)S(1)} %get-tuple-element.48.q, bf16[1536,64]{1,0:T(8,128)(2,1)S(1)} %get-tuple-element.49.near_rim, bf16[1536,64]{1,0:T(8,128)(2,1)S(1)} %copy-done.4, ...), custom_call_target="tpu_custom_call" | custom-call | flops 200000000 | bytes 2500000 | tf_op jit(solution)/shard_map/rim_rows/pallas_call | solution.py:286
  166.5 2.8 %all-to-all-done.4.answers = bf16[16,48,128]{2,1,0:T(8,128)(2,1)S(1)} async-done(((bf16[16,48,128]{2,1,0:T(8,128)(2,1)}), bf16[16,48,128]{2,1,0:T(8,128)(2,1)S(1)}, u32[]{:S(2)}, u32[]{:S(2)}) %all-to-all-start.4) | async-done | bytes 196640 | tf_op jit(solution)/shard_map/all_to_all | solution.py:449
  169.4 2.0 %finish_rows.1 = bf16[1,192,768]{2,1,0:T(8,128)(2,1)} custom-call(s32[48]{0:T(128)S(1)} %get-tuple-element.31.table, bf16[16,48,128]{2,1,0:T(8,128)(2,1)S(1)} %all-to-all-done.4.answers, f32[768,192]{1,0:T(8,128)S(1)} %get-tuple-element.54.local_sum, f32[16,192]{1,0:T(8,128)S(1)} %get-tuple-element.55.local_best, ...), custom_call_target="tpu_custom_call" | custom-call | flops 100000000 | bytes 1500000 | tf_op jit(solution)/shard_map/finish_rows/pallas_call | solution.py:351
  (37 shorter events, 1.9 us)
Async XLA Ops:
  0.0 0.9 copy-start
  0.9 22.2 %collective-permute-start = (bf16[72,768]{1,0:T(8,128)(2,1)S(1)}, bf16[72,768]{1,0:T(8,128)(2,1)S(1)}, u32[]{:S(2)}, u32[]{:S(2)}) collective-permute-start(bf16[72,768]{1,0:T(8,128)(2,1)S(1)} %pad_maximum_fusion.1), channel_id=1, source_target_pairs={{0,449},{1,448},{64,385},{65,384},{128,321},{129,320},{192,257},{1... | collective-permute-start | bytes 331784 | tf_op jit(solution)/shard_map/ppermute | solution.py:361
  38.4 4.9 %copy-start.10 = (bf16[768,72]{0,1:T(8,128)(2,1)S(1)}, bf16[768,72]{0,1:T(8,128)(2,1)}, u32[]{:S(2)}) copy-start(bf16[768,72]{0,1:T(8,128)(2,1)} %param.12) | copy-start | bytes 331780
  38.4 28.3 %all-to-all-start.1 = ((bf16[4,576,768]{2,1,0:T(8,128)(2,1)}), bf16[4,576,768]{2,1,0:T(8,128)(2,1)}, u32[]{:S(2)}, u32[]{:S(2)}) async-start(bf16[4,576,768]{2,1,0:T(8,128)(2,1)} %broadcast_in_dim.10), calls=%async_computation.1 | async-start | bytes 7077888 | tf_op jit(solution)/shard_map/all_to_all | solution.py:405
  43.3 33.3 %copy-start.1 = (bf16[1,192,1536]{2,1,0:T(8,128)(2,1)S(1)}, bf16[1,192,1536]{2,1,0:T(8,128)(2,1)}, u32[]{:S(2)}) copy-start(bf16[1,192,1536]{2,1,0:T(8,128)(2,1)} %ctx.1) | copy-start | bytes 1769476
  43.3 33.3 %copy-start.2 = (bf16[1,192,1536]{2,1,0:T(8,128)(2,1)S(1)}, bf16[1,192,1536]{2,1,0:T(8,128)(2,1)}, u32[]{:S(2)}) copy-start(bf16[1,192,1536]{2,1,0:T(8,128)(2,1)} %res.1) | copy-start | bytes 1769476
  43.3 33.3 %copy-start.7 = (s32[1,1,192]{2,1,0:T(1,128)S(1)}, s32[1,1,192]{2,1,0:T(1,128)}, u32[]{:S(2)}) copy-start(s32[1,1,192]{2,1,0:T(1,128)} %listing.3) | copy-start | bytes 2308
  43.4 33.3 %copy-start.8 = (s32[1,32]{1,0:T(1,128)S(1)}, s32[1,32]{1,0:T(1,128)}, u32[]{:S(2)}) copy-start(s32[1,32]{1,0:T(1,128)} %counts.1) | copy-start | bytes 388
  43.4 33.3 %copy-start.9 = (s32[1,2]{1,0:T(1,128)S(1)}, s32[1,2]{1,0:T(1,128)}, u32[]{:S(2)}) copy-start(s32[1,2]{1,0:T(1,128)} %dilation.1) | copy-start | bytes 28
  43.4 7.8 %collective-permute-start.1 = (bf16[72,384]{1,0:T(8,128)(2,1)S(1)}, bf16[72,384]{1,0:T(8,128)(2,1)S(1)}, u32[]{:S(2)}, u32[]{:S(2)}) collective-permute-start(bf16[72,384]{1,0:T(8,128)(2,1)S(1)} %dynamic-slice_bitcast_fusion.1), channel_id=1, source_target_pairs={{0,449},{1,448},{64,385},{65,384},{128,321},{129,320},{192,257},{1... | collective-permute-start | bytes 165896 | tf_op jit(solution)/shard_map/ppermute | solution.py:361
  68.2 10.8 %collective-permute-start.2 = (bf16[16,144,768]{2,1,0:T(8,128)(2,1)}, bf16[16,144,768]{2,1,0:T(8,128)(2,1)}, u32[]{:S(2)}, u32[]{:S(2)}) collective-permute-start(bf16[16,144,768]{2,1,0:T(8,128)(2,1)} %bitcast.6.own), channel_id=1, source_target_pairs={{0,32},{32,0},{1,33},{33,1},{2,34},{34,2},{3,35},{35,3},{4,36},{36... | collective-permute-start | bytes 10616840 | tf_op jit(solution)/shard_map/ppermute | solution.py:380
  72.8 33.1 %all-to-all-start.2 = ((bf16[16,144,384]{2,1,0:T(8,128)(2,1)}), bf16[16,144,384]{2,1,0:T(8,128)(2,1)S(1)}, u32[]{:S(2)}, u32[]{:S(2)}) async-start(bf16[16,144,384]{2,1,0:T(8,128)(2,1)} %broadcast_in_dim.22), calls=%async_computation.2 | async-start | bytes 3538944 | tf_op jit(solution)/shard_map/all_to_all | solution.py:384
  85.7 11.1 %collective-permute-start.3 = (bf16[64,768]{1,0:T(8,128)(2,1)S(1)}, bf16[64,768]{1,0:T(8,128)(2,1)S(1)}, u32[]{:S(2)}, u32[]{:S(2)}) collective-permute-start(bf16[64,768]{1,0:T(8,128)(2,1)S(1)} %get-tuple-element.37), channel_id=1, source_target_pairs={{0,256},{32,289},{64,320},{96,353},{128,384},{160,417},{192,448},{... | collective-permute-start | bytes 294920 | tf_op jit(solution)/shard_map/ppermute | solution.py:376
  90.1 19.1 %collective-permute-start.5 = (bf16[128,768]{1,0:T(8,128)(2,1)S(1)}, bf16[128,768]{1,0:T(8,128)(2,1)}, u32[]{:S(2)}, u32[]{:S(2)}) collective-permute-start(bf16[128,768]{1,0:T(8,128)(2,1)S(1)} %get-tuple-element.38), channel_id=1, source_target_pairs={{0,256},{32,289},{64,320},{96,353},{128,384},{160,417},{192,448},{... | collective-permute-start | bytes 589832 | tf_op jit(solution)/shard_map/ppermute | solution.py:376
  96.8 12.3 %collective-permute-start.4 = (bf16[64,768]{1,0:T(8,128)(2,1)S(1)}, bf16[64,768]{1,0:T(8,128)(2,1)S(1)}, u32[]{:S(2)}, u32[]{:S(2)}) collective-permute-start(bf16[64,768]{1,0:T(8,128)(2,1)S(1)} %collective-permute-done.3), channel_id=1, source_target_pairs={{0,256},{32,289},{64,320},{96,353},{128,384},{160,417},{192,448},{... | collective-permute-start | bytes 294920 | tf_op jit(solution)/shard_map/ppermute | solution.py:376
  109.1 22.9 %copy-start.5 = (bf16[64,768]{1,0:T(8,128)(2,1)}, bf16[64,768]{1,0:T(8,128)(2,1)S(1)}, u32[]{:S(2)}) copy-start(bf16[64,768]{1,0:T(8,128)(2,1)S(1)} %collective-permute-done.4.lower) | copy-start | bytes 294916
  109.1 14.1 %collective-permute-start.7 = (bf16[2304,384]{1,0:T(8,128)(2,1)S(1)}, bf16[2304,384]{1,0:T(8,128)(2,1)S(1)}, u32[]{:S(2)}, u32[]{:S(2)}) collective-permute-start(bf16[2304,384]{1,0:T(8,128)(2,1)S(1)} %bitcast.12), channel_id=1, source_target_pairs={{0,32},{32,0},{1,33},{33,1},{2,34},{34,2},{3,35},{35,3},{4,36},{36... | collective-permute-start | bytes 5308424 | tf_op jit(solution)/shard_map/ppermute | solution.py:380
  115.4 16.6 %collective-permute-start.6 = (bf16[128,768]{1,0:T(8,128)(2,1)}, bf16[128,768]{1,0:T(8,128)(2,1)S(1)}, u32[]{:S(2)}, u32[]{:S(2)}) collective-permute-start(bf16[128,768]{1,0:T(8,128)(2,1)} %collective-permute-done.5), channel_id=1, source_target_pairs={{0,256},{32,289},{64,320},{96,353},{128,384},{160,417},{192,448},{... | collective-permute-start | bytes 589832 | tf_op jit(solution)/shard_map/ppermute | solution.py:376
  120.8 9.9 %collective-permute-start.8 = (bf16[64,768]{1,0:T(8,128)(2,1)S(1)}, bf16[64,768]{1,0:T(8,128)(2,1)S(1)}, u32[]{:S(2)}, u32[]{:S(2)}) collective-permute-start(bf16[64,768]{1,0:T(8,128)(2,1)S(1)} %collective-permute-done.4.lower), channel_id=1, source_target_pairs={{0,2},{2,4},{4,6},{6,8},{8,10},{10,12},{12,14},{14,16},{16,18},{18... | collective-permute-start | bytes 294920 | tf_op jit(solution)/shard_map/ppermute | solution.py:441
  132.0 0.9 copy-start.6
  137.1 17.1 %copy-start.3 = (bf16[1536,64]{1,0:T(8,128)(2,1)}, bf16[1536,64]{1,0:T(8,128)(2,1)S(1)}, u32[]{:S(2)}) copy-start(bf16[1536,64]{1,0:T(8,128)(2,1)S(1)} %get-tuple-element.50.far_rim) | copy-start | bytes 589828
  158.2 11.1 %all-to-all-start.4 = ((bf16[16,48,128]{2,1,0:T(8,128)(2,1)}), bf16[16,48,128]{2,1,0:T(8,128)(2,1)S(1)}, u32[]{:S(2)}, u32[]{:S(2)}) async-start(bf16[16,48,128]{2,1,0:T(8,128)(2,1)} %far_branch.1), calls=%async_computation.4 | async-start | bytes 393216 | tf_op jit(solution)/shard_map/all_to_all | solution.py:449
  161.8 1.0 copy-start.4
